TPU v7x, 32 devices: a whole 2x2x4 slice. The times are simulated.
32 devices in a mesh: gx: 2 (over core), gy: 2 (over x), gz: 8 (over z, y).
Axes of the slice: x: 2, y: 2, z: 4, core: 2. Of those that a mesh axis runs over, the one named last changes fastest.
Arguments:
- a_diag: bfloat16 [8, 12, 64, 4096], P('gx', 'gy', 'gz'), may hold values from -0.75 to 0.75
- a_face: bfloat16 [3, 8, 12, 64, 4096], P(None, 'gx', 'gy', 'gz'), may hold values from -0.75 to 0.75
- prolong: bfloat16 [8, 12, 64, 4096], P('gx', 'gy', 'gz'), may hold values from -0.75 to 0.75
- aggregate: int32 [8, 12, 64], P('gx', 'gy', 'gz'), may hold values from 0 to 23
- pair_slot: int32 [7, 8, 12, 64], P(None, 'gx', 'gy', 'gz'), may hold values from 0 to 6
- row_owner: int32 [768], P(('gx', 'gy', 'gz')), may hold values from 0 to 7, as said below
Outputs:
- coarse: bfloat16 [2, 2, 8, 24, 7, 4096], P('gx', 'gy', 'gz')
Inputs may be any that keep to these rules, and one draw needn't show every extreme that they name: `row_owner`: all rows of a device go to owners in its own (gx, gy) column. From each device at most 3 rows go to one owner, and in each column one owner receives exactly 3 rows from every device, so at most 24 rows reach one owner.
All inputs are finite; a program needn't handle non-finite values.
Results may differ from a plain program's by a relative error of at most 0.0049.
Values may be sent and summed in bfloat16 or wider, within the bound.
No kernel may reach another device: no remote copies, remote signals or barrier semaphores. Data moves between devices by JAX's collectives and lax.ppermute only.
A program may use at most 256 MiB of HBM per device.

v0:
```python
import functools

import jax
import jax.numpy as jnp
from jax import lax
from jax.experimental import pallas as pl
from jax.experimental.pallas import tpu as pltpu
from jax.sharding import PartitionSpec as P

NODES = 64
SLOTS = 7
AGG_DEV = 24
LANES = 128
HALF = NODES // 2
VMEM_LIMIT = 50 * 1024 * 1024


def passed_along(block, axis, distance):
    devices = range(lax.axis_size(axis))
    route = [(i - distance, i) for i in devices if i - distance in devices]
    return lax.ppermute(block, axis, route)


def pick_rows(match, source_rows):
    count = match.shape[1]
    source = jnp.sum(match * jnp.arange(count, dtype=jnp.int32)[None, :], axis=1)
    present = jnp.sum(match, axis=1) > 0
    taken = jnp.take(source_rows, source, axis=0)
    return (jnp.where(present[:, None, None], taken, jnp.zeros_like(taken)), present)


def low_lanes(rows):
    return lax.broadcasted_iota(jnp.int32, (rows, LANES), 1) < NODES


def swapped(value):
    return pltpu.roll(value, NODES, 1)


def spread(column, stage):
    depth = column.shape[0]
    for k in range(column.shape[1] // LANES):
        stage[depth * k : depth * (k + 1), :] = column[:, LANES * k : LANES * (k + 1)].astype(jnp.float32)


def block_of(stage, z, depth):
    return stage[pl.ds(z, HALF, stride=depth), :]


def stacked_pair(first, second):
    low = low_lanes(HALF)
    even = jnp.where(low, first, swapped(second))
    odd = jnp.where(low, swapped(first), second)
    return jnp.concatenate([even, odd], axis=0).astype(jnp.bfloat16)


def in_order(pair):
    row = lax.broadcasted_iota(jnp.int32, (NODES, NODES), 0)
    col = lax.broadcasted_iota(jnp.int32, (NODES, NODES), 1)
    move = (row == 2 * (col % HALF) + col // HALF).astype(jnp.bfloat16)
    return jnp.dot(move, pair, preferred_element_type=jnp.float32).astype(jnp.bfloat16)


def paired_weights(pair):
    low = low_lanes(NODES)
    zero = jnp.zeros_like(pair)
    first = jnp.where(low, pair, zero)
    second = jnp.where(low, zero, pair)
    left = jnp.concatenate([first, zero, second, zero], axis=0)
    right = jnp.concatenate([zero, first, zero, second], axis=0)
    return jnp.concatenate([left, right], axis=1)


def upright(product):
    return jnp.concatenate([product[:, :LANES], product[:, LANES:]], axis=0).astype(jnp.bfloat16)


def across(left, right):
    return lax.dot_general(left, right, (((0,), (0,)), ((), ())), preferred_element_type=jnp.float32)


def folded(square):
    low = low_lanes(HALF)
    moved = swapped(jnp.where(low, square[HALF : 2 * HALF], square[2 * HALF : 3 * HALF]))
    return (jnp.where(low, square[:HALF], moved), jnp.where(low, moved, square[3 * HALF :]))


def add_to(total, key, value):
    total[key] = total[key] + value


def joined_transposes(left0, right0, left1, right1):
    low = low_lanes(NODES)
    one = across(left0, right0)
    two = across(left1, right1)
    same = jnp.where(low, one[:NODES], two[NODES:])
    other = jnp.where(low, two[:NODES], one[NODES:])
    return (same + swapped(other)).astype(jnp.bfloat16)


def prepare_kernel(p_ref, fx_ref, fy_ref, fz_ref, natural_ref, stacked_ref, shifted_ref, head_x_ref, head_y_ref, head_z_ref,
                   rim_x_ref, rim_y_ref, rim_z_ref, tail_x_ref, tail_y_ref, tail_z_ref, last_z_ref, stage_p, stage_f, first_z, ends_z):
    plane = pl.program_id(0)
    size_y, depth = p_ref.shape[0], p_ref.shape[1]
    pairs = depth // 2

    def tail(blocks, stage, put):
        spread(blocks, stage)
        for z in range(depth):
            put(z, block_of(stage, z, depth).astype(jnp.bfloat16))

    def column(j, carry):
        spread(p_ref[j], stage_p)
        block = [block_of(stage_p, z, depth) for z in range(depth)]
        for p in range(pairs):
            stacked = stacked_pair(block[2 * p], block[2 * p + 1])
            stacked_ref[j, p] = stacked
            natural_ref[j, p] = in_order(stacked)
            shifted_ref[j, p] = stacked_pair(block[(2 * p - 1) % depth], block[2 * p])
        first_z[j] = block[0]
        ends_z[j] = block[depth - 1]
        spread(fz_ref[0, j], stage_f)
        tail_z_ref[j] = block_of(stage_f, depth - 1, depth).astype(jnp.bfloat16)

        @pl.when(plane == pl.num_programs(0) - 1)
        def _():
            spread(fx_ref[0, j], stage_f)
            for p in range(pairs):
                left = [block_of(stage_f, z, depth).astype(jnp.bfloat16) for z in (2 * p, 2 * p + 1)]
                tail_x_ref[j, 2 * p] = left[0]
                tail_x_ref[j, 2 * p + 1] = left[1]
                rim_x_ref[j, p] = joined_transposes(
                    left[0], block[2 * p].astype(jnp.bfloat16), left[1], block[2 * p + 1].astype(jnp.bfloat16))

        return carry

    lax.fori_loop(0, size_y, column, 0)

    spread(fy_ref[0, 0], stage_f)
    block = [block_of(stage_p, z, depth).astype(jnp.bfloat16) for z in range(depth)]
    for p in range(pairs):
        left = [block_of(stage_f, z, depth).astype(jnp.bfloat16) for z in (2 * p, 2 * p + 1)]
        tail_y_ref[0, 2 * p] = left[0]
        tail_y_ref[0, 2 * p + 1] = left[1]
        rim_y_ref[0, p] = joined_transposes(left[0], block[2 * p], left[1], block[2 * p + 1])
    head_y_ref[0] = natural_ref[0]

    @pl.when(plane == 0)
    def _():
        head_x_ref[...] = natural_ref[...]

    for t in range(size_y // 2):
        head_z_ref[t] = in_order(stacked_pair(first_z[2 * t], first_z[2 * t + 1]))
        last_z_ref[t] = stacked_pair(ends_z[2 * t], ends_z[2 * t + 1])
        rim_z_ref[t] = joined_transposes(
            tail_z_ref[2 * t], ends_z[2 * t].astype(jnp.bfloat16),
            tail_z_ref[2 * t + 1], ends_z[2 * t + 1].astype(jnp.bfloat16))


def prepare(prolong, faces, sizes):
    size_x, size_y, depth = sizes
    pairs, block = depth // 2, prolong.shape[-1]
    columns, half = size_x * size_y, size_y // 2
    shape = lambda *dims: jax.ShapeDtypeStruct(dims, jnp.bfloat16)
    by_plane = pl.BlockSpec((size_y, pairs, NODES, LANES), lambda i: (i, 0, 0, 0))
    one_plane = pl.BlockSpec((size_y, pairs, NODES, LANES), lambda i: (0, 0, 0, 0))
    by_column = pl.BlockSpec((1, pairs, NODES, LANES), lambda i: (i, 0, 0, 0))
    by_half = pl.BlockSpec((half, NODES, LANES), lambda i: (i, 0, 0))
    all_pairs = shape(columns, pairs, NODES, LANES)
    return pl.pallas_call(
        prepare_kernel,
        grid=(size_x,),
        in_specs=[
            pl.BlockSpec((size_y, depth, block), lambda i: (i, 0, 0)),
            pl.BlockSpec((1, size_y, depth, block), lambda i: (0, size_x - 1, 0, 0)),
            pl.BlockSpec((1, 1, depth, block), lambda i: (1, i * size_y + size_y - 1, 0, 0)),
            pl.BlockSpec((1, size_y, depth, block), lambda i: (2, i, 0, 0)),
        ],
        out_specs=[
            by_plane, by_plane, by_plane, one_plane, by_column, by_half, one_plane, by_column, by_half,
            pl.BlockSpec((size_y, depth, HALF, LANES), lambda i: (0, 0, 0, 0)),
            pl.BlockSpec((1, depth, HALF, LANES), lambda i: (i, 0, 0, 0)),
            pl.BlockSpec((size_y, HALF, LANES), lambda i: (i, 0, 0)),
            by_half,
        ],
        out_shape=[
            all_pairs, all_pairs, all_pairs,
            shape(size_y, pairs, NODES, LANES), shape(size_x, pairs, NODES, LANES), shape(columns // 2, NODES, LANES),
            shape(size_y, pairs, NODES, LANES), shape(size_x, pairs, NODES, LANES), shape(columns // 2, NODES, LANES),
            shape(size_y, depth, HALF, LANES), shape(size_x, depth, HALF, LANES), shape(columns, HALF, LANES),
            shape(columns // 2, NODES, LANES),
        ],
        scratch_shapes=[
            pltpu.VMEM((depth * HALF, LANES), jnp.float32),
            pltpu.VMEM((depth * HALF, LANES), jnp.float32),
            pltpu.VMEM((size_y, HALF, LANES), jnp.float32),
            pltpu.VMEM((size_y, HALF, LANES), jnp.float32),
        ],
        compiler_params=pltpu.CompilerParams(vmem_limit_bytes=VMEM_LIMIT),
        name="prepare",
    )(prolong, faces, faces, faces)


def interior_kernel(keys, diag_ref, fx_ref, fy_ref, fz_ref, natural_ref, stacked_ref, shifted_ref, out_ref,
                    stages, forward_even, forward_odd, back_even, back_odd):
    plane = pl.program_id(0)
    size_y, depth = diag_ref.shape[0], diag_ref.shape[1]
    pairs = depth // 2
    spare = out_ref.shape[0]
    totals = (forward_even, forward_odd, back_even, back_odd)

    @pl.when(plane == 0)
    def _():
        for total in totals:
            total[...] = jnp.zeros_like(total)

    def column(j, carry):
        here = plane * size_y + j
        below_x = jnp.maximum(here - size_y, 0)
        below_y = jnp.maximum(here - 1, 0)
        row_y = jnp.maximum(j - 1, 0)
        has_x, has_y = plane > 0, j > 0
        for stage, source in zip(range(4), (diag_ref[j], fx_ref[0, j], fy_ref[0, row_y], fz_ref[0, j])):
            spread(source, stages.at[stage])
        for p in range(pairs):
            left = []
            for stage in range(4):
                shift = 1 if stage == 3 else 0
                sides = [block_of(stages.at[stage], (2 * p + side - shift) % depth, depth).astype(jnp.bfloat16) for side in (0, 1)]
                left.append(jnp.concatenate(sides, axis=1))
            product = jnp.dot(
                jnp.concatenate(left, axis=0), paired_weights(natural_ref[j, p]), preferred_element_type=jnp.float32)
            prolongs = (stacked_ref[here, p], stacked_ref[below_x, p], stacked_ref[below_y, p], shifted_ref[j, p])
            for face in range(4):
                couple = upright(product[HALF * face : HALF * (face + 1)])
                square = across(prolongs[face], couple)
                ahead = folded(square)
                for side in (0, 1):
                    z = 2 * p + side
                    if face == 0:
                        key = keys[0, plane, j, z]
                    elif face == 1:
                        key = jnp.where(has_x, keys[2, jnp.maximum(plane - 1, 0), j, z], spare)
                    elif face == 2:
                        key = jnp.where(has_y, keys[4, plane, row_y, z], spare)
                    else:
                        key = keys[6, plane, j, z - 1] if z > 0 else spare
                    add_to(totals[side], key, ahead[side])
                if face == 0:
                    continue
                behind = folded(across(couple, prolongs[face]))
                for side in (0, 1):
                    z = 2 * p + side
                    if face == 1:
                        key = jnp.where(has_x, keys[1, plane, j, z], spare)
                    elif face == 2:
                        key = jnp.where(has_y, keys[3, plane, j, z], spare)
                    else:
                        key = keys[5, plane, j, z] if z > 0 else spare
                    add_to(totals[2 + side], key, behind[side])
        return carry

    lax.fori_loop(0, size_y, column, 0)

    @pl.when(plane == pl.num_programs(0) - 1)
    def _():
        def gather(r, carry):
            for s in range(SLOTS):
                key = r * SLOTS + s
                out_ref[key] = (forward_even[key] + forward_odd[key]) + (back_even[key] + back_odd[key])
            return carry

        lax.fori_loop(0, spare // SLOTS, gather, 0)


def interior(keys, diag, faces, natural, stacked, shifted, sizes):
    size_x, size_y, depth = sizes
    pairs, block = depth // 2, diag.shape[-1]
    columns, rows = size_x * size_y, AGG_DEV * SLOTS
    by_plane = pl.BlockSpec((size_y, pairs, NODES, LANES), lambda i: (i, 0, 0, 0))
    total = pltpu.VMEM((rows + 1, HALF, LANES), jnp.float32)
    return pl.pallas_call(
        interior_kernel,
        grid=(size_x,),
        in_specs=[
            pl.BlockSpec(memory_space=pltpu.SMEM),
            pl.BlockSpec((size_y, depth, block), lambda i: (i, 0, 0)),
            pl.BlockSpec((1, size_y, depth, block), lambda i: (0, jnp.maximum(i - 1, 0), 0, 0)),
            pl.BlockSpec((1, size_y, depth, block), lambda i: (1, i, 0, 0)),
            pl.BlockSpec((1, size_y, depth, block), lambda i: (2, i, 0, 0)),
            by_plane,
            pl.BlockSpec((columns, pairs, NODES, LANES), lambda i: (0, 0, 0, 0)),
            by_plane,
        ],
        out_specs=pl.BlockSpec((rows, HALF, LANES), lambda i: (0, 0, 0)),
        out_shape=jax.ShapeDtypeStruct((rows, HALF, LANES), jnp.float32),
        scratch_shapes=[pltpu.VMEM((4, depth * HALF, LANES), jnp.float32), total, total, total, total],
        compiler_params=pltpu.CompilerParams(vmem_limit_bytes=VMEM_LIMIT),
        cost_estimate=pl.CostEstimate(flops=columns * depth * 14 * NODES**3, bytes_accessed=columns * depth * 6 * block * 2, transcendentals=0),
        name="interior",
    )(keys, diag, faces, faces, faces, natural, stacked, shifted)


def border_kernel(capacity, keys, owners, head_x, head_y, head_z, rim_x, rim_y, rim_z, tail_x, tail_y, tail_z,
                  natural, stacked, first_z, last_z, total_ref, out_ref, ahead_total, back_total, stage, filled):
    size_y, depth = tail_x.shape[0], tail_x.shape[1]
    size_x = tail_y.shape[0]
    pairs = depth // 2
    rows = total_ref.shape[0] // SLOTS
    places = out_ref.shape[0]

    ahead_total[...] = total_ref[...]
    back_total[...] = jnp.zeros_like(back_total)

    def ahead(left0, left1, head, prolong):
        product = jnp.dot(jnp.concatenate([left0, left1], axis=1), paired_weights(head), preferred_element_type=jnp.float32)
        return folded(across(prolong, upright(product)))

    def over_x(j, carry):
        for p in range(pairs):
            sums = ahead(tail_x[j, 2 * p], tail_x[j, 2 * p + 1], head_x[j, p], stacked[(size_x - 1) * size_y + j, p])
            back = folded(across(natural[j, p], rim_x[j, p]))
            for side in (0, 1):
                add_to(ahead_total, keys[2, size_x - 1, j, 2 * p + side], sums[side])
                add_to(back_total, keys[1, 0, j, 2 * p + side], back[side])
        return carry

    def over_y(i, carry):
        for p in range(pairs):
            sums = ahead(tail_y[i, 2 * p], tail_y[i, 2 * p + 1], head_y[i, p], stacked[i * size_y + size_y - 1, p])
            back = folded(across(natural[i * size_y, p], rim_y[i, p]))
            for side in (0, 1):
                add_to(ahead_total, keys[4, i, size_y - 1, 2 * p + side], sums[side])
                add_to(back_total, keys[3, i, 0, 2 * p + side], back[side])
        return carry

    def over_z(i, carry):
        for u in range(size_y // 2):
            t = i * (size_y // 2) + u
            sums = ahead(tail_z[2 * t], tail_z[2 * t + 1], head_z[t], last_z[t])
            back = folded(across(first_z[t], rim_z[t]))
            for side in (0, 1):
                add_to(ahead_total, keys[6, i, 2 * u + side, depth - 1], sums[side])
                add_to(back_total, keys[5, i, 2 * u + side, 0], back[side])
        return carry

    lax.fori_loop(0, size_y, over_x, 0)
    lax.fori_loop(0, size_x, over_y, 0)
    lax.fori_loop(0, size_x, over_z, 0)

    for owner in range(places // capacity):
        filled[owner] = 0
    if places != rows:
        out_ref[...] = jnp.zeros_like(out_ref)

    def emit(r, carry):
        low = low_lanes(HALF // 2)
        owner = owners[r]
        place = owner * capacity + filled[owner]
        filled[owner] = filled[owner] + 1
        for s in range(SLOTS):
            key = r * SLOTS + s
            ahead_total[key] = ahead_total[key] + back_total[key]
            even = ahead_total[key, pl.ds(0, HALF // 2, stride=2), :]
            odd = ahead_total[key, pl.ds(1, HALF // 2, stride=2), :]
            top = jnp.where(low, even, swapped(odd))
            bottom = jnp.where(low, swapped(even), odd)
            stage[pl.ds(s, HALF, stride=8), :] = jnp.concatenate([top, bottom], axis=0)
        for k in range(HALF):
            out_ref[place, :, LANES * k : LANES * (k + 1)] = stage[8 * k : 8 * k + SLOTS, :].astype(jnp.bfloat16)
        return carry

    lax.fori_loop(0, rows, emit, 0)


def border(keys, owners, operands, capacity, places, block):
    rows = AGG_DEV * SLOTS
    smem = pl.BlockSpec(memory_space=pltpu.SMEM)
    total = pltpu.VMEM((rows, HALF, LANES), jnp.float32)
    return pl.pallas_call(
        functools.partial(border_kernel, capacity),
        in_specs=[smem, smem] + [pl.BlockSpec(memory_space=pltpu.VMEM)] * len(operands),
        out_specs=pl.BlockSpec(memory_space=pltpu.VMEM),
        out_shape=jax.ShapeDtypeStruct((places, SLOTS, block), jnp.bfloat16),
        scratch_shapes=[total, total, pltpu.VMEM((8 * HALF, LANES), jnp.float32), pltpu.SMEM((places // capacity,), jnp.int32)],
        compiler_params=pltpu.CompilerParams(vmem_limit_bytes=VMEM_LIMIT),
        name="border",
    )(keys, owners, *operands)


def shards(a_diag, a_face, prolong, aggregate, pair_slot, row_owner):
    size_x, size_y, size_z, block = a_diag.shape
    sizes = (size_x, size_y, size_z)
    columns = size_x * size_y
    depth = lax.axis_size("gz")
    capacity = max(2, (AGG_DEV + depth - 1) // depth)
    holding = capacity * depth
    diag = a_diag.reshape(columns, size_z, block)
    faces = a_face.reshape(3, columns, size_z, block)
    keys = aggregate[None] * SLOTS + pair_slot

    (natural, stacked, shifted, head_x, head_y, head_z, rim_x, rim_y, rim_z, tail_x, tail_y, tail_z, last_z) = prepare(
        prolong.reshape(columns, size_z, block), faces, sizes)
    over_x = passed_along(head_x, "gx", -1)
    over_y = passed_along(head_y, "gy", -1)
    over_z = passed_along(head_z, "gz", -1)
    back_y = passed_along(rim_y, "gy", 1)
    back_z = passed_along(rim_z, "gz", 1)
    back_x = passed_along(rim_x, "gx", 1)
    inner = interior(keys, diag, faces, natural, stacked, shifted, sizes)
    outgoing = border(
        keys, row_owner,
        (over_x, over_y, over_z, back_x, back_y, back_z, tail_x, tail_y, tail_z, natural, stacked, head_z, last_z, inner),
        capacity, holding, block)
    result = lax.all_to_all(outgoing, "gz", 0, 0, tiled=True)
    if holding != AGG_DEV:
        owner_ids = jnp.arange(depth, dtype=jnp.int32)
        counts = jnp.sum((row_owner[:, None] == owner_ids[None, :]).astype(jnp.int32), axis=0)
        arrived_counts = lax.all_to_all(counts, "gz", 0, 0, tiled=True)
        slots = jnp.arange(holding, dtype=jnp.int32)
        arrived = (slots % capacity < jnp.repeat(arrived_counts, capacity)).astype(jnp.int32)
        target = jnp.cumsum(arrived) - 1
        match = ((arrived[None, :] > 0) & (target[None, :] == slots[:, None])).astype(jnp.int32)
        result, _ = pick_rows(match, result)
    return result.reshape(1, 1, 1, holding, SLOTS, block)


def solution(mesh):
    return jax.shard_map(
        shards,
        mesh=mesh,
        in_specs=(
            P("gx", "gy", "gz", None),
            P(None, "gx", "gy", "gz", None),
            P("gx", "gy", "gz", None),
            P("gx", "gy", "gz"),
            P(None, "gx", "gy", "gz"),
            P(("gx", "gy", "gz")),
        ),
        out_specs=P("gx", "gy", "gz", None, None, None),
        check_vma=False,
    )
```

profile of v0, /device:TPU:0, one launch (start us, length us, event | category | flops | bytes accessed | tf_op | source)
XLA Modules:
  0.0 128.8 jit_solution(8540554213846102467)
XLA Ops:
  0.0 0.0 copy-start.4
  0.0 0.0 copy-start.3
  0.0 0.0 copy-start.1
  0.0 13.2 %prepare.1 = (bf16[24,4,64,128]{3,2,1,0:T(8,128)(2,1)}, bf16[24,4,64,128]{3,2,1,0:T(8,128)(2,1)}, bf16[24,4,64,128]{3,2,1,0:T(8,128)(2,1)}, bf16[6,4,64,128]{3,2...) custom-call(bf16[24,8,4096]{2,1,0:T(8,128)(2,1)} %bitcast.12, ...), custom_call_target="tpu_custom_call" | custom-call | tf_op jit(solution)/shard_map/prepare/pallas_call | solution.py:170
  13.2 4.9 %collective-permute-start.5 = (bf16[12,64,128]{2,1,0:T(8,128)(2,1)S(1)}, bf16[12,64,128]{2,1,0:T(8,128)(2,1)S(1)}, u32[]{:S(2)}, u32[]{:S(2)}) collective-permute-start(bf16[12,64,128]{2,1,0:T(8,128)(2,1)S(1)} %get-tuple-element.23), channel_id=1, source_target_pairs={{0,1},{1,2},{2,3},{3,4},{4,5},{5,6},{6,7},{8,9},{9,10},{10,11},{11... | collective-permute-start | bytes 589832 | tf_op jit(solution)/shard_map/ppermute | solution.py:21
  18.1 1.3 %collective-permute-start.2 = (bf16[12,64,128]{2,1,0:T(8,128)(2,1)S(1)}, bf16[12,64,128]{2,1,0:T(8,128)(2,1)S(1)}, u32[]{:S(2)}, u32[]{:S(2)}) collective-permute-start(bf16[12,64,128]{2,1,0:T(8,128)(2,1)S(1)} %get-tuple-element.20.first_z), channel_id=1, source_target_pairs={{1,0},{2,1},{3,2},{4,3},{5,4},{6,5},{7,6},{9,8},{10,9},{11,10},{12... | collective-permute-start | bytes 589832 | tf_op jit(solution)/shard_map/ppermute | solution.py:21
  19.4 1.3 %collective-permute-start.1 = (bf16[4,4,64,128]{3,2,1,0:T(8,128)(2,1)S(1)}, bf16[4,4,64,128]{3,2,1,0:T(8,128)(2,1)S(1)}, u32[]{:S(2)}, u32[]{:S(2)}) collective-permute-start(bf16[4,4,64,128]{3,2,1,0:T(8,128)(2,1)S(1)} %get-tuple-element.19), channel_id=1, source_target_pairs={{8,0},{9,1},{10,2},{11,3},{12,4},{13,5},{14,6},{15,7},{24,16},{25,... | collective-permute-start | bytes 786440 | tf_op jit(solution)/shard_map/ppermute | solution.py:21
  20.7 1.3 %collective-permute-start = (bf16[6,4,64,128]{3,2,1,0:T(8,128)(2,1)S(1)}, bf16[6,4,64,128]{3,2,1,0:T(8,128)(2,1)S(1)}, u32[]{:S(2)}, u32[]{:S(2)}) collective-permute-start(bf16[6,4,64,128]{3,2,1,0:T(8,128)(2,1)S(1)} %get-tuple-element.18), channel_id=1, source_target_pairs={{16,0},{17,1},{18,2},{19,3},{20,4},{21,5},{22,6},{23,7},{24,8},{25... | collective-permute-start | bytes 1179656 | tf_op jit(solution)/shard_map/ppermute | solution.py:21
  22.0 3.1 %collective-permute-start.3 = (bf16[6,4,64,128]{3,2,1,0:T(8,128)(2,1)S(1)}, bf16[6,4,64,128]{3,2,1,0:T(8,128)(2,1)S(1)}, u32[]{:S(2)}, u32[]{:S(2)}) collective-permute-start(bf16[6,4,64,128]{3,2,1,0:T(8,128)(2,1)S(1)} %get-tuple-element.21), channel_id=1, source_target_pairs={{0,16},{1,17},{2,18},{3,19},{4,20},{5,21},{6,22},{7,23},{8,24},{9,... | collective-permute-start | bytes 1179656 | tf_op jit(solution)/shard_map/ppermute | solution.py:21
  25.1 0.0 copy-done.4
  25.2 0.0 collective-permute-done.5.rim_z
  25.2 4.6 %collective-permute-start.4 = (bf16[4,4,64,128]{3,2,1,0:T(8,128)(2,1)S(1)}, bf16[4,4,64,128]{3,2,1,0:T(8,128)(2,1)S(1)}, u32[]{:S(2)}, u32[]{:S(2)}) collective-permute-start(bf16[4,4,64,128]{3,2,1,0:T(8,128)(2,1)S(1)} %get-tuple-element.22), channel_id=1, source_target_pairs={{0,8},{1,9},{2,10},{3,11},{4,12},{5,13},{6,14},{7,15},{16,24},{17,... | collective-permute-start | bytes 786440 | tf_op jit(solution)/shard_map/ppermute | solution.py:21
  29.8 0.0 copy-done.3
  29.8 0.0 copy-done.1
  29.8 0.0 copy-start
  29.8 1.4 %copy-done = bf16[24,4,64,128]{3,2,1,0:T(8,128)(2,1)S(1)} copy-done((bf16[24,4,64,128]{3,2,1,0:T(8,128)(2,1)S(1)}, bf16[24,4,64,128]{3,2,1,0:T(8,128)(2,1)}, u32[]{:S(2)}) %copy-start) | copy-done | bytes 1572888
  31.2 0.0 copy-start.2
  31.2 32.9 %interior.1.total_ref = f32[168,32,128]{2,1,0:T(8,128)} custom-call(s32[7,4,6,8]{3,2,1,0:T(8,128)S(1)} %copy_add_fusion.keys, bf16[24,8,4096]{2,1,0:T(8,128)(2,1)S(1)} %bitcast.4, bf16[3,24,8,4096]{3,2,1,0:T(8,128)(2,1)} %bitcast.8, bf16[3,24,8,4096]{3,2,1,0:T(8,128)(2,1)} %bitcast.9, bf16[3,24,8,4096]{3,2,1,0:T(8,128)(2,1)} %bitcast.10, ...), custom_call_target="tpu_custom_call" | custom-call | flops 704643072 | bytes 9437184 | tf_op jit(solution)/shard_map/interior/pallas_call | solution.py:282
  64.1 0.0 collective-permute-done.2.head_z
  64.1 0.0 collective-permute-done.1.head_y
  64.1 0.0 collective-permute-done.4.rim_y
  64.1 0.0 collective-permute-done.head_x
  64.1 0.0 collective-permute-done.3.rim_x
  64.1 0.0 copy-done.2
  64.1 19.5 %border.1 = bf16[24,7,4096]{2,1,0:T(8,128)(2,1)} custom-call(s32[7,4,6,8]{3,2,1,0:T(8,128)S(1)} %copy_add_fusion.keys, s32[24]{0:T(128)S(1)} %copy-done.2, bf16[6,4,64,128]{3,2,1,0:T(8,128)(2,1)S(1)} %collective-permute-done.head_x, bf16[4,4,64,128]{3,2,1,0:T(8,128)(2,1)S(1)} %collective-permute-done.1.head_y, ...), custom_call_target="tpu_custom_call" | custom-call | tf_op jit(solution)/shard_map/border/pallas_call | solution.py:380
  83.6 43.2 %all_to_all.5 = bf16[24,7,4096]{2,1,0:T(8,128)(2,1)S(1)} all-to-all(bf16[24,7,4096]{2,1,0:T(8,128)(2,1)} %border.1), channel_id=1, replica_groups=mesh['gx'=2,'gy'=2,'gz'=8] {'gz'}, dimensions={0} | all-to-all | bytes 2752512 | tf_op jit(solution)/shard_map/all_to_all | solution.py:415
  126.9 1.9 %copy.9 = bf16[1,1,1,24,7,4096]{5,3,4,2,1,0:T(8,128)(2,1)} copy(bf16[1,1,1,24,7,4096]{5,4,3,2,1,0:T(8,128)(2,1)S(1)} %bitcast.11) | data formatting | bytes 2752512 | tf_op jit(solution)/shard_map/reshape | solution.py:425
  (3 shorter events, 0.0 us)
Async XLA Ops:
  0.0 25.1 %copy-start.4 = (s32[4,6,8]{2,0,1:T(4,128)S(1)}, s32[4,6,8]{2,0,1:T(4,128)}, u32[]{:S(2)}) copy-start(s32[4,6,8]{2,0,1:T(4,128)} %param.9) | copy-start | bytes 2308
  0.0 29.8 %copy-start.3 = (s32[7,4,6,8]{3,1,2,0:T(4,128)S(1)}, s32[7,4,6,8]{3,1,2,0:T(4,128)}, u32[]{:S(2)}) copy-start(s32[7,4,6,8]{3,1,2,0:T(4,128)} %param.10) | copy-start | bytes 16132
  0.0 29.8 %copy-start.1 = (bf16[4,6,8,4096]{3,2,1,0:T(8,128)(2,1)S(1)}, bf16[4,6,8,4096]{3,2,1,0:T(8,128)(2,1)}, u32[]{:S(2)}) copy-start(bf16[4,6,8,4096]{3,2,1,0:T(8,128)(2,1)} %param.6) | copy-start | bytes 4718596
  13.2 11.9 %collective-permute-start.5 = (bf16[12,64,128]{2,1,0:T(8,128)(2,1)S(1)}, bf16[12,64,128]{2,1,0:T(8,128)(2,1)S(1)}, u32[]{:S(2)}, u32[]{:S(2)}) collective-permute-start(bf16[12,64,128]{2,1,0:T(8,128)(2,1)S(1)} %get-tuple-element.23), channel_id=1, source_target_pairs={{0,1},{1,2},{2,3},{3,4},{4,5},{5,6},{6,7},{8,9},{9,10},{10,11},{11... | collective-permute-start | bytes 589832 | tf_op jit(solution)/shard_map/ppermute | solution.py:21
  18.1 45.9 %collective-permute-start.2 = (bf16[12,64,128]{2,1,0:T(8,128)(2,1)S(1)}, bf16[12,64,128]{2,1,0:T(8,128)(2,1)S(1)}, u32[]{:S(2)}, u32[]{:S(2)}) collective-permute-start(bf16[12,64,128]{2,1,0:T(8,128)(2,1)S(1)} %get-tuple-element.20.first_z), channel_id=1, source_target_pairs={{1,0},{2,1},{3,2},{4,3},{5,4},{6,5},{7,6},{9,8},{10,9},{11,10},{12... | collective-permute-start | bytes 589832 | tf_op jit(solution)/shard_map/ppermute | solution.py:21
  19.4 44.6 %collective-permute-start.1 = (bf16[4,4,64,128]{3,2,1,0:T(8,128)(2,1)S(1)}, bf16[4,4,64,128]{3,2,1,0:T(8,128)(2,1)S(1)}, u32[]{:S(2)}, u32[]{:S(2)}) collective-permute-start(bf16[4,4,64,128]{3,2,1,0:T(8,128)(2,1)S(1)} %get-tuple-element.19), channel_id=1, source_target_pairs={{8,0},{9,1},{10,2},{11,3},{12,4},{13,5},{14,6},{15,7},{24,16},{25,... | collective-permute-start | bytes 786440 | tf_op jit(solution)/shard_map/ppermute | solution.py:21
  20.7 43.4 %collective-permute-start = (bf16[6,4,64,128]{3,2,1,0:T(8,128)(2,1)S(1)}, bf16[6,4,64,128]{3,2,1,0:T(8,128)(2,1)S(1)}, u32[]{:S(2)}, u32[]{:S(2)}) collective-permute-start(bf16[6,4,64,128]{3,2,1,0:T(8,128)(2,1)S(1)} %get-tuple-element.18), channel_id=1, source_target_pairs={{16,0},{17,1},{18,2},{19,3},{20,4},{21,5},{22,6},{23,7},{24,8},{25... | collective-permute-start | bytes 1179656 | tf_op jit(solution)/shard_map/ppermute | solution.py:21
  22.0 42.1 %collective-permute-start.3 = (bf16[6,4,64,128]{3,2,1,0:T(8,128)(2,1)S(1)}, bf16[6,4,64,128]{3,2,1,0:T(8,128)(2,1)S(1)}, u32[]{:S(2)}, u32[]{:S(2)}) collective-permute-start(bf16[6,4,64,128]{3,2,1,0:T(8,128)(2,1)S(1)} %get-tuple-element.21), channel_id=1, source_target_pairs={{0,16},{1,17},{2,18},{3,19},{4,20},{5,21},{6,22},{7,23},{8,24},{9,... | collective-permute-start | bytes 1179656 | tf_op jit(solution)/shard_map/ppermute | solution.py:21
  25.2 38.9 %collective-permute-start.4 = (bf16[4,4,64,128]{3,2,1,0:T(8,128)(2,1)S(1)}, bf16[4,4,64,128]{3,2,1,0:T(8,128)(2,1)S(1)}, u32[]{:S(2)}, u32[]{:S(2)}) collective-permute-start(bf16[4,4,64,128]{3,2,1,0:T(8,128)(2,1)S(1)} %get-tuple-element.22), channel_id=1, source_target_pairs={{0,8},{1,9},{2,10},{3,11},{4,12},{5,13},{6,14},{7,15},{16,24},{17,... | collective-permute-start | bytes 786440 | tf_op jit(solution)/shard_map/ppermute | solution.py:21
  29.8 1.4 %copy-start = (bf16[24,4,64,128]{3,2,1,0:T(8,128)(2,1)S(1)}, bf16[24,4,64,128]{3,2,1,0:T(8,128)(2,1)}, u32[]{:S(2)}) copy-start(bf16[24,4,64,128]{3,2,1,0:T(8,128)(2,1)} %get-tuple-element.27.natural_ref.natural) | copy-start | bytes 4718596
  31.2 32.9 %copy-start.2 = (s32[24]{0:T(128)S(1)}, s32[24]{0:T(128)}, u32[]{:S(2)}) copy-start(s32[24]{0:T(128)} %owners.1) | copy-start | bytes 292
where the time goes:
time: 129 us
  Pallas kernels  65.6 us (51%)
  blocking collectives  43.2 us (33%)
  starting transfers between devices  16.4 us (13%)
  local copies, waits for them, and re-layouts  3.36 us (3%)
    all_to_all x1, blocking collectives, shards(): result = lax.all_to_all(outgoing, 'gz', 0, 0, tiled=True)  43.2 us
    pallas_call x1, Pallas kernels, interior(): pl.pallas_call(interior_kernel, grid=(size_x,), in_specs=[pl.BlockSpec(me...  32.9 us
    pallas_call x1, Pallas kernels, border(): pl.pallas_call(functools.partial(border_kernel, capacity), in_specs=[smem...  19.5 us
    ppermute x6, starting transfers between devices, passed_along(): return lax.ppermute(block, axis, route)  16.4 us
    pallas_call x1, Pallas kernels, prepare(): pl.pallas_call(prepare_kernel, grid=(size_x,), in_specs=[pl.BlockSpec((si...  13.2 us
  transfers between devices with their start and end apart: 6, of which 0 were waited for; matrix products, arithmetic and copies ran while one was open for 0% of the time, Pallas kernels for 26%

commit v1 on v0

v1 whole, which is shorter than its diff:
```python
import functools

import jax
import jax.numpy as jnp
from jax import lax
from jax.experimental import pallas as pl
from jax.experimental.pallas import tpu as pltpu
from jax.sharding import PartitionSpec as P

NODES = 64
SLOTS = 7
AGG_DEV = 24
LANES = 128
HALF = NODES // 2
VMEM_LIMIT = 48 * 1024 * 1024
UNROLL = 2


def passed_along(block, axis, distance):
    devices = range(lax.axis_size(axis))
    route = [(i - distance, i) for i in devices if i - distance in devices]
    return lax.ppermute(block, axis, route)


def low_lanes(rows):
    return lax.broadcasted_iota(jnp.int32, (rows, LANES), 1) < NODES


def swapped(value):
    return pltpu.roll(value, NODES, 1)


def spread(column, stage):
    depth = column.shape[0]
    for k in range(column.shape[1] // LANES):
        stage[depth * k : depth * (k + 1), :] = column[:, LANES * k : LANES * (k + 1)].astype(jnp.float32)


def block_of(stage, z, depth):
    return stage[pl.ds(z, HALF, stride=depth), :]


def stacked_pair(first, second):
    low = low_lanes(HALF)
    even = jnp.where(low, first, swapped(second))
    odd = jnp.where(low, swapped(first), second)
    return jnp.concatenate([even, odd], axis=0).astype(jnp.bfloat16)


def in_order(pair):
    row = lax.broadcasted_iota(jnp.int32, (NODES, NODES), 0)
    col = lax.broadcasted_iota(jnp.int32, (NODES, NODES), 1)
    move = (row == 2 * (col % HALF) + col // HALF).astype(jnp.bfloat16)
    return jnp.dot(move, pair, preferred_element_type=jnp.float32).astype(jnp.bfloat16)


def paired_weights(pair):
    low = low_lanes(NODES)
    zero = jnp.zeros_like(pair)
    first = jnp.where(low, pair, zero)
    second = jnp.where(low, zero, pair)
    left = jnp.concatenate([first, zero, second, zero], axis=0)
    right = jnp.concatenate([zero, first, zero, second], axis=0)
    return jnp.concatenate([left, right], axis=1)


def upright(product):
    return jnp.concatenate([product[:, :LANES], product[:, LANES:]], axis=0).astype(jnp.bfloat16)


def across(left, right):
    return lax.dot_general(left, right, (((0,), (0,)), ((), ())), preferred_element_type=jnp.float32)


def folded(square):
    low = low_lanes(HALF)
    moved = swapped(jnp.where(low, square[HALF : 2 * HALF], square[2 * HALF : 3 * HALF]))
    return (jnp.where(low, square[:HALF], moved), jnp.where(low, moved, square[3 * HALF :]))


def add_to(total, key, value):
    total[key] = total[key] + value


def diagonal(square):
    return jnp.where(low_lanes(NODES), square[:NODES], square[NODES:]).astype(jnp.bfloat16)


def prepare_kernel(place_ref, p_ref, fx_ref, fy_ref, fz_ref, natural_ref, stacked_ref, shifted_ref, swap_x_ref, swap_y_ref, head_z_ref, rim_z_ref, last_z_ref,
                   tail_x_ref, tail_y_ref, tail_z_ref, stages, stages_f, ends):
    plane = pl.program_id(0)
    size_y, depth = p_ref.shape[0], p_ref.shape[1]
    pairs = depth // 2

    for j in range(size_y):
        stage = stages.at[j]
        spread(p_ref[j], stage)
        block = [block_of(stage, z, depth) for z in range(depth)]
        for p in range(pairs):
            stacked = stacked_pair(block[2 * p], block[2 * p + 1])
            stacked_ref[j, p] = stacked
            shifted_ref[j, p] = stacked_pair(block[(2 * p - 1) % depth], block[2 * p])
            natural_ref[j, p] = in_order(stacked)
        ends[0, j] = block[0]
        ends[1, j] = block[depth - 1]
        stage_f = stages_f.at[j]
        spread(fz_ref[0, j], stage_f)
        last = block_of(stage_f, depth - 1, depth)
        ends[2, j] = last
        tail_z_ref[j] = last.astype(jnp.bfloat16)

    for t in range(size_y // 2):
        first, last, face = [stacked_pair(ends[kind, 2 * t], ends[kind, 2 * t + 1]) for kind in range(3)]
        head_z_ref[t] = in_order(first)
        last_z_ref[t] = last
        rim_z_ref[t] = diagonal(across(face, last))

    def faces(source, stage, j, tails, rims):
        spread(source, stage)
        block = [block_of(stage, z, depth) for z in range(depth)]
        for z in range(depth):
            tails[z] = block[z].astype(jnp.bfloat16)
        for p in range(pairs):
            rims[p] = diagonal(across(stacked_pair(block[2 * p], block[2 * p + 1]), stacked_ref[j, p]))

    @pl.when(place_ref[1] == 0)
    def _():
        faces(fy_ref[0, 0], stages_f.at[0], size_y - 1, tail_y_ref.at[0], swap_y_ref.at[0])

    @pl.when(place_ref[1] != 0)
    def _():
        swap_y_ref[0] = natural_ref[0]

    @pl.when((place_ref[0] == 0) & (plane == pl.num_programs(0) - 1))
    def _():
        for j in range(size_y):
            faces(fx_ref[0, j], stages_f.at[j], j, tail_x_ref.at[j], swap_x_ref.at[j])

    @pl.when((place_ref[0] != 0) & (plane == 0))
    def _():
        swap_x_ref[...] = natural_ref[...]


def prepare(place, prolong, faces, sizes):
    size_x, size_y, depth = sizes
    pairs, block = depth // 2, prolong.shape[-1]
    columns, half = size_x * size_y, size_y // 2
    shape = lambda *dims: jax.ShapeDtypeStruct(dims, jnp.bfloat16)
    by_half = pl.BlockSpec((half, NODES, LANES), lambda i: (i, 0, 0))
    stage = pltpu.VMEM((size_y, depth * HALF, LANES), jnp.float32)
    return pl.pallas_call(
        prepare_kernel,
        grid=(size_x,),
        in_specs=[
            pl.BlockSpec(memory_space=pltpu.SMEM),
            pl.BlockSpec((size_y, depth, block), lambda i: (i, 0, 0)),
            pl.BlockSpec((1, size_y, depth, block), lambda i: (0, size_x - 1, 0, 0)),
            pl.BlockSpec((1, 1, depth, block), lambda i: (1, i * size_y + size_y - 1, 0, 0)),
            pl.BlockSpec((1, size_y, depth, block), lambda i: (2, i, 0, 0)),
        ],
        out_specs=[
            pl.BlockSpec((size_y, pairs, NODES, LANES), lambda i: (i, 0, 0, 0)),
            pl.BlockSpec((size_y, pairs, NODES, LANES), lambda i: (i, 0, 0, 0)),
            pl.BlockSpec((size_y, pairs, NODES, LANES), lambda i: (i, 0, 0, 0)),
            pl.BlockSpec((size_y, pairs, NODES, LANES), lambda i: (0, 0, 0, 0)),
            pl.BlockSpec((1, pairs, NODES, LANES), lambda i: (i, 0, 0, 0)),
            by_half, by_half, by_half,
            pl.BlockSpec((size_y, depth, HALF, LANES), lambda i: (0, 0, 0, 0)),
            pl.BlockSpec((1, depth, HALF, LANES), lambda i: (i, 0, 0, 0)),
            pl.BlockSpec((size_y, HALF, LANES), lambda i: (i, 0, 0)),
        ],
        out_shape=[
            shape(columns, pairs, NODES, LANES), shape(columns, pairs, NODES, LANES), shape(columns, pairs, NODES, LANES),
            shape(size_y, pairs, NODES, LANES), shape(size_x, pairs, NODES, LANES),
            shape(columns // 2, NODES, LANES), shape(columns // 2, NODES, LANES), shape(columns // 2, NODES, LANES),
            shape(size_y, depth, HALF, LANES), shape(size_x, depth, HALF, LANES), shape(columns, HALF, LANES),
        ],
        scratch_shapes=[
            stage, stage,
            pltpu.VMEM((3, size_y, HALF, LANES), jnp.float32),
        ],
        compiler_params=pltpu.CompilerParams(vmem_limit_bytes=VMEM_LIMIT),
        name="prepare",
    )(place, prolong, faces, faces, faces)


def interior_kernel(keys, diag_ref, fx_ref, fy_ref, fz_ref, natural_ref, stacked_ref, below_ref, shifted_ref, ahead_ref, behind_ref,
                    stages, ahead_even, ahead_odd, behind_even, behind_odd):
    plane = pl.program_id(0)
    size_y, depth = diag_ref.shape[0], diag_ref.shape[1]
    pairs = depth // 2
    spare = ahead_ref.shape[0]
    ahead, behind = (ahead_even, ahead_odd), (behind_even, behind_odd)

    @pl.when(plane == 0)
    def _():
        for total in ahead + behind:
            total[...] = jnp.zeros_like(total)

    def column(j, stage):
        row_y = jnp.maximum(j - 1, 0)
        row_x = jnp.maximum(plane - 1, 0)
        has_x, has_y = plane > 0, j > 0
        for face, source in zip(range(4), (diag_ref[j], fx_ref[0, j], fy_ref[0, row_y], fz_ref[0, j])):
            spread(source, stage.at[face])
        for p in range(pairs):
            left = []
            for face in range(4):
                shift = 1 if face == 3 else 0
                sides = [block_of(stage.at[face], (2 * p + side - shift) % depth, depth).astype(jnp.bfloat16) for side in (0, 1)]
                left.append(jnp.concatenate(sides, axis=1))
            product = jnp.dot(
                jnp.concatenate(left, axis=0), paired_weights(natural_ref[j, p]), preferred_element_type=jnp.float32)
            stacked = (stacked_ref[j, p], below_ref[j, p], stacked_ref[row_y, p], shifted_ref[j, p])
            for face in range(4):
                couple = upright(product[HALF * face : HALF * (face + 1)])
                sums = folded(across(stacked[face], couple))
                for side in (0, 1):
                    z = 2 * p + side
                    if face == 0:
                        add_to(ahead[side], keys[0, plane, j, z], sums[side])
                        continue
                    if face == 1:
                        here, there = keys[2, row_x, j, z], keys[1, plane, j, z]
                        here, there = jnp.where(has_x, here, spare), jnp.where(has_x, there, spare)
                    elif face == 2:
                        here, there = keys[4, plane, row_y, z], keys[3, plane, j, z]
                        here, there = jnp.where(has_y, here, spare), jnp.where(has_y, there, spare)
                    elif z > 0:
                        here, there = keys[6, plane, j, z - 1], keys[5, plane, j, z]
                    else:
                        continue
                    add_to(ahead[side], here, sums[side])
                    add_to(behind[side], there, sums[side])

    def columns(step, carry):
        for u in range(UNROLL):
            column(step * UNROLL + u, stages.at[u])
        return carry

    lax.fori_loop(0, size_y // UNROLL, columns, 0)

    @pl.when(plane == pl.num_programs(0) - 1)
    def _():
        def gather(r, carry):
            for s in range(SLOTS):
                key = r * SLOTS + s
                ahead_ref[key] = ahead_even[key] + ahead_odd[key]
                behind_ref[key] = behind_even[key] + behind_odd[key]
            return carry

        lax.fori_loop(0, spare // SLOTS, gather, 0)


def interior(keys, diag, faces, natural, stacked, shifted, sizes):
    size_x, size_y, depth = sizes
    pairs, block = depth // 2, diag.shape[-1]
    columns, rows = size_x * size_y, AGG_DEV * SLOTS
    total = pltpu.VMEM((rows + 1, HALF, LANES), jnp.float32)
    sums = jax.ShapeDtypeStruct((rows, HALF, LANES), jnp.float32)
    all_rows = pl.BlockSpec((rows, HALF, LANES), lambda i: (0, 0, 0))
    return pl.pallas_call(
        interior_kernel,
        grid=(size_x,),
        in_specs=[
            pl.BlockSpec(memory_space=pltpu.SMEM),
            pl.BlockSpec((size_y, depth, block), lambda i: (i, 0, 0)),
            pl.BlockSpec((1, size_y, depth, block), lambda i: (0, jnp.maximum(i - 1, 0), 0, 0)),
            pl.BlockSpec((1, size_y, depth, block), lambda i: (1, i, 0, 0)),
            pl.BlockSpec((1, size_y, depth, block), lambda i: (2, i, 0, 0)),
            pl.BlockSpec((size_y, pairs, NODES, LANES), lambda i: (i, 0, 0, 0)),
            pl.BlockSpec((size_y, pairs, NODES, LANES), lambda i: (i, 0, 0, 0)),
            pl.BlockSpec((size_y, pairs, NODES, LANES), lambda i: (jnp.maximum(i - 1, 0), 0, 0, 0)),
            pl.BlockSpec((size_y, pairs, NODES, LANES), lambda i: (i, 0, 0, 0)),
        ],
        out_specs=[all_rows, all_rows],
        out_shape=[sums, sums],
        scratch_shapes=[pltpu.VMEM((UNROLL, 4, depth * HALF, LANES), jnp.float32), total, total, total, total],
        compiler_params=pltpu.CompilerParams(vmem_limit_bytes=VMEM_LIMIT),
        cost_estimate=pl.CostEstimate(flops=columns * depth * 14 * NODES**3, bytes_accessed=columns * depth * 6 * block * 2, transcendentals=0),
        name="interior",
    )(keys, diag, faces, faces, faces, natural, stacked, stacked, shifted)


def border_kernel(capacity, keys, owners, place_ref, got_x, got_y, got_z, back_z, tail_x, tail_y, tail_z,
                  natural, stacked, first_z, last_z, ahead_ref, behind_ref, out_ref, extra_ahead, extra_back, wide, filled):
    size_y, depth = tail_x.shape[0], tail_x.shape[1]
    size_x = tail_y.shape[0]
    pairs = depth // 2
    rows = ahead_ref.shape[0] // SLOTS
    places = out_ref.shape[0]
    low = low_lanes(HALF)

    extra_ahead[...] = jnp.zeros_like(extra_ahead)
    extra_back[...] = jnp.zeros_like(extra_back)

    def ahead(left0, left1, head, prolong):
        product = jnp.dot(jnp.concatenate([left0, left1], axis=1), paired_weights(head), preferred_element_type=jnp.float32)
        return folded(across(prolong, upright(product)))

    def back(prolong, rim):
        return folded(across(prolong, rim))

    @pl.when(place_ref[0] == 0)
    def _():
        def over(j, carry):
            for p in range(pairs):
                sums = ahead(tail_x[j, 2 * p], tail_x[j, 2 * p + 1], got_x[j, p],
                             stacked[(size_x - 1) * size_y + j, p])
                for side in (0, 1):
                    add_to(extra_ahead, keys[2, size_x - 1, j, 2 * p + side], sums[side])
            return carry

        lax.fori_loop(0, size_y, over, 0)

    @pl.when(place_ref[0] != 0)
    def _():
        def over(j, carry):
            for p in range(pairs):
                sums = back(natural[j, p], got_x[j, p])
                for side in (0, 1):
                    add_to(extra_back, keys[1, 0, j, 2 * p + side], sums[side])
            return carry

        lax.fori_loop(0, size_y, over, 0)

    @pl.when(place_ref[1] == 0)
    def _():
        def over(i, carry):
            for p in range(pairs):
                sums = ahead(tail_y[i, 2 * p], tail_y[i, 2 * p + 1], got_y[i, p],
                             stacked[i * size_y + size_y - 1, p])
                for side in (0, 1):
                    add_to(extra_ahead, keys[4, i, size_y - 1, 2 * p + side], sums[side])
            return carry

        lax.fori_loop(0, size_x, over, 0)

    @pl.when(place_ref[1] != 0)
    def _():
        def over(i, carry):
            for p in range(pairs):
                sums = back(natural[i * size_y, p], got_y[i, p])
                for side in (0, 1):
                    add_to(extra_back, keys[3, i, 0, 2 * p + side], sums[side])
            return carry

        lax.fori_loop(0, size_x, over, 0)

    def over_z(i, carry):
        for u in range(size_y // 2):
            t = i * (size_y // 2) + u
            sums = ahead(tail_z[2 * t], tail_z[2 * t + 1], got_z[t], last_z[t])
            past = back(first_z[t], back_z[t])
            for side in (0, 1):
                add_to(extra_ahead, keys[6, i, 2 * u + side, depth - 1], sums[side])
                add_to(extra_back, keys[5, i, 2 * u + side, 0], past[side])
        return carry

    lax.fori_loop(0, size_x, over_z, 0)

    for owner in range(places // capacity):
        filled[owner] = 0
    if places != rows:
        out_ref[...] = jnp.zeros_like(out_ref)

    def emit(pair, carry):
        spots = []
        for side in (0, 1):
            owner = owners[2 * pair + side]
            spots.append(owner * capacity + filled[owner])
            filled[owner] = filled[owner] + 1
        for s in range(SLOTS):
            key = [(2 * pair + side) * SLOTS + s for side in (0, 1)]
            one, two = behind_ref[key[0]], behind_ref[key[1]]
            upper = jnp.where(low, one, swapped(two))
            lower = jnp.where(low, swapped(one), two)
            wide[s, :, :NODES] = jnp.concatenate([upper, lower], axis=0).T
            for side in (0, 1):
                extra_ahead[key[side]] = ahead_ref[key[side]] + (extra_ahead[key[side]] + extra_back[key[side]])
                even = extra_ahead[key[side], pl.ds(0, HALF // 2, stride=2), :]
                odd = extra_ahead[key[side], pl.ds(1, HALF // 2, stride=2), :]
                narrow = low[: HALF // 2]
                straight = jnp.concatenate(
                    [jnp.where(narrow, even, swapped(odd)), jnp.where(narrow, swapped(even), odd)], axis=0)
                even = wide[s, pl.ds(NODES * side, HALF, stride=2), :]
                odd = wide[s, pl.ds(NODES * side + 1, HALF, stride=2), :]
                total = straight + jnp.where(low, even, swapped(odd))
                out_ref[spots[side], HALF * s : HALF * (s + 1), :] = total.astype(jnp.bfloat16)
        return carry

    lax.fori_loop(0, rows // 2, emit, 0)


def border(keys, owners, place, operands, capacity, places):
    rows = AGG_DEV * SLOTS
    smem = pl.BlockSpec(memory_space=pltpu.SMEM)
    total = pltpu.VMEM((rows, HALF, LANES), jnp.float32)
    return pl.pallas_call(
        functools.partial(border_kernel, capacity),
        in_specs=[smem, smem, smem] + [pl.BlockSpec(memory_space=pltpu.VMEM)] * len(operands),
        out_specs=pl.BlockSpec(memory_space=pltpu.VMEM),
        out_shape=jax.ShapeDtypeStruct((places, SLOTS * HALF, LANES), jnp.bfloat16),
        scratch_shapes=[total, total, pltpu.VMEM((SLOTS, LANES, LANES), jnp.float32), pltpu.SMEM((places // capacity,), jnp.int32)],
        compiler_params=pltpu.CompilerParams(vmem_limit_bytes=VMEM_LIMIT),
        name="border",
    )(keys, owners, place, *operands)


def layout_kernel(source, rows_ref, out_ref, stage):
    group = pl.program_id(0)
    height = out_ref.shape[1]
    for s in range(SLOTS):
        for r in range(height):
            row = source[group * height + r]
            block = rows_ref[jnp.maximum(row, 0), HALF * s : HALF * (s + 1), :].astype(jnp.float32)
            stage[s, pl.ds(r, HALF, stride=height), :] = jnp.where(row >= 0, block, jnp.zeros_like(block))
        for k in range(HALF):
            out_ref[s, :, LANES * k : LANES * (k + 1)] = stage[s, height * k : height * (k + 1), :].astype(jnp.bfloat16)


def laid_out(source, rows, block):
    places, height = rows.shape[0], 8
    return pl.pallas_call(
        layout_kernel,
        grid=(places // height,),
        in_specs=[pl.BlockSpec(memory_space=pltpu.SMEM), pl.BlockSpec(rows.shape, lambda g: (0, 0, 0))],
        out_specs=pl.BlockSpec((SLOTS, height, block), lambda g: (0, g, 0)),
        out_shape=jax.ShapeDtypeStruct((SLOTS, places, block), jnp.bfloat16),
        scratch_shapes=[pltpu.VMEM((SLOTS, height * HALF, LANES), jnp.float32)],
        compiler_params=pltpu.CompilerParams(vmem_limit_bytes=VMEM_LIMIT),
        name="layout",
    )(source, rows)


def swap(block, axis):
    assert lax.axis_size(axis) == 2
    return lax.ppermute(block, axis, [(0, 1), (1, 0)])


def shards(a_diag, a_face, prolong, aggregate, pair_slot, row_owner):
    size_x, size_y, size_z, block = a_diag.shape
    sizes = (size_x, size_y, size_z)
    columns = size_x * size_y
    depth = lax.axis_size("gz")
    capacity = max(2, (AGG_DEV + depth - 1) // depth)
    holding = capacity * depth
    diag = a_diag.reshape(columns, size_z, block)
    faces = a_face.reshape(3, columns, size_z, block)
    keys = aggregate[None] * SLOTS + pair_slot
    place = jnp.stack([lax.axis_index("gx"), lax.axis_index("gy")]).astype(jnp.int32)

    natural, stacked, shifted, swap_x, swap_y, head_z, rim_z, last_z, tail_x, tail_y, tail_z = prepare(
        place, prolong.reshape(columns, size_z, block), faces, sizes)
    got_z = passed_along(head_z, "gz", -1)
    back_z = passed_along(rim_z, "gz", 1)
    got_y = swap(swap_y, "gy")
    got_x = swap(swap_x, "gx")
    ahead, behind = interior(keys, diag, faces, natural, stacked, shifted, sizes)
    outgoing = border(
        keys, row_owner, place,
        (got_x, got_y, got_z, back_z, tail_x, tail_y, tail_z, natural, stacked, head_z, last_z, ahead, behind), capacity, holding)
    arrived = lax.all_to_all(outgoing, "gz", 0, 0, tiled=True)
    source = jnp.arange(holding, dtype=jnp.int32)
    if holding != AGG_DEV:
        owner_ids = jnp.arange(depth, dtype=jnp.int32)
        counts = jnp.sum((row_owner[:, None] == owner_ids[None, :]).astype(jnp.int32), axis=0)
        arrived_counts = lax.all_to_all(counts, "gz", 0, 0, tiled=True)
        present = source % capacity < jnp.repeat(arrived_counts, capacity)
        target = jnp.cumsum(present.astype(jnp.int32)) - 1
        match = (present[None, :] & (target[None, :] == source[:, None])).astype(jnp.int32)
        source = jnp.sum(match * (source[None, :] + 1), axis=1) - 1
    result = laid_out(source, arrived, block)
    return jnp.transpose(result, (1, 0, 2)).reshape(1, 1, 1, holding, SLOTS, block)


def solution(mesh):
    return jax.shard_map(
        shards,
        mesh=mesh,
        in_specs=(
            P("gx", "gy", "gz", None),
            P(None, "gx", "gy", "gz", None),
            P("gx", "gy", "gz", None),
            P("gx", "gy", "gz"),
            P(None, "gx", "gy", "gz"),
            P(("gx", "gy", "gz")),
        ),
        out_specs=P("gx", "gy", "gz", None, None, None),
        check_vma=False,
    )
```

time: 129 us -> 108 us (0.84)
  starting transfers between devices: 16.4 us -> 8.03 us
  blocking collectives: 43.2 us -> 35.6 us
  local copies, waits for them, and re-layouts: 3.36 us -> 0.03 us
  Pallas kernels: 65.6 us -> 64 us
    ppermute x6 -> x2, starting transfers between devices: 16.4 us -> 5.83 us  [passed_along(): return lax.ppermute(block, axis, route)]
    all_to_all x1, blocking collectives: 43.2 us -> 35.6 us  [shards(): arrived = lax.all_to_all(outgoing, 'gz', 0, 0, tiled=True)]
    pallas_call x1, Pallas kernels: 19.5 us -> 25.5 us  [border(): pl.pallas_call(functools.partial(border_kernel, capacity), in_specs=[smem...]
    pallas_call x1, Pallas kernels: 32.9 us -> 28.9 us  [interior(): pl.pallas_call(interior_kernel, grid=(size_x,), in_specs=[pl.BlockSpec(me...]
    pallas_call x1 -> x2, Pallas kernels: 13.2 us -> 9.55 us  [the longest x1 6.92 us: prepare(): pl.pallas_call(prepare_kernel, grid=(size_x,), in_specs=[pl.BlockSpec(mem...]
    ppermute x0 -> x2, starting transfers between devices: none -> 2.2 us  [swap(): return lax.ppermute(block, axis, [(0, 1), (1, 0)])]
    reshape x1 -> x0, local copies, waits for them, and re-layouts: 1.94 us -> none  [shards(): return result.reshape(1, 1, 1, holding, SLOTS, block)]
    unnamed x10, local copies, waits for them, and re-layouts: 1.42 us -> 0.02 us
  transfers between devices with their start and end apart: 6 -> 4, of which waited for: 0 -> 0; matrix products, arithmetic and copies ran while one was open for 0% -> 0% of each run, Pallas kernels for 26% -> 27%
where the time goes in v1:
time: 108 us
  Pallas kernels  64 us (59%)
  blocking collectives  35.6 us (33%)
  starting transfers between devices  8.03 us (7%)
    all_to_all x1, blocking collectives, shards(): arrived = lax.all_to_all(outgoing, 'gz', 0, 0, tiled=True)  35.6 us
    pallas_call x1, Pallas kernels, interior(): pl.pallas_call(interior_kernel, grid=(size_x,), in_specs=[pl.BlockSpec(me...  28.9 us
    pallas_call x1, Pallas kernels, border(): pl.pallas_call(functools.partial(border_kernel, capacity), in_specs=[smem...  25.5 us
    pallas_call x1, Pallas kernels, prepare(): pl.pallas_call(prepare_kernel, grid=(size_x,), in_specs=[pl.BlockSpec(mem...  6.92 us
    ppermute x2, starting transfers between devices, passed_along(): return lax.ppermute(block, axis, route)  5.83 us
    pallas_call x1, Pallas kernels, laid_out(): pl.pallas_call(layout_kernel, grid=(places // height,), in_specs=[pl.Bloc...  2.63 us
    ppermute x2, starting transfers between devices, swap(): return lax.ppermute(block, axis, [(0, 1), (1, 0)])  2.2 us
  transfers between devices with their start and end apart: 4, of which 0 were waited for; matrix products, arithmetic and copies ran while one was open for 0% of the time, Pallas kernels for 27%

profile of v1, /device:TPU:0, one launch (start us, length us, event | category | flops | bytes accessed | tf_op | source)
XLA Modules:
  0.0 107.9 jit_solution(12471580793007686330)
XLA Ops:
  0.0 0.1 pad_add_fusion.place_ref
  0.1 0.0 copy-start.4
  0.1 0.0 copy-start.3
  0.1 0.0 copy-start.1
  0.1 6.9 %prepare.1 = (bf16[24,4,64,128]{3,2,1,0:T(8,128)(2,1)S(1)}, bf16[24,4,64,128]{3,2,1,0:T(8,128)(2,1)S(1)}, bf16[24,4,64,128]{3,2,1,0:T(8,128)(2,1)}, bf16[6,4,64,...) custom-call(s32[2]{0:T(128)S(1)} %pad_add_fusion.place_ref, ...), custom_call_target="tpu_custom_call" | custom-call | tf_op jit(solution)/shard_map/prepare/pallas_call | solution.py:151
  7.0 0.0 copy-start
  7.0 1.3 %collective-permute-start.2 = (bf16[12,64,128]{2,1,0:T(8,128)(2,1)S(1)}, bf16[12,64,128]{2,1,0:T(8,128)(2,1)S(1)}, u32[]{:S(2)}, u32[]{:S(2)}) collective-permute-start(bf16[12,64,128]{2,1,0:T(8,128)(2,1)S(1)} %get-tuple-element.20.first_z), channel_id=1, source_target_pairs={{1,0},{2,1},{3,2},{4,3},{5,4},{6,5},{7,6},{9,8},{10,9},{11,10},{12... | collective-permute-start | bytes 589832 | tf_op jit(solution)/shard_map/ppermute | solution.py:22
  8.3 0.1 collective-permute-start
  8.4 2.1 %collective-permute-start.1 = (bf16[4,4,64,128]{3,2,1,0:T(8,128)(2,1)S(1)}, bf16[4,4,64,128]{3,2,1,0:T(8,128)(2,1)S(1)}, u32[]{:S(2)}, u32[]{:S(2)}) collective-permute-start(bf16[4,4,64,128]{3,2,1,0:T(8,128)(2,1)S(1)} %get-tuple-element.19), channel_id=1, source_target_pairs={{0,8},{8,0},{1,9},{9,1},{2,10},{10,2},{3,11},{11,3},{4,12},{12,4},... | collective-permute-start | bytes 786440 | tf_op jit(solution)/shard_map/ppermute | solution.py:438
  10.5 4.5 %collective-permute-start.3 = (bf16[12,64,128]{2,1,0:T(8,128)(2,1)S(1)}, bf16[12,64,128]{2,1,0:T(8,128)(2,1)S(1)}, u32[]{:S(2)}, u32[]{:S(2)}) collective-permute-start(bf16[12,64,128]{2,1,0:T(8,128)(2,1)S(1)} %get-tuple-element.21), channel_id=1, source_target_pairs={{0,1},{1,2},{2,3},{3,4},{4,5},{5,6},{6,7},{8,9},{9,10},{10,11},{11... | collective-permute-start | bytes 589832 | tf_op jit(solution)/shard_map/ppermute | solution.py:22
  15.1 0.0 copy-done.4
  15.1 0.0 copy-done.3
  15.1 0.0 copy-done.1
  15.1 0.0 copy-start.2
  15.1 28.9 %interior.1 = (f32[168,32,128]{2,1,0:T(8,128)}, f32[168,32,128]{2,1,0:T(8,128)}) custom-call(s32[7,4,6,8]{3,2,1,0:T(8,128)S(1)} %copy_add_fusion.keys, bf16[24,8,4096]{2,1,0:T(8,128)(2,1)S(1)} %bitcast.8, bf16[3,24,8,4096]{3,2,1,0:T(8,128)(2,1)} %bitcast.12, bf16[3,24,8,4096]{3,2,1,0:T(8,128)(2,1)} %bitcast.13, bf16[3,24,8,4096]{3,2,1,0:T(8,128)(2,1)} %bitcast.14, ...), custom_call_target="tpu_custom_call" | custom-call | flops 704643072 | bytes 9437184 | tf_op jit(solution)/shard_map/interior/pallas_call | solution.py:262
  44.0 0.0 copy-done
  44.0 0.0 collective-permute-done.2.got_z
  44.0 0.0 collective-permute-done.3.back_z
  44.1 0.0 collective-permute-done.1.got_y
  44.1 0.0 collective-permute-done.got_x
  44.1 0.0 copy-done.2
  44.1 25.5 %border.1 = bf16[24,224,128]{2,1,0:T(8,128)(2,1)S(1)} custom-call(s32[7,4,6,8]{3,2,1,0:T(8,128)S(1)} %copy_add_fusion.keys, s32[24]{0:T(128)S(1)} %copy-done.2, s32[2]{0:T(128)S(1)} %pad_add_fusion.place_ref, bf16[6,4,64,128]{3,2,1,0:T(8,128)(2,1)S(1)} %collective-permute-done.got_x, bf16[4,4,64,128]{3,2,1,0:T(8,128)(2,1)S(1)} %collective-permute-done.1.got_y, ...), custom_call_target="tpu_custom_call" | custom-call | tf_op jit(solution)/shard_map/border/pallas_call | solution.py:399
  69.6 35.6 %all_to_all.5.rows_ref = bf16[24,224,128]{2,1,0:T(8,128)(2,1)S(1)} all-to-all(bf16[24,224,128]{2,1,0:T(8,128)(2,1)S(1)} %border.1), channel_id=1, replica_groups=mesh['gx'=2,'gy'=2,'gz'=8] {'gz'}, dimensions={0} | all-to-all | bytes 2752512 | tf_op jit(solution)/shard_map/all_to_all | solution.py:463
  105.2 2.6 %layout.1 = bf16[7,24,4096]{2,1,0:T(8,128)(2,1)} custom-call(s32[24]{0:T(128)S(1)} %iota.3.source, bf16[24,224,128]{2,1,0:T(8,128)(2,1)S(1)} %all_to_all.5.rows_ref), custom_call_target="tpu_custom_call" | custom-call | tf_op jit(solution)/shard_map/layout/pallas_call | solution.py:424
  (4 shorter events, 0.0 us)
Async XLA Ops:
  0.1 15.0 %copy-start.4 = (s32[4,6,8]{2,0,1:T(4,128)S(1)}, s32[4,6,8]{2,0,1:T(4,128)}, u32[]{:S(2)}) copy-start(s32[4,6,8]{2,0,1:T(4,128)} %param.9) | copy-start | bytes 2308
  0.1 15.0 %copy-start.3 = (s32[7,4,6,8]{3,1,2,0:T(4,128)S(1)}, s32[7,4,6,8]{3,1,2,0:T(4,128)}, u32[]{:S(2)}) copy-start(s32[7,4,6,8]{3,1,2,0:T(4,128)} %param.10) | copy-start | bytes 16132
  0.1 15.0 %copy-start.1 = (bf16[4,6,8,4096]{3,2,1,0:T(8,128)(2,1)S(1)}, bf16[4,6,8,4096]{3,2,1,0:T(8,128)(2,1)}, u32[]{:S(2)}) copy-start(bf16[4,6,8,4096]{3,2,1,0:T(8,128)(2,1)} %param.6) | copy-start | bytes 4718596
  7.0 37.0 %copy-start = (bf16[24,4,64,128]{3,2,1,0:T(8,128)(2,1)}, bf16[24,4,64,128]{3,2,1,0:T(8,128)(2,1)S(1)}, u32[]{:S(2)}) copy-start(bf16[24,4,64,128]{3,2,1,0:T(8,128)(2,1)S(1)} %get-tuple-element.26.stacked_ref.below_ref.stacked) | copy-start | bytes 4718596
  7.0 37.0 %collective-permute-start.2 = (bf16[12,64,128]{2,1,0:T(8,128)(2,1)S(1)}, bf16[12,64,128]{2,1,0:T(8,128)(2,1)S(1)}, u32[]{:S(2)}, u32[]{:S(2)}) collective-permute-start(bf16[12,64,128]{2,1,0:T(8,128)(2,1)S(1)} %get-tuple-element.20.first_z), channel_id=1, source_target_pairs={{1,0},{2,1},{3,2},{4,3},{5,4},{6,5},{7,6},{9,8},{10,9},{11,10},{12... | collective-permute-start | bytes 589832 | tf_op jit(solution)/shard_map/ppermute | solution.py:22
  8.3 35.8 %collective-permute-start = (bf16[6,4,64,128]{3,2,1,0:T(8,128)(2,1)S(1)}, bf16[6,4,64,128]{3,2,1,0:T(8,128)(2,1)S(1)}, u32[]{:S(2)}, u32[]{:S(2)}) collective-permute-start(bf16[6,4,64,128]{3,2,1,0:T(8,128)(2,1)S(1)} %get-tuple-element.18), channel_id=1, source_target_pairs={{0,16},{16,0},{1,17},{17,1},{2,18},{18,2},{3,19},{19,3},{4,20},{20... | collective-permute-start | bytes 1179656 | tf_op jit(solution)/shard_map/ppermute | solution.py:438
  8.4 35.7 %collective-permute-start.1 = (bf16[4,4,64,128]{3,2,1,0:T(8,128)(2,1)S(1)}, bf16[4,4,64,128]{3,2,1,0:T(8,128)(2,1)S(1)}, u32[]{:S(2)}, u32[]{:S(2)}) collective-permute-start(bf16[4,4,64,128]{3,2,1,0:T(8,128)(2,1)S(1)} %get-tuple-element.19), channel_id=1, source_target_pairs={{0,8},{8,0},{1,9},{9,1},{2,10},{10,2},{3,11},{11,3},{4,12},{12,4},... | collective-permute-start | bytes 786440 | tf_op jit(solution)/shard_map/ppermute | solution.py:438
  10.5 33.6 %collective-permute-start.3 = (bf16[12,64,128]{2,1,0:T(8,128)(2,1)S(1)}, bf16[12,64,128]{2,1,0:T(8,128)(2,1)S(1)}, u32[]{:S(2)}, u32[]{:S(2)}) collective-permute-start(bf16[12,64,128]{2,1,0:T(8,128)(2,1)S(1)} %get-tuple-element.21), channel_id=1, source_target_pairs={{0,1},{1,2},{2,3},{3,4},{4,5},{5,6},{6,7},{8,9},{9,10},{10,11},{11... | collective-permute-start | bytes 589832 | tf_op jit(solution)/shard_map/ppermute | solution.py:22
  15.1 29.0 %copy-start.2 = (s32[24]{0:T(128)S(1)}, s32[24]{0:T(128)}, u32[]{:S(2)}) copy-start(s32[24]{0:T(128)} %owners.1) | copy-start | bytes 292

commit v2 on v1

v2 whole, which is shorter than its diff:
```python
import functools

import jax
import jax.numpy as jnp
from jax import lax
from jax.experimental import pallas as pl
from jax.experimental.pallas import tpu as pltpu
from jax.sharding import PartitionSpec as P

NODES = 64
SLOTS = 7
AGG_DEV = 24
LANES = 128
HALF = NODES // 2
VMEM_LIMIT = 48 * 1024 * 1024
STEP = 8


def passed_along(block, axis, distance):
    devices = range(lax.axis_size(axis))
    route = [(i - distance, i) for i in devices if i - distance in devices]
    return lax.ppermute(block, axis, route)


def low_lanes(rows):
    return lax.broadcasted_iota(jnp.int32, (rows, LANES), 1) < NODES


def swapped(value):
    return pltpu.roll(value, NODES, 1)


def spread(column, stage):
    depth = column.shape[0]
    for k in range(column.shape[1] // LANES):
        stage[depth * k : depth * (k + 1), :] = column[:, LANES * k : LANES * (k + 1)].astype(jnp.float32)


def block_of(stage, z, depth):
    return stage[pl.ds(z, HALF, stride=depth), :]


def stacked_pair(first, second):
    low = low_lanes(HALF)
    even = jnp.where(low, first, swapped(second))
    odd = jnp.where(low, swapped(first), second)
    return jnp.concatenate([even, odd], axis=0).astype(jnp.bfloat16)


def in_order(pair):
    row = lax.broadcasted_iota(jnp.int32, (NODES, NODES), 0)
    col = lax.broadcasted_iota(jnp.int32, (NODES, NODES), 1)
    move = (row == 2 * (col % HALF) + col // HALF).astype(jnp.bfloat16)
    return jnp.dot(move, pair, preferred_element_type=jnp.float32).astype(jnp.bfloat16)


def paired_weights(pair):
    low = low_lanes(NODES)
    zero = jnp.zeros_like(pair)
    first = jnp.where(low, pair, zero)
    second = jnp.where(low, zero, pair)
    left = jnp.concatenate([first, zero, second, zero], axis=0)
    right = jnp.concatenate([zero, first, zero, second], axis=0)
    return jnp.concatenate([left, right], axis=1)


def upright(product):
    return jnp.concatenate([product[:, :LANES], product[:, LANES:]], axis=0).astype(jnp.bfloat16)


def across(left, right):
    return lax.dot_general(left, right, (((0,), (0,)), ((), ())), preferred_element_type=jnp.float32)


def folded(square):
    low = low_lanes(HALF)
    moved = swapped(jnp.where(low, square[HALF : 2 * HALF], square[2 * HALF : 3 * HALF]))
    return (jnp.where(low, square[:HALF], moved), jnp.where(low, moved, square[3 * HALF :]))


def diagonal(square):
    return jnp.where(low_lanes(NODES), square[:NODES], square[NODES:]).astype(jnp.bfloat16)


def turned_pairs(first, second):
    row = lax.broadcasted_iota(jnp.int32, (LANES, LANES), 0)
    col = lax.broadcasted_iota(jnp.int32, (LANES, LANES), 1)
    return across(jnp.concatenate([first, second], axis=0), (row == col).astype(jnp.bfloat16)).astype(jnp.bfloat16)


def two_pairs(turned, first, second):
    zero = jnp.zeros_like(first)
    couples = jnp.concatenate([jnp.concatenate([first, zero], axis=1), jnp.concatenate([zero, second], axis=1)], axis=0)
    product = jnp.dot(turned, couples, preferred_element_type=jnp.float32)
    return folded(product[:, :LANES]) + folded(product[:, LANES:])


def put(stage, z, term):
    stage[pl.ds(z, HALF, stride=STEP), :] = term


def chosen(keys, rows):
    return (lax.broadcasted_iota(jnp.int32, (rows, keys.shape[1]), 0) == keys).astype(jnp.float32).astype(jnp.bfloat16)


def straightened(first, second):
    low = low_lanes(first.shape[0])
    return jnp.where(low, first, swapped(second)), jnp.where(low, swapped(first), second)


def prepare_kernel(place_ref, p_ref, fx_ref, fy_ref, fz_ref, natural_ref, turned_ref, shifted_ref, swap_x_ref, swap_y_ref, head_z_ref, rim_z_ref,
                   last_z_ref, tail_x_ref, tail_y_ref, tail_z_ref, stages, stages_f, stacks, ends):
    plane = pl.program_id(0)
    size_y, depth = p_ref.shape[0], p_ref.shape[1]
    pairs = depth // 2

    for j in range(size_y):
        stage = stages.at[j]
        spread(p_ref[j], stage)
        block = [block_of(stage, z, depth) for z in range(depth)]
        stacked = [stacked_pair(block[2 * p], block[2 * p + 1]) for p in range(pairs)]
        moved = [stacked_pair(block[(2 * p - 1) % depth], block[2 * p]) for p in range(pairs)]
        for p in range(pairs):
            stacks[j, p] = stacked[p]
            natural_ref[j, p] = in_order(stacked[p])
        for h in range(pairs // 2):
            turned_ref[j, h] = turned_pairs(stacked[2 * h], stacked[2 * h + 1])
            shifted_ref[j, h] = turned_pairs(moved[2 * h], moved[2 * h + 1])
        ends[0, j] = block[0]
        ends[1, j] = block[depth - 1]
        stage_f = stages_f.at[j]
        spread(fz_ref[0, j], stage_f)
        last = block_of(stage_f, depth - 1, depth)
        ends[2, j] = last
        tail_z_ref[j] = last.astype(jnp.bfloat16)

    for t in range(size_y // 2):
        first, last, face = [stacked_pair(ends[kind, 2 * t], ends[kind, 2 * t + 1]) for kind in range(3)]
        head_z_ref[t] = in_order(first)
        last_z_ref[t] = last
        rim_z_ref[t] = diagonal(across(face, last))

    def faces(source, stage, j, tails, rims):
        spread(source, stage)
        block = [block_of(stage, z, depth) for z in range(depth)]
        for z in range(depth):
            tails[z] = block[z].astype(jnp.bfloat16)
        for p in range(pairs):
            rims[p] = diagonal(across(stacked_pair(block[2 * p], block[2 * p + 1]), stacks[j, p]))

    @pl.when(place_ref[1] == 0)
    def _():
        faces(fy_ref[0, 0], stages_f.at[0], size_y - 1, tail_y_ref.at[0], swap_y_ref.at[0])

    @pl.when(place_ref[1] != 0)
    def _():
        swap_y_ref[0] = natural_ref[0]

    @pl.when((place_ref[0] == 0) & (plane == pl.num_programs(0) - 1))
    def _():
        for j in range(size_y):
            faces(fx_ref[0, j], stages_f.at[j], j, tail_x_ref.at[j], swap_x_ref.at[j])

    @pl.when((place_ref[0] != 0) & (plane == 0))
    def _():
        swap_x_ref[...] = natural_ref[...]


def prepare(place, prolong, faces, sizes):
    size_x, size_y, depth = sizes
    pairs, block = depth // 2, prolong.shape[-1]
    columns, half = size_x * size_y, size_y // 2
    shape = lambda *dims: jax.ShapeDtypeStruct(dims, jnp.bfloat16)
    by_half = pl.BlockSpec((half, NODES, LANES), lambda i: (i, 0, 0))
    by_plane = pl.BlockSpec((size_y, pairs // 2, LANES, LANES), lambda i: (i, 0, 0, 0))
    stage = pltpu.VMEM((size_y, depth * HALF, LANES), jnp.float32)
    return pl.pallas_call(
        prepare_kernel,
        grid=(size_x,),
        in_specs=[
            pl.BlockSpec(memory_space=pltpu.SMEM),
            pl.BlockSpec((size_y, depth, block), lambda i: (i, 0, 0)),
            pl.BlockSpec((1, size_y, depth, block), lambda i: (0, size_x - 1, 0, 0)),
            pl.BlockSpec((1, 1, depth, block), lambda i: (1, i * size_y + size_y - 1, 0, 0)),
            pl.BlockSpec((1, size_y, depth, block), lambda i: (2, i, 0, 0)),
        ],
        out_specs=[
            pl.BlockSpec((size_y, pairs, NODES, LANES), lambda i: (i, 0, 0, 0)),
            by_plane, by_plane,
            pl.BlockSpec((size_y, pairs, NODES, LANES), lambda i: (0, 0, 0, 0)),
            pl.BlockSpec((1, pairs, NODES, LANES), lambda i: (i, 0, 0, 0)),
            by_half, by_half, by_half,
            pl.BlockSpec((size_y, depth, HALF, LANES), lambda i: (0, 0, 0, 0)),
            pl.BlockSpec((1, depth, HALF, LANES), lambda i: (i, 0, 0, 0)),
            pl.BlockSpec((size_y, HALF, LANES), lambda i: (i, 0, 0)),
        ],
        out_shape=[
            shape(columns, pairs, NODES, LANES), shape(columns, pairs // 2, LANES, LANES), shape(columns, pairs // 2, LANES, LANES),
            shape(size_y, pairs, NODES, LANES), shape(size_x, pairs, NODES, LANES),
            shape(columns // 2, NODES, LANES), shape(columns // 2, NODES, LANES), shape(columns // 2, NODES, LANES),
            shape(size_y, depth, HALF, LANES), shape(size_x, depth, HALF, LANES), shape(columns, HALF, LANES),
        ],
        scratch_shapes=[
            stage, stage,
            pltpu.VMEM((size_y, pairs, NODES, LANES), jnp.bfloat16),
            pltpu.VMEM((3, size_y, HALF, LANES), jnp.float32),
        ],
        compiler_params=pltpu.CompilerParams(vmem_limit_bytes=VMEM_LIMIT),
        name="prepare",
    )(place, prolong, faces, faces, faces)


def interior_kernel(keys_ref, diag_ref, fx_ref, fy_ref, fz_ref, natural_ref, turned_ref, below_ref, shifted_ref, out_ref,
                    stages, terms, flat, behind, wide):
    plane = pl.program_id(0)
    size_y, depth = diag_ref.shape[0], diag_ref.shape[1]
    pairs = depth // 2
    groups = out_ref.shape[0]
    rows = groups * STEP

    def column(j, stage, term):
        row_y = jnp.maximum(j - 1, 0)
        for face, source in zip(range(4), (diag_ref[j], fx_ref[0, j], fy_ref[0, row_y], fz_ref[0, j])):
            spread(source, stage.at[face])
        couples = []
        for p in range(pairs):
            left = []
            for face in range(4):
                shift = 1 if face == 3 else 0
                sides = [block_of(stage.at[face], (2 * p + side - shift) % depth, depth).astype(jnp.bfloat16) for side in (0, 1)]
                left.append(jnp.concatenate(sides, axis=1))
            product = jnp.dot(
                jnp.concatenate(left, axis=0), paired_weights(natural_ref[j, p]), preferred_element_type=jnp.float32)
            couples.append([upright(product[HALF * face : HALF * (face + 1)]) for face in range(4)])
        for h in range(pairs // 2):
            turned = (turned_ref[j, h], below_ref[j, h], turned_ref[row_y, h], shifted_ref[j, h])
            for face in range(4):
                four = two_pairs(turned[face], couples[2 * h][face], couples[2 * h + 1][face])
                for z in range(4):
                    put(term.at[face], 4 * h + z, four[z])

    def columns(step, carry):
        for u in range(2):
            column(2 * step + u, stages.at[u], terms.at[u])
        for face in range(4):
            for k in range(HALF):
                both = [terms[u, face, STEP * k : STEP * (k + 1), :] for u in range(2)]
                flat[face, plane * (size_y // 2) + step, :, LANES * k : LANES * (k + 1)] = jnp.concatenate(both, axis=0).astype(jnp.bfloat16)
        return carry

    lax.fori_loop(0, size_y // 2, columns, 0)

    @pl.when(plane == pl.num_programs(0) - 1)
    def _():
        count = flat.shape[1] * flat.shape[2]
        ahead_keys = [chosen(keys_ref[face : face + 1, :], rows) for face in range(4)]
        behind_keys = [chosen(keys_ref[3 + face : 4 + face, :], rows) for face in range(1, 4)]

        def tiles(t, carry):
            lanes = pl.ds(pl.multiple_of(2 * LANES * t, 2 * LANES), 2 * LANES)
            part = [flat[face, :, :, lanes].reshape(count, 2 * LANES) for face in range(4)]
            ahead = jnp.zeros((rows, 2 * LANES), jnp.float32)
            for face in range(4):
                ahead += jnp.dot(ahead_keys[face], part[face], preferred_element_type=jnp.float32)
            upper, lower = straightened(ahead[:, :LANES], ahead[:, LANES:])
            out_ref[:, pl.ds(pl.multiple_of(STEP * t, STEP), STEP), :] = upper.reshape(groups, STEP, LANES)
            out_ref[:, pl.ds(pl.multiple_of(STEP * (t + HALF // 2), STEP), STEP), :] = lower.reshape(groups, STEP, LANES)
            back = jnp.zeros((rows, 2 * LANES), jnp.float32)
            for face in range(1, 4):
                back += jnp.dot(behind_keys[face - 1], part[face], preferred_element_type=jnp.float32)
            for side in (0, 1):
                behind[:, pl.ds(pl.multiple_of(STEP * (2 * t + side), STEP), STEP), :] = (
                    back[:, LANES * side : LANES * (side + 1)].reshape(groups, STEP, LANES))
            return carry

        lax.fori_loop(0, HALF // 2, tiles, 0)

        def turn(g, carry):
            low = low_lanes(HALF)
            for p in range(STEP // 2):
                one, two = [block_of(behind.at[g], 2 * p + side, STEP) for side in (0, 1)]
                upper = jnp.where(low, one, swapped(two))
                lower = jnp.where(low, swapped(one), two)
                wide[p, :, :NODES] = jnp.concatenate([upper, lower], axis=0).T
            for p in range(STEP // 2):
                for side in (0, 1):
                    even = wide[p, pl.ds(NODES * side, HALF, stride=2), :]
                    odd = wide[p, pl.ds(NODES * side + 1, HALF, stride=2), :]
                    where = pl.ds(2 * p + side, HALF, stride=STEP)
                    out_ref[g, where, :] = out_ref[g, where, :] + jnp.where(low, even, swapped(odd))
            return carry

        lax.fori_loop(0, groups, turn, 0)


def interior(keys, diag, faces, natural, turned, shifted, sizes):
    size_x, size_y, depth = sizes
    pairs, block = depth // 2, diag.shape[-1]
    columns, groups = size_x * size_y, AGG_DEV * SLOTS // STEP
    by_plane = lambda shift: pl.BlockSpec((size_y, pairs // 2, LANES, LANES), lambda i: (jnp.maximum(i - shift, 0), 0, 0, 0))
    spot = pltpu.VMEM((2, 4, depth * HALF, LANES), jnp.float32)
    total = (groups, STEP * HALF, LANES)
    return pl.pallas_call(
        interior_kernel,
        grid=(size_x,),
        in_specs=[
            pl.BlockSpec(keys.shape, lambda i: (0, 0)),
            pl.BlockSpec((size_y, depth, block), lambda i: (i, 0, 0)),
            pl.BlockSpec((1, size_y, depth, block), lambda i: (0, jnp.maximum(i - 1, 0), 0, 0)),
            pl.BlockSpec((1, size_y, depth, block), lambda i: (1, i, 0, 0)),
            pl.BlockSpec((1, size_y, depth, block), lambda i: (2, i, 0, 0)),
            pl.BlockSpec((size_y, pairs, NODES, LANES), lambda i: (i, 0, 0, 0)),
            by_plane(0), by_plane(1), by_plane(0),
        ],
        out_specs=pl.BlockSpec(total, lambda i: (0, 0, 0)),
        out_shape=jax.ShapeDtypeStruct(total, jnp.float32),
        scratch_shapes=[
            spot, spot,
            pltpu.VMEM((4, columns // 2, 2 * depth, block), jnp.bfloat16),
            pltpu.VMEM(total, jnp.float32),
            pltpu.VMEM((STEP // 2, LANES, LANES), jnp.float32),
        ],
        compiler_params=pltpu.CompilerParams(vmem_limit_bytes=VMEM_LIMIT),
        cost_estimate=pl.CostEstimate(flops=columns * depth * 14 * NODES**3, bytes_accessed=columns * depth * 6 * block * 2, transcendentals=0),
        name="interior",
    )(keys, diag, faces, faces, faces, natural, turned, turned, shifted)


def border_kernel(capacity, owners, place_ref, keys_ref, got_x, got_y, got_z, back_z, tail_x, tail_y, tail_z, turned_x, turned_y,
                  natural_x, natural_y, first_z, last_z, total_ref, out_ref, terms, flat, sums, filled):
    size_y, depth = tail_x.shape[0], tail_x.shape[1]
    size_x = tail_y.shape[0]
    pairs = depth // 2
    groups = total_ref.shape[0]
    rows = groups * STEP
    places = out_ref.shape[0]
    quarter = STEP // 2

    def couple(left0, left1, head):
        product = jnp.dot(jnp.concatenate([left0, left1], axis=1), paired_weights(head), preferred_element_type=jnp.float32)
        return upright(product)

    def ahead(tail, head, turned, term):
        couples = [couple(tail[2 * p], tail[2 * p + 1], head[p]) for p in range(pairs)]
        for h in range(pairs // 2):
            four = two_pairs(turned[h], couples[2 * h], couples[2 * h + 1])
            for z in range(4):
                put(term, 4 * h + z, four[z])

    def back(natural, rim, term):
        for p in range(pairs):
            two = folded(across(natural[p], rim[p]))
            for side in (0, 1):
                put(term, 2 * p + side, two[side])

    for first, count, axis, tail, got, turned, natural in (
            (0, size_y, 0, tail_x, got_x, turned_x, natural_x),
            (size_y, size_x, 1, tail_y, got_y, turned_y.at[:, 0], natural_y.at[:, 0])):
        @pl.when(place_ref[axis] == 0)
        def _():
            for j in range(count):
                ahead(tail.at[j], got.at[j], turned.at[j], terms.at[first + j])

        @pl.when(place_ref[axis] != 0)
        def _():
            for j in range(count):
                back(natural.at[j], got.at[j], terms.at[first + j])

    base = size_x + size_y
    columns_z = got_z.shape[0] // quarter
    for t in range(got_z.shape[0]):
        sums_z = folded(across(last_z[t], couple(tail_z[2 * t], tail_z[2 * t + 1], got_z[t])))
        past = folded(across(first_z[t], back_z[t]))
        for side in (0, 1):
            put(terms.at[base + t // quarter], 2 * (t % quarter) + side, sums_z[side])
            put(terms.at[base + columns_z + t // quarter], 2 * (t % quarter) + side, past[side])

    def pack(g, carry):
        for k in range(HALF):
            both = [terms[2 * g + u, STEP * k : STEP * (k + 1), :] for u in range(2)]
            flat[g, :, LANES * k : LANES * (k + 1)] = jnp.concatenate(both, axis=0).astype(jnp.bfloat16)
        return carry

    lax.fori_loop(0, flat.shape[0], pack, 0)
    picks = chosen(keys_ref[...], rows)

    def tiles(t, carry):
        lanes = pl.ds(pl.multiple_of(2 * LANES * t, 2 * LANES), 2 * LANES)
        part = flat[:, :, lanes].reshape(flat.shape[0] * flat.shape[1], 2 * LANES)
        extra = jnp.dot(picks, part, preferred_element_type=jnp.float32)
        for where, value in zip((t, t + HALF // 2), straightened(extra[:, :LANES], extra[:, LANES:])):
            spot = pl.ds(pl.multiple_of(STEP * where, STEP), STEP)
            sums[:, spot, :] = total_ref[:, spot, :] + value.reshape(groups, STEP, LANES)
        return carry

    lax.fori_loop(0, HALF // 2, tiles, 0)

    for owner in range(places // capacity):
        filled[owner] = 0
    if places * SLOTS != rows:
        out_ref[...] = jnp.zeros_like(out_ref)
    for r in range(rows // SLOTS):
        owner = owners[r]
        spot = owner * capacity + filled[owner]
        filled[owner] = filled[owner] + 1
        for s in range(SLOTS):
            key = r * SLOTS + s
            out_ref[spot, HALF * s : HALF * (s + 1), :] = block_of(sums.at[key // STEP], key % STEP, STEP).astype(jnp.bfloat16)


def border(owners, place, keys, operands, turned, natural, ends, capacity, places, sizes):
    size_x, size_y, depth = sizes
    pairs, groups = depth // 2, AGG_DEV * SLOTS // STEP
    count = keys.shape[1]
    smem = pl.BlockSpec(memory_space=pltpu.SMEM)
    whole = pl.BlockSpec(memory_space=pltpu.VMEM)
    planes = lambda array: array.reshape((size_x, size_y) + array.shape[1:])
    return pl.pallas_call(
        functools.partial(border_kernel, capacity),
        grid=(1,),
        in_specs=[smem, smem, whole] + [whole] * len(operands) + [
            pl.BlockSpec((size_y, pairs // 2, LANES, LANES), lambda i: (size_x - 1, 0, 0, 0)),
            pl.BlockSpec((size_x, 1, pairs // 2, LANES, LANES), lambda i: (0, size_y - 1, 0, 0, 0)),
            pl.BlockSpec((size_y, pairs, NODES, LANES), lambda i: (0, 0, 0, 0)),
            pl.BlockSpec((size_x, 1, pairs, NODES, LANES), lambda i: (0, 0, 0, 0, 0)),
        ] + [whole] * len(ends),
        out_specs=whole,
        out_shape=jax.ShapeDtypeStruct((places, SLOTS * HALF, LANES), jnp.bfloat16),
        scratch_shapes=[
            pltpu.VMEM((count // STEP, STEP * HALF, LANES), jnp.float32),
            pltpu.VMEM((count // (2 * STEP), 2 * STEP, HALF * LANES), jnp.bfloat16),
            pltpu.VMEM((groups, STEP * HALF, LANES), jnp.float32),
            pltpu.SMEM((places // capacity,), jnp.int32),
        ],
        compiler_params=pltpu.CompilerParams(vmem_limit_bytes=VMEM_LIMIT),
        name="border",
    )(owners, place, keys, *operands, turned, planes(turned), natural, planes(natural), *ends)


def layout_kernel(source, rows_ref, out_ref, stage):
    group = pl.program_id(0)
    height = out_ref.shape[1]
    for s in range(SLOTS):
        for r in range(height):
            row = source[group * height + r]
            block = rows_ref[jnp.maximum(row, 0), HALF * s : HALF * (s + 1), :].astype(jnp.float32)
            stage[s, pl.ds(r, HALF, stride=height), :] = jnp.where(row >= 0, block, jnp.zeros_like(block))
        for k in range(HALF):
            out_ref[s, :, LANES * k : LANES * (k + 1)] = stage[s, height * k : height * (k + 1), :].astype(jnp.bfloat16)


def laid_out(source, rows, block):
    places, height = rows.shape[0], 8
    return pl.pallas_call(
        layout_kernel,
        grid=(places // height,),
        in_specs=[pl.BlockSpec(memory_space=pltpu.SMEM), pl.BlockSpec(rows.shape, lambda g: (0, 0, 0))],
        out_specs=pl.BlockSpec((SLOTS, height, block), lambda g: (0, g, 0)),
        out_shape=jax.ShapeDtypeStruct((SLOTS, places, block), jnp.bfloat16),
        scratch_shapes=[pltpu.VMEM((SLOTS, height * HALF, LANES), jnp.float32)],
        compiler_params=pltpu.CompilerParams(vmem_limit_bytes=VMEM_LIMIT),
        name="layout",
    )(source, rows)


def swap(block, axis):
    assert lax.axis_size(axis) == 2
    return lax.ppermute(block, axis, [(0, 1), (1, 0)])


def pair_keys(keys, place):
    def moved(values, axis):
        return jnp.pad(values, [(1, 0) if dim == axis else (0, 0) for dim in range(3)], constant_values=-1)

    own = [keys[0]]
    own += [moved(lax.slice_in_dim(keys[2 * axis + 2], 0, -1, axis=axis), axis) for axis in range(3)]
    own += [moved(lax.slice_in_dim(keys[2 * axis + 1], 1, None, axis=axis), axis) for axis in range(3)]
    inner = jnp.stack(own).reshape(7, -1)
    outer = jnp.concatenate([
        jnp.where(place[0] == 0, keys[2, -1], keys[1, 0]).reshape(1, -1),
        jnp.where(place[1] == 0, keys[4, :, -1], keys[3, :, 0]).reshape(1, -1),
        keys[6, :, :, -1].reshape(1, -1),
        keys[5, :, :, 0].reshape(1, -1),
    ], axis=1)
    return inner, outer


def shards(a_diag, a_face, prolong, aggregate, pair_slot, row_owner):
    size_x, size_y, size_z, block = a_diag.shape
    sizes = (size_x, size_y, size_z)
    columns = size_x * size_y
    depth = lax.axis_size("gz")
    capacity = max(2, (AGG_DEV + depth - 1) // depth)
    holding = capacity * depth
    diag = a_diag.reshape(columns, size_z, block)
    faces = a_face.reshape(3, columns, size_z, block)
    place = jnp.stack([lax.axis_index("gx"), lax.axis_index("gy")]).astype(jnp.int32)
    inner_keys, outer_keys = pair_keys(aggregate[None] * SLOTS + pair_slot, place)

    natural, turned, shifted, swap_x, swap_y, head_z, rim_z, last_z, tail_x, tail_y, tail_z = prepare(
        place, prolong.reshape(columns, size_z, block), faces, sizes)
    got_z = passed_along(head_z, "gz", -1)
    back_z = passed_along(rim_z, "gz", 1)
    got_y = swap(swap_y, "gy")
    got_x = swap(swap_x, "gx")
    total = interior(inner_keys, diag, faces, natural, turned, shifted, sizes)
    outgoing = border(
        row_owner, place, outer_keys, (got_x, got_y, got_z, back_z, tail_x, tail_y, tail_z), turned, natural,
        (head_z, last_z, total), capacity, holding, sizes)
    arrived = lax.all_to_all(outgoing, "gz", 0, 0, tiled=True)
    source = jnp.arange(holding, dtype=jnp.int32)
    if holding != AGG_DEV:
        owner_ids = jnp.arange(depth, dtype=jnp.int32)
        counts = jnp.sum((row_owner[:, None] == owner_ids[None, :]).astype(jnp.int32), axis=0)
        arrived_counts = lax.all_to_all(counts, "gz", 0, 0, tiled=True)
        present = source % capacity < jnp.repeat(arrived_counts, capacity)
        target = jnp.cumsum(present.astype(jnp.int32)) - 1
        match = (present[None, :] & (target[None, :] == source[:, None])).astype(jnp.int32)
        source = jnp.sum(match * (source[None, :] + 1), axis=1) - 1
    result = laid_out(source, arrived, block)
    return jnp.transpose(result, (1, 0, 2)).reshape(1, 1, 1, holding, SLOTS, block)


def solution(mesh):
    return jax.shard_map(
        shards,
        mesh=mesh,
        in_specs=(
            P("gx", "gy", "gz", None),
            P(None, "gx", "gy", "gz", None),
            P("gx", "gy", "gz", None),
            P("gx", "gy", "gz"),
            P(None, "gx", "gy", "gz"),
            P(("gx", "gy", "gz")),
        ),
        out_specs=P("gx", "gy", "gz", None, None, None),
        check_vma=False,
    )
```

time: 108 us -> 133 us (1.23); the launches traced: 108 us -> 131 us
  local copies, waits for them, and re-layouts: 0.03 us -> 32 us
  Pallas kernels: 64 us -> 50.1 us
  other arithmetic: 0.1 us -> 2.77 us
  blocking collectives: 35.6 us -> 37.5 us
    pallas_call x2, Pallas kernels: 54.4 us -> 38.9 us  [the longest x1 27 us: interior(): pl.pallas_call(interior_kernel, grid=(size_x,), in_specs=[pl.BlockSpec(ke...]
    another operation x0 -> x10, local copies, waits for them, and re-layouts: none -> 12.4 us  [the longest x8 10.4 us: pair_keys(): inner = jnp.stack(own).reshape(7, -1)]
    slice x0 -> x8, local copies, waits for them, and re-layouts: none -> 6.85 us  [the longest x3 2.09 us: pair_keys(): lax.slice_in_dim(keys[2 * axis + 1], 1, None, axis=axis)]
    unnamed x10 -> x36, local copies, waits for them, and re-layouts: 0.02 us -> 5.68 us
    pad x0 -> x6, local copies, waits for them, and re-layouts: none -> 3.77 us  [moved(): jnp.pad(values, [(1, 0) if dim == axis else (0, 0) for dim in range(3)],...]
    select_n x0 -> x2, local copies, waits for them, and re-layouts: none -> 2.68 us  [the longest x1 1.34 us: pair_keys(): jnp.where(place[0] == 0, keys[2, -1], keys[1, 0]).reshape(1, -1)]
    select_n x0 -> x2, other arithmetic: none -> 2.6 us  [the longest x1 1.33 us: pair_keys(): jnp.where(place[0] == 0, keys[2, -1], keys[1, 0]).reshape(1, -1)]
    all_to_all x1, blocking collectives: 35.6 us -> 37.5 us  [shards(): arrived = lax.all_to_all(outgoing, 'gz', 0, 0, tiled=True)]
  transfers between devices with their start and end apart: 4 -> 4, of which waited for: 0 -> 0; matrix products, arithmetic and copies ran while one was open for 0% -> 24% of each run, Pallas kernels for 27% -> 21%
where the time goes in v2:
time: 133 us; the launch traced here: 131 us
  Pallas kernels  50.1 us (38%)
  blocking collectives  37.5 us (28%)
  local copies, waits for them, and re-layouts  32 us (24%)
  starting transfers between devices  8.62 us (6%)
  other arithmetic  2.77 us (2%)
    all_to_all x1, blocking collectives, shards(): arrived = lax.all_to_all(outgoing, 'gz', 0, 0, tiled=True)  37.5 us
    pallas_call x1, Pallas kernels, interior(): pl.pallas_call(interior_kernel, grid=(size_x,), in_specs=[pl.BlockSpec(ke...  27 us
    pallas_call x1, Pallas kernels, border(): pl.pallas_call(functools.partial(border_kernel, capacity), grid=(1,), in_...  11.9 us
    another operation x8, local copies, waits for them, and re-layouts, pair_keys(): inner = jnp.stack(own).reshape(7, -1)  10.4 us
    pallas_call x1, Pallas kernels, prepare(): pl.pallas_call(prepare_kernel, grid=(size_x,), in_specs=[pl.BlockSpec(mem...  8.49 us
    ppermute x2, starting transfers between devices, passed_along(): return lax.ppermute(block, axis, route)  6.5 us
    unnamed x36, local copies, waits for them, and re-layouts  5.68 us
    pad x6, local copies, waits for them, and re-layouts, moved(): jnp.pad(values, [(1, 0) if dim == axis else (0, 0) for dim in range(3)],...  3.77 us
  transfers between devices with their start and end apart: 4, of which 0 were waited for; matrix products, arithmetic and copies ran while one was open for 24% of the time, Pallas kernels for 21%

profile of v2, /device:TPU:0, one launch (start us, length us, event | category | flops | bytes accessed | tf_op | source)
XLA Modules:
  0.0 131.1 jit_solution(11965120429098983831)
XLA Ops:
  0.0 0.1 pad_add_fusion.place_ref
  0.1 8.5 %prepare.1 = (bf16[24,4,64,128]{3,2,1,0:T(8,128)(2,1)S(1)}, bf16[24,2,128,128]{3,2,1,0:T(8,128)(2,1)S(1)}, bf16[24,2,128,128]{3,2,1,0:T(8,128)(2,1)}, bf16[6,4,6...) custom-call(s32[2]{0:T(128)S(1)} %pad_add_fusion.place_ref, ...), custom_call_target="tpu_custom_call" | custom-call | tf_op jit(solution)/shard_map/prepare/pallas_call | solution.py:177
  8.6 0.0 copy-start.2
  8.6 0.7 copy-done.2
  9.3 0.7 copy-done.4
  10.0 0.7 copy-done.6
  10.7 1.3 collective-permute-start.2
  12.0 0.1 collective-permute-start
  12.1 2.1 %collective-permute-start.1 = (bf16[4,4,64,128]{3,2,1,0:T(8,128)(2,1)}, bf16[4,4,64,128]{3,2,1,0:T(8,128)(2,1)}, u32[]{:S(2)}, u32[]{:S(2)}) collective-permute-start(bf16[4,4,64,128]{3,2,1,0:T(8,128)(2,1)} %get-tuple-element.17), channel_id=1, source_target_pairs={{0,8},{8,0},{1,9},{9,1},{2,10},{10,2},{3,11},{11,3},{4,12},{12,4},... | collective-permute-start | bytes 786440 | tf_op jit(solution)/shard_map/ppermute | solution.py:468
  14.1 5.2 %collective-permute-start.3 = (bf16[12,64,128]{2,1,0:T(8,128)(2,1)}, bf16[12,64,128]{2,1,0:T(8,128)(2,1)}, u32[]{:S(2)}, u32[]{:S(2)}) collective-permute-start(bf16[12,64,128]{2,1,0:T(8,128)(2,1)} %get-tuple-element.19), channel_id=1, source_target_pairs={{0,1},{1,2},{2,3},{3,4},{4,5},{5,6},{6,7},{8,9},{9,10},{10,11},{11... | collective-permute-start | bytes 589832 | tf_op jit(solution)/shard_map/ppermute | solution.py:22
  19.3 0.0 copy-done.11
  19.3 0.0 copy-done.10
  19.4 0.0 copy-start.9
  19.4 0.7 slice_bitcast_fusion
  20.0 0.6 slice_bitcast_fusion.2
  20.6 0.0 copy-done.9
  20.6 0.7 fusion.1
  21.3 1.3 slice_select_fusion
  22.6 1.3 %fusion = s32[6,8]{1,0:T(8,128)} fusion(pred[]{:T(512)S(6)} %eq.6, s32[7,4,6,8]{3,1,2,0:T(4,128)} %bitcast.46), kind=kLoop, calls=%fused_computation.9 | loop fusion | flops 48 | bytes 577 | tf_op jit(solution)/shard_map/jit(_where)/select_n | solution.py:480
  23.9 0.8 slice.96
  24.7 0.7 pad.26.clone
  25.4 1.4 %stack.41 = s32[1,192]{1,0:T(1,128)} reshape(s32[4,6,8]{2,1,0:T(8,128)} %pad.26.clone) | data formatting | bytes 1536 | tf_op jit(solution)/shard_map/stack | solution.py:478
  26.7 0.7 slice.89
  27.5 0.6 pad.22.clone
  28.1 1.3 %stack.37 = s32[1,192]{1,0:T(1,128)} reshape(s32[4,6,8]{2,1,0:T(8,128)} %pad.22.clone) | data formatting | bytes 1536 | tf_op jit(solution)/shard_map/stack | solution.py:478
  29.4 0.7 slice.94
  30.1 0.6 pad.25.clone
  30.7 1.4 %stack.40 = s32[1,192]{1,0:T(1,128)} reshape(s32[4,6,8]{2,1,0:T(8,128)} %pad.25.clone) | data formatting | bytes 1536 | tf_op jit(solution)/shard_map/stack | solution.py:478
  32.1 0.7 copy.27
  32.8 0.7 pad.23.clone
  33.5 1.3 %stack.38 = s32[1,192]{1,0:T(1,128)} reshape(s32[4,6,8]{2,1,0:T(8,128)} %pad.23.clone) | data formatting | bytes 1536 | tf_op jit(solution)/shard_map/stack | solution.py:478
  34.9 1.3 copy.18
  36.2 1.4 %stack.35 = s32[1,192]{1,0:T(1,128)} reshape(s32[1,4,6,8]{3,2,1,0:T(8,128)} %copy.18) | data formatting | bytes 1536 | tf_op jit(solution)/shard_map/stack | solution.py:478
  37.5 0.7 copy.25
  38.2 0.6 pad.21.clone
  38.8 1.4 %stack.36 = s32[1,192]{1,0:T(1,128)} reshape(s32[4,6,8]{2,1,0:T(8,128)} %pad.21.clone) | data formatting | bytes 1536 | tf_op jit(solution)/shard_map/stack | solution.py:478
  40.2 0.7 copy.28
  41.0 0.6 pad.24.clone
  41.6 1.4 %stack.39 = s32[1,192]{1,0:T(1,128)} reshape(s32[4,6,8]{2,1,0:T(8,128)} %pad.24.clone) | data formatting | bytes 1536 | tf_op jit(solution)/shard_map/stack | solution.py:478
  42.9 1.3 %select_n.38 = s32[1,48]{1,0:T(1,128)} reshape(s32[6,8]{1,0:T(8,128)} %fusion) | data formatting | bytes 384 | tf_op jit(solution)/shard_map/jit(_where)/select_n | solution.py:480
  44.3 1.3 %select_n.41 = s32[1,32]{1,0:T(1,128)} reshape(s32[1,4,1,8]{3,1,2,0:T(4,128)} %slice_select_fusion) | data formatting | bytes 256 | tf_op jit(solution)/shard_map/jit(_where)/select_n | solution.py:481
  45.6 1.4 %copy.16 = s32[1,4,6,1]{2,1,3,0:T(4,128)} copy(s32[1,4,6,1]{3,1,2,0:T(4,128)} %get-tuple-element.34) | data formatting | bytes 192 | tf_op jit(solution)/shard_map/slice | solution.py:482
  47.0 1.3 reshape_squeeze.6
  48.3 0.7 copy.17
  49.0 0.8 reshape_squeeze.7
  49.7 0.7 stack.42.keys_ref
  50.5 0.0 copy-start.1
  50.5 1.4 %copy-done.1 = bf16[4,6,8,4096]{3,2,1,0:T(8,128)(2,1)S(1)} copy-done((bf16[4,6,8,4096]{3,2,1,0:T(8,128)(2,1)S(1)}, bf16[4,6,8,4096]{3,2,1,0:T(8,128)(2,1)}, u32[]{:S(2)}) %copy-start.1) | copy-done | bytes 1572888
  51.9 0.0 copy-start.5
  51.9 0.0 copy-start.7
  51.9 0.0 copy-start.8
  51.9 27.0 %interior.1.total_ref = f32[21,256,128]{2,1,0:T(8,128)} custom-call(s32[7,192]{1,0:T(8,128)S(1)} %stack.42.keys_ref, bf16[24,8,4096]{2,1,0:T(8,128)(2,1)S(1)} %bitcast.34, bf16[3,24,8,4096]{3,2,1,0:T(8,128)(2,1)} %bitcast.38, bf16[3,24,8,4096]{3,2,1,0:T(8,128)(2,1)} %bitcast.39, bf16[3,24,8,4096]{3,2,1,0:T(8,128)(2,1)} %bitcast.40, ...), custom_call_target="tpu_custom_call" | custom-call | flops 704643072 | bytes 9437184 | tf_op jit(solution)/shard_map/interior/pallas_call | solution.py:303
  78.9 0.0 copy-done
  78.9 0.0 copy-done.12
  78.9 0.0 copy-done.13
  78.9 0.0 copy-done.14
  78.9 0.1 pad_add_fusion.1.keys_ref
  79.0 0.0 collective-permute-done.2.got_z
  79.0 0.0 collective-permute-done.3.back_z
  79.0 0.0 collective-permute-done.1.got_y
  79.0 0.0 collective-permute-done.got_x
  79.1 11.9 %border.1 = bf16[24,224,128]{2,1,0:T(8,128)(2,1)S(1)} custom-call(s32[24]{0:T(128)S(1)} %copy-done.8, s32[2]{0:T(128)S(1)} %pad_add_fusion.place_ref, s32[1,128]{1,0:T(1,128)S(1)} %pad_add_fusion.1.keys_ref, bf16[6,4,64,128]{3,2,1,0:T(8,128)(2,1)} %collective-permute-done.got_x, bf16[4,4,64,128]{3,2,1,0:T(8,128)(2,1)} %collective-permute-done.1.got_y, ...), custom_call_target="tpu_custom_call" | custom-call | tf_op jit(solution)/shard_map/border/pallas_call | solution.py:418
  91.0 37.5 %all_to_all.5.rows_ref = bf16[24,224,128]{2,1,0:T(8,128)(2,1)S(1)} all-to-all(bf16[24,224,128]{2,1,0:T(8,128)(2,1)S(1)} %border.1), channel_id=1, replica_groups=mesh['gx'=2,'gy'=2,'gz'=8] {'gz'}, dimensions={0} | all-to-all | bytes 2752512 | tf_op jit(solution)/shard_map/all_to_all | solution.py:510
  128.5 2.6 %layout.1 = bf16[7,24,4096]{2,1,0:T(8,128)(2,1)} custom-call(s32[24]{0:T(128)S(1)} %iota.3.source, bf16[24,224,128]{2,1,0:T(8,128)(2,1)S(1)} %all_to_all.5.rows_ref), custom_call_target="tpu_custom_call" | custom-call | tf_op jit(solution)/shard_map/layout/pallas_call | solution.py:454
  (19 shorter events, 0.1 us)
Async XLA Ops:
  0.1 19.3 %copy-start.11 = (s32[4,6,8]{2,0,1:T(4,128)S(1)}, s32[4,6,8]{2,0,1:T(4,128)}, u32[]{:S(2)}) copy-start(s32[4,6,8]{2,0,1:T(4,128)} %param.9) | copy-start | bytes 2308
  0.1 19.3 %copy-start.10 = (s32[7,4,6,8]{3,1,2,0:T(4,128)S(1)}, s32[7,4,6,8]{3,1,2,0:T(4,128)}, u32[]{:S(2)}) copy-start(s32[7,4,6,8]{3,1,2,0:T(4,128)} %param.10) | copy-start | bytes 16132
  8.6 0.7 copy-start.2
  9.3 0.7 copy-start.4
  10.0 0.7 copy-start.6
  10.7 68.2 %copy-start = (bf16[24,4,64,128]{3,2,1,0:T(8,128)(2,1)}, bf16[24,4,64,128]{3,2,1,0:T(8,128)(2,1)S(1)}, u32[]{:S(2)}) copy-start(bf16[24,4,64,128]{3,2,1,0:T(8,128)(2,1)S(1)} %get-tuple-element.24.natural_ref.natural_x) | copy-start | bytes 4718596
  10.7 68.3 %collective-permute-start.2 = (bf16[12,64,128]{2,1,0:T(8,128)(2,1)}, bf16[12,64,128]{2,1,0:T(8,128)(2,1)}, u32[]{:S(2)}, u32[]{:S(2)}) collective-permute-start(bf16[12,64,128]{2,1,0:T(8,128)(2,1)} %get-tuple-element.18.first_z), channel_id=1, source_target_pairs={{1,0},{2,1},{3,2},{4,3},{5,4},{6,5},{7,6},{9,8},{10,9},{11,10},{12... | collective-permute-start | bytes 589832 | tf_op jit(solution)/shard_map/ppermute | solution.py:22
  12.0 67.1 %collective-permute-start = (bf16[6,4,64,128]{3,2,1,0:T(8,128)(2,1)}, bf16[6,4,64,128]{3,2,1,0:T(8,128)(2,1)}, u32[]{:S(2)}, u32[]{:S(2)}) collective-permute-start(bf16[6,4,64,128]{3,2,1,0:T(8,128)(2,1)} %get-tuple-element.16), channel_id=1, source_target_pairs={{0,16},{16,0},{1,17},{17,1},{2,18},{18,2},{3,19},{19,3},{4,20},{20... | collective-permute-start | bytes 1179656 | tf_op jit(solution)/shard_map/ppermute | solution.py:468
  12.1 67.0 %collective-permute-start.1 = (bf16[4,4,64,128]{3,2,1,0:T(8,128)(2,1)}, bf16[4,4,64,128]{3,2,1,0:T(8,128)(2,1)}, u32[]{:S(2)}, u32[]{:S(2)}) collective-permute-start(bf16[4,4,64,128]{3,2,1,0:T(8,128)(2,1)} %get-tuple-element.17), channel_id=1, source_target_pairs={{0,8},{8,0},{1,9},{9,1},{2,10},{10,2},{3,11},{11,3},{4,12},{12,4},... | collective-permute-start | bytes 786440 | tf_op jit(solution)/shard_map/ppermute | solution.py:468
  14.1 64.9 %collective-permute-start.3 = (bf16[12,64,128]{2,1,0:T(8,128)(2,1)}, bf16[12,64,128]{2,1,0:T(8,128)(2,1)}, u32[]{:S(2)}, u32[]{:S(2)}) collective-permute-start(bf16[12,64,128]{2,1,0:T(8,128)(2,1)} %get-tuple-element.19), channel_id=1, source_target_pairs={{0,1},{1,2},{2,3},{3,4},{4,5},{5,6},{6,7},{8,9},{9,10},{10,11},{11... | collective-permute-start | bytes 589832 | tf_op jit(solution)/shard_map/ppermute | solution.py:22
  19.4 1.3 copy-start.9
  50.5 1.4 %copy-start.1 = (bf16[4,6,8,4096]{3,2,1,0:T(8,128)(2,1)S(1)}, bf16[4,6,8,4096]{3,2,1,0:T(8,128)(2,1)}, u32[]{:S(2)}) copy-start(bf16[4,6,8,4096]{3,2,1,0:T(8,128)(2,1)} %param.6) | copy-start | bytes 4718596
  51.9 27.0 %copy-start.12 = (s32[1,48]{1,0:T(1,128)S(1)}, s32[1,48]{1,0:T(1,128)}, u32[]{:S(2)}) copy-start(s32[1,48]{1,0:T(1,128)} %select_n.38) | copy-start | bytes 580
  51.9 27.1 %copy-start.13 = (s32[1,32]{1,0:T(1,128)S(1)}, s32[1,32]{1,0:T(1,128)}, u32[]{:S(2)}) copy-start(s32[1,32]{1,0:T(1,128)} %select_n.41) | copy-start | bytes 388
  51.9 27.1 %copy-start.14 = (s32[1,24]{1,0:T(1,128)S(1)}, s32[1,24]{1,0:T(1,128)}, u32[]{:S(2)}) copy-start(s32[1,24]{1,0:T(1,128)} %reshape_squeeze.6) | copy-start | bytes 292
  51.9 27.2 %copy-start.3 = (bf16[4,8,32,128]{3,2,1,0:T(8,128)(2,1)S(1)}, bf16[4,8,32,128]{3,2,1,0:T(8,128)(2,1)}, u32[]{:S(2)}) copy-start(bf16[4,8,32,128]{3,2,1,0:T(8,128)(2,1)} %copy-done.2) | copy-start | bytes 786436
  51.9 27.2 %copy-start.5 = (bf16[12,64,128]{2,1,0:T(8,128)(2,1)S(1)}, bf16[12,64,128]{2,1,0:T(8,128)(2,1)}, u32[]{:S(2)}) copy-start(bf16[12,64,128]{2,1,0:T(8,128)(2,1)} %copy-done.4) | copy-start | bytes 589828
  51.9 27.2 %copy-start.7 = (bf16[24,32,128]{2,1,0:T(8,128)(2,1)S(1)}, bf16[24,32,128]{2,1,0:T(8,128)(2,1)}, u32[]{:S(2)}) copy-start(bf16[24,32,128]{2,1,0:T(8,128)(2,1)} %copy-done.6) | copy-start | bytes 589828
  51.9 27.2 %copy-start.8 = (s32[24]{0:T(128)S(1)}, s32[24]{0:T(128)}, u32[]{:S(2)}) copy-start(s32[24]{0:T(128)} %owners.1) | copy-start | bytes 292

commit v3 on v2

v3 whole, which is shorter than its diff:
```python
import functools

import jax
import jax.numpy as jnp
from jax import lax
from jax.experimental import pallas as pl
from jax.experimental.pallas import tpu as pltpu
from jax.sharding import PartitionSpec as P

NODES = 64
SLOTS = 7
AGG_DEV = 24
LANES = 128
HALF = NODES // 2
VMEM_LIMIT = 48 * 1024 * 1024
STEP = 8


def passed_along(block, axis, distance):
    devices = range(lax.axis_size(axis))
    route = [(i - distance, i) for i in devices if i - distance in devices]
    return lax.ppermute(block, axis, route)


def low_lanes(rows):
    return lax.broadcasted_iota(jnp.int32, (rows, LANES), 1) < NODES


def swapped(value):
    return pltpu.roll(value, NODES, 1)


def zero_one(mask):
    return mask.astype(jnp.float32).astype(jnp.bfloat16)


def grid_of(rows, cols):
    return lax.broadcasted_iota(jnp.int32, (rows, cols), 0), lax.broadcasted_iota(jnp.int32, (rows, cols), 1)


def to_blocks():
    row, col = grid_of(STEP * HALF, STEP * HALF)
    return zero_one(col == (row % HALF) * STEP + row // HALF)


def to_lines():
    row, col = grid_of(STEP * HALF, STEP * HALF)
    return zero_one(col == (row % STEP) * HALF + row // STEP)


def product(left, right):
    return jnp.dot(left, right, preferred_element_type=jnp.float32)


def across(left, right):
    return lax.dot_general(left, right, (((0,), (0,)), ((), ())), preferred_element_type=jnp.float32)


def tiled(column):
    tiles = [column[:, LANES * k : LANES * (k + 1)].astype(jnp.float32) for k in range(HALF)]
    return jnp.concatenate(tiles, axis=0).astype(jnp.bfloat16)


def blocks_of(move, first, second):
    rows = product(move, jnp.concatenate([first, second], axis=1))
    return [[rows[HALF * z : HALF * (z + 1), LANES * side : LANES * (side + 1)] for z in range(STEP)] for side in (0, 1)]


def lines_of(move, first, second):
    return product(move, jnp.concatenate([jnp.concatenate(first, axis=0), jnp.concatenate(second, axis=0)], axis=1))


def stacked_pair(first, second):
    low = low_lanes(HALF)
    even = jnp.where(low, first, swapped(second))
    odd = jnp.where(low, swapped(first), second)
    return jnp.concatenate([even, odd], axis=0).astype(jnp.bfloat16)


def in_order(pair):
    row, col = grid_of(NODES, NODES)
    return product(zero_one(row == 2 * (col % HALF) + col // HALF), pair).astype(jnp.bfloat16)


def paired_weights(pair):
    low = low_lanes(NODES)
    zero = jnp.zeros_like(pair)
    first = jnp.where(low, pair, zero)
    second = jnp.where(low, zero, pair)
    left = jnp.concatenate([first, zero, second, zero], axis=0)
    right = jnp.concatenate([zero, first, zero, second], axis=0)
    return jnp.concatenate([left, right], axis=1)


def upright(value):
    return jnp.concatenate([value[:, :LANES], value[:, LANES:]], axis=0).astype(jnp.bfloat16)


def folded(square):
    low = low_lanes(HALF)
    moved = swapped(jnp.where(low, square[HALF : 2 * HALF], square[2 * HALF : 3 * HALF]))
    return [jnp.where(low, square[:HALF], moved).astype(jnp.bfloat16), jnp.where(low, moved, square[3 * HALF :]).astype(jnp.bfloat16)]


def diagonal(square):
    return jnp.where(low_lanes(NODES), square[:NODES], square[NODES:]).astype(jnp.bfloat16)


def turned_pairs(first, second):
    row, col = grid_of(LANES, LANES)
    return across(jnp.concatenate([first, second], axis=0), zero_one(row == col)).astype(jnp.bfloat16)


def apart(first, second):
    zero = jnp.zeros_like(first)
    return jnp.concatenate([jnp.concatenate([first, zero], axis=1), jnp.concatenate([zero, second], axis=1)], axis=0)


def two_pairs(squares):
    return folded(squares[:, :LANES]) + folded(squares[:, LANES:])


def chosen(keys, rows):
    return zero_one(lax.broadcasted_iota(jnp.int32, (rows, keys.shape[1]), 0) == keys)


def straightened(first, second):
    low = low_lanes(first.shape[0])
    return jnp.where(low, first, swapped(second)), jnp.where(low, swapped(first), second)


def keys_along(keys_ref, number, width, target):
    _, size_x, size_y, depth = keys_ref.shape
    total = jnp.zeros((1, width), jnp.float32)
    z, lane_z = grid_of(depth, width)
    row, lane = grid_of(size_y, width)
    for i in range(size_x):
        reach_z, reach_y = target(i, row, z, lane, lane_z)
        if reach_z is None:
            continue
        keys = (keys_ref[number, i] + 1).astype(jnp.float32).astype(jnp.bfloat16)
        wide = product(keys, zero_one(reach_z))
        total += jnp.sum(jnp.where(reach_y, wide, 0.0), axis=0, keepdims=True)
    return total.astype(jnp.int32) - 1


def prepare_kernel(place_ref, p_ref, fx_ref, fy_ref, fz_ref, natural_ref, stacked_ref, moved_ref, turned_ref, shifted_ref,
                   swap_x_ref, swap_y_ref, head_z_ref, rim_z_ref, last_z_ref, tail_x_ref, tail_y_ref, tail_z_ref, move_ref, ends):
    plane = pl.program_id(0)
    size_y, depth = p_ref.shape[0], p_ref.shape[1]
    pairs = depth // 2

    @pl.when(plane == 0)
    def _():
        move_ref[...] = to_blocks()

    for t in range(size_y // 2):
        both = blocks_of(move_ref[...], tiled(p_ref[2 * t]), tiled(p_ref[2 * t + 1]))
        faces_z = jnp.concatenate([tiled(fz_ref[0, 2 * t]), tiled(fz_ref[0, 2 * t + 1])], axis=1)
        last = product(move_ref[HALF * (depth - 1) : HALF * depth, :], faces_z)
        for side in (0, 1):
            j, block = 2 * t + side, both[side]
            stacked = [stacked_pair(block[2 * p], block[2 * p + 1]) for p in range(pairs)]
            moved = [stacked_pair(block[(2 * p - 1) % depth], block[2 * p]) for p in range(pairs)]
            for p in range(pairs):
                stacked_ref[j, p] = stacked[p]
                moved_ref[j, p] = moved[p]
                natural_ref[j, p] = in_order(stacked[p])
            for h in range(pairs // 2):
                turned_ref[j, h] = turned_pairs(stacked[2 * h], stacked[2 * h + 1])
                shifted_ref[j, h] = turned_pairs(moved[2 * h], moved[2 * h + 1])
            tail_z_ref[j] = last[:, LANES * side : LANES * (side + 1)].astype(jnp.bfloat16)
        head_z_ref[t] = in_order(stacked_pair(both[0][0], both[1][0]))
        end = stacked_pair(both[0][depth - 1], both[1][depth - 1])
        last_z_ref[t] = end
        rim_z_ref[t] = diagonal(across(stacked_pair(last[:, :LANES], last[:, LANES:]), end))

    def faces(block, j, tails, rims):
        for z in range(depth):
            tails[z] = block[z].astype(jnp.bfloat16)
        for p in range(pairs):
            rims[p] = diagonal(across(stacked_pair(block[2 * p], block[2 * p + 1]), stacked_ref[j, p]))

    @pl.when(place_ref[1] == 0)
    def _():
        source = tiled(fy_ref[0, 0])
        faces(blocks_of(move_ref[...], source, source)[0], size_y - 1, tail_y_ref.at[0], swap_y_ref.at[0])

    @pl.when(place_ref[1] != 0)
    def _():
        swap_y_ref[0] = natural_ref[0]

    @pl.when((place_ref[0] == 0) & (plane == pl.num_programs(0) - 1))
    def _():
        for t in range(size_y // 2):
            both = blocks_of(move_ref[...], tiled(fx_ref[0, 2 * t]), tiled(fx_ref[0, 2 * t + 1]))
            for side in (0, 1):
                faces(both[side], 2 * t + side, tail_x_ref.at[2 * t + side], swap_x_ref.at[2 * t + side])

    @pl.when((place_ref[0] != 0) & (plane == 0))
    def _():
        swap_x_ref[...] = natural_ref[...]


def prepare(place, prolong, faces, sizes):
    size_x, size_y, depth = sizes
    pairs, block = depth // 2, prolong.shape[-1]
    columns, half = size_x * size_y, size_y // 2
    shape = lambda *dims: jax.ShapeDtypeStruct(dims, jnp.bfloat16)
    by_half = pl.BlockSpec((half, NODES, LANES), lambda i: (i, 0, 0))
    by_plane = pl.BlockSpec((size_y, pairs, NODES, LANES), lambda i: (i, 0, 0, 0))
    by_square = pl.BlockSpec((size_y, pairs // 2, LANES, LANES), lambda i: (i, 0, 0, 0))
    all_pairs, all_squares = shape(columns, pairs, NODES, LANES), shape(columns, pairs // 2, LANES, LANES)
    edge = shape(columns // 2, NODES, LANES)
    return pl.pallas_call(
        prepare_kernel,
        grid=(size_x,),
        in_specs=[
            pl.BlockSpec(memory_space=pltpu.SMEM),
            pl.BlockSpec((size_y, depth, block), lambda i: (i, 0, 0)),
            pl.BlockSpec((1, size_y, depth, block), lambda i: (0, size_x - 1, 0, 0)),
            pl.BlockSpec((1, 1, depth, block), lambda i: (1, i * size_y + size_y - 1, 0, 0)),
            pl.BlockSpec((1, size_y, depth, block), lambda i: (2, i, 0, 0)),
        ],
        out_specs=[
            by_plane, by_plane, by_plane, by_square, by_square,
            pl.BlockSpec((size_y, pairs, NODES, LANES), lambda i: (0, 0, 0, 0)),
            pl.BlockSpec((1, pairs, NODES, LANES), lambda i: (i, 0, 0, 0)),
            by_half, by_half, by_half,
            pl.BlockSpec((size_y, depth, HALF, LANES), lambda i: (0, 0, 0, 0)),
            pl.BlockSpec((1, depth, HALF, LANES), lambda i: (i, 0, 0, 0)),
            pl.BlockSpec((size_y, HALF, LANES), lambda i: (i, 0, 0)),
        ],
        out_shape=[
            all_pairs, all_pairs, all_pairs, all_squares, all_squares,
            shape(size_y, pairs, NODES, LANES), shape(size_x, pairs, NODES, LANES), edge, edge, edge,
            shape(size_y, depth, HALF, LANES), shape(size_x, depth, HALF, LANES), shape(columns, HALF, LANES),
        ],
        scratch_shapes=[
            pltpu.VMEM((STEP * HALF, STEP * HALF), jnp.bfloat16),
            pltpu.VMEM((3, size_y, HALF, LANES), jnp.float32),
        ],
        compiler_params=pltpu.CompilerParams(vmem_limit_bytes=VMEM_LIMIT),
        name="prepare",
    )(place, prolong, faces, faces, faces)


def interior_kernel(keys_ref, diag_ref, fx_ref, fy_ref, fz_ref, natural_ref, stacked_ref, under_ref, moved_ref,
                    turned_ref, below_ref, shifted_ref, out_ref, blocks_ref, lines_ref, flat):
    plane = pl.program_id(0)
    size_y, depth = diag_ref.shape[0], diag_ref.shape[1]
    pairs = depth // 2
    groups = out_ref.shape[0]
    rows = groups * STEP

    @pl.when(plane == 0)
    def _():
        blocks_ref[...] = to_blocks()
        lines_ref[...] = to_lines()

    def column(j):
        row_y = jnp.maximum(j - 1, 0)
        sources = [tiled(source) for source in (diag_ref[j], fx_ref[0, j], fy_ref[0, row_y], fz_ref[0, j])]
        block = blocks_of(blocks_ref[...], sources[0], sources[1]) + blocks_of(blocks_ref[...], sources[2], sources[3])
        couples = []
        for p in range(pairs):
            left = []
            for face in range(4):
                shift = 1 if face == 3 else 0
                sides = [block[face][(2 * p + side - shift) % depth].astype(jnp.bfloat16) for side in (0, 1)]
                left.append(jnp.concatenate(sides, axis=1))
            pair = product(jnp.concatenate(left, axis=0), paired_weights(natural_ref[j, p]))
            couples.append([upright(pair[HALF * face : HALF * (face + 1)]) for face in range(4)])
        terms = [[] for _ in range(7)]
        for h in range(pairs // 2):
            turned = (turned_ref[j, h], below_ref[j, h], turned_ref[row_y, h], shifted_ref[j, h])
            straight = ((stacked_ref, j), (under_ref, j), (stacked_ref, row_y), (moved_ref, j))
            for face in range(4):
                first, second = couples[2 * h][face], couples[2 * h + 1][face]
                terms[face] += two_pairs(product(turned[face], apart(first, second)))
                if face:
                    source, at = straight[face]
                    weights = apart(source[at, 2 * h], source[at, 2 * h + 1])
                    terms[3 + face] += two_pairs(across(jnp.concatenate([first, second], axis=0), weights))
        return terms

    def columns(step, carry):
        both = [column(2 * step + u) for u in range(2)]
        for number in range(7):
            lines = lines_of(lines_ref[...], both[0][number], both[1][number])
            for k in range(HALF):
                part = lines[STEP * k : STEP * (k + 1)]
                line = jnp.concatenate([part[:, :LANES], part[:, LANES:]], axis=0).astype(jnp.bfloat16)
                flat[number, plane * (size_y // 2) + step, :, LANES * k : LANES * (k + 1)] = line
        return carry

    lax.fori_loop(0, size_y // 2, columns, 0)

    @pl.when(plane == pl.num_programs(0) - 1)
    def _():
        count = flat.shape[1] * flat.shape[2]

        def keys_of(number, step, least):
            def target(i, row, z, lane, lane_z):
                if i < least[0] or i + step[0] >= keys_ref.shape[1]:
                    return None, None
                here = (lane // (depth * size_y) == i + step[0]) & (lane // depth % size_y == row + step[1]) & (row >= least[1])
                return (lane_z % depth == z + step[2]) & (z >= least[2]), here

            return chosen(keys_along(keys_ref, number, count, target), rows)

        none = (0, 0, 0)
        unit = ((1, 0, 0), (0, 1, 0), (0, 0, 1))
        picks = [keys_of(0, none, none)]
        picks += [keys_of(2 * axis + 2, unit[axis], none) for axis in range(3)]
        picks += [keys_of(2 * axis + 1, none, unit[axis]) for axis in range(3)]

        def tiles(t, carry):
            lanes = pl.ds(pl.multiple_of(2 * LANES * t, 2 * LANES), 2 * LANES)
            total = jnp.zeros((rows, 2 * LANES), jnp.float32)
            for number in range(7):
                total += product(picks[number], flat[number, :, :, lanes].reshape(count, 2 * LANES))
            upper, lower = straightened(total[:, :LANES], total[:, LANES:])
            out_ref[:, pl.ds(pl.multiple_of(STEP * t, STEP), STEP), :] = upper.reshape(groups, STEP, LANES)
            out_ref[:, pl.ds(pl.multiple_of(STEP * (t + HALF // 2), STEP), STEP), :] = lower.reshape(groups, STEP, LANES)
            return carry

        lax.fori_loop(0, HALF // 2, tiles, 0)


def interior(keys, diag, faces, natural, stacked, moved, turned, shifted, sizes):
    size_x, size_y, depth = sizes
    pairs, block = depth // 2, diag.shape[-1]
    columns, groups = size_x * size_y, AGG_DEV * SLOTS // STEP
    squares = lambda shift: pl.BlockSpec((size_y, pairs // 2, LANES, LANES), lambda i: (jnp.maximum(i - shift, 0), 0, 0, 0))
    planes = lambda shift: pl.BlockSpec((size_y, pairs, NODES, LANES), lambda i: (jnp.maximum(i - shift, 0), 0, 0, 0))
    total = (groups, STEP * HALF, LANES)
    move = pltpu.VMEM((STEP * HALF, STEP * HALF), jnp.bfloat16)
    return pl.pallas_call(
        interior_kernel,
        grid=(size_x,),
        in_specs=[
            pl.BlockSpec(keys.shape, lambda i: (0, 0, 0, 0)),
            pl.BlockSpec((size_y, depth, block), lambda i: (i, 0, 0)),
            pl.BlockSpec((1, size_y, depth, block), lambda i: (0, jnp.maximum(i - 1, 0), 0, 0)),
            pl.BlockSpec((1, size_y, depth, block), lambda i: (1, i, 0, 0)),
            pl.BlockSpec((1, size_y, depth, block), lambda i: (2, i, 0, 0)),
            planes(0), planes(0), planes(1), planes(0), squares(0), squares(1), squares(0),
        ],
        out_specs=pl.BlockSpec(total, lambda i: (0, 0, 0)),
        out_shape=jax.ShapeDtypeStruct(total, jnp.float32),
        scratch_shapes=[move, move, pltpu.VMEM((7, columns // 2, 2 * depth, block), jnp.bfloat16)],
        compiler_params=pltpu.CompilerParams(vmem_limit_bytes=VMEM_LIMIT),
        cost_estimate=pl.CostEstimate(flops=columns * depth * 14 * NODES**3, bytes_accessed=columns * depth * 6 * block * 2, transcendentals=0),
        name="interior",
    )(keys, diag, faces, faces, faces, natural, stacked, stacked, moved, turned, turned, shifted)


def border_kernel(capacity, owners, place_ref, keys_ref, got_x, got_y, got_z, back_z, tail_x, tail_y, tail_z, turned_x, turned_y,
                  natural_x, natural_y, first_z, last_z, total_ref, out_ref, terms, flat, sums, lane_keys, filled):
    size_y, depth = tail_x.shape[0], tail_x.shape[1]
    size_x = tail_y.shape[0]
    pairs = depth // 2
    groups = total_ref.shape[0]
    rows = groups * STEP
    places = out_ref.shape[0]
    quarter = STEP // 2
    width = lane_keys.shape[1]

    def couple(left0, left1, head):
        return upright(product(jnp.concatenate([left0, left1], axis=1), paired_weights(head)))

    def put(group, z, term):
        terms[group, HALF * z : HALF * (z + 1), :] = term

    def ahead(tail, head, turned, group):
        couples = [couple(tail[2 * p], tail[2 * p + 1], head[p]) for p in range(pairs)]
        for h in range(pairs // 2):
            four = two_pairs(product(turned[h], apart(couples[2 * h], couples[2 * h + 1])))
            for z in range(4):
                put(group, 4 * h + z, four[z])

    def back(natural, rim, group):
        for p in range(pairs):
            two = folded(across(natural[p], rim[p]))
            for side in (0, 1):
                put(group, 2 * p + side, two[side])

    def keys_x(number, at):
        def target(i, row, z, lane, lane_z):
            if i != at:
                return None, None
            return lane_z % depth == z, lane // depth == row

        return keys_along(keys_ref, number, width, target)

    def keys_y(number, at):
        def target(i, row, z, lane, lane_z):
            return lane_z % depth == z, (lane // depth == size_y + i) & (row == at)

        return keys_along(keys_ref, number, width, target)

    def keys_z(number, at, base):
        def target(i, row, z, lane, lane_z):
            return z == at, lane == base + size_y * i + row

        return keys_along(keys_ref, number, width, target)

    for first, count, axis, tail, got, turned, natural in (
            (0, size_y, 0, tail_x, got_x, turned_x, natural_x),
            (size_y, size_x, 1, tail_y, got_y, turned_y.at[:, 0], natural_y.at[:, 0])):
        @pl.when(place_ref[axis] == 0)
        def _():
            for j in range(count):
                ahead(tail.at[j], got.at[j], turned.at[j], first + j)
            lane_keys[axis : axis + 1, :] = keys_x(2, size_x - 1) if axis == 0 else keys_y(4, size_y - 1)

        @pl.when(place_ref[axis] != 0)
        def _():
            for j in range(count):
                back(natural.at[j], got.at[j], first + j)
            lane_keys[axis : axis + 1, :] = keys_x(1, 0) if axis == 0 else keys_y(3, 0)

    base = size_x + size_y
    columns_z = got_z.shape[0] // quarter
    for t in range(got_z.shape[0]):
        front = folded(across(last_z[t], couple(tail_z[2 * t], tail_z[2 * t + 1], got_z[t])))
        past = folded(across(first_z[t], back_z[t]))
        for side in (0, 1):
            put(base + t // quarter, 2 * (t % quarter) + side, front[side])
            put(base + columns_z + t // quarter, 2 * (t % quarter) + side, past[side])
    keys = jnp.maximum(lane_keys[0:1, :], lane_keys[1:2, :])
    keys = jnp.maximum(keys, keys_z(6, depth - 1, STEP * base))
    keys = jnp.maximum(keys, keys_z(5, 0, STEP * base + size_x * size_y))
    picks = chosen(keys, rows)

    lines_move = to_lines()
    for g in range(flat.shape[0]):
        lines = product(lines_move, jnp.concatenate([terms[2 * g], terms[2 * g + 1]], axis=1))
        for k in range(HALF):
            part = lines[STEP * k : STEP * (k + 1)]
            flat[g, :, LANES * k : LANES * (k + 1)] = jnp.concatenate([part[:, :LANES], part[:, LANES:]], axis=0).astype(jnp.bfloat16)

    def tiles(t, carry):
        lanes = pl.ds(pl.multiple_of(2 * LANES * t, 2 * LANES), 2 * LANES)
        extra = product(picks, flat[:, :, lanes].reshape(flat.shape[0] * flat.shape[1], 2 * LANES))
        for where, value in zip((t, t + HALF // 2), straightened(extra[:, :LANES], extra[:, LANES:])):
            spot = pl.ds(pl.multiple_of(STEP * where, STEP), STEP)
            sums[:, spot, :] = total_ref[:, spot, :] + value.reshape(groups, STEP, LANES)
        return carry

    lax.fori_loop(0, HALF // 2, tiles, 0)

    for owner in range(places // capacity):
        filled[owner] = 0
    if places * SLOTS != rows:
        out_ref[...] = jnp.zeros_like(out_ref)
    spots = []
    for r in range(rows // SLOTS):
        owner = owners[r]
        spots.append(owner * capacity + filled[owner])
        filled[owner] = filled[owner] + 1
    blocks_move = to_blocks()
    for g in range(0, groups, 2):
        other = min(g + 1, groups - 1)
        both = blocks_of(blocks_move, sums[g].astype(jnp.bfloat16), sums[other].astype(jnp.bfloat16))
        for side in range(other - g + 1):
            for z in range(STEP):
                key = STEP * (g + side) + z
                s = key % SLOTS
                out_ref[spots[key // SLOTS], HALF * s : HALF * (s + 1), :] = both[side][z].astype(jnp.bfloat16)


def border(owners, place, keys, operands, turned, natural, ends, capacity, places, sizes):
    size_x, size_y, depth = sizes
    pairs, groups = depth // 2, AGG_DEV * SLOTS // STEP
    count = STEP * (size_x + size_y) + 2 * size_x * size_y
    smem = pl.BlockSpec(memory_space=pltpu.SMEM)
    whole = pl.BlockSpec(memory_space=pltpu.VMEM)
    planes = lambda array: array.reshape((size_x, size_y) + array.shape[1:])
    return pl.pallas_call(
        functools.partial(border_kernel, capacity),
        grid=(1,),
        in_specs=[smem, smem, whole] + [whole] * len(operands) + [
            pl.BlockSpec((size_y, pairs // 2, LANES, LANES), lambda i: (size_x - 1, 0, 0, 0)),
            pl.BlockSpec((size_x, 1, pairs // 2, LANES, LANES), lambda i: (0, size_y - 1, 0, 0, 0)),
            pl.BlockSpec((size_y, pairs, NODES, LANES), lambda i: (0, 0, 0, 0)),
            pl.BlockSpec((size_x, 1, pairs, NODES, LANES), lambda i: (0, 0, 0, 0, 0)),
        ] + [whole] * len(ends),
        out_specs=whole,
        out_shape=jax.ShapeDtypeStruct((places, SLOTS * HALF, LANES), jnp.bfloat16),
        scratch_shapes=[
            pltpu.VMEM((count // STEP, STEP * HALF, LANES), jnp.bfloat16),
            pltpu.VMEM((count // (2 * STEP), 2 * STEP, HALF * LANES), jnp.bfloat16),
            pltpu.VMEM((groups, STEP * HALF, LANES), jnp.float32),
            pltpu.VMEM((2, count), jnp.int32),
            pltpu.SMEM((places // capacity,), jnp.int32),
        ],
        compiler_params=pltpu.CompilerParams(vmem_limit_bytes=VMEM_LIMIT),
        name="border",
    )(owners, place, keys, *operands, turned, planes(turned), natural, planes(natural), *ends)


def layout_kernel(source, rows_ref, out_ref):
    group = pl.program_id(0)
    move = to_lines()

    def blocks(s):
        found = []
        for r in range(STEP):
            row = source[group * STEP + r]
            block = rows_ref[jnp.maximum(row, 0), HALF * s : HALF * (s + 1), :]
            found.append(jnp.where(row >= 0, block, jnp.zeros_like(block)))
        return found

    for s in range(0, SLOTS, 2):
        other = min(s + 1, SLOTS - 1)
        lines = lines_of(move, blocks(s), blocks(other))
        for side in range(other - s + 1):
            for k in range(HALF):
                part = lines[STEP * k : STEP * (k + 1), LANES * side : LANES * (side + 1)]
                out_ref[s + side, :, LANES * k : LANES * (k + 1)] = part.astype(jnp.bfloat16)


def laid_out(source, rows, block):
    places = rows.shape[0]
    return pl.pallas_call(
        layout_kernel,
        grid=(places // STEP,),
        in_specs=[pl.BlockSpec(memory_space=pltpu.SMEM), pl.BlockSpec(rows.shape, lambda g: (0, 0, 0))],
        out_specs=pl.BlockSpec((SLOTS, STEP, block), lambda g: (0, g, 0)),
        out_shape=jax.ShapeDtypeStruct((SLOTS, places, block), jnp.bfloat16),
        compiler_params=pltpu.CompilerParams(vmem_limit_bytes=VMEM_LIMIT),
        name="layout",
    )(source, rows)


def swap(block, axis):
    assert lax.axis_size(axis) == 2
    return lax.ppermute(block, axis, [(0, 1), (1, 0)])


def shards(a_diag, a_face, prolong, aggregate, pair_slot, row_owner):
    size_x, size_y, size_z, block = a_diag.shape
    sizes = (size_x, size_y, size_z)
    columns = size_x * size_y
    depth = lax.axis_size("gz")
    capacity = max(2, (AGG_DEV + depth - 1) // depth)
    holding = capacity * depth
    diag = a_diag.reshape(columns, size_z, block)
    faces = a_face.reshape(3, columns, size_z, block)
    place = jnp.stack([lax.axis_index("gx"), lax.axis_index("gy")]).astype(jnp.int32)
    keys = aggregate[None] * SLOTS + pair_slot

    natural, stacked, moved, turned, shifted, swap_x, swap_y, head_z, rim_z, last_z, tail_x, tail_y, tail_z = prepare(
        place, prolong.reshape(columns, size_z, block), faces, sizes)
    got_z = passed_along(head_z, "gz", -1)
    back_z = passed_along(rim_z, "gz", 1)
    got_y = swap(swap_y, "gy")
    got_x = swap(swap_x, "gx")
    total = interior(keys, diag, faces, natural, stacked, moved, turned, shifted, sizes)
    outgoing = border(
        row_owner, place, keys, (got_x, got_y, got_z, back_z, tail_x, tail_y, tail_z), turned, natural,
        (head_z, last_z, total), capacity, holding, sizes)
    arrived = lax.all_to_all(outgoing, "gz", 0, 0, tiled=True)
    source = jnp.arange(holding, dtype=jnp.int32)
    if holding != AGG_DEV:
        owner_ids = jnp.arange(depth, dtype=jnp.int32)
        counts = jnp.sum((row_owner[:, None] == owner_ids[None, :]).astype(jnp.int32), axis=0)
        arrived_counts = lax.all_to_all(counts, "gz", 0, 0, tiled=True)
        present = source % capacity < jnp.repeat(arrived_counts, capacity)
        target = jnp.cumsum(present.astype(jnp.int32)) - 1
        match = (present[None, :] & (target[None, :] == source[:, None])).astype(jnp.int32)
        source = jnp.sum(match * (source[None, :] + 1), axis=1) - 1
    result = laid_out(source, arrived, block)
    return jnp.transpose(result, (1, 0, 2)).reshape(1, 1, 1, holding, SLOTS, block)


def solution(mesh):
    return jax.shard_map(
        shards,
        mesh=mesh,
        in_specs=(
            P("gx", "gy", "gz", None),
            P(None, "gx", "gy", "gz", None),
            P("gx", "gy", "gz", None),
            P("gx", "gy", "gz"),
            P(None, "gx", "gy", "gz"),
            P(("gx", "gy", "gz")),
        ),
        out_specs=P("gx", "gy", "gz", None, None, None),
        check_vma=False,
    )
```

time: 133 us -> 104 us (0.78); the launches traced: 131 us -> 104 us
  local copies, waits for them, and re-layouts: 32 us -> 0.03 us
  Pallas kernels: 50.1 us -> 57.5 us
  other arithmetic: 2.77 us -> 0.1 us
  starting transfers between devices: 8.62 us -> 7.16 us
    another operation x10 -> x0, local copies, waits for them, and re-layouts: 12.4 us -> none  [the longest x8 10.4 us: pair_keys(): inner = jnp.stack(own).reshape(7, -1)]
    slice x8 -> x0, local copies, waits for them, and re-layouts: 6.85 us -> none  [the longest x3 2.09 us: pair_keys(): lax.slice_in_dim(keys[2 * axis + 1], 1, None, axis=axis)]
    unnamed x36 -> x12, local copies, waits for them, and re-layouts: 5.68 us -> 0.03 us
    pallas_call x1, Pallas kernels: 27 us -> 31 us  [interior(): pl.pallas_call(interior_kernel, grid=(size_x,), in_specs=[pl.BlockSpec(ke...]
    pad x6 -> x0, local copies, waits for them, and re-layouts: 3.77 us -> none  [moved(): jnp.pad(values, [(1, 0) if dim == axis else (0, 0) for dim in range(3)],...]
    pallas_call x1, Pallas kernels: 8.49 us -> 11.9 us  [prepare(): pl.pallas_call(prepare_kernel, grid=(size_x,), in_specs=[pl.BlockSpec(mem...]
    select_n x2 -> x0, local copies, waits for them, and re-layouts: 2.68 us -> none  [the longest x1 1.34 us: pair_keys(): jnp.where(place[0] == 0, keys[2, -1], keys[1, 0]).reshape(1, -1)]
    select_n x2 -> x0, other arithmetic: 2.6 us -> none  [the longest x1 1.33 us: pair_keys(): jnp.where(place[0] == 0, keys[2, -1], keys[1, 0]).reshape(1, -1)]
  transfers between devices with their start and end apart: 4 -> 4, of which waited for: 0 -> 0; matrix products, arithmetic and copies ran while one was open for 24% -> 0% of each run, Pallas kernels for 21% -> 30%
where the time goes in v3:
time: 104 us
  Pallas kernels  57.5 us (55%)
  blocking collectives  38.6 us (37%)
  starting transfers between devices  7.16 us (7%)
    all_to_all x1, blocking collectives, shards(): arrived = lax.all_to_all(outgoing, 'gz', 0, 0, tiled=True)  38.6 us
    pallas_call x1, Pallas kernels, interior(): pl.pallas_call(interior_kernel, grid=(size_x,), in_specs=[pl.BlockSpec(ke...  31 us
    pallas_call x1, Pallas kernels, prepare(): pl.pallas_call(prepare_kernel, grid=(size_x,), in_specs=[pl.BlockSpec(mem...  11.9 us
    pallas_call x1, Pallas kernels, border(): pl.pallas_call(functools.partial(border_kernel, capacity), grid=(1,), in_...  11.8 us
    ppermute x2, starting transfers between devices, passed_along(): return lax.ppermute(block, axis, route)  5.83 us
    pallas_call x1, Pallas kernels, laid_out(): pl.pallas_call(layout_kernel, grid=(places // STEP,), in_specs=[pl.BlockS...  2.76 us
  transfers between devices with their start and end apart: 4, of which 0 were waited for; matrix products, arithmetic and copies ran while one was open for 0% of the time, Pallas kernels for 30%

profile of v3, /device:TPU:0, one launch (start us, length us, event | category | flops | bytes accessed | tf_op | source)
XLA Modules:
  0.0 103.6 jit_solution(12045699485739259822)
XLA Ops:
  0.0 0.1 pad_add_fusion.place_ref
  0.1 0.0 copy-start.5
  0.1 0.0 copy-start.4
  0.1 0.0 copy-start.2
  0.1 11.9 %prepare.1 = (bf16[24,4,64,128]{3,2,1,0:T(8,128)(2,1)S(1)}, bf16[24,4,64,128]{3,2,1,0:T(8,128)(2,1)S(1)}, bf16[24,4,64,128]{3,2,1,0:T(8,128)(2,1)}, bf16[24,2,12...) custom-call(s32[2]{0:T(128)S(1)} %pad_add_fusion.place_ref, ...), custom_call_target="tpu_custom_call" | custom-call | tf_op jit(solution)/shard_map/prepare/pallas_call | solution.py:215
  12.0 0.0 copy-start.1
  12.0 1.3 %collective-permute-start.2 = (bf16[12,64,128]{2,1,0:T(8,128)(2,1)S(1)}, bf16[12,64,128]{2,1,0:T(8,128)(2,1)S(1)}, u32[]{:S(2)}, u32[]{:S(2)}) collective-permute-start(bf16[12,64,128]{2,1,0:T(8,128)(2,1)S(1)} %get-tuple-element.20.first_z), channel_id=1, source_target_pairs={{1,0},{2,1},{3,2},{4,3},{5,4},{6,5},{7,6},{9,8},{10,9},{11,10},{12... | collective-permute-start | bytes 589832 | tf_op jit(solution)/shard_map/ppermute | solution.py:22
  13.3 0.1 collective-permute-start
  13.4 1.3 %collective-permute-start.1 = (bf16[4,4,64,128]{3,2,1,0:T(8,128)(2,1)S(1)}, bf16[4,4,64,128]{3,2,1,0:T(8,128)(2,1)S(1)}, u32[]{:S(2)}, u32[]{:S(2)}) collective-permute-start(bf16[4,4,64,128]{3,2,1,0:T(8,128)(2,1)S(1)} %get-tuple-element.19), channel_id=1, source_target_pairs={{0,8},{8,0},{1,9},{9,1},{2,10},{10,2},{3,11},{11,3},{4,12},{12,4},... | collective-permute-start | bytes 786440 | tf_op jit(solution)/shard_map/ppermute | solution.py:540
  14.6 4.5 %collective-permute-start.3 = (bf16[12,64,128]{2,1,0:T(8,128)(2,1)S(1)}, bf16[12,64,128]{2,1,0:T(8,128)(2,1)S(1)}, u32[]{:S(2)}, u32[]{:S(2)}) collective-permute-start(bf16[12,64,128]{2,1,0:T(8,128)(2,1)S(1)} %get-tuple-element.21), channel_id=1, source_target_pairs={{0,1},{1,2},{2,3},{3,4},{4,5},{5,6},{6,7},{8,9},{9,10},{10,11},{11... | collective-permute-start | bytes 589832 | tf_op jit(solution)/shard_map/ppermute | solution.py:22
  19.2 0.0 copy-done.5
  19.2 0.0 copy-done.4
  19.3 0.0 copy-done.2
  19.3 0.0 copy-start
  19.3 0.0 copy-start.3
  19.3 31.0 %interior.1.total_ref = f32[21,256,128]{2,1,0:T(8,128)} custom-call(s32[7,4,6,8]{3,2,1,0:T(8,128)S(1)} %copy_add_fusion.keys_ref, bf16[24,8,4096]{2,1,0:T(8,128)(2,1)S(1)} %bitcast.12, bf16[3,24,8,4096]{3,2,1,0:T(8,128)(2,1)} %bitcast.16, bf16[3,24,8,4096]{3,2,1,0:T(8,128)(2,1)} %bitcast.17, bf16[3,24,8,4096]{3,2,1,0:T(8,128)(2,1)} %bitcast.18, ...), custom_call_target="tpu_custom_call" | custom-call | flops 704643072 | bytes 9437184 | tf_op jit(solution)/shard_map/interior/pallas_call | solution.py:339
  50.3 0.0 copy-done.1
  50.3 0.0 collective-permute-done.2.got_z
  50.3 0.0 collective-permute-done.3.back_z
  50.3 0.0 collective-permute-done.1.got_y
  50.3 0.0 collective-permute-done.got_x
  50.3 0.0 copy-done
  50.4 0.0 copy-done.3
  50.4 11.8 %border.1 = bf16[24,224,128]{2,1,0:T(8,128)(2,1)S(1)} custom-call(s32[24]{0:T(128)S(1)} %copy-done.3, s32[2]{0:T(128)S(1)} %pad_add_fusion.place_ref, s32[7,4,6,8]{3,2,1,0:T(8,128)S(1)} %copy_add_fusion.keys_ref, bf16[6,4,64,128]{3,2,1,0:T(8,128)(2,1)S(1)} %collective-permute-done.got_x, bf16[4,4,64,128]{3,2,1,0:T(8,128)(2,1)S(1)} %collective-permute-done.1.got_y, ...), custom_call_target="tpu_custom_call" | custom-call | tf_op jit(solution)/shard_map/border/pallas_call | solution.py:481
  62.2 38.6 %all_to_all.5.rows_ref = bf16[24,224,128]{2,1,0:T(8,128)(2,1)S(1)} all-to-all(bf16[24,224,128]{2,1,0:T(8,128)(2,1)S(1)} %border.1), channel_id=1, replica_groups=mesh['gx'=2,'gy'=2,'gz'=8] {'gz'}, dimensions={0} | all-to-all | bytes 2752512 | tf_op jit(solution)/shard_map/all_to_all | solution.py:565
  100.9 2.8 %layout.1 = bf16[7,24,4096]{2,1,0:T(8,128)(2,1)} custom-call(s32[24]{0:T(128)S(1)} %iota.3.source, bf16[24,224,128]{2,1,0:T(8,128)(2,1)S(1)} %all_to_all.5.rows_ref), custom_call_target="tpu_custom_call" | custom-call | tf_op jit(solution)/shard_map/layout/pallas_call | solution.py:527
  (4 shorter events, 0.0 us)
Async XLA Ops:
  0.1 19.1 %copy-start.5 = (s32[4,6,8]{2,0,1:T(4,128)S(1)}, s32[4,6,8]{2,0,1:T(4,128)}, u32[]{:S(2)}) copy-start(s32[4,6,8]{2,0,1:T(4,128)} %param.9) | copy-start | bytes 2308
  0.1 19.1 %copy-start.4 = (s32[7,4,6,8]{3,1,2,0:T(4,128)S(1)}, s32[7,4,6,8]{3,1,2,0:T(4,128)}, u32[]{:S(2)}) copy-start(s32[7,4,6,8]{3,1,2,0:T(4,128)} %param.10) | copy-start | bytes 16132
  0.1 19.2 %copy-start.2 = (bf16[4,6,8,4096]{3,2,1,0:T(8,128)(2,1)S(1)}, bf16[4,6,8,4096]{3,2,1,0:T(8,128)(2,1)}, u32[]{:S(2)}) copy-start(bf16[4,6,8,4096]{3,2,1,0:T(8,128)(2,1)} %param.6) | copy-start | bytes 4718596
  12.0 38.3 %copy-start.1 = (bf16[24,4,64,128]{3,2,1,0:T(8,128)(2,1)}, bf16[24,4,64,128]{3,2,1,0:T(8,128)(2,1)S(1)}, u32[]{:S(2)}) copy-start(bf16[24,4,64,128]{3,2,1,0:T(8,128)(2,1)S(1)} %get-tuple-element.26.natural_ref.natural_x) | copy-start | bytes 4718596
  12.0 38.3 %collective-permute-start.2 = (bf16[12,64,128]{2,1,0:T(8,128)(2,1)S(1)}, bf16[12,64,128]{2,1,0:T(8,128)(2,1)S(1)}, u32[]{:S(2)}, u32[]{:S(2)}) collective-permute-start(bf16[12,64,128]{2,1,0:T(8,128)(2,1)S(1)} %get-tuple-element.20.first_z), channel_id=1, source_target_pairs={{1,0},{2,1},{3,2},{4,3},{5,4},{6,5},{7,6},{9,8},{10,9},{11,10},{12... | collective-permute-start | bytes 589832 | tf_op jit(solution)/shard_map/ppermute | solution.py:22
  13.3 37.0 %collective-permute-start = (bf16[6,4,64,128]{3,2,1,0:T(8,128)(2,1)S(1)}, bf16[6,4,64,128]{3,2,1,0:T(8,128)(2,1)S(1)}, u32[]{:S(2)}, u32[]{:S(2)}) collective-permute-start(bf16[6,4,64,128]{3,2,1,0:T(8,128)(2,1)S(1)} %get-tuple-element.18), channel_id=1, source_target_pairs={{0,16},{16,0},{1,17},{17,1},{2,18},{18,2},{3,19},{19,3},{4,20},{20... | collective-permute-start | bytes 1179656 | tf_op jit(solution)/shard_map/ppermute | solution.py:540
  13.4 37.0 %collective-permute-start.1 = (bf16[4,4,64,128]{3,2,1,0:T(8,128)(2,1)S(1)}, bf16[4,4,64,128]{3,2,1,0:T(8,128)(2,1)S(1)}, u32[]{:S(2)}, u32[]{:S(2)}) collective-permute-start(bf16[4,4,64,128]{3,2,1,0:T(8,128)(2,1)S(1)} %get-tuple-element.19), channel_id=1, source_target_pairs={{0,8},{8,0},{1,9},{9,1},{2,10},{10,2},{3,11},{11,3},{4,12},{12,4},... | collective-permute-start | bytes 786440 | tf_op jit(solution)/shard_map/ppermute | solution.py:540
  14.6 35.7 %collective-permute-start.3 = (bf16[12,64,128]{2,1,0:T(8,128)(2,1)S(1)}, bf16[12,64,128]{2,1,0:T(8,128)(2,1)S(1)}, u32[]{:S(2)}, u32[]{:S(2)}) collective-permute-start(bf16[12,64,128]{2,1,0:T(8,128)(2,1)S(1)} %get-tuple-element.21), channel_id=1, source_target_pairs={{0,1},{1,2},{2,3},{3,4},{4,5},{5,6},{6,7},{8,9},{9,10},{10,11},{11... | collective-permute-start | bytes 589832 | tf_op jit(solution)/shard_map/ppermute | solution.py:22
  19.3 31.1 %copy-start = (bf16[24,2,128,128]{3,2,1,0:T(8,128)(2,1)S(1)}, bf16[24,2,128,128]{3,2,1,0:T(8,128)(2,1)}, u32[]{:S(2)}) copy-start(bf16[24,2,128,128]{3,2,1,0:T(8,128)(2,1)} %get-tuple-element.25.turned_ref.below_ref.turned_x) | copy-start | bytes 4718596
  19.3 31.1 %copy-start.3 = (s32[24]{0:T(128)S(1)}, s32[24]{0:T(128)}, u32[]{:S(2)}) copy-start(s32[24]{0:T(128)} %owners.1) | copy-start | bytes 292

commit v4 on v1

v4 whole, which is shorter than its diff:
```python
import functools

import jax
import jax.numpy as jnp
from jax import lax
from jax.experimental import pallas as pl
from jax.experimental.pallas import tpu as pltpu
from jax.sharding import PartitionSpec as P

NODES = 64
SLOTS = 7
AGG_DEV = 24
LANES = 128
HALF = NODES // 2
VMEM_LIMIT = 48 * 1024 * 1024
STEP = 8


def passed_along(block, axis, distance):
    devices = range(lax.axis_size(axis))
    route = [(i - distance, i) for i in devices if i - distance in devices]
    return lax.ppermute(block, axis, route)


def low_lanes(rows):
    return lax.broadcasted_iota(jnp.int32, (rows, LANES), 1) < NODES


def swapped(value):
    return pltpu.roll(value, NODES, 1)


def zero_one(mask):
    return mask.astype(jnp.float32).astype(jnp.bfloat16)


def product(left, right):
    return jnp.dot(left, right, preferred_element_type=jnp.float32)


def across(left, right):
    return lax.dot_general(left, right, (((0,), (0,)), ((), ())), preferred_element_type=jnp.float32)


def spread(column, stage):
    depth = column.shape[0]
    for k in range(column.shape[1] // LANES):
        stage[depth * k : depth * (k + 1), :] = column[:, LANES * k : LANES * (k + 1)].astype(jnp.float32)


def block_of(stage, z, depth):
    return stage[pl.ds(z, HALF, stride=depth), :]


def stacked_pair(first, second):
    low = low_lanes(HALF)
    even = jnp.where(low, first, swapped(second))
    odd = jnp.where(low, swapped(first), second)
    return jnp.concatenate([even, odd], axis=0).astype(jnp.bfloat16)


def in_order(pair):
    row = lax.broadcasted_iota(jnp.int32, (NODES, NODES), 0)
    col = lax.broadcasted_iota(jnp.int32, (NODES, NODES), 1)
    return product(zero_one(row == 2 * (col % HALF) + col // HALF), pair).astype(jnp.bfloat16)


def paired_weights(pair):
    low = low_lanes(NODES)
    zero = jnp.zeros_like(pair)
    first = jnp.where(low, pair, zero)
    second = jnp.where(low, zero, pair)
    left = jnp.concatenate([first, zero, second, zero], axis=0)
    right = jnp.concatenate([zero, first, zero, second], axis=0)
    return jnp.concatenate([left, right], axis=1)


def upright(value):
    return jnp.concatenate([value[:, :LANES], value[:, LANES:]], axis=0)


def folded(square):
    low = low_lanes(HALF)
    moved = swapped(jnp.where(low, square[HALF : 2 * HALF], square[2 * HALF : 3 * HALF]))
    return [jnp.where(low, square[:HALF], moved), jnp.where(low, moved, square[3 * HALF :])]


def straightened(even, odd):
    low = low_lanes(HALF // 2)
    return jnp.concatenate([jnp.where(low, even, swapped(odd)), jnp.where(low, swapped(even), odd)], axis=0)


def diagonal(square):
    return jnp.where(low_lanes(NODES), square[:NODES], square[NODES:]).astype(jnp.bfloat16)


def apart(first, second):
    zero = jnp.zeros_like(first)
    return jnp.concatenate([jnp.concatenate([first, zero], axis=1), jnp.concatenate([zero, second], axis=1)], axis=0)


def two_pairs(squares):
    return folded(squares[:, :LANES]) + folded(squares[:, LANES:])


def add_all(updates):
    olds = [total[key] for total, key, _ in updates]
    news = []
    for number, (total, key, value) in enumerate(updates):
        for other, other_key, other_value in updates[:number]:
            if other is total:
                value = value + jnp.where(key == other_key, other_value, jnp.zeros_like(other_value))
        news.append(olds[number] + value)
    for (total, key, _), new in zip(updates, news):
        total[key] = new


def prepare_kernel(place_ref, p_ref, fx_ref, fy_ref, fz_ref, natural_ref, turned_ref, swap_x_ref, swap_y_ref, head_z_ref, rim_z_ref,
                   last_z_ref, tail_x_ref, tail_y_ref, tail_z_ref, stages, stages_f, stacks, ends):
    plane = pl.program_id(0)
    size_y, depth = p_ref.shape[0], p_ref.shape[1]
    pairs = depth // 2

    for j in range(size_y):
        stage = stages.at[j]
        spread(p_ref[j], stage)
        block = [block_of(stage, z, depth) for z in range(depth)]
        stacked = [stacked_pair(block[2 * p], block[2 * p + 1]) for p in range(pairs)]
        for p in range(pairs):
            stacks[j, p] = stacked[p]
            natural_ref[j, p] = in_order(stacked[p])
        for h in range(pairs // 2):
            turned_ref[j, h] = jnp.concatenate([stacked[2 * h], stacked[2 * h + 1]], axis=0).T
        ends[0, j] = block[0]
        ends[1, j] = block[depth - 1]
        stage_f = stages_f.at[j]
        spread(fz_ref[0, j], stage_f)
        last = block_of(stage_f, depth - 1, depth)
        ends[2, j] = last
        tail_z_ref[j] = last.astype(jnp.bfloat16)

    for t in range(size_y // 2):
        first, last, face = [stacked_pair(ends[kind, 2 * t], ends[kind, 2 * t + 1]) for kind in range(3)]
        head_z_ref[t] = in_order(first)
        last_z_ref[t] = last
        rim_z_ref[t] = diagonal(across(face, last))

    def faces(source, stage, j, tails, rims):
        spread(source, stage)
        block = [block_of(stage, z, depth) for z in range(depth)]
        for z in range(depth):
            tails[z] = block[z].astype(jnp.bfloat16)
        for p in range(pairs):
            rims[p] = diagonal(across(stacked_pair(block[2 * p], block[2 * p + 1]), stacks[j, p]))

    @pl.when(place_ref[1] == 0)
    def _():
        faces(fy_ref[0, 0], stages_f.at[0], size_y - 1, tail_y_ref.at[0], swap_y_ref.at[0])

    @pl.when(place_ref[1] != 0)
    def _():
        swap_y_ref[0] = natural_ref[0]

    @pl.when((place_ref[0] == 0) & (plane == pl.num_programs(0) - 1))
    def _():
        for j in range(size_y):
            faces(fx_ref[0, j], stages_f.at[j], j, tail_x_ref.at[j], swap_x_ref.at[j])

    @pl.when((place_ref[0] != 0) & (plane == 0))
    def _():
        swap_x_ref[...] = natural_ref[...]


def prepare(place, prolong, faces, sizes):
    size_x, size_y, depth = sizes
    pairs, block = depth // 2, prolong.shape[-1]
    columns, half = size_x * size_y, size_y // 2
    shape = lambda *dims: jax.ShapeDtypeStruct(dims, jnp.bfloat16)
    by_half = pl.BlockSpec((half, NODES, LANES), lambda i: (i, 0, 0))
    edge = shape(columns // 2, NODES, LANES)
    stage = pltpu.VMEM((size_y, depth * HALF, LANES), jnp.float32)
    return pl.pallas_call(
        prepare_kernel,
        grid=(size_x,),
        in_specs=[
            pl.BlockSpec(memory_space=pltpu.SMEM),
            pl.BlockSpec((size_y, depth, block), lambda i: (i, 0, 0)),
            pl.BlockSpec((1, size_y, depth, block), lambda i: (0, size_x - 1, 0, 0)),
            pl.BlockSpec((1, 1, depth, block), lambda i: (1, i * size_y + size_y - 1, 0, 0)),
            pl.BlockSpec((1, size_y, depth, block), lambda i: (2, i, 0, 0)),
        ],
        out_specs=[
            pl.BlockSpec((size_y, pairs, NODES, LANES), lambda i: (i, 0, 0, 0)),
            pl.BlockSpec((size_y, pairs // 2, LANES, LANES), lambda i: (i, 0, 0, 0)),
            pl.BlockSpec((size_y, pairs, NODES, LANES), lambda i: (0, 0, 0, 0)),
            pl.BlockSpec((1, pairs, NODES, LANES), lambda i: (i, 0, 0, 0)),
            by_half, by_half, by_half,
            pl.BlockSpec((size_y, depth, HALF, LANES), lambda i: (0, 0, 0, 0)),
            pl.BlockSpec((1, depth, HALF, LANES), lambda i: (i, 0, 0, 0)),
            pl.BlockSpec((size_y, HALF, LANES), lambda i: (i, 0, 0)),
        ],
        out_shape=[
            shape(columns, pairs, NODES, LANES), shape(columns, pairs // 2, LANES, LANES),
            shape(size_y, pairs, NODES, LANES), shape(size_x, pairs, NODES, LANES), edge, edge, edge,
            shape(size_y, depth, HALF, LANES), shape(size_x, depth, HALF, LANES), shape(columns, HALF, LANES),
        ],
        scratch_shapes=[
            stage, stage,
            pltpu.VMEM((size_y, pairs, NODES, LANES), jnp.bfloat16),
            pltpu.VMEM((3, size_y, HALF, LANES), jnp.float32),
        ],
        compiler_params=pltpu.CompilerParams(vmem_limit_bytes=VMEM_LIMIT),
        name="prepare",
    )(place, prolong, faces, faces, faces)


def interior_kernel(keys, diag_ref, fx_ref, fy_ref, fz_ref, natural_ref, turned_ref, below_ref, out_ref,
                    stages, ahead_even, ahead_odd, behind_even, behind_odd, wide):
    plane = pl.program_id(0)
    size_y, depth = diag_ref.shape[0], diag_ref.shape[1]
    pairs = depth // 2
    spare = out_ref.shape[0]
    ahead, behind = (ahead_even, ahead_odd), (behind_even, behind_odd)
    row_x = jnp.maximum(plane - 1, 0)
    has_x = plane > 0

    @pl.when(plane == 0)
    def _():
        for total in ahead + behind:
            total[...] = jnp.zeros_like(total)

    def couplings(j, stage):
        row_y = jnp.maximum(j - 1, 0)
        for face, source in zip(range(4), (diag_ref[j], fx_ref[0, j], fy_ref[0, row_y], fz_ref[0, j])):
            spread(source, stage.at[face])
        couples = [[] for _ in range(4)]
        for p in range(pairs):
            left = []
            for face in range(4):
                shift = 1 if face == 3 else 0
                sides = [block_of(stage.at[face], (2 * p + side - shift) % depth, depth).astype(jnp.bfloat16) for side in (0, 1)]
                left.append(jnp.concatenate(sides, axis=1))
            pair = product(jnp.concatenate(left, axis=0), paired_weights(natural_ref[j, p]))
            for face in range(4):
                couple = upright(pair[HALF * face : HALF * (face + 1)])
                couples[face].append(swapped(couple) if face == 3 else couple.astype(jnp.bfloat16))
        low = low_lanes(NODES)
        along = couples[3]
        couples[3] = [jnp.where(low, along[p], along[min(p + 1, pairs - 1)]).astype(jnp.bfloat16) for p in range(pairs)]
        return couples

    def sums(j, couples):
        row_y = jnp.maximum(j - 1, 0)
        has_y = j > 0
        for h in range(pairs // 2):
            turned = (turned_ref[j, h], below_ref[j, h], turned_ref[row_y, h], turned_ref[j, h])
            for face in range(4):
                four = two_pairs(product(turned[face], apart(couples[face][2 * h], couples[face][2 * h + 1])))
                updates = []
                for number, term in enumerate(four):
                    z, side = 4 * h + number, number % 2
                    if face == 0:
                        updates.append((ahead[side], keys[0, plane, j, z], term))
                        continue
                    if face == 1:
                        here, there = keys[2, row_x, j, z], keys[1, plane, j, z]
                        here, there = jnp.where(has_x, here, spare), jnp.where(has_x, there, spare)
                    elif face == 2:
                        here, there = keys[4, plane, row_y, z], keys[3, plane, j, z]
                        here, there = jnp.where(has_y, here, spare), jnp.where(has_y, there, spare)
                    elif z + 1 < depth:
                        here, there = keys[6, plane, j, z], keys[5, plane, j, z + 1]
                    else:
                        continue
                    updates.append((ahead[side], here, term))
                    updates.append((behind[side], there, term))
                add_all(updates)

    def columns(step, carry):
        couples = [couplings(2 * step + u, stages.at[u]) for u in range(2)]
        for u in range(2):
            sums(2 * step + u, couples[u])
        return carry

    lax.fori_loop(0, size_y // 2, columns, 0)

    @pl.when(plane == pl.num_programs(0) - 1)
    def _():
        def finish(g, carry):
            low = low_lanes(HALF)
            for p in range(STEP // 2):
                one, two = [behind_even[STEP * g + 2 * p + side] + behind_odd[STEP * g + 2 * p + side] for side in (0, 1)]
                upper = jnp.where(low, one, swapped(two))
                lower = jnp.where(low, swapped(one), two)
                wide[p, :, :NODES] = jnp.concatenate([upper, lower], axis=0).T
            for p in range(STEP // 2):
                for side in (0, 1):
                    key = STEP * g + 2 * p + side
                    even, odd = [
                        ahead_even[key, pl.ds(first, HALF // 2, stride=2), :] + ahead_odd[key, pl.ds(first, HALF // 2, stride=2), :]
                        for first in (0, 1)]
                    turned = [wide[p, pl.ds(NODES * side + first, HALF, stride=2), :] for first in (0, 1)]
                    out_ref[key] = straightened(even, odd) + jnp.where(low, turned[0], swapped(turned[1]))
            return carry

        lax.fori_loop(0, spare // STEP, finish, 0)


def interior(keys, diag, faces, natural, turned, sizes):
    size_x, size_y, depth = sizes
    pairs, block = depth // 2, diag.shape[-1]
    columns, rows = size_x * size_y, AGG_DEV * SLOTS
    squares = lambda shift: pl.BlockSpec((size_y, pairs // 2, LANES, LANES), lambda i: (jnp.maximum(i - shift, 0), 0, 0, 0))
    total = pltpu.VMEM((rows + 1, HALF, LANES), jnp.float32)
    return pl.pallas_call(
        interior_kernel,
        grid=(size_x,),
        in_specs=[
            pl.BlockSpec(memory_space=pltpu.SMEM),
            pl.BlockSpec((size_y, depth, block), lambda i: (i, 0, 0)),
            pl.BlockSpec((1, size_y, depth, block), lambda i: (0, jnp.maximum(i - 1, 0), 0, 0)),
            pl.BlockSpec((1, size_y, depth, block), lambda i: (1, i, 0, 0)),
            pl.BlockSpec((1, size_y, depth, block), lambda i: (2, i, 0, 0)),
            pl.BlockSpec((size_y, pairs, NODES, LANES), lambda i: (i, 0, 0, 0)),
            squares(0), squares(1),
        ],
        out_specs=pl.BlockSpec((rows, HALF, LANES), lambda i: (0, 0, 0)),
        out_shape=jax.ShapeDtypeStruct((rows, HALF, LANES), jnp.float32),
        scratch_shapes=[
            pltpu.VMEM((2, 4, depth * HALF, LANES), jnp.float32), total, total, total, total,
            pltpu.VMEM((STEP // 2, LANES, LANES), jnp.float32),
        ],
        compiler_params=pltpu.CompilerParams(vmem_limit_bytes=VMEM_LIMIT),
        cost_estimate=pl.CostEstimate(flops=columns * depth * 14 * NODES**3, bytes_accessed=columns * depth * 6 * block * 2, transcendentals=0),
        name="interior",
    )(keys, diag, faces, faces, faces, natural, turned, turned)


def border_kernel(capacity, owners, place_ref, keys, got_x, got_y, got_z, back_z, tail_x, tail_y, tail_z, turned_x, turned_y,
                  natural_x, natural_y, first_z, last_z, total_ref, out_ref, even_total, odd_total, filled):
    size_y, depth = tail_x.shape[0], tail_x.shape[1]
    size_x = tail_y.shape[0]
    pairs = depth // 2
    rows = total_ref.shape[0]
    places = out_ref.shape[0]
    totals = (even_total, odd_total)

    for total in totals:
        total[...] = jnp.zeros_like(total)

    def couple(left0, left1, head):
        return upright(product(jnp.concatenate([left0, left1], axis=1), paired_weights(head))).astype(jnp.bfloat16)

    def ahead(tail, head, turned, key):
        couples = [couple(tail[2 * p], tail[2 * p + 1], head[p]) for p in range(pairs)]
        for h in range(pairs // 2):
            four = two_pairs(product(turned[h], apart(couples[2 * h], couples[2 * h + 1])))
            add_all([(totals[number % 2], key(4 * h + number), term) for number, term in enumerate(four)])

    def back(natural, rim, key):
        for h in range(pairs // 2):
            four = [term for p in (2 * h, 2 * h + 1) for term in folded(across(natural[p], rim[p]))]
            add_all([(totals[number % 2], key(4 * h + number), term) for number, term in enumerate(four)])

    @pl.when(place_ref[0] == 0)
    def _():
        for j in range(size_y):
            ahead(tail_x.at[j], got_x.at[j], turned_x.at[j], lambda z: keys[2, size_x - 1, j, z])

    @pl.when(place_ref[0] != 0)
    def _():
        for j in range(size_y):
            back(natural_x.at[j], got_x.at[j], lambda z: keys[1, 0, j, z])

    @pl.when(place_ref[1] == 0)
    def _():
        for i in range(size_x):
            ahead(tail_y.at[i], got_y.at[i], turned_y.at[i, 0], lambda z: keys[4, i, size_y - 1, z])

    @pl.when(place_ref[1] != 0)
    def _():
        for i in range(size_x):
            back(natural_y.at[i, 0], got_y.at[i], lambda z: keys[3, i, 0, z])

    for t in range(got_z.shape[0]):
        i, j = 2 * t // size_y, 2 * t % size_y
        front = folded(across(last_z[t], couple(tail_z[2 * t], tail_z[2 * t + 1], got_z[t])))
        past = folded(across(first_z[t], back_z[t]))
        add_all([(totals[side], keys[6, i, j + side, depth - 1], front[side]) for side in (0, 1)]
                + [(totals[side], keys[5, i, j + side, 0], past[side]) for side in (0, 1)])

    for owner in range(places // capacity):
        filled[owner] = 0
    if places * SLOTS != rows:
        out_ref[...] = jnp.zeros_like(out_ref)
    for r in range(rows // SLOTS):
        owner = owners[r]
        spot = owner * capacity + filled[owner]
        filled[owner] = filled[owner] + 1
        for s in range(SLOTS):
            key = r * SLOTS + s
            even, odd = [
                even_total[key, pl.ds(first, HALF // 2, stride=2), :] + odd_total[key, pl.ds(first, HALF // 2, stride=2), :]
                for first in (0, 1)]
            out_ref[spot, HALF * s : HALF * (s + 1), :] = (total_ref[key] + straightened(even, odd)).astype(jnp.bfloat16)


def border(owners, place, keys, operands, turned, natural, ends, capacity, places, sizes):
    size_x, size_y, depth = sizes
    pairs, rows = depth // 2, AGG_DEV * SLOTS
    smem = pl.BlockSpec(memory_space=pltpu.SMEM)
    whole = pl.BlockSpec(memory_space=pltpu.VMEM)
    planes = lambda array: array.reshape((size_x, size_y) + array.shape[1:])
    total = pltpu.VMEM((rows, HALF, LANES), jnp.float32)
    return pl.pallas_call(
        functools.partial(border_kernel, capacity),
        grid=(1,),
        in_specs=[smem, smem, smem] + [whole] * len(operands) + [
            pl.BlockSpec((size_y, pairs // 2, LANES, LANES), lambda i: (size_x - 1, 0, 0, 0)),
            pl.BlockSpec((size_x, 1, pairs // 2, LANES, LANES), lambda i: (0, size_y - 1, 0, 0, 0)),
            pl.BlockSpec((size_y, pairs, NODES, LANES), lambda i: (0, 0, 0, 0)),
            pl.BlockSpec((size_x, 1, pairs, NODES, LANES), lambda i: (0, 0, 0, 0, 0)),
        ] + [whole] * len(ends),
        out_specs=whole,
        out_shape=jax.ShapeDtypeStruct((places, SLOTS * HALF, LANES), jnp.bfloat16),
        scratch_shapes=[total, total, pltpu.SMEM((places // capacity,), jnp.int32)],
        compiler_params=pltpu.CompilerParams(vmem_limit_bytes=VMEM_LIMIT),
        name="border",
    )(owners, place, keys, *operands, turned, planes(turned), natural, planes(natural), *ends)


def layout_kernel(source, rows_ref, out_ref, stage):
    group = pl.program_id(0)
    height = out_ref.shape[1]
    for s in range(SLOTS):
        for r in range(height):
            row = source[group * height + r]
            block = rows_ref[jnp.maximum(row, 0), HALF * s : HALF * (s + 1), :].astype(jnp.float32)
            stage[s, pl.ds(r, HALF, stride=height), :] = jnp.where(row >= 0, block, jnp.zeros_like(block))
        for k in range(HALF):
            out_ref[s, :, LANES * k : LANES * (k + 1)] = stage[s, height * k : height * (k + 1), :].astype(jnp.bfloat16)


def laid_out(source, rows, block):
    places, height = rows.shape[0], 8
    return pl.pallas_call(
        layout_kernel,
        grid=(places // height,),
        in_specs=[pl.BlockSpec(memory_space=pltpu.SMEM), pl.BlockSpec(rows.shape, lambda g: (0, 0, 0))],
        out_specs=pl.BlockSpec((SLOTS, height, block), lambda g: (0, g, 0)),
        out_shape=jax.ShapeDtypeStruct((SLOTS, places, block), jnp.bfloat16),
        scratch_shapes=[pltpu.VMEM((SLOTS, height * HALF, LANES), jnp.float32)],
        compiler_params=pltpu.CompilerParams(vmem_limit_bytes=VMEM_LIMIT),
        name="layout",
    )(source, rows)


def swap(block, axis):
    assert lax.axis_size(axis) == 2
    return lax.ppermute(block, axis, [(0, 1), (1, 0)])


def shards(a_diag, a_face, prolong, aggregate, pair_slot, row_owner):
    size_x, size_y, size_z, block = a_diag.shape
    sizes = (size_x, size_y, size_z)
    columns = size_x * size_y
    depth = lax.axis_size("gz")
    capacity = max(2, (AGG_DEV + depth - 1) // depth)
    holding = capacity * depth
    diag = a_diag.reshape(columns, size_z, block)
    faces = a_face.reshape(3, columns, size_z, block)
    place = jnp.stack([lax.axis_index("gx"), lax.axis_index("gy")]).astype(jnp.int32)
    keys = aggregate[None] * SLOTS + pair_slot

    natural, turned, swap_x, swap_y, head_z, rim_z, last_z, tail_x, tail_y, tail_z = prepare(
        place, prolong.reshape(columns, size_z, block), faces, sizes)
    got_z = passed_along(head_z, "gz", -1)
    back_z = passed_along(rim_z, "gz", 1)
    got_y = swap(swap_y, "gy")
    got_x = swap(swap_x, "gx")
    total = interior(keys, diag, faces, natural, turned, sizes)
    outgoing = border(
        row_owner, place, keys, (got_x, got_y, got_z, back_z, tail_x, tail_y, tail_z), turned, natural,
        (head_z, last_z, total), capacity, holding, sizes)
    arrived = lax.all_to_all(outgoing, "gz", 0, 0, tiled=True)
    source = jnp.arange(holding, dtype=jnp.int32)
    if holding != AGG_DEV:
        owner_ids = jnp.arange(depth, dtype=jnp.int32)
        counts = jnp.sum((row_owner[:, None] == owner_ids[None, :]).astype(jnp.int32), axis=0)
        arrived_counts = lax.all_to_all(counts, "gz", 0, 0, tiled=True)
        present = source % capacity < jnp.repeat(arrived_counts, capacity)
        target = jnp.cumsum(present.astype(jnp.int32)) - 1
        match = (present[None, :] & (target[None, :] == source[:, None])).astype(jnp.int32)
        source = jnp.sum(match * (source[None, :] + 1), axis=1) - 1
    result = laid_out(source, arrived, block)
    return jnp.transpose(result, (1, 0, 2)).reshape(1, 1, 1, holding, SLOTS, block)


def solution(mesh):
    return jax.shard_map(
        shards,
        mesh=mesh,
        in_specs=(
            P("gx", "gy", "gz", None),
            P(None, "gx", "gy", "gz", None),
            P("gx", "gy", "gz", None),
            P("gx", "gy", "gz"),
            P(None, "gx", "gy", "gz"),
            P(("gx", "gy", "gz")),
        ),
        out_specs=P("gx", "gy", "gz", None, None, None),
        check_vma=False,
    )
```

time: 108 us -> 85.7 us (0.79)
  Pallas kernels: 64 us -> 39 us
  blocking collectives: 35.6 us -> 38.1 us
    pallas_call x1, Pallas kernels: 25.5 us -> 8.41 us  [border(): pl.pallas_call(functools.partial(border_kernel, capacity), grid=(1,), in_...]
    pallas_call x1, Pallas kernels: 28.9 us -> 21.5 us  [interior(): pl.pallas_call(interior_kernel, grid=(size_x,), in_specs=[pl.BlockSpec(me...]
    all_to_all x1, blocking collectives: 35.6 us -> 38.1 us  [shards(): arrived = lax.all_to_all(outgoing, 'gz', 0, 0, tiled=True)]
  transfers between devices with their start and end apart: 4 -> 4, of which waited for: 0 -> 0; matrix products, arithmetic and copies ran while one was open for 0% -> 0% of each run, Pallas kernels for 27% -> 25%
where the time goes in v4:
time: 85.7 us; the launch traced here: 85.5 us
  Pallas kernels  39 us (46%)
  blocking collectives  38.1 us (44%)
  starting transfers between devices  8.07 us (9%)
    all_to_all x1, blocking collectives, shards(): arrived = lax.all_to_all(outgoing, 'gz', 0, 0, tiled=True)  38.1 us
    pallas_call x1, Pallas kernels, interior(): pl.pallas_call(interior_kernel, grid=(size_x,), in_specs=[pl.BlockSpec(me...  21.5 us
    pallas_call x1, Pallas kernels, border(): pl.pallas_call(functools.partial(border_kernel, capacity), grid=(1,), in_...  8.41 us
    pallas_call x1, Pallas kernels, prepare(): pl.pallas_call(prepare_kernel, grid=(size_x,), in_specs=[pl.BlockSpec(mem...  6.53 us
    ppermute x2, starting transfers between devices, passed_along(): return lax.ppermute(block, axis, route)  5.84 us
    pallas_call x1, Pallas kernels, laid_out(): pl.pallas_call(layout_kernel, grid=(places // height,), in_specs=[pl.Bloc...  2.63 us
    ppermute x2, starting transfers between devices, swap(): return lax.ppermute(block, axis, [(0, 1), (1, 0)])  2.24 us
  transfers between devices with their start and end apart: 4, of which 0 were waited for; matrix products, arithmetic and copies ran while one was open for 0% of the time, Pallas kernels for 25%

profile of v4, /device:TPU:0, one launch (start us, length us, event | category | flops | bytes accessed | tf_op | source)
XLA Modules:
  0.0 85.5 jit_solution(1880058647610874841)
XLA Ops:
  0.0 0.1 pad_add_fusion.place_ref
  0.1 0.0 copy-start.4
  0.1 0.0 copy-start.3
  0.1 0.0 copy-start.1
  0.1 6.5 %prepare.1 = (bf16[24,4,64,128]{3,2,1,0:T(8,128)(2,1)S(1)}, bf16[24,2,128,128]{3,2,1,0:T(8,128)(2,1)S(1)}, bf16[6,4,64,128]{3,2,1,0:T(8,128)(2,1)S(1)}, bf16[4,4...) custom-call(s32[2]{0:T(128)S(1)} %pad_add_fusion.place_ref, ...), custom_call_target="tpu_custom_call" | custom-call | tf_op jit(solution)/shard_map/prepare/pallas_call | solution.py:182
  6.6 0.0 copy-start
  6.6 1.3 %collective-permute-start.2 = (bf16[12,64,128]{2,1,0:T(8,128)(2,1)S(1)}, bf16[12,64,128]{2,1,0:T(8,128)(2,1)S(1)}, u32[]{:S(2)}, u32[]{:S(2)}) collective-permute-start(bf16[12,64,128]{2,1,0:T(8,128)(2,1)S(1)} %get-tuple-element.17.first_z), channel_id=1, source_target_pairs={{1,0},{2,1},{3,2},{4,3},{5,4},{6,5},{7,6},{9,8},{10,9},{11,10},{12... | collective-permute-start | bytes 589832 | tf_op jit(solution)/shard_map/ppermute | solution.py:22
  7.9 0.1 collective-permute-start
  8.0 2.2 %collective-permute-start.1 = (bf16[4,4,64,128]{3,2,1,0:T(8,128)(2,1)S(1)}, bf16[4,4,64,128]{3,2,1,0:T(8,128)(2,1)S(1)}, u32[]{:S(2)}, u32[]{:S(2)}) collective-permute-start(bf16[4,4,64,128]{3,2,1,0:T(8,128)(2,1)S(1)} %get-tuple-element.16), channel_id=1, source_target_pairs={{0,8},{8,0},{1,9},{9,1},{2,10},{10,2},{3,11},{11,3},{4,12},{12,4},... | collective-permute-start | bytes 786440 | tf_op jit(solution)/shard_map/ppermute | solution.py:460
  10.2 4.5 %collective-permute-start.3 = (bf16[12,64,128]{2,1,0:T(8,128)(2,1)S(1)}, bf16[12,64,128]{2,1,0:T(8,128)(2,1)S(1)}, u32[]{:S(2)}, u32[]{:S(2)}) collective-permute-start(bf16[12,64,128]{2,1,0:T(8,128)(2,1)S(1)} %get-tuple-element.18), channel_id=1, source_target_pairs={{0,1},{1,2},{2,3},{3,4},{4,5},{5,6},{6,7},{8,9},{9,10},{10,11},{11... | collective-permute-start | bytes 589832 | tf_op jit(solution)/shard_map/ppermute | solution.py:22
  14.7 0.0 copy-done.4
  14.8 0.0 copy-done.3
  14.8 0.0 copy-done.1
  14.8 0.0 copy-start.2
  14.8 21.5 %interior.1.total_ref = f32[168,32,128]{2,1,0:T(8,128)} custom-call(s32[7,4,6,8]{3,2,1,0:T(8,128)S(1)} %copy_add_fusion.keys, bf16[24,8,4096]{2,1,0:T(8,128)(2,1)S(1)} %bitcast.12, bf16[3,24,8,4096]{3,2,1,0:T(8,128)(2,1)} %bitcast.16, bf16[3,24,8,4096]{3,2,1,0:T(8,128)(2,1)} %bitcast.17, bf16[3,24,8,4096]{3,2,1,0:T(8,128)(2,1)} %bitcast.18, ...), custom_call_target="tpu_custom_call" | custom-call | flops 704643072 | bytes 9437184 | tf_op jit(solution)/shard_map/interior/pallas_call | solution.py:315
  36.3 0.0 copy-done
  36.3 0.0 collective-permute-done.2.got_z
  36.3 0.0 collective-permute-done.3.back_z
  36.3 0.0 collective-permute-done.1.got_y
  36.3 0.0 collective-permute-done.got_x
  36.3 0.0 copy-done.2
  36.3 8.4 %border.1 = bf16[24,224,128]{2,1,0:T(8,128)(2,1)S(1)} custom-call(s32[24]{0:T(128)S(1)} %copy-done.2, s32[2]{0:T(128)S(1)} %pad_add_fusion.place_ref, s32[7,4,6,8]{3,2,1,0:T(8,128)S(1)} %copy_add_fusion.keys, bf16[6,4,64,128]{3,2,1,0:T(8,128)(2,1)S(1)} %collective-permute-done.got_x, bf16[4,4,64,128]{3,2,1,0:T(8,128)(2,1)S(1)} %collective-permute-done.1.got_y, ...), custom_call_target="tpu_custom_call" | custom-call | tf_op jit(solution)/shard_map/border/pallas_call | solution.py:415
  44.8 38.1 %all_to_all.5.rows_ref = bf16[24,224,128]{2,1,0:T(8,128)(2,1)S(1)} all-to-all(bf16[24,224,128]{2,1,0:T(8,128)(2,1)S(1)} %border.1), channel_id=1, replica_groups=mesh['gx'=2,'gy'=2,'gz'=8] {'gz'}, dimensions={0} | all-to-all | bytes 2752512 | tf_op jit(solution)/shard_map/all_to_all | solution.py:485
  82.8 2.6 %layout.1 = bf16[7,24,4096]{2,1,0:T(8,128)(2,1)} custom-call(s32[24]{0:T(128)S(1)} %iota.3.source, bf16[24,224,128]{2,1,0:T(8,128)(2,1)S(1)} %all_to_all.5.rows_ref), custom_call_target="tpu_custom_call" | custom-call | tf_op jit(solution)/shard_map/layout/pallas_call | solution.py:446
  (4 shorter events, 0.0 us)
Async XLA Ops:
  0.1 14.7 %copy-start.4 = (s32[4,6,8]{2,0,1:T(4,128)S(1)}, s32[4,6,8]{2,0,1:T(4,128)}, u32[]{:S(2)}) copy-start(s32[4,6,8]{2,0,1:T(4,128)} %param.9) | copy-start | bytes 2308
  0.1 14.7 %copy-start.3 = (s32[7,4,6,8]{3,1,2,0:T(4,128)S(1)}, s32[7,4,6,8]{3,1,2,0:T(4,128)}, u32[]{:S(2)}) copy-start(s32[7,4,6,8]{3,1,2,0:T(4,128)} %param.10) | copy-start | bytes 16132
  0.1 14.7 %copy-start.1 = (bf16[4,6,8,4096]{3,2,1,0:T(8,128)(2,1)S(1)}, bf16[4,6,8,4096]{3,2,1,0:T(8,128)(2,1)}, u32[]{:S(2)}) copy-start(bf16[4,6,8,4096]{3,2,1,0:T(8,128)(2,1)} %param.6) | copy-start | bytes 4718596
  6.6 29.7 %copy-start = (bf16[24,4,64,128]{3,2,1,0:T(8,128)(2,1)}, bf16[24,4,64,128]{3,2,1,0:T(8,128)(2,1)S(1)}, u32[]{:S(2)}) copy-start(bf16[24,4,64,128]{3,2,1,0:T(8,128)(2,1)S(1)} %get-tuple-element.23.natural_ref.natural_x) | copy-start | bytes 4718596
  6.6 29.7 %collective-permute-start.2 = (bf16[12,64,128]{2,1,0:T(8,128)(2,1)S(1)}, bf16[12,64,128]{2,1,0:T(8,128)(2,1)S(1)}, u32[]{:S(2)}, u32[]{:S(2)}) collective-permute-start(bf16[12,64,128]{2,1,0:T(8,128)(2,1)S(1)} %get-tuple-element.17.first_z), channel_id=1, source_target_pairs={{1,0},{2,1},{3,2},{4,3},{5,4},{6,5},{7,6},{9,8},{10,9},{11,10},{12... | collective-permute-start | bytes 589832 | tf_op jit(solution)/shard_map/ppermute | solution.py:22
  7.9 28.4 %collective-permute-start = (bf16[6,4,64,128]{3,2,1,0:T(8,128)(2,1)S(1)}, bf16[6,4,64,128]{3,2,1,0:T(8,128)(2,1)S(1)}, u32[]{:S(2)}, u32[]{:S(2)}) collective-permute-start(bf16[6,4,64,128]{3,2,1,0:T(8,128)(2,1)S(1)} %get-tuple-element.15), channel_id=1, source_target_pairs={{0,16},{16,0},{1,17},{17,1},{2,18},{18,2},{3,19},{19,3},{4,20},{20... | collective-permute-start | bytes 1179656 | tf_op jit(solution)/shard_map/ppermute | solution.py:460
  8.0 28.3 %collective-permute-start.1 = (bf16[4,4,64,128]{3,2,1,0:T(8,128)(2,1)S(1)}, bf16[4,4,64,128]{3,2,1,0:T(8,128)(2,1)S(1)}, u32[]{:S(2)}, u32[]{:S(2)}) collective-permute-start(bf16[4,4,64,128]{3,2,1,0:T(8,128)(2,1)S(1)} %get-tuple-element.16), channel_id=1, source_target_pairs={{0,8},{8,0},{1,9},{9,1},{2,10},{10,2},{3,11},{11,3},{4,12},{12,4},... | collective-permute-start | bytes 786440 | tf_op jit(solution)/shard_map/ppermute | solution.py:460
  10.2 26.1 %collective-permute-start.3 = (bf16[12,64,128]{2,1,0:T(8,128)(2,1)S(1)}, bf16[12,64,128]{2,1,0:T(8,128)(2,1)S(1)}, u32[]{:S(2)}, u32[]{:S(2)}) collective-permute-start(bf16[12,64,128]{2,1,0:T(8,128)(2,1)S(1)} %get-tuple-element.18), channel_id=1, source_target_pairs={{0,1},{1,2},{2,3},{3,4},{4,5},{5,6},{6,7},{8,9},{9,10},{10,11},{11... | collective-permute-start | bytes 589832 | tf_op jit(solution)/shard_map/ppermute | solution.py:22
  14.8 21.5 %copy-start.2 = (s32[24]{0:T(128)S(1)}, s32[24]{0:T(128)}, u32[]{:S(2)}) copy-start(s32[24]{0:T(128)} %owners.1) | copy-start | bytes 292

commit v5 on v4

--- a/solution.py
+++ b/solution.py
@@ -12,7 +12,7 @@
 AGG_DEV = 24
 LANES = 128
 HALF = NODES // 2
-VMEM_LIMIT = 48 * 1024 * 1024
+MIB = 1024 * 1024
 STEP = 8
 
 
@@ -209,7 +209,7 @@
             pltpu.VMEM((size_y, pairs, NODES, LANES), jnp.bfloat16),
             pltpu.VMEM((3, size_y, HALF, LANES), jnp.float32),
         ],
-        compiler_params=pltpu.CompilerParams(vmem_limit_bytes=VMEM_LIMIT),
+        compiler_params=pltpu.CompilerParams(vmem_limit_bytes=48 * MIB),
         name="prepare",
     )(place, prolong, faces, faces, faces)
 
@@ -330,7 +330,7 @@
             pltpu.VMEM((2, 4, depth * HALF, LANES), jnp.float32), total, total, total, total,
             pltpu.VMEM((STEP // 2, LANES, LANES), jnp.float32),
         ],
-        compiler_params=pltpu.CompilerParams(vmem_limit_bytes=VMEM_LIMIT),
+        compiler_params=pltpu.CompilerParams(vmem_limit_bytes=28 * MIB),
         cost_estimate=pl.CostEstimate(flops=columns * depth * 14 * NODES**3, bytes_accessed=columns * depth * 6 * block * 2, transcendentals=0),
         name="interior",
     )(keys, diag, faces, faces, faces, natural, turned, turned)
@@ -365,22 +365,22 @@
     @pl.when(place_ref[0] == 0)
     def _():
         for j in range(size_y):
-            ahead(tail_x.at[j], got_x.at[j], turned_x.at[j], lambda z: keys[2, size_x - 1, j, z])
+            ahead(tail_x.at[j], got_x.at[1, j], turned_x.at[j], lambda z: keys[2, size_x - 1, j, z])
 
     @pl.when(place_ref[0] != 0)
     def _():
         for j in range(size_y):
-            back(natural_x.at[j], got_x.at[j], lambda z: keys[1, 0, j, z])
+            back(natural_x.at[j], got_x.at[0, j], lambda z: keys[1, 0, j, z])
 
     @pl.when(place_ref[1] == 0)
     def _():
         for i in range(size_x):
-            ahead(tail_y.at[i], got_y.at[i], turned_y.at[i, 0], lambda z: keys[4, i, size_y - 1, z])
+            ahead(tail_y.at[i], got_y.at[1, i], turned_y.at[i, 0], lambda z: keys[4, i, size_y - 1, z])
 
     @pl.when(place_ref[1] != 0)
     def _():
         for i in range(size_x):
-            back(natural_y.at[i, 0], got_y.at[i], lambda z: keys[3, i, 0, z])
+            back(natural_y.at[i, 0], got_y.at[0, i], lambda z: keys[3, i, 0, z])
 
     for t in range(got_z.shape[0]):
         i, j = 2 * t // size_y, 2 * t % size_y
@@ -424,7 +424,7 @@
         out_specs=whole,
         out_shape=jax.ShapeDtypeStruct((places, SLOTS * HALF, LANES), jnp.bfloat16),
         scratch_shapes=[total, total, pltpu.SMEM((places // capacity,), jnp.int32)],
-        compiler_params=pltpu.CompilerParams(vmem_limit_bytes=VMEM_LIMIT),
+        compiler_params=pltpu.CompilerParams(vmem_limit_bytes=18 * MIB),
         name="border",
     )(owners, place, keys, *operands, turned, planes(turned), natural, planes(natural), *ends)
 
@@ -450,14 +450,14 @@
         out_specs=pl.BlockSpec((SLOTS, height, block), lambda g: (0, g, 0)),
         out_shape=jax.ShapeDtypeStruct((SLOTS, places, block), jnp.bfloat16),
         scratch_shapes=[pltpu.VMEM((SLOTS, height * HALF, LANES), jnp.float32)],
-        compiler_params=pltpu.CompilerParams(vmem_limit_bytes=VMEM_LIMIT),
+        compiler_params=pltpu.CompilerParams(vmem_limit_bytes=10 * MIB),
         name="layout",
     )(source, rows)
 
 
-def swap(block, axis):
+def shared(block, axis):
     assert lax.axis_size(axis) == 2
-    return lax.ppermute(block, axis, [(0, 1), (1, 0)])
+    return lax.all_gather(block, axis, axis=0, tiled=False)
 
 
 def shards(a_diag, a_face, prolong, aggregate, pair_slot, row_owner):
@@ -476,8 +476,8 @@
         place, prolong.reshape(columns, size_z, block), faces, sizes)
     got_z = passed_along(head_z, "gz", -1)
     back_z = passed_along(rim_z, "gz", 1)
-    got_y = swap(swap_y, "gy")
-    got_x = swap(swap_x, "gx")
+    got_y = shared(swap_y, "gy")
+    got_x = shared(swap_x, "gx")
     total = interior(keys, diag, faces, natural, turned, sizes)
     outgoing = border(
         row_owner, place, keys, (got_x, got_y, got_z, back_z, tail_x, tail_y, tail_z), turned, natural,

time: 85.7 us -> 93.4 us (1.090)
  blocking collectives: 38.1 us -> 48.8 us
  Pallas kernels: 39 us -> 37.4 us
  starting transfers between devices: 8.07 us -> 6.8 us
    all_gather x0 -> x2, blocking collectives: none -> 10.2 us  [shared(): return lax.all_gather(block, axis, axis=0, tiled=False)]
    ppermute x2 -> x0, starting transfers between devices: 2.24 us -> none  [swap(): return lax.ppermute(block, axis, [(0, 1), (1, 0)])]
    pallas_call x1, Pallas kernels: 21.5 us -> 19.8 us  [interior(): pl.pallas_call(interior_kernel, grid=(size_x,), in_specs=[pl.BlockSpec(me...]
    ppermute x2, starting transfers between devices: 5.84 us -> 6.8 us  [passed_along(): return lax.ppermute(block, axis, route)]
  transfers between devices with their start and end apart: 4 -> 2, of which waited for: 0 -> 0; matrix products, arithmetic and copies ran while one was open for 0% -> 0% of each run, Pallas kernels for 25% -> 21%
where the time goes in v5:
time: 93.4 us; the launch traced here: 93.2 us
  blocking collectives  48.8 us (52%)
  Pallas kernels  37.4 us (40%)
  starting transfers between devices  6.8 us (7%)
    all_to_all x1, blocking collectives, shards(): arrived = lax.all_to_all(outgoing, 'gz', 0, 0, tiled=True)  38.6 us
    pallas_call x1, Pallas kernels, interior(): pl.pallas_call(interior_kernel, grid=(size_x,), in_specs=[pl.BlockSpec(me...  19.8 us
    all_gather x2, blocking collectives, shared(): return lax.all_gather(block, axis, axis=0, tiled=False)  10.2 us
    pallas_call x1, Pallas kernels, border(): pl.pallas_call(functools.partial(border_kernel, capacity), grid=(1,), in_...  8.4 us
    ppermute x2, starting transfers between devices, passed_along(): return lax.ppermute(block, axis, route)  6.8 us
    pallas_call x1, Pallas kernels, prepare(): pl.pallas_call(prepare_kernel, grid=(size_x,), in_specs=[pl.BlockSpec(mem...  6.58 us
    pallas_call x1, Pallas kernels, laid_out(): pl.pallas_call(layout_kernel, grid=(places // height,), in_specs=[pl.Bloc...  2.63 us
  transfers between devices with their start and end apart: 2, of which 0 were waited for; matrix products, arithmetic and copies ran while one was open for 0% of the time, Pallas kernels for 21%

profile of v5, /device:TPU:0, one launch (start us, length us, event | category | flops | bytes accessed | tf_op | source)
XLA Modules:
  0.0 93.2 jit_solution(3595106554252902794)
XLA Ops:
  0.0 0.1 pad_add_fusion.place_ref
  0.1 0.0 slice-start
  0.1 0.0 copy-start.3
  0.1 0.0 copy-start.2
  0.1 0.0 slice-start.1
  0.1 0.0 copy-start
  0.1 6.6 %prepare.1 = (bf16[24,4,64,128]{3,2,1,0:T(8,128)(2,1)S(1)}, bf16[24,2,128,128]{3,2,1,0:T(8,128)(2,1)S(1)}, bf16[6,4,64,128]{3,2,1,0:T(8,128)(2,1)S(1)}, bf16[4,4...) custom-call(s32[2]{0:T(128)S(1)} %pad_add_fusion.place_ref, ...), custom_call_target="tpu_custom_call" | custom-call | tf_op jit(solution)/shard_map/prepare/pallas_call | solution.py:182
  6.7 1.3 %collective-permute-start = (bf16[12,64,128]{2,1,0:T(8,128)(2,1)S(1)}, bf16[12,64,128]{2,1,0:T(8,128)(2,1)S(1)}, u32[]{:S(2)}, u32[]{:S(2)}) collective-permute-start(bf16[12,64,128]{2,1,0:T(8,128)(2,1)S(1)} %get-tuple-element.17.first_z), channel_id=1, source_target_pairs={{1,0},{2,1},{3,2},{4,3},{5,4},{6,5},{7,6},{9,8},{10,9},{11,10},{12... | collective-permute-start | bytes 589832 | tf_op jit(solution)/shard_map/ppermute | solution.py:22
  8.0 5.5 %collective-permute-start.1 = (bf16[12,64,128]{2,1,0:T(8,128)(2,1)S(1)}, bf16[12,64,128]{2,1,0:T(8,128)(2,1)S(1)}, u32[]{:S(2)}, u32[]{:S(2)}) collective-permute-start(bf16[12,64,128]{2,1,0:T(8,128)(2,1)S(1)} %get-tuple-element.18), channel_id=1, source_target_pairs={{0,1},{1,2},{2,3},{3,4},{4,5},{5,6},{6,7},{8,9},{9,10},{10,11},{11... | collective-permute-start | bytes 589832 | tf_op jit(solution)/shard_map/ppermute | solution.py:22
  13.5 0.0 copy-done.3
  13.5 7.8 %all-gather.1 = bf16[8,4,64,128]{3,2,1,0:T(8,128)(2,1)S(1)} all-gather(bf16[4,4,64,128]{3,2,1,0:T(8,128)(2,1)S(1)} %get-tuple-element.16), channel_id=3, replica_groups=mesh['gx'=2,'gy'=2,'gz'=8] {'gy'}, dimensions={0}, use_global_device_ids=true | all-gather | bytes 786432 | tf_op jit(solution)/shard_map/all_gather | solution.py:460
  21.4 0.0 copy-done.2
  21.4 0.0 slice-done
  21.4 0.0 slice-done.1
  21.4 0.0 copy-done
  21.4 0.0 copy-start.1
  21.4 19.8 %interior.1.total_ref = f32[168,32,128]{2,1,0:T(8,128)S(1)} custom-call(s32[7,4,6,8]{3,2,1,0:T(8,128)S(1)} %copy_add_fusion.keys, bf16[24,8,4096]{2,1,0:T(8,128)(2,1)S(1)} %bitcast.24, bf16[3,24,8,4096]{3,2,1,0:T(8,128)(2,1)S(1)} %bitcast.17, bf16[3,24,8,4096]{3,2,1,0:T(8,128)(2,1)S(1)} %bitcast.18, bf16[3,24,8,4096]{3,2,1,0:T(8,128)(2,1)S(1)} %bitcast.19, ...), custom_call_target="tpu_custom_call" | custom-call | flops 704643072 | bytes 9437184 | tf_op jit(solution)/shard_map/interior/pallas_call | solution.py:315
  41.2 2.4 %all-gather = bf16[12,4,64,128]{3,2,1,0:T(8,128)(2,1)S(1)} all-gather(bf16[6,4,64,128]{3,2,1,0:T(8,128)(2,1)S(1)} %get-tuple-element.15), channel_id=2, replica_groups=mesh['gx'=2,'gy'=2,'gz'=8] {'gx'}, dimensions={0}, use_global_device_ids=true | all-gather | bytes 1179648 | tf_op jit(solution)/shard_map/all_gather | solution.py:460
  43.6 0.0 collective-permute-done.got_z
  43.6 0.0 collective-permute-done.1.back_z
  43.6 0.0 copy-done.1
  43.6 8.4 %border.1 = bf16[24,224,128]{2,1,0:T(8,128)(2,1)S(1)} custom-call(s32[24]{0:T(128)S(1)} %copy-done.1, s32[2]{0:T(128)S(1)} %pad_add_fusion.place_ref, s32[7,4,6,8]{3,2,1,0:T(8,128)S(1)} %copy_add_fusion.keys, bf16[2,6,4,64,128]{4,3,2,1,0:T(8,128)(2,1)S(1)} %bitcast.22, bf16[2,4,4,64,128]{4,3,2,1,0:T(8,128)(2,1)S(1)} %bitcast.23, ...), custom_call_target="tpu_custom_call" | custom-call | tf_op jit(solution)/shard_map/border/pallas_call | solution.py:415
  52.0 38.6 %all_to_all.5.rows_ref = bf16[24,224,128]{2,1,0:T(8,128)(2,1)S(1)} all-to-all(bf16[24,224,128]{2,1,0:T(8,128)(2,1)S(1)} %border.1), channel_id=1, replica_groups=mesh['gx'=2,'gy'=2,'gz'=8] {'gz'}, dimensions={0} | all-to-all | bytes 2752512 | tf_op jit(solution)/shard_map/all_to_all | solution.py:485
  90.6 2.6 %layout.1 = bf16[7,24,4096]{2,1,0:T(8,128)(2,1)} custom-call(s32[24]{0:T(128)S(1)} %iota.3.source, bf16[24,224,128]{2,1,0:T(8,128)(2,1)S(1)} %all_to_all.5.rows_ref), custom_call_target="tpu_custom_call" | custom-call | tf_op jit(solution)/shard_map/layout/pallas_call | solution.py:446
  (5 shorter events, 0.0 us)
Async XLA Ops:
  0.1 21.3 %slice-start = ((s8[4718592]{0:T(1024)(128)(4,1)}), s8[4194304]{0:T(1024)(128)(4,1)S(1)}, s32[]{:S(2)}) async-start(s8[4718592]{0:T(1024)(128)(4,1)} %bitcast.15), calls=%async_computation.1 | async-start | bytes 8388608
  0.1 13.4 %copy-start.3 = (s32[4,6,8]{2,0,1:T(4,128)S(1)}, s32[4,6,8]{2,0,1:T(4,128)}, u32[]{:S(2)}) copy-start(s32[4,6,8]{2,0,1:T(4,128)} %param.9) | copy-start | bytes 2308
  0.1 21.3 %copy-start.2 = (s32[7,4,6,8]{3,1,2,0:T(4,128)S(1)}, s32[7,4,6,8]{3,1,2,0:T(4,128)}, u32[]{:S(2)}) copy-start(s32[7,4,6,8]{3,1,2,0:T(4,128)} %param.10) | copy-start | bytes 16132
  0.1 21.3 %slice-start.1 = ((s8[4718592]{0:T(1024)(128)(4,1)}), s8[524288]{0:T(1024)(128)(4,1)S(1)}, s32[]{:S(2)}) async-start(s8[4718592]{0:T(1024)(128)(4,1)} %bitcast.15), calls=%async_computation.2 | async-start | bytes 1048576
  0.1 21.3 %copy-start = (bf16[4,6,8,4096]{3,2,1,0:T(8,128)(2,1)S(1)}, bf16[4,6,8,4096]{3,2,1,0:T(8,128)(2,1)}, u32[]{:S(2)}) copy-start(bf16[4,6,8,4096]{3,2,1,0:T(8,128)(2,1)} %param.6) | copy-start | bytes 4718596
  6.7 36.9 %collective-permute-start = (bf16[12,64,128]{2,1,0:T(8,128)(2,1)S(1)}, bf16[12,64,128]{2,1,0:T(8,128)(2,1)S(1)}, u32[]{:S(2)}, u32[]{:S(2)}) collective-permute-start(bf16[12,64,128]{2,1,0:T(8,128)(2,1)S(1)} %get-tuple-element.17.first_z), channel_id=1, source_target_pairs={{1,0},{2,1},{3,2},{4,3},{5,4},{6,5},{7,6},{9,8},{10,9},{11,10},{12... | collective-permute-start | bytes 589832 | tf_op jit(solution)/shard_map/ppermute | solution.py:22
  8.0 35.6 %collective-permute-start.1 = (bf16[12,64,128]{2,1,0:T(8,128)(2,1)S(1)}, bf16[12,64,128]{2,1,0:T(8,128)(2,1)S(1)}, u32[]{:S(2)}, u32[]{:S(2)}) collective-permute-start(bf16[12,64,128]{2,1,0:T(8,128)(2,1)S(1)} %get-tuple-element.18), channel_id=1, source_target_pairs={{0,1},{1,2},{2,3},{3,4},{4,5},{5,6},{6,7},{8,9},{9,10},{10,11},{11... | collective-permute-start | bytes 589832 | tf_op jit(solution)/shard_map/ppermute | solution.py:22
  21.4 22.2 %copy-start.1 = (s32[24]{0:T(128)S(1)}, s32[24]{0:T(128)}, u32[]{:S(2)}) copy-start(s32[24]{0:T(128)} %owners.1) | copy-start | bytes 292

commit v6 on v5

--- a/solution.py
+++ b/solution.py
@@ -252,6 +252,7 @@
     def sums(j, couples):
         row_y = jnp.maximum(j - 1, 0)
         has_y = j > 0
+        batches = []
         for h in range(pairs // 2):
             turned = (turned_ref[j, h], below_ref[j, h], turned_ref[row_y, h], turned_ref[j, h])
             for face in range(4):
@@ -274,12 +275,13 @@
                         continue
                     updates.append((ahead[side], here, term))
                     updates.append((behind[side], there, term))
-                add_all(updates)
+                batches.append(updates)
+        return batches
 
     def columns(step, carry):
         couples = [couplings(2 * step + u, stages.at[u]) for u in range(2)]
-        for u in range(2):
-            sums(2 * step + u, couples[u])
+        for updates in [updates for u in range(2) for updates in sums(2 * step + u, couples[u])]:
+            add_all(updates)
         return carry
 
     lax.fori_loop(0, size_y // 2, columns, 0)
@@ -348,6 +350,9 @@
     for total in totals:
         total[...] = jnp.zeros_like(total)
 
+    def key_at(number, i, j, z):
+        return keys[number, i, j, z]
+
     def couple(left0, left1, head):
         return upright(product(jnp.concatenate([left0, left1], axis=1), paired_weights(head))).astype(jnp.bfloat16)
 
@@ -355,39 +360,47 @@
         couples = [couple(tail[2 * p], tail[2 * p + 1], head[p]) for p in range(pairs)]
         for h in range(pairs // 2):
             four = two_pairs(product(turned[h], apart(couples[2 * h], couples[2 * h + 1])))
-            add_all([(totals[number % 2], key(4 * h + number), term) for number, term in enumerate(four)])
+            yield [(totals[number % 2], key(4 * h + number), term) for number, term in enumerate(four)]
 
     def back(natural, rim, key):
         for h in range(pairs // 2):
             four = [term for p in (2 * h, 2 * h + 1) for term in folded(across(natural[p], rim[p]))]
-            add_all([(totals[number % 2], key(4 * h + number), term) for number, term in enumerate(four)])
+            yield [(totals[number % 2], key(4 * h + number), term) for number, term in enumerate(four)]
+
+    def add_batches(batches):
+        for updates in list(batches):
+            add_all(updates)
 
     @pl.when(place_ref[0] == 0)
     def _():
-        for j in range(size_y):
-            ahead(tail_x.at[j], got_x.at[1, j], turned_x.at[j], lambda z: keys[2, size_x - 1, j, z])
+        add_batches(
+            batch for j in range(size_y)
+            for batch in ahead(tail_x.at[j], got_x.at[j], turned_x.at[j], functools.partial(key_at, 2, size_x - 1, j)))
 
     @pl.when(place_ref[0] != 0)
     def _():
-        for j in range(size_y):
-            back(natural_x.at[j], got_x.at[0, j], lambda z: keys[1, 0, j, z])
+        add_batches(
+            batch for j in range(size_y) for batch in back(natural_x.at[j], got_x.at[j], functools.partial(key_at, 1, 0, j)))
 
     @pl.when(place_ref[1] == 0)
     def _():
-        for i in range(size_x):
-            ahead(tail_y.at[i], got_y.at[1, i], turned_y.at[i, 0], lambda z: keys[4, i, size_y - 1, z])
+        add_batches(
+            batch for i in range(size_x)
+            for batch in ahead(tail_y.at[i], got_y.at[i], turned_y.at[i, 0], functools.partial(key_at, 4, i, size_y - 1)))
 
     @pl.when(place_ref[1] != 0)
     def _():
-        for i in range(size_x):
-            back(natural_y.at[i, 0], got_y.at[0, i], lambda z: keys[3, i, 0, z])
-
+        add_batches(
+            batch for i in range(size_x) for batch in back(natural_y.at[i, 0], got_y.at[i], functools.partial(key_at, 3, i, 0)))
+
+    batches = []
     for t in range(got_z.shape[0]):
         i, j = 2 * t // size_y, 2 * t % size_y
         front = folded(across(last_z[t], couple(tail_z[2 * t], tail_z[2 * t + 1], got_z[t])))
         past = folded(across(first_z[t], back_z[t]))
-        add_all([(totals[side], keys[6, i, j + side, depth - 1], front[side]) for side in (0, 1)]
-                + [(totals[side], keys[5, i, j + side, 0], past[side]) for side in (0, 1)])
+        batches.append([(totals[side], keys[6, i, j + side, depth - 1], front[side]) for side in (0, 1)]
+                       + [(totals[side], keys[5, i, j + side, 0], past[side]) for side in (0, 1)])
+    add_batches(batches)
 
     for owner in range(places // capacity):
         filled[owner] = 0
@@ -455,9 +468,9 @@
     )(source, rows)
 
 
-def shared(block, axis):
+def swap(block, axis):
     assert lax.axis_size(axis) == 2
-    return lax.all_gather(block, axis, axis=0, tiled=False)
+    return lax.ppermute(block, axis, [(0, 1), (1, 0)])
 
 
 def shards(a_diag, a_face, prolong, aggregate, pair_slot, row_owner):
@@ -476,8 +489,8 @@
         place, prolong.reshape(columns, size_z, block), faces, sizes)
     got_z = passed_along(head_z, "gz", -1)
     back_z = passed_along(rim_z, "gz", 1)
-    got_y = shared(swap_y, "gy")
-    got_x = shared(swap_x, "gx")
+    got_y = swap(swap_y, "gy")
+    got_x = swap(swap_x, "gx")
     total = interior(keys, diag, faces, natural, turned, sizes)
     outgoing = border(
         row_owner, place, keys, (got_x, got_y, got_z, back_z, tail_x, tail_y, tail_z), turned, natural,

time: 93.4 us -> 84.3 us (0.903)
  blocking collectives: 48.8 us -> 38.1 us
  starting transfers between devices: 6.8 us -> 8.3 us
    all_gather x2 -> x0, blocking collectives: 10.2 us -> none  [shared(): return lax.all_gather(block, axis, axis=0, tiled=False)]
    ppermute x0 -> x2, starting transfers between devices: none -> 2.47 us  [swap(): return lax.ppermute(block, axis, [(0, 1), (1, 0)])]
    ppermute x2, starting transfers between devices: 6.8 us -> 5.84 us  [passed_along(): return lax.ppermute(block, axis, route)]
  transfers between devices with their start and end apart: 2 -> 4, of which waited for: 0 -> 0; matrix products, arithmetic and copies ran while one was open for 0% -> 0% of each run, Pallas kernels for 21% -> 24%
where the time goes in v6:
time: 84.3 us; the launch traced here: 84.1 us
  blocking collectives  38.1 us (45%)
  Pallas kernels  37.4 us (44%)
  starting transfers between devices  8.3 us (10%)
    all_to_all x1, blocking collectives, shards(): arrived = lax.all_to_all(outgoing, 'gz', 0, 0, tiled=True)  38.1 us
    pallas_call x1, Pallas kernels, interior(): pl.pallas_call(interior_kernel, grid=(size_x,), in_specs=[pl.BlockSpec(me...  19.8 us
    pallas_call x1, Pallas kernels, border(): pl.pallas_call(functools.partial(border_kernel, capacity), grid=(1,), in_...  8.39 us
    pallas_call x1, Pallas kernels, prepare(): pl.pallas_call(prepare_kernel, grid=(size_x,), in_specs=[pl.BlockSpec(mem...  6.58 us
    ppermute x2, starting transfers between devices, passed_along(): return lax.ppermute(block, axis, route)  5.84 us
    pallas_call x1, Pallas kernels, laid_out(): pl.pallas_call(layout_kernel, grid=(places // height,), in_specs=[pl.Bloc...  2.63 us
    ppermute x2, starting transfers between devices, swap(): return lax.ppermute(block, axis, [(0, 1), (1, 0)])  2.47 us
  transfers between devices with their start and end apart: 4, of which 0 were waited for; matrix products, arithmetic and copies ran while one was open for 0% of the time, Pallas kernels for 24%

profile of v6, /device:TPU:0, one launch (start us, length us, event | category | flops | bytes accessed | tf_op | source)
XLA Modules:
  0.0 84.1 jit_solution(8573493591061905838)
XLA Ops:
  0.0 0.1 pad_add_fusion.place_ref
  0.1 0.0 slice-start
  0.1 0.0 copy-start.3
  0.1 0.0 copy-start.2
  0.1 0.0 slice-start.1
  0.1 0.0 copy-start
  0.1 6.6 %prepare.1 = (bf16[24,4,64,128]{3,2,1,0:T(8,128)(2,1)S(1)}, bf16[24,2,128,128]{3,2,1,0:T(8,128)(2,1)S(1)}, bf16[6,4,64,128]{3,2,1,0:T(8,128)(2,1)S(1)}, bf16[4,4...) custom-call(s32[2]{0:T(128)S(1)} %pad_add_fusion.place_ref, ...), custom_call_target="tpu_custom_call" | custom-call | tf_op jit(solution)/shard_map/prepare/pallas_call | solution.py:182
  6.7 1.3 %collective-permute-start.2 = (bf16[12,64,128]{2,1,0:T(8,128)(2,1)S(1)}, bf16[12,64,128]{2,1,0:T(8,128)(2,1)S(1)}, u32[]{:S(2)}, u32[]{:S(2)}) collective-permute-start(bf16[12,64,128]{2,1,0:T(8,128)(2,1)S(1)} %get-tuple-element.17.first_z), channel_id=1, source_target_pairs={{1,0},{2,1},{3,2},{4,3},{5,4},{6,5},{7,6},{9,8},{10,9},{11,10},{12... | collective-permute-start | bytes 589832 | tf_op jit(solution)/shard_map/ppermute | solution.py:22
  8.0 0.1 collective-permute-start
  8.1 2.4 %collective-permute-start.1 = (bf16[4,4,64,128]{3,2,1,0:T(8,128)(2,1)S(1)}, bf16[4,4,64,128]{3,2,1,0:T(8,128)(2,1)S(1)}, u32[]{:S(2)}, u32[]{:S(2)}) collective-permute-start(bf16[4,4,64,128]{3,2,1,0:T(8,128)(2,1)S(1)} %get-tuple-element.16), channel_id=1, source_target_pairs={{0,8},{8,0},{1,9},{9,1},{2,10},{10,2},{3,11},{11,3},{4,12},{12,4},... | collective-permute-start | bytes 786440 | tf_op jit(solution)/shard_map/ppermute | solution.py:473
  10.5 4.5 %collective-permute-start.3 = (bf16[12,64,128]{2,1,0:T(8,128)(2,1)S(1)}, bf16[12,64,128]{2,1,0:T(8,128)(2,1)S(1)}, u32[]{:S(2)}, u32[]{:S(2)}) collective-permute-start(bf16[12,64,128]{2,1,0:T(8,128)(2,1)S(1)} %get-tuple-element.18), channel_id=1, source_target_pairs={{0,1},{1,2},{2,3},{3,4},{4,5},{5,6},{6,7},{8,9},{9,10},{10,11},{11... | collective-permute-start | bytes 589832 | tf_op jit(solution)/shard_map/ppermute | solution.py:22
  15.0 0.0 copy-done.3
  15.0 0.0 copy-done.2
  15.1 0.0 slice-done
  15.1 0.0 slice-done.1
  15.1 0.0 copy-done
  15.1 0.0 copy-start.1
  15.1 19.8 %interior.1.total_ref = f32[168,32,128]{2,1,0:T(8,128)S(1)} custom-call(s32[7,4,6,8]{3,2,1,0:T(8,128)S(1)} %copy_add_fusion.keys, bf16[24,8,4096]{2,1,0:T(8,128)(2,1)S(1)} %bitcast.20, bf16[3,24,8,4096]{3,2,1,0:T(8,128)(2,1)S(1)} %bitcast.15, bf16[3,24,8,4096]{3,2,1,0:T(8,128)(2,1)S(1)} %bitcast.16, bf16[3,24,8,4096]{3,2,1,0:T(8,128)(2,1)S(1)} %bitcast.17, ...), custom_call_target="tpu_custom_call" | custom-call | flops 704643072 | bytes 9437184 | tf_op jit(solution)/shard_map/interior/pallas_call | solution.py:317
  34.9 0.0 collective-permute-done.2.got_z
  34.9 0.0 collective-permute-done.3.back_z
  34.9 0.0 collective-permute-done.1.got_y
  35.0 0.0 collective-permute-done.got_x
  35.0 0.0 copy-done.1
  35.0 8.4 %border.1 = bf16[24,224,128]{2,1,0:T(8,128)(2,1)S(1)} custom-call(s32[24]{0:T(128)S(1)} %copy-done.1, s32[2]{0:T(128)S(1)} %pad_add_fusion.place_ref, s32[7,4,6,8]{3,2,1,0:T(8,128)S(1)} %copy_add_fusion.keys, bf16[6,4,64,128]{3,2,1,0:T(8,128)(2,1)S(1)} %collective-permute-done.got_x, bf16[4,4,64,128]{3,2,1,0:T(8,128)(2,1)S(1)} %collective-permute-done.1.got_y, ...), custom_call_target="tpu_custom_call" | custom-call | tf_op jit(solution)/shard_map/border/pallas_call | solution.py:428
  43.4 38.1 %all_to_all.5.rows_ref = bf16[24,224,128]{2,1,0:T(8,128)(2,1)S(1)} all-to-all(bf16[24,224,128]{2,1,0:T(8,128)(2,1)S(1)} %border.1), channel_id=1, replica_groups=mesh['gx'=2,'gy'=2,'gz'=8] {'gz'}, dimensions={0} | all-to-all | bytes 2752512 | tf_op jit(solution)/shard_map/all_to_all | solution.py:498
  81.4 2.6 %layout.1 = bf16[7,24,4096]{2,1,0:T(8,128)(2,1)} custom-call(s32[24]{0:T(128)S(1)} %iota.3.source, bf16[24,224,128]{2,1,0:T(8,128)(2,1)S(1)} %all_to_all.5.rows_ref), custom_call_target="tpu_custom_call" | custom-call | tf_op jit(solution)/shard_map/layout/pallas_call | solution.py:459
  (5 shorter events, 0.0 us)
Async XLA Ops:
  0.1 15.0 %slice-start = ((s8[4718592]{0:T(1024)(128)(4,1)}), s8[4194304]{0:T(1024)(128)(4,1)S(1)}, s32[]{:S(2)}) async-start(s8[4718592]{0:T(1024)(128)(4,1)} %bitcast.13), calls=%async_computation.1 | async-start | bytes 8388608
  0.1 14.9 %copy-start.3 = (s32[4,6,8]{2,0,1:T(4,128)S(1)}, s32[4,6,8]{2,0,1:T(4,128)}, u32[]{:S(2)}) copy-start(s32[4,6,8]{2,0,1:T(4,128)} %param.9) | copy-start | bytes 2308
  0.1 15.0 %copy-start.2 = (s32[7,4,6,8]{3,1,2,0:T(4,128)S(1)}, s32[7,4,6,8]{3,1,2,0:T(4,128)}, u32[]{:S(2)}) copy-start(s32[7,4,6,8]{3,1,2,0:T(4,128)} %param.10) | copy-start | bytes 16132
  0.1 15.0 %slice-start.1 = ((s8[4718592]{0:T(1024)(128)(4,1)}), s8[524288]{0:T(1024)(128)(4,1)S(1)}, s32[]{:S(2)}) async-start(s8[4718592]{0:T(1024)(128)(4,1)} %bitcast.13), calls=%async_computation.2 | async-start | bytes 1048576
  0.1 15.0 %copy-start = (bf16[4,6,8,4096]{3,2,1,0:T(8,128)(2,1)S(1)}, bf16[4,6,8,4096]{3,2,1,0:T(8,128)(2,1)}, u32[]{:S(2)}) copy-start(bf16[4,6,8,4096]{3,2,1,0:T(8,128)(2,1)} %param.6) | copy-start | bytes 4718596
  6.7 28.2 %collective-permute-start.2 = (bf16[12,64,128]{2,1,0:T(8,128)(2,1)S(1)}, bf16[12,64,128]{2,1,0:T(8,128)(2,1)S(1)}, u32[]{:S(2)}, u32[]{:S(2)}) collective-permute-start(bf16[12,64,128]{2,1,0:T(8,128)(2,1)S(1)} %get-tuple-element.17.first_z), channel_id=1, source_target_pairs={{1,0},{2,1},{3,2},{4,3},{5,4},{6,5},{7,6},{9,8},{10,9},{11,10},{12... | collective-permute-start | bytes 589832 | tf_op jit(solution)/shard_map/ppermute | solution.py:22
  8.0 27.0 %collective-permute-start = (bf16[6,4,64,128]{3,2,1,0:T(8,128)(2,1)S(1)}, bf16[6,4,64,128]{3,2,1,0:T(8,128)(2,1)S(1)}, u32[]{:S(2)}, u32[]{:S(2)}) collective-permute-start(bf16[6,4,64,128]{3,2,1,0:T(8,128)(2,1)S(1)} %get-tuple-element.15), channel_id=1, source_target_pairs={{0,16},{16,0},{1,17},{17,1},{2,18},{18,2},{3,19},{19,3},{4,20},{20... | collective-permute-start | bytes 1179656 | tf_op jit(solution)/shard_map/ppermute | solution.py:473
  8.1 26.9 %collective-permute-start.1 = (bf16[4,4,64,128]{3,2,1,0:T(8,128)(2,1)S(1)}, bf16[4,4,64,128]{3,2,1,0:T(8,128)(2,1)S(1)}, u32[]{:S(2)}, u32[]{:S(2)}) collective-permute-start(bf16[4,4,64,128]{3,2,1,0:T(8,128)(2,1)S(1)} %get-tuple-element.16), channel_id=1, source_target_pairs={{0,8},{8,0},{1,9},{9,1},{2,10},{10,2},{3,11},{11,3},{4,12},{12,4},... | collective-permute-start | bytes 786440 | tf_op jit(solution)/shard_map/ppermute | solution.py:473
  10.5 24.5 %collective-permute-start.3 = (bf16[12,64,128]{2,1,0:T(8,128)(2,1)S(1)}, bf16[12,64,128]{2,1,0:T(8,128)(2,1)S(1)}, u32[]{:S(2)}, u32[]{:S(2)}) collective-permute-start(bf16[12,64,128]{2,1,0:T(8,128)(2,1)S(1)} %get-tuple-element.18), channel_id=1, source_target_pairs={{0,1},{1,2},{2,3},{3,4},{4,5},{5,6},{6,7},{8,9},{9,10},{10,11},{11... | collective-permute-start | bytes 589832 | tf_op jit(solution)/shard_map/ppermute | solution.py:22
  15.1 19.8 %copy-start.1 = (s32[24]{0:T(128)S(1)}, s32[24]{0:T(128)}, u32[]{:S(2)}) copy-start(s32[24]{0:T(128)} %owners.1) | copy-start | bytes 292

commit v7 on v6

--- a/solution.py
+++ b/solution.py
@@ -16,10 +16,9 @@
 STEP = 8
 
 
-def passed_along(block, axis, distance):
-    devices = range(lax.axis_size(axis))
-    route = [(i - distance, i) for i in devices if i - distance in devices]
-    return lax.ppermute(block, axis, route)
+def swapped_along(block, axis, first):
+    pairs = [(i, i + 1) for i in range(first, lax.axis_size(axis) - 1, 2)]
+    return lax.ppermute(block, axis, pairs + [(i + 1, i) for i, _ in pairs])
 
 
 def low_lanes(rows):
@@ -49,14 +48,14 @@
 
 
 def block_of(stage, z, depth):
-    return stage[pl.ds(z, HALF, stride=depth), :]
+    return stage[pl.ds(z, HALF, stride=depth), :].astype(jnp.bfloat16)
 
 
 def stacked_pair(first, second):
     low = low_lanes(HALF)
     even = jnp.where(low, first, swapped(second))
     odd = jnp.where(low, swapped(first), second)
-    return jnp.concatenate([even, odd], axis=0).astype(jnp.bfloat16)
+    return jnp.concatenate([even, odd], axis=0)
 
 
 def in_order(pair):
@@ -65,18 +64,12 @@
     return product(zero_one(row == 2 * (col % HALF) + col // HALF), pair).astype(jnp.bfloat16)
 
 
-def paired_weights(pair):
+def four_weights(first, second):
     low = low_lanes(NODES)
-    zero = jnp.zeros_like(pair)
-    first = jnp.where(low, pair, zero)
-    second = jnp.where(low, zero, pair)
-    left = jnp.concatenate([first, zero, second, zero], axis=0)
-    right = jnp.concatenate([zero, first, zero, second], axis=0)
-    return jnp.concatenate([left, right], axis=1)
-
-
-def upright(value):
-    return jnp.concatenate([value[:, :LANES], value[:, LANES:]], axis=0)
+    zero = jnp.zeros_like(first)
+    left = [jnp.where(low, first, zero), jnp.where(low, zero, first), zero, zero]
+    right = [zero, zero, jnp.where(low, second, zero), jnp.where(low, zero, second)]
+    return jnp.concatenate([jnp.concatenate(left, axis=0), jnp.concatenate(right, axis=0)], axis=1)
 
 
 def folded(square):
@@ -115,8 +108,8 @@
         total[key] = new
 
 
-def prepare_kernel(place_ref, p_ref, fx_ref, fy_ref, fz_ref, natural_ref, turned_ref, swap_x_ref, swap_y_ref, head_z_ref, rim_z_ref,
-                   last_z_ref, tail_x_ref, tail_y_ref, tail_z_ref, stages, stages_f, stacks, ends):
+def prepare_kernel(place_ref, p_ref, fx_ref, fy_ref, fz_ref, natural_ref, turned_ref, swap_x_ref, swap_y_ref, near_z_ref, far_z_ref,
+                   first_z_ref, last_z_ref, tail_x_ref, tail_y_ref, tail_z_ref, stages, stages_f, stacks, ends):
     plane = pl.program_id(0)
     size_y, depth = p_ref.shape[0], p_ref.shape[1]
     pairs = depth // 2
@@ -137,21 +130,23 @@
         spread(fz_ref[0, j], stage_f)
         last = block_of(stage_f, depth - 1, depth)
         ends[2, j] = last
-        tail_z_ref[j] = last.astype(jnp.bfloat16)
 
     for t in range(size_y // 2):
         first, last, face = [stacked_pair(ends[kind, 2 * t], ends[kind, 2 * t + 1]) for kind in range(3)]
-        head_z_ref[t] = in_order(first)
+        head = in_order(first)
+        rim = diagonal(across(face, last))
+        first_z_ref[t] = head
         last_z_ref[t] = last
-        rim_z_ref[t] = diagonal(across(face, last))
+        tail_z_ref[t] = face
+        near_z_ref[t] = jnp.where(place_ref[2] == 0, rim, head)
+        far_z_ref[t] = jnp.where(place_ref[2] == 0, head, rim)
 
     def faces(source, stage, j, tails, rims):
         spread(source, stage)
         block = [block_of(stage, z, depth) for z in range(depth)]
-        for z in range(depth):
-            tails[z] = block[z].astype(jnp.bfloat16)
         for p in range(pairs):
-            rims[p] = diagonal(across(stacked_pair(block[2 * p], block[2 * p + 1]), stacks[j, p]))
+            tails[p] = stacked_pair(block[2 * p], block[2 * p + 1])
+            rims[p] = diagonal(across(tails[p], stacks[j, p]))
 
     @pl.when(place_ref[1] == 0)
     def _():
@@ -194,20 +189,20 @@
             pl.BlockSpec((size_y, pairs // 2, LANES, LANES), lambda i: (i, 0, 0, 0)),
             pl.BlockSpec((size_y, pairs, NODES, LANES), lambda i: (0, 0, 0, 0)),
             pl.BlockSpec((1, pairs, NODES, LANES), lambda i: (i, 0, 0, 0)),
-            by_half, by_half, by_half,
-            pl.BlockSpec((size_y, depth, HALF, LANES), lambda i: (0, 0, 0, 0)),
-            pl.BlockSpec((1, depth, HALF, LANES), lambda i: (i, 0, 0, 0)),
-            pl.BlockSpec((size_y, HALF, LANES), lambda i: (i, 0, 0)),
+            by_half, by_half, by_half, by_half,
+            pl.BlockSpec((size_y, pairs, NODES, LANES), lambda i: (0, 0, 0, 0)),
+            pl.BlockSpec((1, pairs, NODES, LANES), lambda i: (i, 0, 0, 0)),
+            by_half,
         ],
         out_shape=[
             shape(columns, pairs, NODES, LANES), shape(columns, pairs // 2, LANES, LANES),
-            shape(size_y, pairs, NODES, LANES), shape(size_x, pairs, NODES, LANES), edge, edge, edge,
-            shape(size_y, depth, HALF, LANES), shape(size_x, depth, HALF, LANES), shape(columns, HALF, LANES),
+            shape(size_y, pairs, NODES, LANES), shape(size_x, pairs, NODES, LANES), edge, edge, edge, edge,
+            shape(size_y, pairs, NODES, LANES), shape(size_x, pairs, NODES, LANES), edge,
         ],
         scratch_shapes=[
             stage, stage,
             pltpu.VMEM((size_y, pairs, NODES, LANES), jnp.bfloat16),
-            pltpu.VMEM((3, size_y, HALF, LANES), jnp.float32),
+            pltpu.VMEM((3, size_y, HALF, LANES), jnp.bfloat16),
         ],
         compiler_params=pltpu.CompilerParams(vmem_limit_bytes=48 * MIB),
         name="prepare",
@@ -233,20 +228,23 @@
         row_y = jnp.maximum(j - 1, 0)
         for face, source in zip(range(4), (diag_ref[j], fx_ref[0, j], fy_ref[0, row_y], fz_ref[0, j])):
             spread(source, stage.at[face])
+        stacked = []
+        for face in range(4):
+            shift = 1 if face == 3 else 0
+            block = [block_of(stage.at[face], z, depth) for z in range(depth)]
+            stacked.append([stacked_pair(block[(2 * p - shift) % depth], block[2 * p + 1 - shift]) for p in range(pairs)])
         couples = [[] for _ in range(4)]
-        for p in range(pairs):
-            left = []
+        for h in range(pairs // 2):
+            left = [jnp.concatenate([stacked[face][2 * h], stacked[face][2 * h + 1]], axis=1) for face in range(4)]
+            weights = four_weights(natural_ref[j, 2 * h], natural_ref[j, 2 * h + 1])
+            four = product(jnp.concatenate(left, axis=0), weights).astype(jnp.bfloat16)
             for face in range(4):
-                shift = 1 if face == 3 else 0
-                sides = [block_of(stage.at[face], (2 * p + side - shift) % depth, depth).astype(jnp.bfloat16) for side in (0, 1)]
-                left.append(jnp.concatenate(sides, axis=1))
-            pair = product(jnp.concatenate(left, axis=0), paired_weights(natural_ref[j, p]))
-            for face in range(4):
-                couple = upright(pair[HALF * face : HALF * (face + 1)])
-                couples[face].append(swapped(couple) if face == 3 else couple.astype(jnp.bfloat16))
+                rows = four[NODES * face : NODES * (face + 1)]
+                for couple in (rows[:, :LANES], rows[:, LANES:]):
+                    couples[face].append(swapped(couple) if face == 3 else couple)
         low = low_lanes(NODES)
         along = couples[3]
-        couples[3] = [jnp.where(low, along[p], along[min(p + 1, pairs - 1)]).astype(jnp.bfloat16) for p in range(pairs)]
+        couples[3] = [jnp.where(low, along[p], along[min(p + 1, pairs - 1)]) for p in range(pairs)]
         return couples
 
     def sums(j, couples):
@@ -290,22 +288,21 @@
     def _():
         def finish(g, carry):
             low = low_lanes(HALF)
-            for p in range(STEP // 2):
-                one, two = [behind_even[STEP * g + 2 * p + side] + behind_odd[STEP * g + 2 * p + side] for side in (0, 1)]
+            spots = [(p, [wide.shape[0] * 2 * g + 2 * p + side for side in (0, 1)]) for p in range(wide.shape[0])]
+            for p, key in spots:
+                one, two = [behind_even[key[side]] + behind_odd[key[side]] for side in (0, 1)]
                 upper = jnp.where(low, one, swapped(two))
                 lower = jnp.where(low, swapped(one), two)
                 wide[p, :, :NODES] = jnp.concatenate([upper, lower], axis=0).T
-            for p in range(STEP // 2):
+            for p, key in spots:
                 for side in (0, 1):
-                    key = STEP * g + 2 * p + side
-                    even, odd = [
-                        ahead_even[key, pl.ds(first, HALF // 2, stride=2), :] + ahead_odd[key, pl.ds(first, HALF // 2, stride=2), :]
-                        for first in (0, 1)]
-                    turned = [wide[p, pl.ds(NODES * side + first, HALF, stride=2), :] for first in (0, 1)]
-                    out_ref[key] = straightened(even, odd) + jnp.where(low, turned[0], swapped(turned[1]))
+                    first = wide[p, NODES * side : NODES * side + HALF, :]
+                    second = wide[p, NODES * side + HALF : NODES * (side + 1), :]
+                    turned = jnp.where(low, first, swapped(second))
+                    out_ref[key[side]] = (ahead_even[key[side]] + ahead_odd[key[side]]) + turned
             return carry
 
-        lax.fori_loop(0, spare // STEP, finish, 0)
+        lax.fori_loop(0, spare // (2 * wide.shape[0]), finish, 0)
 
 
 def interior(keys, diag, faces, natural, turned, sizes):
@@ -330,7 +327,7 @@
         out_shape=jax.ShapeDtypeStruct((rows, HALF, LANES), jnp.float32),
         scratch_shapes=[
             pltpu.VMEM((2, 4, depth * HALF, LANES), jnp.float32), total, total, total, total,
-            pltpu.VMEM((STEP // 2, LANES, LANES), jnp.float32),
+            pltpu.VMEM((12, LANES, LANES), jnp.float32),
         ],
         compiler_params=pltpu.CompilerParams(vmem_limit_bytes=28 * MIB),
         cost_estimate=pl.CostEstimate(flops=columns * depth * 14 * NODES**3, bytes_accessed=columns * depth * 6 * block * 2, transcendentals=0),
@@ -338,11 +335,10 @@
     )(keys, diag, faces, faces, faces, natural, turned, turned)
 
 
-def border_kernel(capacity, owners, place_ref, keys, got_x, got_y, got_z, back_z, tail_x, tail_y, tail_z, turned_x, turned_y,
+def border_kernel(capacity, owners, place_ref, keys, got_x, got_y, near_z, far_z, tail_x, tail_y, tail_z, turned_x, turned_y,
                   natural_x, natural_y, first_z, last_z, total_ref, out_ref, even_total, odd_total, filled):
-    size_y, depth = tail_x.shape[0], tail_x.shape[1]
-    size_x = tail_y.shape[0]
-    pairs = depth // 2
+    size_y, pairs = tail_x.shape[0], tail_x.shape[1]
+    size_x, depth = tail_y.shape[0], 2 * pairs
     rows = total_ref.shape[0]
     places = out_ref.shape[0]
     totals = (even_total, odd_total)
@@ -353,13 +349,15 @@
     def key_at(number, i, j, z):
         return keys[number, i, j, z]
 
-    def couple(left0, left1, head):
-        return upright(product(jnp.concatenate([left0, left1], axis=1), paired_weights(head))).astype(jnp.bfloat16)
+    def couplings(tail, head):
+        left = jnp.concatenate(tail, axis=1)
+        four = product(left, four_weights(*head)).astype(jnp.bfloat16)
+        return four[:, :LANES], four[:, LANES:]
 
     def ahead(tail, head, turned, key):
-        couples = [couple(tail[2 * p], tail[2 * p + 1], head[p]) for p in range(pairs)]
         for h in range(pairs // 2):
-            four = two_pairs(product(turned[h], apart(couples[2 * h], couples[2 * h + 1])))
+            couples = couplings([tail[2 * h], tail[2 * h + 1]], [head[2 * h], head[2 * h + 1]])
+            four = two_pairs(product(turned[h], apart(*couples)))
             yield [(totals[number % 2], key(4 * h + number), term) for number, term in enumerate(four)]
 
     def back(natural, rim, key):
@@ -394,12 +392,16 @@
             batch for i in range(size_x) for batch in back(natural_y.at[i, 0], got_y.at[i], functools.partial(key_at, 3, i, 0)))
 
     batches = []
-    for t in range(got_z.shape[0]):
-        i, j = 2 * t // size_y, 2 * t % size_y
-        front = folded(across(last_z[t], couple(tail_z[2 * t], tail_z[2 * t + 1], got_z[t])))
-        past = folded(across(first_z[t], back_z[t]))
-        batches.append([(totals[side], keys[6, i, j + side, depth - 1], front[side]) for side in (0, 1)]
-                       + [(totals[side], keys[5, i, j + side, 0], past[side]) for side in (0, 1)])
+    even = place_ref[2] == 0
+    for t in range(0, near_z.shape[0], 2):
+        heads = [jnp.where(even, near_z[u], far_z[u]) for u in (t, t + 1)]
+        couples = couplings([tail_z[t], tail_z[t + 1]], heads)
+        for u in (t, t + 1):
+            i, j = 2 * u // size_y, 2 * u % size_y
+            front = folded(across(last_z[u], couples[u - t]))
+            past = folded(across(first_z[u], jnp.where(even, far_z[u], near_z[u])))
+            batches.append([(totals[side], keys[6, i, j + side, depth - 1], front[side]) for side in (0, 1)]
+                           + [(totals[side], keys[5, i, j + side, 0], past[side]) for side in (0, 1)])
     add_batches(batches)
 
     for owner in range(places // capacity):
@@ -413,9 +415,8 @@
         for s in range(SLOTS):
             key = r * SLOTS + s
             even, odd = [
-                even_total[key, pl.ds(first, HALF // 2, stride=2), :] + odd_total[key, pl.ds(first, HALF // 2, stride=2), :]
-                for first in (0, 1)]
-            out_ref[spot, HALF * s : HALF * (s + 1), :] = (total_ref[key] + straightened(even, odd)).astype(jnp.bfloat16)
+                sum(total[key, pl.ds(first, HALF // 2, stride=2), :] for total in (total_ref,) + totals) for first in (0, 1)]
+            out_ref[spot, HALF * s : HALF * (s + 1), :] = straightened(even, odd).astype(jnp.bfloat16)
 
 
 def border(owners, place, keys, operands, turned, natural, ends, capacity, places, sizes):
@@ -468,11 +469,6 @@
     )(source, rows)
 
 
-def swap(block, axis):
-    assert lax.axis_size(axis) == 2
-    return lax.ppermute(block, axis, [(0, 1), (1, 0)])
-
-
 def shards(a_diag, a_face, prolong, aggregate, pair_slot, row_owner):
     size_x, size_y, size_z, block = a_diag.shape
     sizes = (size_x, size_y, size_z)
@@ -482,19 +478,20 @@
     holding = capacity * depth
     diag = a_diag.reshape(columns, size_z, block)
     faces = a_face.reshape(3, columns, size_z, block)
-    place = jnp.stack([lax.axis_index("gx"), lax.axis_index("gy")]).astype(jnp.int32)
+    assert lax.axis_size("gx") == 2 and lax.axis_size("gy") == 2
+    place = jnp.stack([lax.axis_index("gx"), lax.axis_index("gy"), lax.axis_index("gz") % 2]).astype(jnp.int32)
     keys = aggregate[None] * SLOTS + pair_slot
 
-    natural, turned, swap_x, swap_y, head_z, rim_z, last_z, tail_x, tail_y, tail_z = prepare(
+    natural, turned, swap_x, swap_y, near_z, far_z, first_z, last_z, tail_x, tail_y, tail_z = prepare(
         place, prolong.reshape(columns, size_z, block), faces, sizes)
-    got_z = passed_along(head_z, "gz", -1)
-    back_z = passed_along(rim_z, "gz", 1)
-    got_y = swap(swap_y, "gy")
-    got_x = swap(swap_x, "gx")
+    near_z = swapped_along(near_z, "gz", 0)
+    far_z = swapped_along(far_z, "gz", 1)
+    got_y = swapped_along(swap_y, "gy", 0)
+    got_x = swapped_along(swap_x, "gx", 0)
     total = interior(keys, diag, faces, natural, turned, sizes)
     outgoing = border(
-        row_owner, place, keys, (got_x, got_y, got_z, back_z, tail_x, tail_y, tail_z), turned, natural,
-        (head_z, last_z, total), capacity, holding, sizes)
+        row_owner, place, keys, (got_x, got_y, near_z, far_z, tail_x, tail_y, tail_z), turned, natural,
+        (first_z, last_z, total), capacity, holding, sizes)
     arrived = lax.all_to_all(outgoing, "gz", 0, 0, tiled=True)
     source = jnp.arange(holding, dtype=jnp.int32)
     if holding != AGG_DEV:

time: 84.3 us -> 79.3 us (0.941)
  starting transfers between devices: 8.3 us -> 4.64 us
  Pallas kernels: 37.4 us -> 35.4 us
    ppermute x4, starting transfers between devices: 8.3 us -> 4.64 us  [swapped_along(): return lax.ppermute(block, axis, pairs + [(i + 1, i) for i, _ in pairs])]
    pallas_call x1, Pallas kernels: 19.8 us -> 17.9 us  [interior(): pl.pallas_call(interior_kernel, grid=(size_x,), in_specs=[pl.BlockSpec(me...]
  transfers between devices with their start and end apart: 4 -> 4, of which waited for: 0 -> 0; matrix products, arithmetic and copies ran while one was open for 0% -> 0% of each run, Pallas kernels for 24% -> 23%
where the time goes in v7:
time: 79.3 us; the launch traced here: 79.1 us
  blocking collectives  38.7 us (49%)
  Pallas kernels  35.4 us (45%)
  starting transfers between devices  4.64 us (6%)
    all_to_all x1, blocking collectives, shards(): arrived = lax.all_to_all(outgoing, 'gz', 0, 0, tiled=True)  38.7 us
    pallas_call x1, Pallas kernels, interior(): pl.pallas_call(interior_kernel, grid=(size_x,), in_specs=[pl.BlockSpec(me...  17.9 us
    pallas_call x1, Pallas kernels, border(): pl.pallas_call(functools.partial(border_kernel, capacity), grid=(1,), in_...  8.68 us
    pallas_call x1, Pallas kernels, prepare(): pl.pallas_call(prepare_kernel, grid=(size_x,), in_specs=[pl.BlockSpec(mem...  6.2 us
    ppermute x4, starting transfers between devices, swapped_along(): return lax.ppermute(block, axis, pairs + [(i + 1, i) for i, _ in pairs])  4.64 us
    pallas_call x1, Pallas kernels, laid_out(): pl.pallas_call(layout_kernel, grid=(places // height,), in_specs=[pl.Bloc...  2.63 us
  transfers between devices with their start and end apart: 4, of which 0 were waited for; matrix products, arithmetic and copies ran while one was open for 0% of the time, Pallas kernels for 23%

profile of v7, /device:TPU:0, one launch (start us, length us, event | category | flops | bytes accessed | tf_op | source)
XLA Modules:
  0.0 79.1 jit_solution(17240918700987208773)
XLA Ops:
  0.0 0.1 pad_add_fusion.place_ref
  0.1 0.0 slice-start
  0.1 0.0 copy-start.3
  0.1 0.0 copy-start.2
  0.1 0.0 slice-start.1
  0.1 0.0 copy-start
  0.1 6.2 %prepare.1 = (bf16[24,4,64,128]{3,2,1,0:T(8,128)(2,1)S(1)}, bf16[24,2,128,128]{3,2,1,0:T(8,128)(2,1)S(1)}, bf16[6,4,64,128]{3,2,1,0:T(8,128)(2,1)S(1)}, bf16[4,4...) custom-call(s32[3]{0:T(128)S(1)} %pad_add_fusion.place_ref, ...), custom_call_target="tpu_custom_call" | custom-call | tf_op jit(solution)/shard_map/prepare/pallas_call | solution.py:177
  6.3 0.1 collective-permute-start
  6.4 2.4 %collective-permute-start.1 = (bf16[4,4,64,128]{3,2,1,0:T(8,128)(2,1)S(1)}, bf16[4,4,64,128]{3,2,1,0:T(8,128)(2,1)S(1)}, u32[]{:S(2)}, u32[]{:S(2)}) collective-permute-start(bf16[4,4,64,128]{3,2,1,0:T(8,128)(2,1)S(1)} %get-tuple-element.17), channel_id=1, source_target_pairs={{0,8},{8,0},{1,9},{9,1},{2,10},{10,2},{3,11},{11,3},{4,12},{12,4},... | collective-permute-start | bytes 786440 | tf_op jit(solution)/shard_map/ppermute | solution.py:21
  8.8 1.5 %collective-permute-start.2 = (bf16[12,64,128]{2,1,0:T(8,128)(2,1)S(1)}, bf16[12,64,128]{2,1,0:T(8,128)(2,1)S(1)}, u32[]{:S(2)}, u32[]{:S(2)}) collective-permute-start(bf16[12,64,128]{2,1,0:T(8,128)(2,1)S(1)} %get-tuple-element.18), channel_id=1, source_target_pairs={{0,1},{2,3},{4,5},{6,7},{1,0},{3,2},{5,4},{7,6},{8,9},{10,11},{12,... | collective-permute-start | bytes 589832 | tf_op jit(solution)/shard_map/ppermute | solution.py:21
  10.3 0.7 collective-permute-start.3
  11.0 0.0 copy-done.3
  11.0 0.0 copy-done.2
  11.0 0.0 slice-done
  11.0 0.0 slice-done.1
  11.1 0.0 copy-done
  11.1 0.0 copy-start.1
  11.1 17.9 %interior.1.total_ref = f32[168,32,128]{2,1,0:T(8,128)S(1)} custom-call(s32[7,4,6,8]{3,2,1,0:T(8,128)S(1)} %copy_add_fusion.keys, bf16[24,8,4096]{2,1,0:T(8,128)(2,1)S(1)} %bitcast.21, bf16[3,24,8,4096]{3,2,1,0:T(8,128)(2,1)S(1)} %bitcast.16, bf16[3,24,8,4096]{3,2,1,0:T(8,128)(2,1)S(1)} %bitcast.17, bf16[3,24,8,4096]{3,2,1,0:T(8,128)(2,1)S(1)} %bitcast.18, ...), custom_call_target="tpu_custom_call" | custom-call | flops 704643072 | bytes 9437184 | tf_op jit(solution)/shard_map/interior/pallas_call | solution.py:314
  29.0 0.0 collective-permute-done.2.near_z
  29.0 0.0 collective-permute-done.3.far_z
  29.0 0.0 collective-permute-done.1.got_y
  29.0 0.0 collective-permute-done.got_x
  29.0 0.0 copy-done.1
  29.0 8.7 %border.1 = bf16[24,224,128]{2,1,0:T(8,128)(2,1)S(1)} custom-call(s32[24]{0:T(128)S(1)} %copy-done.1, s32[3]{0:T(128)S(1)} %pad_add_fusion.place_ref, s32[7,4,6,8]{3,2,1,0:T(8,128)S(1)} %copy_add_fusion.keys, bf16[6,4,64,128]{3,2,1,0:T(8,128)(2,1)S(1)} %collective-permute-done.got_x, bf16[4,4,64,128]{3,2,1,0:T(8,128)(2,1)S(1)} %collective-permute-done.1.got_y, ...), custom_call_target="tpu_custom_call" | custom-call | tf_op jit(solution)/shard_map/border/pallas_call | solution.py:429
  37.7 38.7 %all_to_all.5.rows_ref = bf16[24,224,128]{2,1,0:T(8,128)(2,1)S(1)} all-to-all(bf16[24,224,128]{2,1,0:T(8,128)(2,1)S(1)} %border.1), channel_id=1, replica_groups=mesh['gx'=2,'gy'=2,'gz'=8] {'gz'}, dimensions={0} | all-to-all | bytes 2752512 | tf_op jit(solution)/shard_map/all_to_all | solution.py:495
  76.5 2.6 %layout.1 = bf16[7,24,4096]{2,1,0:T(8,128)(2,1)} custom-call(s32[24]{0:T(128)S(1)} %iota.3.source, bf16[24,224,128]{2,1,0:T(8,128)(2,1)S(1)} %all_to_all.5.rows_ref), custom_call_target="tpu_custom_call" | custom-call | tf_op jit(solution)/shard_map/layout/pallas_call | solution.py:460
  (5 shorter events, 0.0 us)
Async XLA Ops:
  0.1 11.0 %slice-start = ((s8[4718592]{0:T(1024)(128)(4,1)}), s8[4194304]{0:T(1024)(128)(4,1)S(1)}, s32[]{:S(2)}) async-start(s8[4718592]{0:T(1024)(128)(4,1)} %bitcast.14), calls=%async_computation.1 | async-start | bytes 8388608
  0.1 10.9 %copy-start.3 = (s32[4,6,8]{2,0,1:T(4,128)S(1)}, s32[4,6,8]{2,0,1:T(4,128)}, u32[]{:S(2)}) copy-start(s32[4,6,8]{2,0,1:T(4,128)} %param.9) | copy-start | bytes 2308
  0.1 10.9 %copy-start.2 = (s32[7,4,6,8]{3,1,2,0:T(4,128)S(1)}, s32[7,4,6,8]{3,1,2,0:T(4,128)}, u32[]{:S(2)}) copy-start(s32[7,4,6,8]{3,1,2,0:T(4,128)} %param.10) | copy-start | bytes 16132
  0.1 11.0 %slice-start.1 = ((s8[4718592]{0:T(1024)(128)(4,1)}), s8[524288]{0:T(1024)(128)(4,1)S(1)}, s32[]{:S(2)}) async-start(s8[4718592]{0:T(1024)(128)(4,1)} %bitcast.14), calls=%async_computation.2 | async-start | bytes 1048576
  0.1 11.0 %copy-start = (bf16[4,6,8,4096]{3,2,1,0:T(8,128)(2,1)S(1)}, bf16[4,6,8,4096]{3,2,1,0:T(8,128)(2,1)}, u32[]{:S(2)}) copy-start(bf16[4,6,8,4096]{3,2,1,0:T(8,128)(2,1)} %param.6) | copy-start | bytes 4718596
  6.3 22.7 %collective-permute-start = (bf16[6,4,64,128]{3,2,1,0:T(8,128)(2,1)S(1)}, bf16[6,4,64,128]{3,2,1,0:T(8,128)(2,1)S(1)}, u32[]{:S(2)}, u32[]{:S(2)}) collective-permute-start(bf16[6,4,64,128]{3,2,1,0:T(8,128)(2,1)S(1)} %get-tuple-element.16), channel_id=1, source_target_pairs={{0,16},{16,0},{1,17},{17,1},{2,18},{18,2},{3,19},{19,3},{4,20},{20... | collective-permute-start | bytes 1179656 | tf_op jit(solution)/shard_map/ppermute | solution.py:21
  6.4 22.6 %collective-permute-start.1 = (bf16[4,4,64,128]{3,2,1,0:T(8,128)(2,1)S(1)}, bf16[4,4,64,128]{3,2,1,0:T(8,128)(2,1)S(1)}, u32[]{:S(2)}, u32[]{:S(2)}) collective-permute-start(bf16[4,4,64,128]{3,2,1,0:T(8,128)(2,1)S(1)} %get-tuple-element.17), channel_id=1, source_target_pairs={{0,8},{8,0},{1,9},{9,1},{2,10},{10,2},{3,11},{11,3},{4,12},{12,4},... | collective-permute-start | bytes 786440 | tf_op jit(solution)/shard_map/ppermute | solution.py:21
  8.8 20.2 %collective-permute-start.2 = (bf16[12,64,128]{2,1,0:T(8,128)(2,1)S(1)}, bf16[12,64,128]{2,1,0:T(8,128)(2,1)S(1)}, u32[]{:S(2)}, u32[]{:S(2)}) collective-permute-start(bf16[12,64,128]{2,1,0:T(8,128)(2,1)S(1)} %get-tuple-element.18), channel_id=1, source_target_pairs={{0,1},{2,3},{4,5},{6,7},{1,0},{3,2},{5,4},{7,6},{8,9},{10,11},{12,... | collective-permute-start | bytes 589832 | tf_op jit(solution)/shard_map/ppermute | solution.py:21
  10.3 18.7 %collective-permute-start.3 = (bf16[12,64,128]{2,1,0:T(8,128)(2,1)S(1)}, bf16[12,64,128]{2,1,0:T(8,128)(2,1)S(1)}, u32[]{:S(2)}, u32[]{:S(2)}) collective-permute-start(bf16[12,64,128]{2,1,0:T(8,128)(2,1)S(1)} %get-tuple-element.19), channel_id=1, source_target_pairs={{1,2},{3,4},{5,6},{2,1},{4,3},{6,5},{9,10},{11,12},{13,14},{10,9},... | collective-permute-start | bytes 589832 | tf_op jit(solution)/shard_map/ppermute | solution.py:21
  11.1 18.0 %copy-start.1 = (s32[24]{0:T(128)S(1)}, s32[24]{0:T(128)}, u32[]{:S(2)}) copy-start(s32[24]{0:T(128)} %owners.1) | copy-start | bytes 292

commit v8 on v7

v8 whole, which is shorter than its diff:
```python
import functools

import jax
import jax.numpy as jnp
from jax import lax
from jax.experimental import pallas as pl
from jax.experimental.pallas import tpu as pltpu
from jax.sharding import PartitionSpec as P

NODES = 64
SLOTS = 7
AGG_DEV = 24
LANES = 128
HALF = NODES // 2
MIB = 1024 * 1024
STEP = 8


def swapped_along(block, axis, first):
    pairs = [(i, i + 1) for i in range(first, lax.axis_size(axis) - 1, 2)]
    return lax.ppermute(block, axis, pairs + [(i + 1, i) for i, _ in pairs])


def low_lanes(rows):
    return lax.broadcasted_iota(jnp.int32, (rows, LANES), 1) < NODES


def swapped(value):
    return pltpu.roll(value, NODES, 1)


def zero_one(mask):
    return mask.astype(jnp.float32).astype(jnp.bfloat16)


def product(left, right):
    return jnp.dot(left, right, preferred_element_type=jnp.float32)


def across(left, right):
    return lax.dot_general(left, right, (((0,), (0,)), ((), ())), preferred_element_type=jnp.float32)


def spread(column, stage):
    depth = column.shape[0]
    for k in range(column.shape[1] // LANES):
        stage[depth * k : depth * (k + 1), :] = column[:, LANES * k : LANES * (k + 1)].astype(jnp.float32)


def block_of(stage, z, depth):
    return stage[pl.ds(z, HALF, stride=depth), :].astype(jnp.bfloat16)


def stacked_pair(first, second):
    low = low_lanes(HALF)
    even = jnp.where(low, first, swapped(second))
    odd = jnp.where(low, swapped(first), second)
    return jnp.concatenate([even, odd], axis=0)


def in_order(pair):
    row = lax.broadcasted_iota(jnp.int32, (NODES, NODES), 0)
    col = lax.broadcasted_iota(jnp.int32, (NODES, NODES), 1)
    return product(zero_one(row == 2 * (col % HALF) + col // HALF), pair).astype(jnp.bfloat16)


def four_weights(first, second):
    low = low_lanes(NODES)
    zero = jnp.zeros_like(first)
    left = [jnp.where(low, first, zero), jnp.where(low, zero, first), zero, zero]
    right = [zero, zero, jnp.where(low, second, zero), jnp.where(low, zero, second)]
    return jnp.concatenate([jnp.concatenate(left, axis=0), jnp.concatenate(right, axis=0)], axis=1)


def four_turned(first, second):
    low = low_lanes(NODES)
    zero = jnp.zeros_like(first)
    left = [jnp.where(low, first, zero), zero, jnp.where(low, zero, first), zero]
    right = [zero, jnp.where(low, second, zero), zero, jnp.where(low, zero, second)]
    return jnp.concatenate([jnp.concatenate(left, axis=0), jnp.concatenate(right, axis=0)], axis=1)


def four_across(first, second):
    turned = jnp.concatenate([first, second], axis=0).T
    return jnp.concatenate([turned[:NODES], turned[NODES:]], axis=1)


def folded_pair(pair):
    low = low_lanes(HALF)
    upper, lower = pair[:HALF], pair[HALF:]
    return [jnp.where(low, upper, swapped(lower)), jnp.where(low, swapped(upper), lower)]


def folded(square):
    low = low_lanes(HALF)
    moved = swapped(jnp.where(low, square[HALF : 2 * HALF], square[2 * HALF : 3 * HALF]))
    return [jnp.where(low, square[:HALF], moved), jnp.where(low, moved, square[3 * HALF :])]


def straightened(even, odd):
    low = low_lanes(HALF // 2)
    return jnp.concatenate([jnp.where(low, even, swapped(odd)), jnp.where(low, swapped(even), odd)], axis=0)


def diagonal(square):
    return jnp.where(low_lanes(NODES), square[:NODES], square[NODES:]).astype(jnp.bfloat16)


def apart(first, second):
    zero = jnp.zeros_like(first)
    return jnp.concatenate([jnp.concatenate([first, zero], axis=1), jnp.concatenate([zero, second], axis=1)], axis=0)


def two_pairs(squares):
    return folded(squares[:, :LANES]) + folded(squares[:, LANES:])


def add_all(updates):
    olds = [total[key] for total, key, _ in updates]
    news = []
    for number, (total, key, value) in enumerate(updates):
        for other, other_key, other_value in updates[:number]:
            if other is total:
                value = value + jnp.where(key == other_key, other_value, jnp.zeros_like(other_value))
        news.append(olds[number] + value)
    for (total, key, _), new in zip(updates, news):
        total[key] = new


def prepare_kernel(place_ref, p_ref, fx_ref, fy_ref, fz_ref, natural_ref, stacked_ref, swap_x_ref, swap_y_ref, near_z_ref, far_z_ref,
                   first_z_ref, last_z_ref, tail_x_ref, tail_y_ref, tail_z_ref, turned_x_ref, turned_y_ref, stages, stages_f, ends):
    plane = pl.program_id(0)
    size_y, depth = p_ref.shape[0], p_ref.shape[1]
    pairs = depth // 2

    for j in range(size_y):
        stage = stages.at[j]
        spread(p_ref[j], stage)
        block = [block_of(stage, z, depth) for z in range(depth)]
        stacked = [stacked_pair(block[2 * p], block[2 * p + 1]) for p in range(pairs)]
        for p in range(pairs):
            stacked_ref[j, p] = stacked[p]
            natural_ref[j, p] = in_order(stacked[p])
        ends[0, j] = block[0]
        ends[1, j] = block[depth - 1]
        stage_f = stages_f.at[j]
        spread(fz_ref[0, j], stage_f)
        last = block_of(stage_f, depth - 1, depth)
        ends[2, j] = last

    for t in range(size_y // 2):
        first, last, face = [stacked_pair(ends[kind, 2 * t], ends[kind, 2 * t + 1]) for kind in range(3)]
        head = in_order(first)
        rim = diagonal(across(face, last))
        first_z_ref[t] = head
        last_z_ref[t] = last
        tail_z_ref[t] = face
        near_z_ref[t] = jnp.where(place_ref[2] == 0, rim, head)
        far_z_ref[t] = jnp.where(place_ref[2] == 0, head, rim)

    def faces(source, stage, j, tails, rims, turned):
        spread(source, stage)
        block = [block_of(stage, z, depth) for z in range(depth)]
        for p in range(pairs):
            tails[p] = stacked_pair(block[2 * p], block[2 * p + 1])
            rims[p] = diagonal(across(tails[p], stacked_ref[j, p]))
        for h in range(pairs // 2):
            turned[h] = jnp.concatenate([stacked_ref[j, 2 * h], stacked_ref[j, 2 * h + 1]], axis=0).T

    @pl.when(place_ref[1] == 0)
    def _():
        faces(fy_ref[0, 0], stages_f.at[0], size_y - 1, tail_y_ref.at[0], swap_y_ref.at[0], turned_y_ref.at[0])

    @pl.when(place_ref[1] != 0)
    def _():
        swap_y_ref[0] = natural_ref[0]

    @pl.when((place_ref[0] == 0) & (plane == pl.num_programs(0) - 1))
    def _():
        for j in range(size_y):
            faces(fx_ref[0, j], stages_f.at[j], j, tail_x_ref.at[j], swap_x_ref.at[j], turned_x_ref.at[j])

    @pl.when((place_ref[0] != 0) & (plane == 0))
    def _():
        swap_x_ref[...] = natural_ref[...]


def prepare(place, prolong, faces, sizes):
    size_x, size_y, depth = sizes
    pairs, block = depth // 2, prolong.shape[-1]
    columns, half = size_x * size_y, size_y // 2
    shape = lambda *dims: jax.ShapeDtypeStruct(dims, jnp.bfloat16)
    by_half = pl.BlockSpec((half, NODES, LANES), lambda i: (i, 0, 0))
    edge = shape(columns // 2, NODES, LANES)
    stage = pltpu.VMEM((size_y, depth * HALF, LANES), jnp.float32)
    return pl.pallas_call(
        prepare_kernel,
        grid=(size_x,),
        in_specs=[
            pl.BlockSpec(memory_space=pltpu.SMEM),
            pl.BlockSpec((size_y, depth, block), lambda i: (i, 0, 0)),
            pl.BlockSpec((1, size_y, depth, block), lambda i: (0, size_x - 1, 0, 0)),
            pl.BlockSpec((1, 1, depth, block), lambda i: (1, i * size_y + size_y - 1, 0, 0)),
            pl.BlockSpec((1, size_y, depth, block), lambda i: (2, i, 0, 0)),
        ],
        out_specs=[
            pl.BlockSpec((size_y, pairs, NODES, LANES), lambda i: (i, 0, 0, 0)),
            pl.BlockSpec((size_y, pairs, NODES, LANES), lambda i: (i, 0, 0, 0)),
            pl.BlockSpec((size_y, pairs, NODES, LANES), lambda i: (0, 0, 0, 0)),
            pl.BlockSpec((1, pairs, NODES, LANES), lambda i: (i, 0, 0, 0)),
            by_half, by_half, by_half, by_half,
            pl.BlockSpec((size_y, pairs, NODES, LANES), lambda i: (0, 0, 0, 0)),
            pl.BlockSpec((1, pairs, NODES, LANES), lambda i: (i, 0, 0, 0)),
            by_half,
            pl.BlockSpec((size_y, pairs // 2, LANES, LANES), lambda i: (0, 0, 0, 0)),
            pl.BlockSpec((1, pairs // 2, LANES, LANES), lambda i: (i, 0, 0, 0)),
        ],
        out_shape=[
            shape(columns, pairs, NODES, LANES), shape(columns, pairs, NODES, LANES),
            shape(size_y, pairs, NODES, LANES), shape(size_x, pairs, NODES, LANES), edge, edge, edge, edge,
            shape(size_y, pairs, NODES, LANES), shape(size_x, pairs, NODES, LANES), edge,
            shape(size_y, pairs // 2, LANES, LANES), shape(size_x, pairs // 2, LANES, LANES),
        ],
        scratch_shapes=[
            stage, stage,
            pltpu.VMEM((3, size_y, HALF, LANES), jnp.bfloat16),
        ],
        compiler_params=pltpu.CompilerParams(vmem_limit_bytes=48 * MIB),
        name="prepare",
    )(place, prolong, faces, faces, faces)


def interior_kernel(keys, diag_ref, face_ref, natural_ref, stacked_ref, out_ref,
                    stages, couples, ahead_even, ahead_odd, behind_even, behind_odd, wide):
    _, size_x, size_y, depth = keys.shape
    pairs = depth // 2
    spare = out_ref.shape[0]
    ahead, behind = (ahead_even, ahead_odd), (behind_even, behind_odd)

    for total in ahead + behind:
        total[...] = jnp.zeros_like(total)

    def couplings(column, stage):
        below_x = jnp.maximum(column - size_y, 0)
        below_y = jnp.maximum(column - 1, 0)
        places = (column, below_x, below_y, column)
        sources = (diag_ref[column], face_ref[0, below_x], face_ref[1, below_y], face_ref[2, column])
        stacked = []
        for face in range(4):
            spread(sources[face], stage.at[face])
            shift = 1 if face == 3 else 0
            block = [block_of(stage.at[face], z, depth) for z in range(depth)]
            stacked.append([stacked_pair(block[(2 * p - shift) % depth], block[2 * p + 1 - shift]) for p in range(pairs)])
        found = [[] for _ in range(4)]
        for h in range(pairs // 2):
            left = [jnp.concatenate([stacked[face][2 * h], stacked[face][2 * h + 1]], axis=1) for face in range(4)]
            weights = four_weights(natural_ref[column, 2 * h], natural_ref[column, 2 * h + 1])
            four = product(jnp.concatenate(left, axis=0), weights).astype(jnp.bfloat16)
            for face in range(4):
                rows = four[NODES * face : NODES * (face + 1)]
                for couple in (rows[:, :LANES], rows[:, LANES:]):
                    found[face].append(swapped(couple) if face == 3 else couple)
        low = low_lanes(NODES)
        along = found[3]
        found[3] = [jnp.where(low, along[p], along[min(p + 1, pairs - 1)]) for p in range(pairs)]
        for face in range(4):
            for h in range(pairs // 2):
                couples[places[face], h, face] = four_across(found[face][2 * h], found[face][2 * h + 1])

    def form(step, carry):
        for u in range(2):
            couplings(2 * step + u, stages.at[u])
        return carry

    lax.fori_loop(0, size_x * size_y // 2, form, 0)

    def sums(i, j):
        has_x, has_y = i + 1 < size_x, j + 1 < size_y
        next_x, next_y = jnp.minimum(i + 1, size_x - 1), jnp.minimum(j + 1, size_y - 1)
        batches = []
        for h in range(pairs // 2):
            column = i * size_y + j
            weights = four_turned(stacked_ref[column, 2 * h], stacked_ref[column, 2 * h + 1])
            terms = product(couples[column, h].reshape(4 * NODES, 4 * NODES), weights)
            for face in range(4):
                rows = terms[NODES * face : NODES * (face + 1)]
                four = folded_pair(rows[:, :LANES]) + folded_pair(rows[:, LANES:])
                updates = []
                for number, term in enumerate(four):
                    z, side = 4 * h + number, number % 2
                    if face == 0:
                        updates.append((ahead[side], keys[0, i, j, z], term))
                        continue
                    if face == 1:
                        here, there = keys[2, i, j, z], keys[1, next_x, j, z]
                        here, there = jnp.where(has_x, here, spare), jnp.where(has_x, there, spare)
                    elif face == 2:
                        here, there = keys[4, i, j, z], keys[3, i, next_y, z]
                        here, there = jnp.where(has_y, here, spare), jnp.where(has_y, there, spare)
                    elif z + 1 < depth:
                        here, there = keys[6, i, j, z], keys[5, i, j, z + 1]
                    else:
                        continue
                    updates.append((ahead[side], here, term))
                    updates.append((behind[side], there, term))
                batches.append(updates)
        return batches

    def add(step, carry):
        i, first = step // (size_y // 2), 2 * (step % (size_y // 2))
        for updates in [updates for u in range(2) for updates in sums(i, first + u)]:
            add_all(updates)
        return carry

    lax.fori_loop(0, size_x * size_y // 2, add, 0)

    def finish(g, carry):
        low = low_lanes(HALF)
        spots = [(p, [wide.shape[0] * 2 * g + 2 * p + side for side in (0, 1)]) for p in range(wide.shape[0])]
        for p, key in spots:
            one, two = [ahead_even[key[side]] + ahead_odd[key[side]] for side in (0, 1)]
            upper = jnp.where(low, one, swapped(two))
            lower = jnp.where(low, swapped(one), two)
            wide[p, :, :NODES] = jnp.concatenate([upper, lower], axis=0).T
        for p, key in spots:
            for side in (0, 1):
                first = wide[p, NODES * side : NODES * side + HALF, :]
                second = wide[p, NODES * side + HALF : NODES * (side + 1), :]
                turned = jnp.where(low, first, swapped(second))
                out_ref[key[side]] = (behind_even[key[side]] + behind_odd[key[side]]) + turned
        return carry

    lax.fori_loop(0, spare // (2 * wide.shape[0]), finish, 0)


def interior(keys, diag, faces, natural, stacked, sizes):
    size_x, size_y, depth = sizes
    pairs, block = depth // 2, diag.shape[-1]
    columns, rows = size_x * size_y, AGG_DEV * SLOTS
    total = pltpu.VMEM((rows + 1, HALF, LANES), jnp.float32)
    whole = pl.BlockSpec(memory_space=pltpu.VMEM)
    return pl.pallas_call(
        interior_kernel,
        in_specs=[pl.BlockSpec(memory_space=pltpu.SMEM), whole, whole, whole, whole],
        out_specs=whole,
        out_shape=jax.ShapeDtypeStruct((rows, HALF, LANES), jnp.float32),
        scratch_shapes=[
            pltpu.VMEM((2, 4, depth * HALF, LANES), jnp.float32),
            pltpu.VMEM((columns, pairs // 2, 4, NODES, 4 * NODES), jnp.bfloat16),
            total, total, total, total,
            pltpu.VMEM((12, LANES, LANES), jnp.float32),
        ],
        compiler_params=pltpu.CompilerParams(vmem_limit_bytes=28 * MIB),
        cost_estimate=pl.CostEstimate(flops=columns * depth * 14 * NODES**3, bytes_accessed=columns * depth * 6 * block * 2, transcendentals=0),
        name="interior",
    )(keys, diag, faces, natural, stacked)


def border_kernel(capacity, owners, place_ref, keys, got_x, got_y, near_z, far_z, tail_x, tail_y, tail_z, turned_x, turned_y,
                  natural_x, natural_y, first_z, last_z, start_ref, out_ref, total, filled):
    size_y, pairs = tail_x.shape[0], tail_x.shape[1]
    size_x, depth = tail_y.shape[0], 2 * pairs
    rows = start_ref.shape[0]
    places = out_ref.shape[0]

    def key_at(number, i, j, z):
        return keys[number, i, j, z]

    def couplings(tail, head):
        left = jnp.concatenate(tail, axis=1)
        four = product(left, four_weights(*head)).astype(jnp.bfloat16)
        return four[:, :LANES], four[:, LANES:]

    def ahead(tail, head, turned, key):
        for h in range(pairs // 2):
            couples = couplings([tail[2 * h], tail[2 * h + 1]], [head[2 * h], head[2 * h + 1]])
            four = two_pairs(product(turned[h], apart(*couples)))
            yield [(total, key(4 * h + number), term) for number, term in enumerate(four)]

    def back(natural, rim, key):
        for h in range(pairs // 2):
            four = [term for p in (2 * h, 2 * h + 1) for term in folded(across(natural[p], rim[p]))]
            yield [(total, key(4 * h + number), term) for number, term in enumerate(four)]

    def add_batches(batches):
        for updates in list(batches):
            add_all(updates)

    @pl.when(place_ref[0] == 0)
    def _():
        add_batches(
            batch for j in range(size_y)
            for batch in ahead(tail_x.at[j], got_x.at[j], turned_x.at[j], functools.partial(key_at, 2, size_x - 1, j)))

    @pl.when(place_ref[0] != 0)
    def _():
        add_batches(
            batch for j in range(size_y) for batch in back(natural_x.at[j], got_x.at[j], functools.partial(key_at, 1, 0, j)))

    @pl.when(place_ref[1] == 0)
    def _():
        add_batches(
            batch for i in range(size_x)
            for batch in ahead(tail_y.at[i], got_y.at[i], turned_y.at[i], functools.partial(key_at, 4, i, size_y - 1)))

    @pl.when(place_ref[1] != 0)
    def _():
        add_batches(
            batch for i in range(size_x) for batch in back(natural_y.at[i, 0], got_y.at[i], functools.partial(key_at, 3, i, 0)))

    batches = []
    even = place_ref[2] == 0
    for t in range(0, near_z.shape[0], 2):
        heads = [jnp.where(even, near_z[u], far_z[u]) for u in (t, t + 1)]
        couples = couplings([tail_z[t], tail_z[t + 1]], heads)
        for u in (t, t + 1):
            i, j = 2 * u // size_y, 2 * u % size_y
            front = folded(across(last_z[u], couples[u - t]))
            past = folded(across(first_z[u], jnp.where(even, far_z[u], near_z[u])))
            batches.append([(total, keys[6, i, j + side, depth - 1], front[side]) for side in (0, 1)]
                           + [(total, keys[5, i, j + side, 0], past[side]) for side in (0, 1)])
    add_batches(batches)

    for owner in range(places // capacity):
        filled[owner] = 0
    if places * SLOTS != rows:
        out_ref[...] = jnp.zeros_like(out_ref)
    for r in range(rows // SLOTS):
        owner = owners[r]
        spot = owner * capacity + filled[owner]
        filled[owner] = filled[owner] + 1
        for s in range(SLOTS):
            key = r * SLOTS + s
            even, odd = [total[key, pl.ds(first, HALF // 2, stride=2), :] for first in (0, 1)]
            out_ref[spot, HALF * s : HALF * (s + 1), :] = straightened(even, odd).astype(jnp.bfloat16)


def border(owners, place, keys, operands, natural, ends, total, capacity, places, sizes):
    size_x, size_y, depth = sizes
    pairs = depth // 2
    smem = pl.BlockSpec(memory_space=pltpu.SMEM)
    whole = pl.BlockSpec(memory_space=pltpu.VMEM)
    before = 3 + len(operands) + 2 + len(ends)
    return pl.pallas_call(
        functools.partial(border_kernel, capacity),
        grid=(1,),
        in_specs=[smem, smem, smem] + [whole] * len(operands) + [
            pl.BlockSpec((size_y, pairs, NODES, LANES), lambda i: (0, 0, 0, 0)),
            pl.BlockSpec((size_x, 1, pairs, NODES, LANES), lambda i: (0, 0, 0, 0, 0)),
        ] + [whole] * (len(ends) + 1),
        out_specs=[whole, whole],
        out_shape=[
            jax.ShapeDtypeStruct((places, SLOTS * HALF, LANES), jnp.bfloat16),
            jax.ShapeDtypeStruct(total.shape, total.dtype),
        ],
        input_output_aliases={before: 1},
        scratch_shapes=[pltpu.SMEM((places // capacity,), jnp.int32)],
        compiler_params=pltpu.CompilerParams(vmem_limit_bytes=18 * MIB),
        name="border",
    )(owners, place, keys, *operands, natural, natural.reshape((size_x, size_y) + natural.shape[1:]), *ends, total)[0]


def layout_kernel(*refs):
    source, (rows_ref, out_ref, stage) = refs[:-3], refs[-3:]
    group = pl.program_id(0)
    height = out_ref.shape[1]
    for s in range(SLOTS):
        for r in range(height):
            row = group * height + r
            if source:
                row = source[0][row]
            block = rows_ref[jnp.maximum(row, 0), HALF * s : HALF * (s + 1), :].astype(jnp.float32)
            if source:
                block = jnp.where(row >= 0, block, jnp.zeros_like(block))
            stage[s, pl.ds(r, HALF, stride=height), :] = block
        for k in range(HALF):
            out_ref[s, :, LANES * k : LANES * (k + 1)] = stage[s, height * k : height * (k + 1), :].astype(jnp.bfloat16)


def laid_out(source, rows, block):
    places, height = rows.shape[0], 8
    return pl.pallas_call(
        layout_kernel,
        grid=(places // height,),
        in_specs=[pl.BlockSpec(memory_space=pltpu.SMEM)] * len(source) + [pl.BlockSpec(memory_space=pltpu.VMEM)],
        out_specs=pl.BlockSpec((SLOTS, height, block), lambda g: (0, g, 0)),
        out_shape=jax.ShapeDtypeStruct((SLOTS, places, block), jnp.bfloat16),
        scratch_shapes=[pltpu.VMEM((SLOTS, height * HALF, LANES), jnp.float32)],
        compiler_params=pltpu.CompilerParams(vmem_limit_bytes=10 * MIB),
        name="layout",
    )(*source, rows)


def shards(a_diag, a_face, prolong, aggregate, pair_slot, row_owner):
    size_x, size_y, size_z, block = a_diag.shape
    sizes = (size_x, size_y, size_z)
    columns = size_x * size_y
    depth = lax.axis_size("gz")
    capacity = max(2, (AGG_DEV + depth - 1) // depth)
    holding = capacity * depth
    diag = a_diag.reshape(columns, size_z, block)
    faces = a_face.reshape(3, columns, size_z, block)
    assert lax.axis_size("gx") == 2 and lax.axis_size("gy") == 2
    place = jnp.stack([lax.axis_index("gx"), lax.axis_index("gy"), lax.axis_index("gz") % 2]).astype(jnp.int32)
    keys = aggregate[None] * SLOTS + pair_slot

    (natural, stacked, swap_x, swap_y, near_z, far_z, first_z, last_z, tail_x, tail_y, tail_z, turned_x, turned_y) = prepare(
        place, prolong.reshape(columns, size_z, block), faces, sizes)
    near_z = swapped_along(near_z, "gz", 0)
    far_z = swapped_along(far_z, "gz", 1)
    got_y = swapped_along(swap_y, "gy", 0)
    got_x = swapped_along(swap_x, "gx", 0)
    total = interior(keys, diag, faces, natural, stacked, sizes)
    outgoing = border(
        row_owner, place, keys, (got_x, got_y, near_z, far_z, tail_x, tail_y, tail_z, turned_x, turned_y), natural,
        (first_z, last_z), total, capacity, holding, sizes)
    arrived = lax.all_to_all(outgoing, "gz", 0, 0, tiled=True)
    sources = []
    if holding != AGG_DEV:
        source = jnp.arange(holding, dtype=jnp.int32)
        owner_ids = jnp.arange(depth, dtype=jnp.int32)
        counts = jnp.sum((row_owner[:, None] == owner_ids[None, :]).astype(jnp.int32), axis=0)
        arrived_counts = lax.all_to_all(counts, "gz", 0, 0, tiled=True)
        present = source % capacity < jnp.repeat(arrived_counts, capacity)
        target = jnp.cumsum(present.astype(jnp.int32)) - 1
        match = (present[None, :] & (target[None, :] == source[:, None])).astype(jnp.int32)
        sources = [jnp.sum(match * (source[None, :] + 1), axis=1) - 1]
    result = laid_out(sources, arrived, block)
    return jnp.transpose(result, (1, 0, 2)).reshape(1, 1, 1, holding, SLOTS, block)


def solution(mesh):
    return jax.shard_map(
        shards,
        mesh=mesh,
        in_specs=(
            P("gx", "gy", "gz", None),
            P(None, "gx", "gy", "gz", None),
            P("gx", "gy", "gz", None),
            P("gx", "gy", "gz"),
            P(None, "gx", "gy", "gz"),
            P(("gx", "gy", "gz")),
        ),
        out_specs=P("gx", "gy", "gz", None, None, None),
        check_vma=False,
    )
```

time: 79.3 us -> 82.5 us (1.040)
  Pallas kernels: 35.4 us -> 37.8 us
  blocking collectives: 38.7 us -> 39.6 us
    pallas_call x1, Pallas kernels: 17.9 us -> 21.2 us  [interior(): pl.pallas_call(interior_kernel, in_specs=[pl.BlockSpec(memory_space=pltpu...]
    all_to_all x1, blocking collectives: 38.7 us -> 39.6 us  [shards(): arrived = lax.all_to_all(outgoing, 'gz', 0, 0, tiled=True)]
  transfers between devices with their start and end apart: 4 -> 4, of which waited for: 0 -> 0; matrix products, arithmetic and copies ran while one was open for 0% -> 0% of each run, Pallas kernels for 23% -> 26%
where the time goes in v8:
time: 82.5 us; the launch traced here: 82.3 us
  blocking collectives  39.6 us (48%)
  Pallas kernels  37.8 us (46%)
  starting transfers between devices  4.64 us (6%)
    all_to_all x1, blocking collectives, shards(): arrived = lax.all_to_all(outgoing, 'gz', 0, 0, tiled=True)  39.6 us
    pallas_call x1, Pallas kernels, interior(): pl.pallas_call(interior_kernel, in_specs=[pl.BlockSpec(memory_space=pltpu...  21.2 us
    pallas_call x1, Pallas kernels, border(): pl.pallas_call(functools.partial(border_kernel, capacity), grid=(1,), in_...  8.17 us
    pallas_call x1, Pallas kernels, prepare(): pl.pallas_call(prepare_kernel, grid=(size_x,), in_specs=[pl.BlockSpec(mem...  6.45 us
    ppermute x4, starting transfers between devices, swapped_along(): return lax.ppermute(block, axis, pairs + [(i + 1, i) for i, _ in pairs])  4.64 us
    pallas_call x1, Pallas kernels, laid_out(): pl.pallas_call(layout_kernel, grid=(places // height,), in_specs=[pl.Bloc...  1.94 us
  transfers between devices with their start and end apart: 4, of which 0 were waited for; matrix products, arithmetic and copies ran while one was open for 0% of the time, Pallas kernels for 26%

profile of v8, /device:TPU:0, one launch (start us, length us, event | category | flops | bytes accessed | tf_op | source)
XLA Modules:
  0.0 82.3 jit_solution(14128385808349565104)
XLA Ops:
  0.0 0.1 pad_add_fusion.place_ref
  0.1 0.0 slice-start
  0.1 0.0 copy-start.3
  0.1 0.0 copy-start.2
  0.1 0.0 slice-start.1
  0.1 0.0 copy-start
  0.1 6.4 %prepare.1 = (bf16[24,4,64,128]{3,2,1,0:T(8,128)(2,1)S(1)}, bf16[24,4,64,128]{3,2,1,0:T(8,128)(2,1)S(1)}, bf16[6,4,64,128]{3,2,1,0:T(8,128)(2,1)S(1)}, bf16[4,4,...) custom-call(s32[3]{0:T(128)S(1)} %pad_add_fusion.place_ref, ...), custom_call_target="tpu_custom_call" | custom-call | tf_op jit(solution)/shard_map/prepare/pallas_call | solution.py:196
  6.6 3.0 %collective-permute-start.2 = (bf16[12,64,128]{2,1,0:T(8,128)(2,1)S(1)}, bf16[12,64,128]{2,1,0:T(8,128)(2,1)S(1)}, u32[]{:S(2)}, u32[]{:S(2)}) collective-permute-start(bf16[12,64,128]{2,1,0:T(8,128)(2,1)S(1)} %get-tuple-element.21), channel_id=1, source_target_pairs={{0,1},{2,3},{4,5},{6,7},{1,0},{3,2},{5,4},{7,6},{8,9},{10,11},{12,... | collective-permute-start | bytes 589832 | tf_op jit(solution)/shard_map/ppermute | solution.py:21
  9.6 0.7 collective-permute-start.3
  10.3 0.9 %collective-permute-start.1 = (bf16[4,4,64,128]{3,2,1,0:T(8,128)(2,1)S(1)}, bf16[4,4,64,128]{3,2,1,0:T(8,128)(2,1)S(1)}, u32[]{:S(2)}, u32[]{:S(2)}) collective-permute-start(bf16[4,4,64,128]{3,2,1,0:T(8,128)(2,1)S(1)} %get-tuple-element.20), channel_id=1, source_target_pairs={{0,8},{8,0},{1,9},{9,1},{2,10},{10,2},{3,11},{11,3},{4,12},{12,4},... | collective-permute-start | bytes 786440 | tf_op jit(solution)/shard_map/ppermute | solution.py:21
  11.2 0.0 collective-permute-start
  11.2 0.0 copy-done.3
  11.2 0.0 copy-done.2
  11.3 0.0 slice-done
  11.3 0.0 slice-done.1
  11.3 0.0 copy-done
  11.3 0.0 copy-start.1
  11.3 21.2 %interior.1.start_ref = f32[168,32,128]{2,1,0:T(8,128)S(1)} custom-call(s32[7,4,6,8]{3,2,1,0:T(8,128)S(1)} %copy_add_fusion.keys, bf16[24,8,4096]{2,1,0:T(8,128)(2,1)S(1)} %bitcast.17, bf16[3,24,8,4096]{3,2,1,0:T(8,128)(2,1)S(1)} %bitcast.15, bf16[24,4,64,128]{3,2,1,0:T(8,128)(2,1)S(1)} %get-tuple-element.28.natural_ref.natural_x, ...), custom_call_target="tpu_custom_call" | custom-call | flops 704643072 | bytes 9437184 | tf_op jit(solution)/shard_map/interior/pallas_call | solution.py:342
  32.5 0.0 collective-permute-done.2.near_z
  32.5 0.0 collective-permute-done.3.far_z
  32.5 0.0 collective-permute-done.1.got_y
  32.6 0.0 collective-permute-done.got_x
  32.6 0.0 copy-done.1
  32.6 8.2 %border.1 = (bf16[24,224,128]{2,1,0:T(8,128)(2,1)S(1)}, f32[168,32,128]{2,1,0:T(8,128)S(1)}) custom-call(s32[24]{0:T(128)S(1)} %copy-done.1, s32[3]{0:T(128)S(1)} %pad_add_fusion.place_ref, s32[7,4,6,8]{3,2,1,0:T(8,128)S(1)} %copy_add_fusion.keys, bf16[6,4,64,128]{3,2,1,0:T(8,128)(2,1)S(1)} %collective-permute-done.got_x, ...), custom_call_target="tpu_custom_call", output_to_operand_aliasing={{1}: (16, {})} | custom-call | tf_op jit(solution)/shard_map/border/pallas_call | solution.py:444
  40.8 39.6 %all_to_all.5.refs_0_ = bf16[24,224,128]{2,1,0:T(8,128)(2,1)S(1)} all-to-all(bf16[24,224,128]{2,1,0:T(8,128)(2,1)S(1)} %get-tuple-element.32), channel_id=1, replica_groups=mesh['gx'=2,'gy'=2,'gz'=8] {'gz'}, dimensions={0} | all-to-all | bytes 2752512 | tf_op jit(solution)/shard_map/all_to_all | solution.py:517
  80.4 1.9 %layout.1 = bf16[7,24,4096]{2,1,0:T(8,128)(2,1)} custom-call(bf16[24,224,128]{2,1,0:T(8,128)(2,1)S(1)} %all_to_all.5.refs_0_), custom_call_target="tpu_custom_call" | custom-call | tf_op jit(solution)/shard_map/layout/pallas_call | solution.py:482
  (4 shorter events, 0.0 us)
Async XLA Ops:
  0.1 11.2 %slice-start = ((s8[4718592]{0:T(1024)(128)(4,1)}), s8[4194304]{0:T(1024)(128)(4,1)S(1)}, s32[]{:S(2)}) async-start(s8[4718592]{0:T(1024)(128)(4,1)} %bitcast.13), calls=%async_computation.1 | async-start | bytes 8388608
  0.1 11.1 %copy-start.3 = (s32[4,6,8]{2,0,1:T(4,128)S(1)}, s32[4,6,8]{2,0,1:T(4,128)}, u32[]{:S(2)}) copy-start(s32[4,6,8]{2,0,1:T(4,128)} %param.9) | copy-start | bytes 2308
  0.1 11.1 %copy-start.2 = (s32[7,4,6,8]{3,1,2,0:T(4,128)S(1)}, s32[7,4,6,8]{3,1,2,0:T(4,128)}, u32[]{:S(2)}) copy-start(s32[7,4,6,8]{3,1,2,0:T(4,128)} %param.10) | copy-start | bytes 16132
  0.1 11.2 %slice-start.1 = ((s8[4718592]{0:T(1024)(128)(4,1)}), s8[524288]{0:T(1024)(128)(4,1)S(1)}, s32[]{:S(2)}) async-start(s8[4718592]{0:T(1024)(128)(4,1)} %bitcast.13), calls=%async_computation.2 | async-start | bytes 1048576
  0.1 11.2 %copy-start = (bf16[4,6,8,4096]{3,2,1,0:T(8,128)(2,1)S(1)}, bf16[4,6,8,4096]{3,2,1,0:T(8,128)(2,1)}, u32[]{:S(2)}) copy-start(bf16[4,6,8,4096]{3,2,1,0:T(8,128)(2,1)} %param.6) | copy-start | bytes 4718596
  6.6 26.0 %collective-permute-start.2 = (bf16[12,64,128]{2,1,0:T(8,128)(2,1)S(1)}, bf16[12,64,128]{2,1,0:T(8,128)(2,1)S(1)}, u32[]{:S(2)}, u32[]{:S(2)}) collective-permute-start(bf16[12,64,128]{2,1,0:T(8,128)(2,1)S(1)} %get-tuple-element.21), channel_id=1, source_target_pairs={{0,1},{2,3},{4,5},{6,7},{1,0},{3,2},{5,4},{7,6},{8,9},{10,11},{12,... | collective-permute-start | bytes 589832 | tf_op jit(solution)/shard_map/ppermute | solution.py:21
  9.6 22.9 %collective-permute-start.3 = (bf16[12,64,128]{2,1,0:T(8,128)(2,1)S(1)}, bf16[12,64,128]{2,1,0:T(8,128)(2,1)S(1)}, u32[]{:S(2)}, u32[]{:S(2)}) collective-permute-start(bf16[12,64,128]{2,1,0:T(8,128)(2,1)S(1)} %get-tuple-element.22), channel_id=1, source_target_pairs={{1,2},{3,4},{5,6},{2,1},{4,3},{6,5},{9,10},{11,12},{13,14},{10,9},... | collective-permute-start | bytes 589832 | tf_op jit(solution)/shard_map/ppermute | solution.py:21
  10.3 22.3 %collective-permute-start.1 = (bf16[4,4,64,128]{3,2,1,0:T(8,128)(2,1)S(1)}, bf16[4,4,64,128]{3,2,1,0:T(8,128)(2,1)S(1)}, u32[]{:S(2)}, u32[]{:S(2)}) collective-permute-start(bf16[4,4,64,128]{3,2,1,0:T(8,128)(2,1)S(1)} %get-tuple-element.20), channel_id=1, source_target_pairs={{0,8},{8,0},{1,9},{9,1},{2,10},{10,2},{3,11},{11,3},{4,12},{12,4},... | collective-permute-start | bytes 786440 | tf_op jit(solution)/shard_map/ppermute | solution.py:21
  11.2 21.4 %collective-permute-start = (bf16[6,4,64,128]{3,2,1,0:T(8,128)(2,1)S(1)}, bf16[6,4,64,128]{3,2,1,0:T(8,128)(2,1)S(1)}, u32[]{:S(2)}, u32[]{:S(2)}) collective-permute-start(bf16[6,4,64,128]{3,2,1,0:T(8,128)(2,1)S(1)} %get-tuple-element.19), channel_id=1, source_target_pairs={{0,16},{16,0},{1,17},{17,1},{2,18},{18,2},{3,19},{19,3},{4,20},{20... | collective-permute-start | bytes 1179656 | tf_op jit(solution)/shard_map/ppermute | solution.py:21
  11.3 21.3 %copy-start.1 = (s32[24]{0:T(128)S(1)}, s32[24]{0:T(128)}, u32[]{:S(2)}) copy-start(s32[24]{0:T(128)} %owners.1) | copy-start | bytes 292

commit v9 on v8

--- a/solution.py
+++ b/solution.py
@@ -70,25 +70,6 @@
     left = [jnp.where(low, first, zero), jnp.where(low, zero, first), zero, zero]
     right = [zero, zero, jnp.where(low, second, zero), jnp.where(low, zero, second)]
     return jnp.concatenate([jnp.concatenate(left, axis=0), jnp.concatenate(right, axis=0)], axis=1)
-
-
-def four_turned(first, second):
-    low = low_lanes(NODES)
-    zero = jnp.zeros_like(first)
-    left = [jnp.where(low, first, zero), zero, jnp.where(low, zero, first), zero]
-    right = [zero, jnp.where(low, second, zero), zero, jnp.where(low, zero, second)]
-    return jnp.concatenate([jnp.concatenate(left, axis=0), jnp.concatenate(right, axis=0)], axis=1)
-
-
-def four_across(first, second):
-    turned = jnp.concatenate([first, second], axis=0).T
-    return jnp.concatenate([turned[:NODES], turned[NODES:]], axis=1)
-
-
-def folded_pair(pair):
-    low = low_lanes(HALF)
-    upper, lower = pair[:HALF], pair[HALF:]
-    return [jnp.where(low, upper, swapped(lower)), jnp.where(low, swapped(upper), lower)]
 
 
 def folded(square):
@@ -127,8 +108,8 @@
         total[key] = new
 
 
-def prepare_kernel(place_ref, p_ref, fx_ref, fy_ref, fz_ref, natural_ref, stacked_ref, swap_x_ref, swap_y_ref, near_z_ref, far_z_ref,
-                   first_z_ref, last_z_ref, tail_x_ref, tail_y_ref, tail_z_ref, turned_x_ref, turned_y_ref, stages, stages_f, ends):
+def prepare_kernel(place_ref, p_ref, fx_ref, fy_ref, fz_ref, natural_ref, turned_ref, swap_x_ref, swap_y_ref, near_z_ref, far_z_ref,
+                   first_z_ref, last_z_ref, tail_x_ref, tail_y_ref, tail_z_ref, stages, stages_f, stacks, ends):
     plane = pl.program_id(0)
     size_y, depth = p_ref.shape[0], p_ref.shape[1]
     pairs = depth // 2
@@ -139,8 +120,10 @@
         block = [block_of(stage, z, depth) for z in range(depth)]
         stacked = [stacked_pair(block[2 * p], block[2 * p + 1]) for p in range(pairs)]
         for p in range(pairs):
-            stacked_ref[j, p] = stacked[p]
+            stacks[j, p] = stacked[p]
             natural_ref[j, p] = in_order(stacked[p])
+        for h in range(pairs // 2):
+            turned_ref[j, h] = jnp.concatenate([stacked[2 * h], stacked[2 * h + 1]], axis=0).T
         ends[0, j] = block[0]
         ends[1, j] = block[depth - 1]
         stage_f = stages_f.at[j]
@@ -158,18 +141,16 @@
         near_z_ref[t] = jnp.where(place_ref[2] == 0, rim, head)
         far_z_ref[t] = jnp.where(place_ref[2] == 0, head, rim)
 
-    def faces(source, stage, j, tails, rims, turned):
+    def faces(source, stage, j, tails, rims):
         spread(source, stage)
         block = [block_of(stage, z, depth) for z in range(depth)]
         for p in range(pairs):
             tails[p] = stacked_pair(block[2 * p], block[2 * p + 1])
-            rims[p] = diagonal(across(tails[p], stacked_ref[j, p]))
-        for h in range(pairs // 2):
-            turned[h] = jnp.concatenate([stacked_ref[j, 2 * h], stacked_ref[j, 2 * h + 1]], axis=0).T
+            rims[p] = diagonal(across(tails[p], stacks[j, p]))
 
     @pl.when(place_ref[1] == 0)
     def _():
-        faces(fy_ref[0, 0], stages_f.at[0], size_y - 1, tail_y_ref.at[0], swap_y_ref.at[0], turned_y_ref.at[0])
+        faces(fy_ref[0, 0], stages_f.at[0], size_y - 1, tail_y_ref.at[0], swap_y_ref.at[0])
 
     @pl.when(place_ref[1] != 0)
     def _():
@@ -178,7 +159,7 @@
     @pl.when((place_ref[0] == 0) & (plane == pl.num_programs(0) - 1))
     def _():
         for j in range(size_y):
-            faces(fx_ref[0, j], stages_f.at[j], j, tail_x_ref.at[j], swap_x_ref.at[j], turned_x_ref.at[j])
+            faces(fx_ref[0, j], stages_f.at[j], j, tail_x_ref.at[j], swap_x_ref.at[j])
 
     @pl.when((place_ref[0] != 0) & (plane == 0))
     def _():
@@ -205,24 +186,22 @@
         ],
         out_specs=[
             pl.BlockSpec((size_y, pairs, NODES, LANES), lambda i: (i, 0, 0, 0)),
-            pl.BlockSpec((size_y, pairs, NODES, LANES), lambda i: (i, 0, 0, 0)),
+            pl.BlockSpec((size_y, pairs // 2, LANES, LANES), lambda i: (i, 0, 0, 0)),
             pl.BlockSpec((size_y, pairs, NODES, LANES), lambda i: (0, 0, 0, 0)),
             pl.BlockSpec((1, pairs, NODES, LANES), lambda i: (i, 0, 0, 0)),
             by_half, by_half, by_half, by_half,
             pl.BlockSpec((size_y, pairs, NODES, LANES), lambda i: (0, 0, 0, 0)),
             pl.BlockSpec((1, pairs, NODES, LANES), lambda i: (i, 0, 0, 0)),
             by_half,
-            pl.BlockSpec((size_y, pairs // 2, LANES, LANES), lambda i: (0, 0, 0, 0)),
-            pl.BlockSpec((1, pairs // 2, LANES, LANES), lambda i: (i, 0, 0, 0)),
         ],
         out_shape=[
-            shape(columns, pairs, NODES, LANES), shape(columns, pairs, NODES, LANES),
+            shape(columns, pairs, NODES, LANES), shape(columns, pairs // 2, LANES, LANES),
             shape(size_y, pairs, NODES, LANES), shape(size_x, pairs, NODES, LANES), edge, edge, edge, edge,
             shape(size_y, pairs, NODES, LANES), shape(size_x, pairs, NODES, LANES), edge,
-            shape(size_y, pairs // 2, LANES, LANES), shape(size_x, pairs // 2, LANES, LANES),
         ],
         scratch_shapes=[
             stage, stage,
+            pltpu.VMEM((size_y, pairs, NODES, LANES), jnp.bfloat16),
             pltpu.VMEM((3, size_y, HALF, LANES), jnp.bfloat16),
         ],
         compiler_params=pltpu.CompilerParams(vmem_limit_bytes=48 * MIB),
@@ -230,8 +209,8 @@
     )(place, prolong, faces, faces, faces)
 
 
-def interior_kernel(keys, diag_ref, face_ref, natural_ref, stacked_ref, out_ref,
-                    stages, couples, ahead_even, ahead_odd, behind_even, behind_odd, wide):
+def interior_kernel(keys, diag_ref, face_ref, natural_ref, turned_ref, out_ref,
+                    stages, ahead_even, ahead_odd, behind_even, behind_odd, wide):
     _, size_x, size_y, depth = keys.shape
     pairs = depth // 2
     spare = out_ref.shape[0]
@@ -240,51 +219,39 @@
     for total in ahead + behind:
         total[...] = jnp.zeros_like(total)
 
-    def couplings(column, stage):
-        below_x = jnp.maximum(column - size_y, 0)
-        below_y = jnp.maximum(column - 1, 0)
-        places = (column, below_x, below_y, column)
-        sources = (diag_ref[column], face_ref[0, below_x], face_ref[1, below_y], face_ref[2, column])
-        stacked = []
-        for face in range(4):
-            spread(sources[face], stage.at[face])
+    def couplings(i, j, stage):
+        column = i * size_y + j
+        sources = [diag_ref[column], face_ref[0, jnp.maximum(column - size_y, 0)], face_ref[1, column - 1] if j else None, face_ref[2, column]]
+        stacked = {}
+        for face, source in enumerate(sources):
+            if source is None:
+                continue
+            spread(source, stage.at[face])
             shift = 1 if face == 3 else 0
             block = [block_of(stage.at[face], z, depth) for z in range(depth)]
-            stacked.append([stacked_pair(block[(2 * p - shift) % depth], block[2 * p + 1 - shift]) for p in range(pairs)])
-        found = [[] for _ in range(4)]
+            stacked[face] = [stacked_pair(block[(2 * p - shift) % depth], block[2 * p + 1 - shift]) for p in range(pairs)]
+        couples = {face: [] for face in stacked}
         for h in range(pairs // 2):
-            left = [jnp.concatenate([stacked[face][2 * h], stacked[face][2 * h + 1]], axis=1) for face in range(4)]
+            left = [jnp.concatenate([rows[2 * h], rows[2 * h + 1]], axis=1) for rows in stacked.values()]
             weights = four_weights(natural_ref[column, 2 * h], natural_ref[column, 2 * h + 1])
             four = product(jnp.concatenate(left, axis=0), weights).astype(jnp.bfloat16)
-            for face in range(4):
-                rows = four[NODES * face : NODES * (face + 1)]
+            for number, face in enumerate(stacked):
+                rows = four[NODES * number : NODES * (number + 1)]
                 for couple in (rows[:, :LANES], rows[:, LANES:]):
-                    found[face].append(swapped(couple) if face == 3 else couple)
+                    couples[face].append(swapped(couple) if face == 3 else couple)
         low = low_lanes(NODES)
-        along = found[3]
-        found[3] = [jnp.where(low, along[p], along[min(p + 1, pairs - 1)]) for p in range(pairs)]
-        for face in range(4):
-            for h in range(pairs // 2):
-                couples[places[face], h, face] = four_across(found[face][2 * h], found[face][2 * h + 1])
-
-    def form(step, carry):
-        for u in range(2):
-            couplings(2 * step + u, stages.at[u])
-        return carry
-
-    lax.fori_loop(0, size_x * size_y // 2, form, 0)
-
-    def sums(i, j):
-        has_x, has_y = i + 1 < size_x, j + 1 < size_y
-        next_x, next_y = jnp.minimum(i + 1, size_x - 1), jnp.minimum(j + 1, size_y - 1)
+        along = couples[3]
+        couples[3] = [jnp.where(low, along[p], along[min(p + 1, pairs - 1)]) for p in range(pairs)]
+        return couples
+
+    def sums(i, j, couples):
+        column = i * size_y + j
+        has_x, row_x = i > 0, jnp.maximum(i - 1, 0)
+        origin = {0: column, 1: jnp.maximum(column - size_y, 0), 2: column - 1, 3: column}
         batches = []
         for h in range(pairs // 2):
-            column = i * size_y + j
-            weights = four_turned(stacked_ref[column, 2 * h], stacked_ref[column, 2 * h + 1])
-            terms = product(couples[column, h].reshape(4 * NODES, 4 * NODES), weights)
-            for face in range(4):
-                rows = terms[NODES * face : NODES * (face + 1)]
-                four = folded_pair(rows[:, :LANES]) + folded_pair(rows[:, LANES:])
+            for face, pair in couples.items():
+                four = two_pairs(product(turned_ref[origin[face], h], apart(pair[2 * h], pair[2 * h + 1])))
                 updates = []
                 for number, term in enumerate(four):
                     z, side = 4 * h + number, number % 2
@@ -292,11 +259,10 @@
                         updates.append((ahead[side], keys[0, i, j, z], term))
                         continue
                     if face == 1:
-                        here, there = keys[2, i, j, z], keys[1, next_x, j, z]
+                        here, there = keys[2, row_x, j, z], keys[1, i, j, z]
                         here, there = jnp.where(has_x, here, spare), jnp.where(has_x, there, spare)
                     elif face == 2:
-                        here, there = keys[4, i, j, z], keys[3, i, next_y, z]
-                        here, there = jnp.where(has_y, here, spare), jnp.where(has_y, there, spare)
+                        here, there = keys[4, i, j - 1, z], keys[3, i, j, z]
                     elif z + 1 < depth:
                         here, there = keys[6, i, j, z], keys[5, i, j, z + 1]
                     else:
@@ -306,19 +272,19 @@
                 batches.append(updates)
         return batches
 
-    def add(step, carry):
-        i, first = step // (size_y // 2), 2 * (step % (size_y // 2))
-        for updates in [updates for u in range(2) for updates in sums(i, first + u)]:
+    def plane(i, carry):
+        couples = [couplings(i, j, stages.at[j]) for j in range(size_y)]
+        for updates in [updates for j in range(size_y) for updates in sums(i, j, couples[j])]:
             add_all(updates)
         return carry
 
-    lax.fori_loop(0, size_x * size_y // 2, add, 0)
+    lax.fori_loop(0, size_x, plane, 0)
 
     def finish(g, carry):
         low = low_lanes(HALF)
         spots = [(p, [wide.shape[0] * 2 * g + 2 * p + side for side in (0, 1)]) for p in range(wide.shape[0])]
         for p, key in spots:
-            one, two = [ahead_even[key[side]] + ahead_odd[key[side]] for side in (0, 1)]
+            one, two = [behind_even[key[side]] + behind_odd[key[side]] for side in (0, 1)]
             upper = jnp.where(low, one, swapped(two))
             lower = jnp.where(low, swapped(one), two)
             wide[p, :, :NODES] = jnp.concatenate([upper, lower], axis=0).T
@@ -327,13 +293,13 @@
                 first = wide[p, NODES * side : NODES * side + HALF, :]
                 second = wide[p, NODES * side + HALF : NODES * (side + 1), :]
                 turned = jnp.where(low, first, swapped(second))
-                out_ref[key[side]] = (behind_even[key[side]] + behind_odd[key[side]]) + turned
+                out_ref[key[side]] = (ahead_even[key[side]] + ahead_odd[key[side]]) + turned
         return carry
 
     lax.fori_loop(0, spare // (2 * wide.shape[0]), finish, 0)
 
 
-def interior(keys, diag, faces, natural, stacked, sizes):
+def interior(keys, diag, faces, natural, turned, sizes):
     size_x, size_y, depth = sizes
     pairs, block = depth // 2, diag.shape[-1]
     columns, rows = size_x * size_y, AGG_DEV * SLOTS
@@ -345,15 +311,14 @@
         out_specs=whole,
         out_shape=jax.ShapeDtypeStruct((rows, HALF, LANES), jnp.float32),
         scratch_shapes=[
-            pltpu.VMEM((2, 4, depth * HALF, LANES), jnp.float32),
-            pltpu.VMEM((columns, pairs // 2, 4, NODES, 4 * NODES), jnp.bfloat16),
+            pltpu.VMEM((size_y, 4, depth * HALF, LANES), jnp.float32),
             total, total, total, total,
             pltpu.VMEM((12, LANES, LANES), jnp.float32),
         ],
         compiler_params=pltpu.CompilerParams(vmem_limit_bytes=28 * MIB),
         cost_estimate=pl.CostEstimate(flops=columns * depth * 14 * NODES**3, bytes_accessed=columns * depth * 6 * block * 2, transcendentals=0),
         name="interior",
-    )(keys, diag, faces, natural, stacked)
+    )(keys, diag, faces, natural, turned)
 
 
 def border_kernel(capacity, owners, place_ref, keys, got_x, got_y, near_z, far_z, tail_x, tail_y, tail_z, turned_x, turned_y,
@@ -401,7 +366,7 @@
     def _():
         add_batches(
             batch for i in range(size_x)
-            for batch in ahead(tail_y.at[i], got_y.at[i], turned_y.at[i], functools.partial(key_at, 4, i, size_y - 1)))
+            for batch in ahead(tail_y.at[i], got_y.at[i], turned_y.at[i, 0], functools.partial(key_at, 4, i, size_y - 1)))
 
     @pl.when(place_ref[1] != 0)
     def _():
@@ -435,16 +400,19 @@
             out_ref[spot, HALF * s : HALF * (s + 1), :] = straightened(even, odd).astype(jnp.bfloat16)
 
 
-def border(owners, place, keys, operands, natural, ends, total, capacity, places, sizes):
+def border(owners, place, keys, operands, turned, natural, ends, total, capacity, places, sizes):
     size_x, size_y, depth = sizes
     pairs = depth // 2
     smem = pl.BlockSpec(memory_space=pltpu.SMEM)
     whole = pl.BlockSpec(memory_space=pltpu.VMEM)
-    before = 3 + len(operands) + 2 + len(ends)
+    planes = lambda array: array.reshape((size_x, size_y) + array.shape[1:])
+    before = 3 + len(operands) + 4 + len(ends)
     return pl.pallas_call(
         functools.partial(border_kernel, capacity),
         grid=(1,),
         in_specs=[smem, smem, smem] + [whole] * len(operands) + [
+            pl.BlockSpec((size_y, pairs // 2, LANES, LANES), lambda i: (size_x - 1, 0, 0, 0)),
+            pl.BlockSpec((size_x, 1, pairs // 2, LANES, LANES), lambda i: (0, size_y - 1, 0, 0, 0)),
             pl.BlockSpec((size_y, pairs, NODES, LANES), lambda i: (0, 0, 0, 0)),
             pl.BlockSpec((size_x, 1, pairs, NODES, LANES), lambda i: (0, 0, 0, 0, 0)),
         ] + [whole] * (len(ends) + 1),
@@ -457,7 +425,7 @@
         scratch_shapes=[pltpu.SMEM((places // capacity,), jnp.int32)],
         compiler_params=pltpu.CompilerParams(vmem_limit_bytes=18 * MIB),
         name="border",
-    )(owners, place, keys, *operands, natural, natural.reshape((size_x, size_y) + natural.shape[1:]), *ends, total)[0]
+    )(owners, place, keys, *operands, turned, planes(turned), natural, planes(natural), *ends, total)[0]
 
 
 def layout_kernel(*refs):
@@ -504,15 +472,15 @@
     place = jnp.stack([lax.axis_index("gx"), lax.axis_index("gy"), lax.axis_index("gz") % 2]).astype(jnp.int32)
     keys = aggregate[None] * SLOTS + pair_slot
 
-    (natural, stacked, swap_x, swap_y, near_z, far_z, first_z, last_z, tail_x, tail_y, tail_z, turned_x, turned_y) = prepare(
+    natural, turned, swap_x, swap_y, near_z, far_z, first_z, last_z, tail_x, tail_y, tail_z = prepare(
         place, prolong.reshape(columns, size_z, block), faces, sizes)
     near_z = swapped_along(near_z, "gz", 0)
     far_z = swapped_along(far_z, "gz", 1)
     got_y = swapped_along(swap_y, "gy", 0)
     got_x = swapped_along(swap_x, "gx", 0)
-    total = interior(keys, diag, faces, natural, stacked, sizes)
+    total = interior(keys, diag, faces, natural, turned, sizes)
     outgoing = border(
-        row_owner, place, keys, (got_x, got_y, near_z, far_z, tail_x, tail_y, tail_z, turned_x, turned_y), natural,
+        row_owner, place, keys, (got_x, got_y, near_z, far_z, tail_x, tail_y, tail_z), turned, natural,
         (first_z, last_z), total, capacity, holding, sizes)
     arrived = lax.all_to_all(outgoing, "gz", 0, 0, tiled=True)
     sources = []

time: 82.5 us -> 76.2 us (0.924)
  Pallas kernels: 37.8 us -> 31.4 us
    pallas_call x1, Pallas kernels: 21.2 us -> 15.1 us  [interior(): pl.pallas_call(interior_kernel, in_specs=[pl.BlockSpec(memory_space=pltpu...]
  transfers between devices with their start and end apart: 4 -> 4, of which waited for: 0 -> 0; matrix products, arithmetic and copies ran while one was open for 0% -> 0% of each run, Pallas kernels for 26% -> 20%
where the time goes in v9:
time: 76.2 us; the launch traced here: 76 us
  blocking collectives  39.6 us (52%)
  Pallas kernels  31.4 us (41%)
  starting transfers between devices  4.64 us (6%)
    all_to_all x1, blocking collectives, shards(): arrived = lax.all_to_all(outgoing, 'gz', 0, 0, tiled=True)  39.6 us
    pallas_call x1, Pallas kernels, interior(): pl.pallas_call(interior_kernel, in_specs=[pl.BlockSpec(memory_space=pltpu...  15.1 us
    pallas_call x1, Pallas kernels, border(): pl.pallas_call(functools.partial(border_kernel, capacity), grid=(1,), in_...  8.17 us
    pallas_call x1, Pallas kernels, prepare(): pl.pallas_call(prepare_kernel, grid=(size_x,), in_specs=[pl.BlockSpec(mem...  6.2 us
    ppermute x4, starting transfers between devices, swapped_along(): return lax.ppermute(block, axis, pairs + [(i + 1, i) for i, _ in pairs])  4.64 us
    pallas_call x1, Pallas kernels, laid_out(): pl.pallas_call(layout_kernel, grid=(places // height,), in_specs=[pl.Bloc...  1.94 us
  transfers between devices with their start and end apart: 4, of which 0 were waited for; matrix products, arithmetic and copies ran while one was open for 0% of the time, Pallas kernels for 20%

profile of v9, /device:TPU:0, one launch (start us, length us, event | category | flops | bytes accessed | tf_op | source)
XLA Modules:
  0.0 76.0 jit_solution(6727149351878245638)
XLA Ops:
  0.0 0.1 pad_add_fusion.place_ref
  0.1 0.0 slice-start
  0.1 0.0 copy-start.3
  0.1 0.0 copy-start.2
  0.1 0.0 slice-start.1
  0.1 0.0 copy-start
  0.1 6.2 %prepare.1 = (bf16[24,4,64,128]{3,2,1,0:T(8,128)(2,1)S(1)}, bf16[24,2,128,128]{3,2,1,0:T(8,128)(2,1)S(1)}, bf16[6,4,64,128]{3,2,1,0:T(8,128)(2,1)S(1)}, bf16[4,4...) custom-call(s32[3]{0:T(128)S(1)} %pad_add_fusion.place_ref, ...), custom_call_target="tpu_custom_call" | custom-call | tf_op jit(solution)/shard_map/prepare/pallas_call | solution.py:177
  6.3 3.0 %collective-permute-start.2 = (bf16[12,64,128]{2,1,0:T(8,128)(2,1)S(1)}, bf16[12,64,128]{2,1,0:T(8,128)(2,1)S(1)}, u32[]{:S(2)}, u32[]{:S(2)}) collective-permute-start(bf16[12,64,128]{2,1,0:T(8,128)(2,1)S(1)} %get-tuple-element.19), channel_id=1, source_target_pairs={{0,1},{2,3},{4,5},{6,7},{1,0},{3,2},{5,4},{7,6},{8,9},{10,11},{12,... | collective-permute-start | bytes 589832 | tf_op jit(solution)/shard_map/ppermute | solution.py:21
  9.3 0.7 collective-permute-start.3
  10.0 0.9 %collective-permute-start.1 = (bf16[4,4,64,128]{3,2,1,0:T(8,128)(2,1)S(1)}, bf16[4,4,64,128]{3,2,1,0:T(8,128)(2,1)S(1)}, u32[]{:S(2)}, u32[]{:S(2)}) collective-permute-start(bf16[4,4,64,128]{3,2,1,0:T(8,128)(2,1)S(1)} %get-tuple-element.18), channel_id=1, source_target_pairs={{0,8},{8,0},{1,9},{9,1},{2,10},{10,2},{3,11},{11,3},{4,12},{12,4},... | collective-permute-start | bytes 786440 | tf_op jit(solution)/shard_map/ppermute | solution.py:21
  10.9 0.0 collective-permute-start
  11.0 0.0 copy-done.3
  11.0 0.0 copy-done.2
  11.0 0.0 slice-done
  11.0 0.0 slice-done.1
  11.0 0.0 copy-done
  11.0 0.0 copy-start.1
  11.1 15.1 %interior.1.start_ref = f32[168,32,128]{2,1,0:T(8,128)S(1)} custom-call(s32[7,4,6,8]{3,2,1,0:T(8,128)S(1)} %copy_add_fusion.keys, bf16[24,8,4096]{2,1,0:T(8,128)(2,1)S(1)} %bitcast.19, bf16[3,24,8,4096]{3,2,1,0:T(8,128)(2,1)S(1)} %bitcast.16, bf16[24,4,64,128]{3,2,1,0:T(8,128)(2,1)S(1)} %get-tuple-element.25.natural_ref.natural_x, ...), custom_call_target="tpu_custom_call" | custom-call | flops 704643072 | bytes 9437184 | tf_op jit(solution)/shard_map/interior/pallas_call | solution.py:308
  26.2 0.0 collective-permute-done.2.near_z
  26.2 0.0 collective-permute-done.3.far_z
  26.2 0.0 collective-permute-done.1.got_y
  26.2 0.0 collective-permute-done.got_x
  26.2 0.0 copy-done.1
  26.3 8.2 %border.1 = (bf16[24,224,128]{2,1,0:T(8,128)(2,1)S(1)}, f32[168,32,128]{2,1,0:T(8,128)S(1)}) custom-call(s32[24]{0:T(128)S(1)} %copy-done.1, s32[3]{0:T(128)S(1)} %pad_add_fusion.place_ref, s32[7,4,6,8]{3,2,1,0:T(8,128)S(1)} %copy_add_fusion.keys, bf16[6,4,64,128]{3,2,1,0:T(8,128)(2,1)S(1)} %collective-permute-done.got_x, ...), custom_call_target="tpu_custom_call", output_to_operand_aliasing={{1}: (16, {})} | custom-call | tf_op jit(solution)/shard_map/border/pallas_call | solution.py:410
  34.4 39.6 %all_to_all.5.refs_0_ = bf16[24,224,128]{2,1,0:T(8,128)(2,1)S(1)} all-to-all(bf16[24,224,128]{2,1,0:T(8,128)(2,1)S(1)} %get-tuple-element.28), channel_id=1, replica_groups=mesh['gx'=2,'gy'=2,'gz'=8] {'gz'}, dimensions={0} | all-to-all | bytes 2752512 | tf_op jit(solution)/shard_map/all_to_all | solution.py:485
  74.1 1.9 %layout.1 = bf16[7,24,4096]{2,1,0:T(8,128)(2,1)} custom-call(bf16[24,224,128]{2,1,0:T(8,128)(2,1)S(1)} %all_to_all.5.refs_0_), custom_call_target="tpu_custom_call" | custom-call | tf_op jit(solution)/shard_map/layout/pallas_call | solution.py:450
  (4 shorter events, 0.0 us)
Async XLA Ops:
  0.1 10.9 %slice-start = ((s8[4718592]{0:T(1024)(128)(4,1)}), s8[4194304]{0:T(1024)(128)(4,1)S(1)}, s32[]{:S(2)}) async-start(s8[4718592]{0:T(1024)(128)(4,1)} %bitcast.14), calls=%async_computation.1 | async-start | bytes 8388608
  0.1 10.9 %copy-start.3 = (s32[4,6,8]{2,0,1:T(4,128)S(1)}, s32[4,6,8]{2,0,1:T(4,128)}, u32[]{:S(2)}) copy-start(s32[4,6,8]{2,0,1:T(4,128)} %param.9) | copy-start | bytes 2308
  0.1 10.9 %copy-start.2 = (s32[7,4,6,8]{3,1,2,0:T(4,128)S(1)}, s32[7,4,6,8]{3,1,2,0:T(4,128)}, u32[]{:S(2)}) copy-start(s32[7,4,6,8]{3,1,2,0:T(4,128)} %param.10) | copy-start | bytes 16132
  0.1 10.9 %slice-start.1 = ((s8[4718592]{0:T(1024)(128)(4,1)}), s8[524288]{0:T(1024)(128)(4,1)S(1)}, s32[]{:S(2)}) async-start(s8[4718592]{0:T(1024)(128)(4,1)} %bitcast.14), calls=%async_computation.2 | async-start | bytes 1048576
  0.1 10.9 %copy-start = (bf16[4,6,8,4096]{3,2,1,0:T(8,128)(2,1)S(1)}, bf16[4,6,8,4096]{3,2,1,0:T(8,128)(2,1)}, u32[]{:S(2)}) copy-start(bf16[4,6,8,4096]{3,2,1,0:T(8,128)(2,1)} %param.6) | copy-start | bytes 4718596
  6.3 19.9 %collective-permute-start.2 = (bf16[12,64,128]{2,1,0:T(8,128)(2,1)S(1)}, bf16[12,64,128]{2,1,0:T(8,128)(2,1)S(1)}, u32[]{:S(2)}, u32[]{:S(2)}) collective-permute-start(bf16[12,64,128]{2,1,0:T(8,128)(2,1)S(1)} %get-tuple-element.19), channel_id=1, source_target_pairs={{0,1},{2,3},{4,5},{6,7},{1,0},{3,2},{5,4},{7,6},{8,9},{10,11},{12,... | collective-permute-start | bytes 589832 | tf_op jit(solution)/shard_map/ppermute | solution.py:21
  9.3 16.9 %collective-permute-start.3 = (bf16[12,64,128]{2,1,0:T(8,128)(2,1)S(1)}, bf16[12,64,128]{2,1,0:T(8,128)(2,1)S(1)}, u32[]{:S(2)}, u32[]{:S(2)}) collective-permute-start(bf16[12,64,128]{2,1,0:T(8,128)(2,1)S(1)} %get-tuple-element.20), channel_id=1, source_target_pairs={{1,2},{3,4},{5,6},{2,1},{4,3},{6,5},{9,10},{11,12},{13,14},{10,9},... | collective-permute-start | bytes 589832 | tf_op jit(solution)/shard_map/ppermute | solution.py:21
  10.0 16.2 %collective-permute-start.1 = (bf16[4,4,64,128]{3,2,1,0:T(8,128)(2,1)S(1)}, bf16[4,4,64,128]{3,2,1,0:T(8,128)(2,1)S(1)}, u32[]{:S(2)}, u32[]{:S(2)}) collective-permute-start(bf16[4,4,64,128]{3,2,1,0:T(8,128)(2,1)S(1)} %get-tuple-element.18), channel_id=1, source_target_pairs={{0,8},{8,0},{1,9},{9,1},{2,10},{10,2},{3,11},{11,3},{4,12},{12,4},... | collective-permute-start | bytes 786440 | tf_op jit(solution)/shard_map/ppermute | solution.py:21
  10.9 15.3 %collective-permute-start = (bf16[6,4,64,128]{3,2,1,0:T(8,128)(2,1)S(1)}, bf16[6,4,64,128]{3,2,1,0:T(8,128)(2,1)S(1)}, u32[]{:S(2)}, u32[]{:S(2)}) collective-permute-start(bf16[6,4,64,128]{3,2,1,0:T(8,128)(2,1)S(1)} %get-tuple-element.17), channel_id=1, source_target_pairs={{0,16},{16,0},{1,17},{17,1},{2,18},{18,2},{3,19},{19,3},{4,20},{20... | collective-permute-start | bytes 1179656 | tf_op jit(solution)/shard_map/ppermute | solution.py:21
  11.0 15.2 %copy-start.1 = (s32[24]{0:T(128)S(1)}, s32[24]{0:T(128)}, u32[]{:S(2)}) copy-start(s32[24]{0:T(128)} %owners.1) | copy-start | bytes 292

commit v10 on v9

--- a/solution.py
+++ b/solution.py
@@ -138,8 +138,8 @@
         first_z_ref[t] = head
         last_z_ref[t] = last
         tail_z_ref[t] = face
-        near_z_ref[t] = jnp.where(place_ref[2] == 0, rim, head)
-        far_z_ref[t] = jnp.where(place_ref[2] == 0, head, rim)
+        near_z_ref[t] = jnp.where(place_ref[2] % 2 == 0, rim, head)
+        far_z_ref[t] = jnp.where(place_ref[2] % 2 == 0, head, rim)
 
     def faces(source, stage, j, tails, rims):
         spread(source, stage)
@@ -321,12 +321,12 @@
     )(keys, diag, faces, natural, turned)
 
 
-def border_kernel(capacity, owners, place_ref, keys, got_x, got_y, near_z, far_z, tail_x, tail_y, tail_z, turned_x, turned_y,
-                  natural_x, natural_y, first_z, last_z, start_ref, out_ref, total, filled):
+def border_kernel(capacity, paired, owners, place_ref, keys, got_x, got_y, near_z, far_z, tail_x, tail_y, tail_z, turned_x, turned_y,
+                  natural_x, natural_y, first_z, last_z, start_ref, *refs):
+    out_refs, (total, filled, listed) = refs[:-3], refs[-3:]
     size_y, pairs = tail_x.shape[0], tail_x.shape[1]
     size_x, depth = tail_y.shape[0], 2 * pairs
     rows = start_ref.shape[0]
-    places = out_ref.shape[0]
 
     def key_at(number, i, j, z):
         return keys[number, i, j, z]
@@ -347,60 +347,62 @@
             four = [term for p in (2 * h, 2 * h + 1) for term in folded(across(natural[p], rim[p]))]
             yield [(total, key(4 * h + number), term) for number, term in enumerate(four)]
 
-    def add_batches(batches):
-        for updates in list(batches):
-            add_all(updates)
-
-    @pl.when(place_ref[0] == 0)
-    def _():
-        add_batches(
-            batch for j in range(size_y)
-            for batch in ahead(tail_x.at[j], got_x.at[j], turned_x.at[j], functools.partial(key_at, 2, size_x - 1, j)))
-
-    @pl.when(place_ref[0] != 0)
-    def _():
-        add_batches(
-            batch for j in range(size_y) for batch in back(natural_x.at[j], got_x.at[j], functools.partial(key_at, 1, 0, j)))
-
-    @pl.when(place_ref[1] == 0)
-    def _():
-        add_batches(
-            batch for i in range(size_x)
-            for batch in ahead(tail_y.at[i], got_y.at[i], turned_y.at[i, 0], functools.partial(key_at, 4, i, size_y - 1)))
-
-    @pl.when(place_ref[1] != 0)
-    def _():
-        add_batches(
-            batch for i in range(size_x) for batch in back(natural_y.at[i, 0], got_y.at[i], functools.partial(key_at, 3, i, 0)))
-
-    batches = []
-    even = place_ref[2] == 0
-    for t in range(0, near_z.shape[0], 2):
-        heads = [jnp.where(even, near_z[u], far_z[u]) for u in (t, t + 1)]
-        couples = couplings([tail_z[t], tail_z[t + 1]], heads)
-        for u in (t, t + 1):
-            i, j = 2 * u // size_y, 2 * u % size_y
-            front = folded(across(last_z[u], couples[u - t]))
-            past = folded(across(first_z[u], jnp.where(even, far_z[u], near_z[u])))
-            batches.append([(total, keys[6, i, j + side, depth - 1], front[side]) for side in (0, 1)]
-                           + [(total, keys[5, i, j + side, 0], past[side]) for side in (0, 1)])
-    add_batches(batches)
-
-    for owner in range(places // capacity):
+    def batches_x(first):
+        for j in range(size_y):
+            if first:
+                yield from ahead(tail_x.at[j], got_x.at[j], turned_x.at[j], functools.partial(key_at, 2, size_x - 1, j))
+            else:
+                yield from back(natural_x.at[j], got_x.at[j], functools.partial(key_at, 1, 0, j))
+
+    def batches_y(first):
+        for i in range(size_x):
+            if first:
+                yield from ahead(tail_y.at[i], got_y.at[i], turned_y.at[i, 0], functools.partial(key_at, 4, i, size_y - 1))
+            else:
+                yield from back(natural_y.at[i, 0], got_y.at[i], functools.partial(key_at, 3, i, 0))
+
+    def batches_z():
+        even = place_ref[2] % 2 == 0
+        for t in range(0, near_z.shape[0], 2):
+            heads = [jnp.where(even, near_z[u], far_z[u]) for u in (t, t + 1)]
+            couples = couplings([tail_z[t], tail_z[t + 1]], heads)
+            for u in (t, t + 1):
+                i, j = 2 * u // size_y, 2 * u % size_y
+                front = folded(across(last_z[u], couples[u - t]))
+                past = folded(across(first_z[u], jnp.where(even, far_z[u], near_z[u])))
+                yield ([(total, keys[6, i, j + side, depth - 1], front[side]) for side in (0, 1)]
+                       + [(total, keys[5, i, j + side, 0], past[side]) for side in (0, 1)])
+
+    for first_x in (True, False):
+        for first_y in (True, False):
+            @pl.when(((place_ref[0] == 0) == first_x) & ((place_ref[1] == 0) == first_y))
+            def _():
+                batches = list(batches_x(first_x)) + list(batches_y(first_y)) + list(batches_z())
+                for updates in batches:
+                    add_all(updates)
+
+    places = capacity * len(out_refs)
+    full = places * SLOTS == rows
+    for spot in range(places):
+        listed[spot] = -1
+    for owner in range(len(out_refs)):
         filled[owner] = 0
-    if places * SLOTS != rows:
-        out_ref[...] = jnp.zeros_like(out_ref)
     for r in range(rows // SLOTS):
         owner = owners[r]
-        spot = owner * capacity + filled[owner]
+        listed[jnp.bitwise_xor(owner, place_ref[2] if paired else 0) * capacity + filled[owner]] = r
         filled[owner] = filled[owner] + 1
+    for spot in range(places):
+        row = listed[spot]
         for s in range(SLOTS):
-            key = r * SLOTS + s
+            key = jnp.maximum(row, 0) * SLOTS + s
             even, odd = [total[key, pl.ds(first, HALF // 2, stride=2), :] for first in (0, 1)]
-            out_ref[spot, HALF * s : HALF * (s + 1), :] = straightened(even, odd).astype(jnp.bfloat16)
-
-
-def border(owners, place, keys, operands, turned, natural, ends, total, capacity, places, sizes):
+            block = straightened(even, odd)
+            if not full:
+                block = jnp.where(row >= 0, block, jnp.zeros_like(block))
+            out_refs[spot // capacity][spot % capacity, HALF * s : HALF * (s + 1), :] = block.astype(jnp.bfloat16)
+
+
+def border(owners, place, keys, operands, turned, natural, ends, total, capacity, devices, paired, sizes):
     size_x, size_y, depth = sizes
     pairs = depth // 2
     smem = pl.BlockSpec(memory_space=pltpu.SMEM)
@@ -408,7 +410,7 @@
     planes = lambda array: array.reshape((size_x, size_y) + array.shape[1:])
     before = 3 + len(operands) + 4 + len(ends)
     return pl.pallas_call(
-        functools.partial(border_kernel, capacity),
+        functools.partial(border_kernel, capacity, paired),
         grid=(1,),
         in_specs=[smem, smem, smem] + [whole] * len(operands) + [
             pl.BlockSpec((size_y, pairs // 2, LANES, LANES), lambda i: (size_x - 1, 0, 0, 0)),
@@ -416,31 +418,24 @@
             pl.BlockSpec((size_y, pairs, NODES, LANES), lambda i: (0, 0, 0, 0)),
             pl.BlockSpec((size_x, 1, pairs, NODES, LANES), lambda i: (0, 0, 0, 0, 0)),
         ] + [whole] * (len(ends) + 1),
-        out_specs=[whole, whole],
-        out_shape=[
-            jax.ShapeDtypeStruct((places, SLOTS * HALF, LANES), jnp.bfloat16),
-            jax.ShapeDtypeStruct(total.shape, total.dtype),
-        ],
-        input_output_aliases={before: 1},
-        scratch_shapes=[pltpu.SMEM((places // capacity,), jnp.int32)],
+        out_specs=[whole] * (devices + 1),
+        out_shape=[jax.ShapeDtypeStruct((capacity, SLOTS * HALF, LANES), jnp.bfloat16)] * devices
+        + [jax.ShapeDtypeStruct(total.shape, total.dtype)],
+        input_output_aliases={before: devices},
+        scratch_shapes=[pltpu.SMEM((devices,), jnp.int32), pltpu.SMEM((capacity * devices,), jnp.int32)],
         compiler_params=pltpu.CompilerParams(vmem_limit_bytes=18 * MIB),
         name="border",
-    )(owners, place, keys, *operands, turned, planes(turned), natural, planes(natural), *ends, total)[0]
-
-
-def layout_kernel(*refs):
-    source, (rows_ref, out_ref, stage) = refs[:-3], refs[-3:]
+    )(owners, place, keys, *operands, turned, planes(turned), natural, planes(natural), *ends, total)[:devices]
+
+
+def layout_kernel(source, rows_ref, out_ref, stage):
     group = pl.program_id(0)
     height = out_ref.shape[1]
     for s in range(SLOTS):
         for r in range(height):
-            row = group * height + r
-            if source:
-                row = source[0][row]
+            row = source[group * height + r]
             block = rows_ref[jnp.maximum(row, 0), HALF * s : HALF * (s + 1), :].astype(jnp.float32)
-            if source:
-                block = jnp.where(row >= 0, block, jnp.zeros_like(block))
-            stage[s, pl.ds(r, HALF, stride=height), :] = block
+            stage[s, pl.ds(r, HALF, stride=height), :] = jnp.where(row >= 0, block, jnp.zeros_like(block))
         for k in range(HALF):
             out_ref[s, :, LANES * k : LANES * (k + 1)] = stage[s, height * k : height * (k + 1), :].astype(jnp.bfloat16)
 
@@ -450,13 +445,41 @@
     return pl.pallas_call(
         layout_kernel,
         grid=(places // height,),
-        in_specs=[pl.BlockSpec(memory_space=pltpu.SMEM)] * len(source) + [pl.BlockSpec(memory_space=pltpu.VMEM)],
+        in_specs=[pl.BlockSpec(memory_space=pltpu.SMEM), pl.BlockSpec(memory_space=pltpu.VMEM)],
         out_specs=pl.BlockSpec((SLOTS, height, block), lambda g: (0, g, 0)),
         out_shape=jax.ShapeDtypeStruct((SLOTS, places, block), jnp.bfloat16),
         scratch_shapes=[pltpu.VMEM((SLOTS, height * HALF, LANES), jnp.float32)],
         compiler_params=pltpu.CompilerParams(vmem_limit_bytes=10 * MIB),
         name="layout",
-    )(*source, rows)
+    )(source, rows)
+
+
+def placed_kernel(place_ref, *refs):
+    parts, (out_ref, stage) = refs[:-2], refs[-2:]
+    capacity, height = parts[0].shape[0], out_ref.shape[1]
+    for number, rows_ref in enumerate(parts):
+        first = jnp.bitwise_xor(place_ref[2], number) * capacity
+        for q in range(capacity):
+            for s in range(SLOTS):
+                block = rows_ref[q, HALF * s : HALF * (s + 1), :].astype(jnp.float32)
+                stage[s, pl.ds(first + q, HALF, stride=height), :] = block
+    for s in range(SLOTS):
+        for k in range(HALF):
+            out_ref[s, :, LANES * k : LANES * (k + 1)] = stage[s, height * k : height * (k + 1), :].astype(jnp.bfloat16)
+
+
+def placed(place, parts, block):
+    places = parts[0].shape[0] * len(parts)
+    whole = pl.BlockSpec(memory_space=pltpu.VMEM)
+    return pl.pallas_call(
+        placed_kernel,
+        in_specs=[pl.BlockSpec(memory_space=pltpu.SMEM)] + [whole] * len(parts),
+        out_specs=whole,
+        out_shape=jax.ShapeDtypeStruct((SLOTS, places, block), jnp.bfloat16),
+        scratch_shapes=[pltpu.VMEM((SLOTS, places * HALF, LANES), jnp.float32)],
+        compiler_params=pltpu.CompilerParams(vmem_limit_bytes=16 * MIB),
+        name="placed",
+    )(place, *parts)
 
 
 def shards(a_diag, a_face, prolong, aggregate, pair_slot, row_owner):
@@ -469,7 +492,7 @@
     diag = a_diag.reshape(columns, size_z, block)
     faces = a_face.reshape(3, columns, size_z, block)
     assert lax.axis_size("gx") == 2 and lax.axis_size("gy") == 2
-    place = jnp.stack([lax.axis_index("gx"), lax.axis_index("gy"), lax.axis_index("gz") % 2]).astype(jnp.int32)
+    place = jnp.stack([lax.axis_index("gx"), lax.axis_index("gy"), lax.axis_index("gz")]).astype(jnp.int32)
     keys = aggregate[None] * SLOTS + pair_slot
 
     natural, turned, swap_x, swap_y, near_z, far_z, first_z, last_z, tail_x, tail_y, tail_z = prepare(
@@ -479,21 +502,26 @@
     got_y = swapped_along(swap_y, "gy", 0)
     got_x = swapped_along(swap_x, "gx", 0)
     total = interior(keys, diag, faces, natural, turned, sizes)
+    paired = holding == AGG_DEV and depth & (depth - 1) == 0
     outgoing = border(
         row_owner, place, keys, (got_x, got_y, near_z, far_z, tail_x, tail_y, tail_z), turned, natural,
-        (first_z, last_z), total, capacity, holding, sizes)
-    arrived = lax.all_to_all(outgoing, "gz", 0, 0, tiled=True)
-    sources = []
-    if holding != AGG_DEV:
-        source = jnp.arange(holding, dtype=jnp.int32)
+        (first_z, last_z), total, capacity, depth, paired, sizes)
+    if paired:
+        parts = list(outgoing)
+        far_first = sorted(range(1, depth), key=lambda k: (k < depth // 2, k))
+        for k in far_first:
+            parts[k] = lax.ppermute(outgoing[k], "gz", [(i, i ^ k) for i in range(depth)])
+        result = placed(place, parts, block)
+    else:
+        arrived = lax.all_to_all(jnp.concatenate(outgoing, axis=0), "gz", 0, 0, tiled=True)
+        slots = jnp.arange(holding, dtype=jnp.int32)
         owner_ids = jnp.arange(depth, dtype=jnp.int32)
         counts = jnp.sum((row_owner[:, None] == owner_ids[None, :]).astype(jnp.int32), axis=0)
         arrived_counts = lax.all_to_all(counts, "gz", 0, 0, tiled=True)
-        present = source % capacity < jnp.repeat(arrived_counts, capacity)
+        present = slots % capacity < jnp.repeat(arrived_counts, capacity)
         target = jnp.cumsum(present.astype(jnp.int32)) - 1
-        match = (present[None, :] & (target[None, :] == source[:, None])).astype(jnp.int32)
-        sources = [jnp.sum(match * (source[None, :] + 1), axis=1) - 1]
-    result = laid_out(sources, arrived, block)
+        match = (present[None, :] & (target[None, :] == slots[:, None])).astype(jnp.int32)
+        result = laid_out(jnp.sum(match * (slots[None, :] + 1), axis=1) - 1, arrived, block)
     return jnp.transpose(result, (1, 0, 2)).reshape(1, 1, 1, holding, SLOTS, block)
 
 

time: 76.2 us -> 73.1 us (0.959)
  the two profiles are of different devices: /device:TPU:0 before, /device:TPU:8 now
where the time goes in v10:
time: 73.1 us; the launch traced here: 72.9 us
  Pallas kernels  31.9 us (44%)
  waiting for transfers between devices  25.2 us (34%)
  starting transfers between devices  15.6 us (21%)
    ppermute x7, waiting for transfers between devices, shards(): lax.ppermute(outgoing[k], 'gz', [(i, i ^ k) for i in range(depth)])  25.2 us
    pallas_call x1, Pallas kernels, interior(): pl.pallas_call(interior_kernel, in_specs=[pl.BlockSpec(memory_space=pltpu...  15.1 us
    ppermute x7, starting transfers between devices, shards(): lax.ppermute(outgoing[k], 'gz', [(i, i ^ k) for i in range(depth)])  10.8 us
    pallas_call x1, Pallas kernels, border(): pl.pallas_call(functools.partial(border_kernel, capacity, paired), grid=(...  8.05 us
    pallas_call x1, Pallas kernels, prepare(): pl.pallas_call(prepare_kernel, grid=(size_x,), in_specs=[pl.BlockSpec(mem...  6.2 us
    ppermute x4, starting transfers between devices, swapped_along(): return lax.ppermute(block, axis, pairs + [(i + 1, i) for i, _ in pairs])  4.82 us
    pallas_call x1, Pallas kernels, placed(): pl.pallas_call(placed_kernel, in_specs=[pl.BlockSpec(memory_space=pltpu.S...  2.51 us
  transfers between devices with their start and end apart: 11, of which 6 were waited for; matrix products, arithmetic and copies ran while one was open for 0% of the time, Pallas kernels for 21%

profile of v10, /device:TPU:8, one launch (start us, length us, event | category | flops | bytes accessed | tf_op | source)
XLA Modules:
  0.0 72.9 jit_solution(5121850402428620973)
XLA Ops:
  0.0 0.1 pad_add_fusion.place_ref
  0.1 0.0 slice-start
  0.1 0.0 copy-start.3
  0.1 0.0 copy-start.2
  0.1 0.0 slice-start.1
  0.1 0.0 copy-start
  0.1 6.2 %prepare.1 = (bf16[24,4,64,128]{3,2,1,0:T(8,128)(2,1)S(1)}, bf16[24,2,128,128]{3,2,1,0:T(8,128)(2,1)S(1)}, bf16[6,4,64,128]{3,2,1,0:T(8,128)(2,1)S(1)}, bf16[4,4...) custom-call(s32[3]{0:T(128)S(1)} %pad_add_fusion.place_ref, ...), custom_call_target="tpu_custom_call" | custom-call | tf_op jit(solution)/shard_map/prepare/pallas_call | solution.py:177
  6.3 1.6 %collective-permute-start.2 = (bf16[12,64,128]{2,1,0:T(8,128)(2,1)S(1)}, bf16[12,64,128]{2,1,0:T(8,128)(2,1)S(1)}, u32[]{:S(2)}, u32[]{:S(2)}) collective-permute-start(bf16[12,64,128]{2,1,0:T(8,128)(2,1)S(1)} %get-tuple-element.26), channel_id=1, source_target_pairs={{0,1},{2,3},{4,5},{6,7},{1,0},{3,2},{5,4},{7,6},{8,9},{10,11},{12,... | collective-permute-start | bytes 589832 | tf_op jit(solution)/shard_map/ppermute | solution.py:21
  7.9 1.9 %collective-permute-start.3 = (bf16[12,64,128]{2,1,0:T(8,128)(2,1)S(1)}, bf16[12,64,128]{2,1,0:T(8,128)(2,1)S(1)}, u32[]{:S(2)}, u32[]{:S(2)}) collective-permute-start(bf16[12,64,128]{2,1,0:T(8,128)(2,1)S(1)} %get-tuple-element.27), channel_id=1, source_target_pairs={{1,2},{3,4},{5,6},{2,1},{4,3},{6,5},{9,10},{11,12},{13,14},{10,9},... | collective-permute-start | bytes 589832 | tf_op jit(solution)/shard_map/ppermute | solution.py:21
  9.8 1.3 %collective-permute-start.1 = (bf16[4,4,64,128]{3,2,1,0:T(8,128)(2,1)S(1)}, bf16[4,4,64,128]{3,2,1,0:T(8,128)(2,1)S(1)}, u32[]{:S(2)}, u32[]{:S(2)}) collective-permute-start(bf16[4,4,64,128]{3,2,1,0:T(8,128)(2,1)S(1)} %get-tuple-element.25), channel_id=1, source_target_pairs={{0,8},{8,0},{1,9},{9,1},{2,10},{10,2},{3,11},{11,3},{4,12},{12,4},... | collective-permute-start | bytes 786440 | tf_op jit(solution)/shard_map/ppermute | solution.py:21
  11.1 0.0 collective-permute-start
  11.1 0.0 copy-done.3
  11.2 0.0 copy-done.2
  11.2 0.0 slice-done
  11.2 0.0 slice-done.1
  11.2 0.0 copy-done
  11.2 0.0 copy-start.1
  11.2 15.1 %interior.1.start_ref = f32[168,32,128]{2,1,0:T(8,128)S(1)} custom-call(s32[7,4,6,8]{3,2,1,0:T(8,128)S(1)} %copy_add_fusion.keys, bf16[24,8,4096]{2,1,0:T(8,128)(2,1)S(1)} %bitcast.19, bf16[3,24,8,4096]{3,2,1,0:T(8,128)(2,1)S(1)} %bitcast.16, bf16[24,4,64,128]{3,2,1,0:T(8,128)(2,1)S(1)} %get-tuple-element.32.natural_ref.natural_x, ...), custom_call_target="tpu_custom_call" | custom-call | flops 704643072 | bytes 9437184 | tf_op jit(solution)/shard_map/interior/pallas_call | solution.py:308
  26.4 0.0 collective-permute-done.2.near_z
  26.4 0.0 collective-permute-done.3.far_z
  26.4 0.0 collective-permute-done.1.got_y
  26.4 0.0 collective-permute-done.got_x
  26.4 0.0 copy-done.1
  26.4 8.0 %border.1 = (bf16[3,224,128]{2,1,0:T(8,128)(2,1)S(1)}, bf16[3,224,128]{2,1,0:T(8,128)(2,1)S(1)}, bf16[3,224,128]{2,1,0:T(8,128)(2,1)S(1)}, bf16[3,224,128]{2,1,0...) custom-call(s32[24]{0:T(128)S(1)} %copy-done.1, ...), custom_call_target="tpu_custom_call", output_to_operand_aliasing={{8}: (16, {})} | custom-call | tf_op jit(solution)/shard_map/border/pallas_call | solution.py:412
  34.5 2.7 %collective-permute-start.4 = (bf16[3,224,128]{2,1,0:T(8,128)(2,1)S(1)}, bf16[3,224,128]{2,1,0:T(8,128)(2,1)S(1)}, u32[]{:S(2)}, u32[]{:S(2)}) collective-permute-start(bf16[3,224,128]{2,1,0:T(8,128)(2,1)S(1)} %get-tuple-element.36), channel_id=1, source_target_pairs={{0,1},{1,0},{2,3},{3,2},{4,5},{5,4},{6,7},{7,6},{8,9},{9,8},{10,11... | collective-permute-start | bytes 516104 | tf_op jit(solution)/shard_map/ppermute | solution.py:513
  37.2 0.5 collective-permute-start.5
  37.6 1.1 %collective-permute-start.6 = (bf16[3,224,128]{2,1,0:T(8,128)(2,1)S(1)}, bf16[3,224,128]{2,1,0:T(8,128)(2,1)S(1)}, u32[]{:S(2)}, u32[]{:S(2)}) collective-permute-start(bf16[3,224,128]{2,1,0:T(8,128)(2,1)S(1)} %get-tuple-element.38), channel_id=1, source_target_pairs={{0,3},{1,2},{2,1},{3,0},{4,7},{5,6},{6,5},{7,4},{8,11},{9,10},{10,... | collective-permute-start | bytes 516104 | tf_op jit(solution)/shard_map/ppermute | solution.py:513
  38.7 1.9 %collective-permute-start.7 = (bf16[3,224,128]{2,1,0:T(8,128)(2,1)S(1)}, bf16[3,224,128]{2,1,0:T(8,128)(2,1)S(1)}, u32[]{:S(2)}, u32[]{:S(2)}) collective-permute-start(bf16[3,224,128]{2,1,0:T(8,128)(2,1)S(1)} %get-tuple-element.39), channel_id=1, source_target_pairs={{0,4},{1,5},{2,6},{3,7},{4,0},{5,1},{6,2},{7,3},{8,12},{9,13},{10,... | collective-permute-start | bytes 516104 | tf_op jit(solution)/shard_map/ppermute | solution.py:513
  40.6 2.4 %collective-permute-start.8 = (bf16[3,224,128]{2,1,0:T(8,128)(2,1)S(1)}, bf16[3,224,128]{2,1,0:T(8,128)(2,1)S(1)}, u32[]{:S(2)}, u32[]{:S(2)}) collective-permute-start(bf16[3,224,128]{2,1,0:T(8,128)(2,1)S(1)} %get-tuple-element.40), channel_id=1, source_target_pairs={{0,5},{1,4},{2,7},{3,6},{4,1},{5,0},{6,3},{7,2},{8,13},{9,12},{10,... | collective-permute-start | bytes 516104 | tf_op jit(solution)/shard_map/ppermute | solution.py:513
  43.0 0.0 collective-permute-done.4.refs_1_
  43.0 1.6 %collective-permute-start.9 = (bf16[3,224,128]{2,1,0:T(8,128)(2,1)S(1)}, bf16[3,224,128]{2,1,0:T(8,128)(2,1)S(1)}, u32[]{:S(2)}, u32[]{:S(2)}) collective-permute-start(bf16[3,224,128]{2,1,0:T(8,128)(2,1)S(1)} %get-tuple-element.41), channel_id=1, source_target_pairs={{0,6},{1,7},{2,4},{3,5},{4,2},{5,3},{6,0},{7,1},{8,14},{9,15},{10,... | collective-permute-start | bytes 516104 | tf_op jit(solution)/shard_map/ppermute | solution.py:513
  44.6 3.5 %collective-permute-done.5.refs_2_ = bf16[3,224,128]{2,1,0:T(8,128)(2,1)S(1)} collective-permute-done((bf16[3,224,128]{2,1,0:T(8,128)(2,1)S(1)}, bf16[3,224,128]{2,1,0:T(8,128)(2,1)S(1)}, u32[]{:S(2)}, u32[]{:S(2)}) %collective-permute-start.5) | collective-permute-done | bytes 172064 | tf_op jit(solution)/shard_map/ppermute | solution.py:513
  48.1 0.6 collective-permute-start.10
  48.7 1.3 %collective-permute-done.6.refs_3_ = bf16[3,224,128]{2,1,0:T(8,128)(2,1)S(1)} collective-permute-done((bf16[3,224,128]{2,1,0:T(8,128)(2,1)S(1)}, bf16[3,224,128]{2,1,0:T(8,128)(2,1)S(1)}, u32[]{:S(2)}, u32[]{:S(2)}) %collective-permute-start.6) | collective-permute-done | bytes 172064 | tf_op jit(solution)/shard_map/ppermute | solution.py:513
  50.0 9.9 %collective-permute-done.7.refs_4_ = bf16[3,224,128]{2,1,0:T(8,128)(2,1)S(1)} collective-permute-done((bf16[3,224,128]{2,1,0:T(8,128)(2,1)S(1)}, bf16[3,224,128]{2,1,0:T(8,128)(2,1)S(1)}, u32[]{:S(2)}, u32[]{:S(2)}) %collective-permute-start.7) | collective-permute-done | bytes 172064 | tf_op jit(solution)/shard_map/ppermute | solution.py:513
  60.0 3.8 %collective-permute-done.8.refs_5_ = bf16[3,224,128]{2,1,0:T(8,128)(2,1)S(1)} collective-permute-done((bf16[3,224,128]{2,1,0:T(8,128)(2,1)S(1)}, bf16[3,224,128]{2,1,0:T(8,128)(2,1)S(1)}, u32[]{:S(2)}, u32[]{:S(2)}) %collective-permute-start.8) | collective-permute-done | bytes 172064 | tf_op jit(solution)/shard_map/ppermute | solution.py:513
  63.8 3.6 %collective-permute-done.9.refs_6_ = bf16[3,224,128]{2,1,0:T(8,128)(2,1)S(1)} collective-permute-done((bf16[3,224,128]{2,1,0:T(8,128)(2,1)S(1)}, bf16[3,224,128]{2,1,0:T(8,128)(2,1)S(1)}, u32[]{:S(2)}, u32[]{:S(2)}) %collective-permute-start.9) | collective-permute-done | bytes 172064 | tf_op jit(solution)/shard_map/ppermute | solution.py:513
  67.4 3.0 %collective-permute-done.10.refs_7_ = bf16[3,224,128]{2,1,0:T(8,128)(2,1)S(1)} collective-permute-done((bf16[3,224,128]{2,1,0:T(8,128)(2,1)S(1)}, bf16[3,224,128]{2,1,0:T(8,128)(2,1)S(1)}, u32[]{:S(2)}, u32[]{:S(2)}) %collective-permute-start.10) | collective-permute-done | bytes 172064 | tf_op jit(solution)/shard_map/ppermute | solution.py:513
  70.4 2.5 %placed.1 = bf16[7,24,4096]{2,1,0:T(8,128)(2,1)} custom-call(s32[3]{0:T(128)S(1)} %pad_add_fusion.place_ref, bf16[3,224,128]{2,1,0:T(8,128)(2,1)S(1)} %get-tuple-element.35.refs_0_, bf16[3,224,128]{2,1,0:T(8,128)(2,1)S(1)} %collective-permute-done.4.refs_1_, bf16[3,224,128]{2,1,0:T(8,128)(2,1)S(1)} %collective-permute-done.5.refs_2_, ...), custom_call_target="tpu_custom_call" | custom-call | tf_op jit(solution)/shard_map/placed/pallas_call | solution.py:474
  (4 shorter events, 0.0 us)
Async XLA Ops:
  0.1 11.1 %slice-start = ((s8[4718592]{0:T(1024)(128)(4,1)}), s8[4194304]{0:T(1024)(128)(4,1)S(1)}, s32[]{:S(2)}) async-start(s8[4718592]{0:T(1024)(128)(4,1)} %bitcast.14), calls=%async_computation | async-start | bytes 8388608
  0.1 11.1 %copy-start.3 = (s32[4,6,8]{2,0,1:T(4,128)S(1)}, s32[4,6,8]{2,0,1:T(4,128)}, u32[]{:S(2)}) copy-start(s32[4,6,8]{2,0,1:T(4,128)} %param.9) | copy-start | bytes 2308
  0.1 11.1 %copy-start.2 = (s32[7,4,6,8]{3,1,2,0:T(4,128)S(1)}, s32[7,4,6,8]{3,1,2,0:T(4,128)}, u32[]{:S(2)}) copy-start(s32[7,4,6,8]{3,1,2,0:T(4,128)} %param.10) | copy-start | bytes 16132
  0.1 11.1 %slice-start.1 = ((s8[4718592]{0:T(1024)(128)(4,1)}), s8[524288]{0:T(1024)(128)(4,1)S(1)}, s32[]{:S(2)}) async-start(s8[4718592]{0:T(1024)(128)(4,1)} %bitcast.14), calls=%async_computation.1 | async-start | bytes 1048576
  0.1 11.1 %copy-start = (bf16[4,6,8,4096]{3,2,1,0:T(8,128)(2,1)S(1)}, bf16[4,6,8,4096]{3,2,1,0:T(8,128)(2,1)}, u32[]{:S(2)}) copy-start(bf16[4,6,8,4096]{3,2,1,0:T(8,128)(2,1)} %param.6) | copy-start | bytes 4718596
  6.3 20.1 %collective-permute-start.2 = (bf16[12,64,128]{2,1,0:T(8,128)(2,1)S(1)}, bf16[12,64,128]{2,1,0:T(8,128)(2,1)S(1)}, u32[]{:S(2)}, u32[]{:S(2)}) collective-permute-start(bf16[12,64,128]{2,1,0:T(8,128)(2,1)S(1)} %get-tuple-element.26), channel_id=1, source_target_pairs={{0,1},{2,3},{4,5},{6,7},{1,0},{3,2},{5,4},{7,6},{8,9},{10,11},{12,... | collective-permute-start | bytes 589832 | tf_op jit(solution)/shard_map/ppermute | solution.py:21
  7.9 18.5 %collective-permute-start.3 = (bf16[12,64,128]{2,1,0:T(8,128)(2,1)S(1)}, bf16[12,64,128]{2,1,0:T(8,128)(2,1)S(1)}, u32[]{:S(2)}, u32[]{:S(2)}) collective-permute-start(bf16[12,64,128]{2,1,0:T(8,128)(2,1)S(1)} %get-tuple-element.27), channel_id=1, source_target_pairs={{1,2},{3,4},{5,6},{2,1},{4,3},{6,5},{9,10},{11,12},{13,14},{10,9},... | collective-permute-start | bytes 589832 | tf_op jit(solution)/shard_map/ppermute | solution.py:21
  9.8 16.6 %collective-permute-start.1 = (bf16[4,4,64,128]{3,2,1,0:T(8,128)(2,1)S(1)}, bf16[4,4,64,128]{3,2,1,0:T(8,128)(2,1)S(1)}, u32[]{:S(2)}, u32[]{:S(2)}) collective-permute-start(bf16[4,4,64,128]{3,2,1,0:T(8,128)(2,1)S(1)} %get-tuple-element.25), channel_id=1, source_target_pairs={{0,8},{8,0},{1,9},{9,1},{2,10},{10,2},{3,11},{11,3},{4,12},{12,4},... | collective-permute-start | bytes 786440 | tf_op jit(solution)/shard_map/ppermute | solution.py:21
  11.1 15.3 %collective-permute-start = (bf16[6,4,64,128]{3,2,1,0:T(8,128)(2,1)S(1)}, bf16[6,4,64,128]{3,2,1,0:T(8,128)(2,1)S(1)}, u32[]{:S(2)}, u32[]{:S(2)}) collective-permute-start(bf16[6,4,64,128]{3,2,1,0:T(8,128)(2,1)S(1)} %get-tuple-element.24), channel_id=1, source_target_pairs={{0,16},{16,0},{1,17},{17,1},{2,18},{18,2},{3,19},{19,3},{4,20},{20... | collective-permute-start | bytes 1179656 | tf_op jit(solution)/shard_map/ppermute | solution.py:21
  11.2 15.2 %copy-start.1 = (s32[24]{0:T(128)S(1)}, s32[24]{0:T(128)}, u32[]{:S(2)}) copy-start(s32[24]{0:T(128)} %owners.1) | copy-start | bytes 292
  34.5 8.6 %collective-permute-start.4 = (bf16[3,224,128]{2,1,0:T(8,128)(2,1)S(1)}, bf16[3,224,128]{2,1,0:T(8,128)(2,1)S(1)}, u32[]{:S(2)}, u32[]{:S(2)}) collective-permute-start(bf16[3,224,128]{2,1,0:T(8,128)(2,1)S(1)} %get-tuple-element.36), channel_id=1, source_target_pairs={{0,1},{1,0},{2,3},{3,2},{4,5},{5,4},{6,7},{7,6},{8,9},{9,8},{10,11... | collective-permute-start | bytes 516104 | tf_op jit(solution)/shard_map/ppermute | solution.py:513
  37.2 10.9 %collective-permute-start.5 = (bf16[3,224,128]{2,1,0:T(8,128)(2,1)S(1)}, bf16[3,224,128]{2,1,0:T(8,128)(2,1)S(1)}, u32[]{:S(2)}, u32[]{:S(2)}) collective-permute-start(bf16[3,224,128]{2,1,0:T(8,128)(2,1)S(1)} %get-tuple-element.37), channel_id=1, source_target_pairs={{0,2},{1,3},{2,0},{3,1},{4,6},{5,7},{6,4},{7,5},{8,10},{9,11},{10,... | collective-permute-start | bytes 516104 | tf_op jit(solution)/shard_map/ppermute | solution.py:513
  37.6 12.4 %collective-permute-start.6 = (bf16[3,224,128]{2,1,0:T(8,128)(2,1)S(1)}, bf16[3,224,128]{2,1,0:T(8,128)(2,1)S(1)}, u32[]{:S(2)}, u32[]{:S(2)}) collective-permute-start(bf16[3,224,128]{2,1,0:T(8,128)(2,1)S(1)} %get-tuple-element.38), channel_id=1, source_target_pairs={{0,3},{1,2},{2,1},{3,0},{4,7},{5,6},{6,5},{7,4},{8,11},{9,10},{10,... | collective-permute-start | bytes 516104 | tf_op jit(solution)/shard_map/ppermute | solution.py:513
  38.7 21.2 %collective-permute-start.7 = (bf16[3,224,128]{2,1,0:T(8,128)(2,1)S(1)}, bf16[3,224,128]{2,1,0:T(8,128)(2,1)S(1)}, u32[]{:S(2)}, u32[]{:S(2)}) collective-permute-start(bf16[3,224,128]{2,1,0:T(8,128)(2,1)S(1)} %get-tuple-element.39), channel_id=1, source_target_pairs={{0,4},{1,5},{2,6},{3,7},{4,0},{5,1},{6,2},{7,3},{8,12},{9,13},{10,... | collective-permute-start | bytes 516104 | tf_op jit(solution)/shard_map/ppermute | solution.py:513
  40.6 23.2 %collective-permute-start.8 = (bf16[3,224,128]{2,1,0:T(8,128)(2,1)S(1)}, bf16[3,224,128]{2,1,0:T(8,128)(2,1)S(1)}, u32[]{:S(2)}, u32[]{:S(2)}) collective-permute-start(bf16[3,224,128]{2,1,0:T(8,128)(2,1)S(1)} %get-tuple-element.40), channel_id=1, source_target_pairs={{0,5},{1,4},{2,7},{3,6},{4,1},{5,0},{6,3},{7,2},{8,13},{9,12},{10,... | collective-permute-start | bytes 516104 | tf_op jit(solution)/shard_map/ppermute | solution.py:513
  43.0 24.4 %collective-permute-start.9 = (bf16[3,224,128]{2,1,0:T(8,128)(2,1)S(1)}, bf16[3,224,128]{2,1,0:T(8,128)(2,1)S(1)}, u32[]{:S(2)}, u32[]{:S(2)}) collective-permute-start(bf16[3,224,128]{2,1,0:T(8,128)(2,1)S(1)} %get-tuple-element.41), channel_id=1, source_target_pairs={{0,6},{1,7},{2,4},{3,5},{4,2},{5,3},{6,0},{7,1},{8,14},{9,15},{10,... | collective-permute-start | bytes 516104 | tf_op jit(solution)/shard_map/ppermute | solution.py:513
  48.1 22.3 %collective-permute-start.10 = (bf16[3,224,128]{2,1,0:T(8,128)(2,1)S(1)}, bf16[3,224,128]{2,1,0:T(8,128)(2,1)S(1)}, u32[]{:S(2)}, u32[]{:S(2)}) collective-permute-start(bf16[3,224,128]{2,1,0:T(8,128)(2,1)S(1)} %get-tuple-element.42), channel_id=1, source_target_pairs={{0,7},{1,6},{2,5},{3,4},{4,3},{5,2},{6,1},{7,0},{8,15},{9,14},{10,... | collective-permute-start | bytes 516104 | tf_op jit(solution)/shard_map/ppermute | solution.py:513

commit v11 on v10

--- a/solution.py
+++ b/solution.py
@@ -58,10 +58,11 @@
     return jnp.concatenate([even, odd], axis=0)
 
 
-def in_order(pair):
+def in_order(pairs):
     row = lax.broadcasted_iota(jnp.int32, (NODES, NODES), 0)
     col = lax.broadcasted_iota(jnp.int32, (NODES, NODES), 1)
-    return product(zero_one(row == 2 * (col % HALF) + col // HALF), pair).astype(jnp.bfloat16)
+    moved = product(zero_one(row == 2 * (col % HALF) + col // HALF), jnp.concatenate(pairs, axis=1)).astype(jnp.bfloat16)
+    return [moved[:, LANES * p : LANES * (p + 1)] for p in range(len(pairs))]
 
 
 def four_weights(first, second):
@@ -119,9 +120,10 @@
         spread(p_ref[j], stage)
         block = [block_of(stage, z, depth) for z in range(depth)]
         stacked = [stacked_pair(block[2 * p], block[2 * p + 1]) for p in range(pairs)]
+        natural = in_order(stacked)
         for p in range(pairs):
             stacks[j, p] = stacked[p]
-            natural_ref[j, p] = in_order(stacked[p])
+            natural_ref[j, p] = natural[p]
         for h in range(pairs // 2):
             turned_ref[j, h] = jnp.concatenate([stacked[2 * h], stacked[2 * h + 1]], axis=0).T
         ends[0, j] = block[0]
@@ -131,9 +133,9 @@
         last = block_of(stage_f, depth - 1, depth)
         ends[2, j] = last
 
-    for t in range(size_y // 2):
-        first, last, face = [stacked_pair(ends[kind, 2 * t], ends[kind, 2 * t + 1]) for kind in range(3)]
-        head = in_order(first)
+    heads = in_order([stacked_pair(ends[0, 2 * t], ends[0, 2 * t + 1]) for t in range(size_y // 2)])
+    for t, head in enumerate(heads):
+        last, face = [stacked_pair(ends[kind, 2 * t], ends[kind, 2 * t + 1]) for kind in (1, 2)]
         rim = diagonal(across(face, last))
         first_z_ref[t] = head
         last_z_ref[t] = last
@@ -219,9 +221,9 @@
     for total in ahead + behind:
         total[...] = jnp.zeros_like(total)
 
-    def couplings(i, j, stage):
+    def couplings(i, j, stage, has_x):
         column = i * size_y + j
-        sources = [diag_ref[column], face_ref[0, jnp.maximum(column - size_y, 0)], face_ref[1, column - 1] if j else None, face_ref[2, column]]
+        sources = [diag_ref[column], face_ref[0, column - size_y] if has_x else None, face_ref[1, column - 1] if j else None, face_ref[2, column]]
         stacked = {}
         for face, source in enumerate(sources):
             if source is None:
@@ -246,8 +248,7 @@
 
     def sums(i, j, couples):
         column = i * size_y + j
-        has_x, row_x = i > 0, jnp.maximum(i - 1, 0)
-        origin = {0: column, 1: jnp.maximum(column - size_y, 0), 2: column - 1, 3: column}
+        origin = {0: column, 1: column - size_y, 2: column - 1, 3: column}
         batches = []
         for h in range(pairs // 2):
             for face, pair in couples.items():
@@ -259,8 +260,7 @@
                         updates.append((ahead[side], keys[0, i, j, z], term))
                         continue
                     if face == 1:
-                        here, there = keys[2, row_x, j, z], keys[1, i, j, z]
-                        here, there = jnp.where(has_x, here, spare), jnp.where(has_x, there, spare)
+                        here, there = keys[2, i - 1, j, z], keys[1, i, j, z]
                     elif face == 2:
                         here, there = keys[4, i, j - 1, z], keys[3, i, j, z]
                     elif z + 1 < depth:
@@ -272,13 +272,14 @@
                 batches.append(updates)
         return batches
 
-    def plane(i, carry):
-        couples = [couplings(i, j, stages.at[j]) for j in range(size_y)]
+    def plane(i, carry, has_x=True):
+        couples = [couplings(i, j, stages.at[j], has_x) for j in range(size_y)]
         for updates in [updates for j in range(size_y) for updates in sums(i, j, couples[j])]:
             add_all(updates)
         return carry
 
-    lax.fori_loop(0, size_x, plane, 0)
+    plane(0, 0, has_x=False)
+    lax.fori_loop(1, size_x, plane, 0)
 
     def finish(g, carry):
         low = low_lanes(HALF)
@@ -303,7 +304,7 @@
     size_x, size_y, depth = sizes
     pairs, block = depth // 2, diag.shape[-1]
     columns, rows = size_x * size_y, AGG_DEV * SLOTS
-    total = pltpu.VMEM((rows + 1, HALF, LANES), jnp.float32)
+    total = pltpu.VMEM((rows, HALF, LANES), jnp.float32)
     whole = pl.BlockSpec(memory_space=pltpu.VMEM)
     return pl.pallas_call(
         interior_kernel,
@@ -321,7 +322,7 @@
     )(keys, diag, faces, natural, turned)
 
 
-def border_kernel(capacity, paired, owners, place_ref, keys, got_x, got_y, near_z, far_z, tail_x, tail_y, tail_z, turned_x, turned_y,
+def border_kernel(capacity, paired, first_part, owners, place_ref, keys, got_x, got_y, near_z, far_z, tail_x, tail_y, tail_z, turned_x, turned_y,
                   natural_x, natural_y, first_z, last_z, start_ref, *refs):
     out_refs, (total, filled, listed) = refs[:-3], refs[-3:]
     size_y, pairs = tail_x.shape[0], tail_x.shape[1]
@@ -342,9 +343,12 @@
             four = two_pairs(product(turned[h], apart(*couples)))
             yield [(total, key(4 * h + number), term) for number, term in enumerate(four)]
 
+    def turned_terms(first, second, rims):
+        return two_pairs(product(jnp.concatenate([first, second], axis=0).T, apart(*rims)))
+
     def back(natural, rim, key):
         for h in range(pairs // 2):
-            four = [term for p in (2 * h, 2 * h + 1) for term in folded(across(natural[p], rim[p]))]
+            four = turned_terms(natural[2 * h], natural[2 * h + 1], (rim[2 * h], rim[2 * h + 1]))
             yield [(total, key(4 * h + number), term) for number, term in enumerate(four)]
 
     def batches_x(first):
@@ -366,12 +370,11 @@
         for t in range(0, near_z.shape[0], 2):
             heads = [jnp.where(even, near_z[u], far_z[u]) for u in (t, t + 1)]
             couples = couplings([tail_z[t], tail_z[t + 1]], heads)
-            for u in (t, t + 1):
-                i, j = 2 * u // size_y, 2 * u % size_y
-                front = folded(across(last_z[u], couples[u - t]))
-                past = folded(across(first_z[u], jnp.where(even, far_z[u], near_z[u])))
-                yield ([(total, keys[6, i, j + side, depth - 1], front[side]) for side in (0, 1)]
-                       + [(total, keys[5, i, j + side, 0], past[side]) for side in (0, 1)])
+            front = turned_terms(last_z[t], last_z[t + 1], couples)
+            past = turned_terms(first_z[t], first_z[t + 1], [jnp.where(even, far_z[u], near_z[u]) for u in (t, t + 1)])
+            spots = [(2 * u // size_y, 2 * u % size_y + side) for u in (t, t + 1) for side in (0, 1)]
+            yield [(total, keys[6, i, j, depth - 1], term) for (i, j), term in zip(spots, front)]
+            yield [(total, keys[5, i, j, 0], term) for (i, j), term in zip(spots, past)]
 
     for first_x in (True, False):
         for first_y in (True, False):
@@ -381,36 +384,59 @@
                 for updates in batches:
                     add_all(updates)
 
-    places = capacity * len(out_refs)
-    full = places * SLOTS == rows
-    for spot in range(places):
+    emit(capacity, paired, first_part, owners, place_ref, total, out_refs, filled, listed)
+
+
+def emit(capacity, paired, first_part, owners, place_ref, total, out_refs, filled, listed):
+    rows, devices = total.shape[0] // SLOTS, filled.shape[0]
+    for spot in range(capacity * devices):
         listed[spot] = -1
-    for owner in range(len(out_refs)):
+    for owner in range(devices):
         filled[owner] = 0
-    for r in range(rows // SLOTS):
+    for r in range(rows):
         owner = owners[r]
         listed[jnp.bitwise_xor(owner, place_ref[2] if paired else 0) * capacity + filled[owner]] = r
         filled[owner] = filled[owner] + 1
-    for spot in range(places):
-        row = listed[spot]
-        for s in range(SLOTS):
-            key = jnp.maximum(row, 0) * SLOTS + s
-            even, odd = [total[key, pl.ds(first, HALF // 2, stride=2), :] for first in (0, 1)]
-            block = straightened(even, odd)
-            if not full:
-                block = jnp.where(row >= 0, block, jnp.zeros_like(block))
-            out_refs[spot // capacity][spot % capacity, HALF * s : HALF * (s + 1), :] = block.astype(jnp.bfloat16)
-
-
-def border(owners, place, keys, operands, turned, natural, ends, total, capacity, devices, paired, sizes):
+    for part, out_ref in enumerate(out_refs):
+        for q in range(capacity):
+            row = listed[(first_part + part) * capacity + q]
+            for s in range(SLOTS):
+                key = jnp.maximum(row, 0) * SLOTS + s
+                even, odd = [total[key, pl.ds(first, HALF // 2, stride=2), :] for first in (0, 1)]
+                block = straightened(even, odd)
+                if capacity * devices != rows:
+                    block = jnp.where(row >= 0, block, jnp.zeros_like(block))
+                out_ref[q, HALF * s : HALF * (s + 1), :] = block.astype(jnp.bfloat16)
+
+
+def near_kernel(capacity, owners, place_ref, total, arrived, *refs):
+    emit(capacity, True, 0, owners, place_ref, total, refs[:-2], *refs[-2:])
+
+
+def near_parts(owners, place, total, arrived, capacity, count, devices):
+    smem = pl.BlockSpec(memory_space=pltpu.SMEM)
+    whole = pl.BlockSpec(memory_space=pltpu.VMEM)
+    return pl.pallas_call(
+        functools.partial(near_kernel, capacity),
+        in_specs=[smem, smem, whole, pl.BlockSpec(memory_space=pl.ANY)],
+        out_specs=[whole] * count,
+        out_shape=[jax.ShapeDtypeStruct((capacity, SLOTS * HALF, LANES), jnp.bfloat16)] * count,
+        scratch_shapes=[pltpu.SMEM((devices,), jnp.int32), pltpu.SMEM((capacity * devices,), jnp.int32)],
+        compiler_params=pltpu.CompilerParams(vmem_limit_bytes=10 * MIB),
+        name="near",
+    )(owners, place, total, arrived)
+
+
+def border(owners, place, keys, operands, turned, natural, ends, total, capacity, devices, paired, first_part, sizes):
     size_x, size_y, depth = sizes
     pairs = depth // 2
     smem = pl.BlockSpec(memory_space=pltpu.SMEM)
     whole = pl.BlockSpec(memory_space=pltpu.VMEM)
     planes = lambda array: array.reshape((size_x, size_y) + array.shape[1:])
     before = 3 + len(operands) + 4 + len(ends)
+    count = devices - first_part
     return pl.pallas_call(
-        functools.partial(border_kernel, capacity, paired),
+        functools.partial(border_kernel, capacity, paired, first_part),
         grid=(1,),
         in_specs=[smem, smem, smem] + [whole] * len(operands) + [
             pl.BlockSpec((size_y, pairs // 2, LANES, LANES), lambda i: (size_x - 1, 0, 0, 0)),
@@ -418,14 +444,14 @@
             pl.BlockSpec((size_y, pairs, NODES, LANES), lambda i: (0, 0, 0, 0)),
             pl.BlockSpec((size_x, 1, pairs, NODES, LANES), lambda i: (0, 0, 0, 0, 0)),
         ] + [whole] * (len(ends) + 1),
-        out_specs=[whole] * (devices + 1),
-        out_shape=[jax.ShapeDtypeStruct((capacity, SLOTS * HALF, LANES), jnp.bfloat16)] * devices
+        out_specs=[whole] * (count + 1),
+        out_shape=[jax.ShapeDtypeStruct((capacity, SLOTS * HALF, LANES), jnp.bfloat16)] * count
         + [jax.ShapeDtypeStruct(total.shape, total.dtype)],
-        input_output_aliases={before: devices},
+        input_output_aliases={before: count},
         scratch_shapes=[pltpu.SMEM((devices,), jnp.int32), pltpu.SMEM((capacity * devices,), jnp.int32)],
         compiler_params=pltpu.CompilerParams(vmem_limit_bytes=18 * MIB),
         name="border",
-    )(owners, place, keys, *operands, turned, planes(turned), natural, planes(natural), *ends, total)[:devices]
+    )(owners, place, keys, *operands, turned, planes(turned), natural, planes(natural), *ends, total)
 
 
 def layout_kernel(source, rows_ref, out_ref, stage):
@@ -503,14 +529,17 @@
     got_x = swapped_along(swap_x, "gx", 0)
     total = interior(keys, diag, faces, natural, turned, sizes)
     paired = holding == AGG_DEV and depth & (depth - 1) == 0
-    outgoing = border(
+    first_part = depth // 2 if paired else 0
+    *outgoing, total = border(
         row_owner, place, keys, (got_x, got_y, near_z, far_z, tail_x, tail_y, tail_z), turned, natural,
-        (first_z, last_z), total, capacity, depth, paired, sizes)
+        (first_z, last_z), total, capacity, depth, paired, first_part, sizes)
     if paired:
-        parts = list(outgoing)
-        far_first = sorted(range(1, depth), key=lambda k: (k < depth // 2, k))
-        for k in far_first:
-            parts[k] = lax.ppermute(outgoing[k], "gz", [(i, i ^ k) for i in range(depth)])
+        def swapped_with(part, k):
+            return lax.ppermute(part, "gz", [(i, i ^ k) for i in range(depth)]) if k else part
+
+        far = [swapped_with(part, first_part + k) for k, part in enumerate(outgoing)]
+        near = [swapped_with(part, k) for k, part in enumerate(near_parts(row_owner, place, total, far[0], capacity, first_part, depth))]
+        parts = near + far
         result = placed(place, parts, block)
     else:
         arrived = lax.all_to_all(jnp.concatenate(outgoing, axis=0), "gz", 0, 0, tiled=True)

time: 73.1 us -> 71 us (0.971)
  the two profiles are of different devices: /device:TPU:8 before, /device:TPU:0 now
where the time goes in v11:
time: 71 us; the launch traced here: 70.8 us
  Pallas kernels  32.2 us (45%)
  waiting for transfers between devices  20.9 us (29%)
  starting transfers between devices  17.5 us (25%)
    ppermute x7, waiting for transfers between devices, swapped_with(): lax.ppermute(part, 'gz', [(i, i ^ k) for i in range(depth)])  20.9 us
    pallas_call x1, Pallas kernels, interior(): pl.pallas_call(interior_kernel, in_specs=[pl.BlockSpec(memory_space=pltpu...  14.7 us
    ppermute x7, starting transfers between devices, swapped_with(): lax.ppermute(part, 'gz', [(i, i ^ k) for i in range(depth)])  12.8 us
    pallas_call x1, Pallas kernels, border(): pl.pallas_call(functools.partial(border_kernel, capacity, paired, first_p...  7.84 us
    pallas_call x1, Pallas kernels, prepare(): pl.pallas_call(prepare_kernel, grid=(size_x,), in_specs=[pl.BlockSpec(mem...  6.21 us
    ppermute x4, starting transfers between devices, swapped_along(): return lax.ppermute(block, axis, pairs + [(i + 1, i) for i, _ in pairs])  4.64 us
    pallas_call x1, Pallas kernels, placed(): pl.pallas_call(placed_kernel, in_specs=[pl.BlockSpec(memory_space=pltpu.S...  2.51 us
  transfers between devices with their start and end apart: 11, of which 4 were waited for; matrix products, arithmetic and copies ran while one was open for 0% of the time, Pallas kernels for 22%

profile of v11, /device:TPU:0, one launch (start us, length us, event | category | flops | bytes accessed | tf_op | source)
XLA Modules:
  0.0 70.8 jit_solution(14373032560849010216)
XLA Ops:
  0.0 0.1 pad_add_fusion.place_ref
  0.1 0.0 slice-start
  0.1 0.0 copy-start.3
  0.1 0.0 copy-start.2
  0.1 0.0 slice-start.1
  0.1 0.0 copy-start
  0.1 6.2 %prepare.1 = (bf16[24,4,64,128]{3,2,1,0:T(8,128)(2,1)S(1)}, bf16[24,2,128,128]{3,2,1,0:T(8,128)(2,1)S(1)}, bf16[6,4,64,128]{3,2,1,0:T(8,128)(2,1)S(1)}, bf16[4,4...) custom-call(s32[3]{0:T(128)S(1)} %pad_add_fusion.place_ref, ...), custom_call_target="tpu_custom_call" | custom-call | tf_op jit(solution)/shard_map/prepare/pallas_call | solution.py:179
  6.3 3.0 %collective-permute-start.2 = (bf16[12,64,128]{2,1,0:T(8,128)(2,1)S(1)}, bf16[12,64,128]{2,1,0:T(8,128)(2,1)S(1)}, u32[]{:S(2)}, u32[]{:S(2)}) collective-permute-start(bf16[12,64,128]{2,1,0:T(8,128)(2,1)S(1)} %get-tuple-element.27), channel_id=1, source_target_pairs={{0,1},{2,3},{4,5},{6,7},{1,0},{3,2},{5,4},{7,6},{8,9},{10,11},{12,... | collective-permute-start | bytes 589832 | tf_op jit(solution)/shard_map/ppermute | solution.py:21
  9.4 0.7 collective-permute-start.3
  10.0 0.9 %collective-permute-start.1 = (bf16[4,4,64,128]{3,2,1,0:T(8,128)(2,1)S(1)}, bf16[4,4,64,128]{3,2,1,0:T(8,128)(2,1)S(1)}, u32[]{:S(2)}, u32[]{:S(2)}) collective-permute-start(bf16[4,4,64,128]{3,2,1,0:T(8,128)(2,1)S(1)} %get-tuple-element.26), channel_id=1, source_target_pairs={{0,8},{8,0},{1,9},{9,1},{2,10},{10,2},{3,11},{11,3},{4,12},{12,4},... | collective-permute-start | bytes 786440 | tf_op jit(solution)/shard_map/ppermute | solution.py:21
  11.0 0.0 collective-permute-start
  11.0 0.0 copy-done.3
  11.0 0.0 copy-done.2
  11.0 0.0 slice-done
  11.0 0.0 slice-done.1
  11.0 0.0 copy-done
  11.1 0.0 copy-start.1
  11.1 14.7 %interior.1.start_ref = f32[168,32,128]{2,1,0:T(8,128)S(1)} custom-call(s32[7,4,6,8]{3,2,1,0:T(8,128)S(1)} %copy_add_fusion.keys, bf16[24,8,4096]{2,1,0:T(8,128)(2,1)S(1)} %bitcast.19, bf16[3,24,8,4096]{3,2,1,0:T(8,128)(2,1)S(1)} %bitcast.16, bf16[24,4,64,128]{3,2,1,0:T(8,128)(2,1)S(1)} %get-tuple-element.33.natural_ref.natural_x, ...), custom_call_target="tpu_custom_call" | custom-call | flops 704643072 | bytes 9437184 | tf_op jit(solution)/shard_map/interior/pallas_call | solution.py:309
  25.8 0.0 collective-permute-done.2.near_z
  25.8 0.0 collective-permute-done.3.far_z
  25.8 0.0 collective-permute-done.1.got_y
  25.8 0.0 collective-permute-done.got_x
  25.8 0.0 copy-done.1
  25.8 7.8 %border.1 = (bf16[3,224,128]{2,1,0:T(8,128)(2,1)S(1)}, bf16[3,224,128]{2,1,0:T(8,128)(2,1)S(1)}, bf16[3,224,128]{2,1,0:T(8,128)(2,1)S(1)}, bf16[3,224,128]{2,1,0:T(8,128)(2,1)S(1)}, f32[168,32,128]{2,1,0:T(8,128)S(1)}) custom-call(s32[24]{0:T(128)S(1)} %copy-done.1, s32[3]{0:T(128)S(1)} %pad_add_fusion.place_ref, ...), custom_call_target="tpu_custom_call", output_to_operand_aliasing={{4}: (16, {})} | custom-call | tf_op jit(solution)/shard_map/border/pallas_call | solution.py:438
  33.7 4.3 %collective-permute-start.4 = (bf16[3,224,128]{2,1,0:T(8,128)(2,1)S(1)}, bf16[3,224,128]{2,1,0:T(8,128)(2,1)S(1)}, u32[]{:S(2)}, u32[]{:S(2)}) collective-permute-start(bf16[3,224,128]{2,1,0:T(8,128)(2,1)S(1)} %get-tuple-element.37), channel_id=1, source_target_pairs={{0,4},{1,5},{2,6},{3,7},{4,0},{5,1},{6,2},{7,3},{8,12},{9,13},{10,... | collective-permute-start | bytes 516104 | tf_op jit(solution)/shard_map/ppermute | solution.py:538
  37.9 2.4 %collective-permute-start.8 = (bf16[3,224,128]{2,1,0:T(8,128)(2,1)S(1)}, bf16[3,224,128]{2,1,0:T(8,128)(2,1)S(1)}, u32[]{:S(2)}, u32[]{:S(2)}) collective-permute-start(bf16[3,224,128]{2,1,0:T(8,128)(2,1)S(1)} %get-tuple-element.42), channel_id=1, source_target_pairs={{0,5},{1,4},{2,7},{3,6},{4,1},{5,0},{6,3},{7,2},{8,13},{9,12},{10,... | collective-permute-start | bytes 516104 | tf_op jit(solution)/shard_map/ppermute | solution.py:538
  40.4 1.1 %collective-permute-start.9 = (bf16[3,224,128]{2,1,0:T(8,128)(2,1)S(1)}, bf16[3,224,128]{2,1,0:T(8,128)(2,1)S(1)}, u32[]{:S(2)}, u32[]{:S(2)}) collective-permute-start(bf16[3,224,128]{2,1,0:T(8,128)(2,1)S(1)} %get-tuple-element.43), channel_id=1, source_target_pairs={{0,6},{1,7},{2,4},{3,5},{4,2},{5,3},{6,0},{7,1},{8,14},{9,15},{10,... | collective-permute-start | bytes 516104 | tf_op jit(solution)/shard_map/ppermute | solution.py:538
  41.4 2.4 %collective-permute-start.10 = (bf16[3,224,128]{2,1,0:T(8,128)(2,1)S(1)}, bf16[3,224,128]{2,1,0:T(8,128)(2,1)S(1)}, u32[]{:S(2)}, u32[]{:S(2)}) collective-permute-start(bf16[3,224,128]{2,1,0:T(8,128)(2,1)S(1)} %get-tuple-element.44), channel_id=1, source_target_pairs={{0,7},{1,6},{2,5},{3,4},{4,3},{5,2},{6,1},{7,0},{8,15},{9,14},{10,... | collective-permute-start | bytes 516104 | tf_op jit(solution)/shard_map/ppermute | solution.py:538
  43.8 12.3 %collective-permute-done.4.arrived.refs_4_ = bf16[3,224,128]{2,1,0:T(8,128)(2,1)S(1)} collective-permute-done((bf16[3,224,128]{2,1,0:T(8,128)(2,1)S(1)}, bf16[3,224,128]{2,1,0:T(8,128)(2,1)S(1)}, u32[]{:S(2)}, u32[]{:S(2)}) %collective-permute-start.4) | collective-permute-done | bytes 172064 | tf_op jit(solution)/shard_map/ppermute | solution.py:538
  56.1 0.9 %near.1 = (bf16[3,224,128]{2,1,0:T(8,128)(2,1)S(1)}, bf16[3,224,128]{2,1,0:T(8,128)(2,1)S(1)}, bf16[3,224,128]{2,1,0:T(8,128)(2,1)S(1)}, bf16[3,224,128]{2,1,0:T(8,128)(2,1)S(1)}) custom-call(s32[24]{0:T(128)S(1)} %copy-done.1, s32[3]{0:T(128)S(1)} %pad_add_fusion.place_ref, f32[168,32,128]{2,1,0:T(8,128)S(1)} %get-tuple-element.36.total, ...), custom_call_target="tpu_custom_call" | custom-call | tf_op jit(solution)/shard_map/near/pallas_call | solution.py:419
  57.1 2.6 %collective-permute-start.5 = (bf16[3,224,128]{2,1,0:T(8,128)(2,1)S(1)}, bf16[3,224,128]{2,1,0:T(8,128)(2,1)S(1)}, u32[]{:S(2)}, u32[]{:S(2)}) collective-permute-start(bf16[3,224,128]{2,1,0:T(8,128)(2,1)S(1)} %get-tuple-element.39), channel_id=1, source_target_pairs={{0,1},{1,0},{2,3},{3,2},{4,5},{5,4},{6,7},{7,6},{8,9},{9,8},{10,11... | collective-permute-start | bytes 516104 | tf_op jit(solution)/shard_map/ppermute | solution.py:538
  59.7 0.0 collective-permute-start.6
  59.7 2.1 %collective-permute-done.8.refs_5_ = bf16[3,224,128]{2,1,0:T(8,128)(2,1)S(1)} collective-permute-done((bf16[3,224,128]{2,1,0:T(8,128)(2,1)S(1)}, bf16[3,224,128]{2,1,0:T(8,128)(2,1)S(1)}, u32[]{:S(2)}, u32[]{:S(2)}) %collective-permute-start.8) | collective-permute-done | bytes 172064 | tf_op jit(solution)/shard_map/ppermute | solution.py:538
  61.8 0.0 collective-permute-start.7
  61.8 0.0 collective-permute-done.9.refs_6_
  61.8 0.0 collective-permute-done.10.refs_7_
  61.9 3.8 %collective-permute-done.5.refs_1_ = bf16[3,224,128]{2,1,0:T(8,128)(2,1)S(1)} collective-permute-done((bf16[3,224,128]{2,1,0:T(8,128)(2,1)S(1)}, bf16[3,224,128]{2,1,0:T(8,128)(2,1)S(1)}, u32[]{:S(2)}, u32[]{:S(2)}) %collective-permute-start.5) | collective-permute-done | bytes 172064 | tf_op jit(solution)/shard_map/ppermute | solution.py:538
  65.6 0.0 collective-permute-done.6.refs_2_
  65.6 2.7 %collective-permute-done.7.refs_3_ = bf16[3,224,128]{2,1,0:T(8,128)(2,1)S(1)} collective-permute-done((bf16[3,224,128]{2,1,0:T(8,128)(2,1)S(1)}, bf16[3,224,128]{2,1,0:T(8,128)(2,1)S(1)}, u32[]{:S(2)}, u32[]{:S(2)}) %collective-permute-start.7) | collective-permute-done | bytes 172064 | tf_op jit(solution)/shard_map/ppermute | solution.py:538
  68.3 2.5 %placed.1 = bf16[7,24,4096]{2,1,0:T(8,128)(2,1)} custom-call(s32[3]{0:T(128)S(1)} %pad_add_fusion.place_ref, bf16[3,224,128]{2,1,0:T(8,128)(2,1)S(1)} %get-tuple-element.38.refs_0_, bf16[3,224,128]{2,1,0:T(8,128)(2,1)S(1)} %collective-permute-done.5.refs_1_, bf16[3,224,128]{2,1,0:T(8,128)(2,1)S(1)} %collective-permute-done.6.refs_2_, ...), custom_call_target="tpu_custom_call" | custom-call | tf_op jit(solution)/shard_map/placed/pallas_call | solution.py:500
  (4 shorter events, 0.0 us)
Async XLA Ops:
  0.1 11.0 %slice-start = ((s8[4718592]{0:T(1024)(128)(4,1)}), s8[4194304]{0:T(1024)(128)(4,1)S(1)}, s32[]{:S(2)}) async-start(s8[4718592]{0:T(1024)(128)(4,1)} %bitcast.14), calls=%async_computation | async-start | bytes 8388608
  0.1 10.9 %copy-start.3 = (s32[4,6,8]{2,0,1:T(4,128)S(1)}, s32[4,6,8]{2,0,1:T(4,128)}, u32[]{:S(2)}) copy-start(s32[4,6,8]{2,0,1:T(4,128)} %param.9) | copy-start | bytes 2308
  0.1 10.9 %copy-start.2 = (s32[7,4,6,8]{3,1,2,0:T(4,128)S(1)}, s32[7,4,6,8]{3,1,2,0:T(4,128)}, u32[]{:S(2)}) copy-start(s32[7,4,6,8]{3,1,2,0:T(4,128)} %param.10) | copy-start | bytes 16132
  0.1 11.0 %slice-start.1 = ((s8[4718592]{0:T(1024)(128)(4,1)}), s8[524288]{0:T(1024)(128)(4,1)S(1)}, s32[]{:S(2)}) async-start(s8[4718592]{0:T(1024)(128)(4,1)} %bitcast.14), calls=%async_computation.1 | async-start | bytes 1048576
  0.1 11.0 %copy-start = (bf16[4,6,8,4096]{3,2,1,0:T(8,128)(2,1)S(1)}, bf16[4,6,8,4096]{3,2,1,0:T(8,128)(2,1)}, u32[]{:S(2)}) copy-start(bf16[4,6,8,4096]{3,2,1,0:T(8,128)(2,1)} %param.6) | copy-start | bytes 4718596
  6.3 19.4 %collective-permute-start.2 = (bf16[12,64,128]{2,1,0:T(8,128)(2,1)S(1)}, bf16[12,64,128]{2,1,0:T(8,128)(2,1)S(1)}, u32[]{:S(2)}, u32[]{:S(2)}) collective-permute-start(bf16[12,64,128]{2,1,0:T(8,128)(2,1)S(1)} %get-tuple-element.27), channel_id=1, source_target_pairs={{0,1},{2,3},{4,5},{6,7},{1,0},{3,2},{5,4},{7,6},{8,9},{10,11},{12,... | collective-permute-start | bytes 589832 | tf_op jit(solution)/shard_map/ppermute | solution.py:21
  9.4 16.4 %collective-permute-start.3 = (bf16[12,64,128]{2,1,0:T(8,128)(2,1)S(1)}, bf16[12,64,128]{2,1,0:T(8,128)(2,1)S(1)}, u32[]{:S(2)}, u32[]{:S(2)}) collective-permute-start(bf16[12,64,128]{2,1,0:T(8,128)(2,1)S(1)} %get-tuple-element.28), channel_id=1, source_target_pairs={{1,2},{3,4},{5,6},{2,1},{4,3},{6,5},{9,10},{11,12},{13,14},{10,9},... | collective-permute-start | bytes 589832 | tf_op jit(solution)/shard_map/ppermute | solution.py:21
  10.0 15.8 %collective-permute-start.1 = (bf16[4,4,64,128]{3,2,1,0:T(8,128)(2,1)S(1)}, bf16[4,4,64,128]{3,2,1,0:T(8,128)(2,1)S(1)}, u32[]{:S(2)}, u32[]{:S(2)}) collective-permute-start(bf16[4,4,64,128]{3,2,1,0:T(8,128)(2,1)S(1)} %get-tuple-element.26), channel_id=1, source_target_pairs={{0,8},{8,0},{1,9},{9,1},{2,10},{10,2},{3,11},{11,3},{4,12},{12,4},... | collective-permute-start | bytes 786440 | tf_op jit(solution)/shard_map/ppermute | solution.py:21
  11.0 14.8 %collective-permute-start = (bf16[6,4,64,128]{3,2,1,0:T(8,128)(2,1)S(1)}, bf16[6,4,64,128]{3,2,1,0:T(8,128)(2,1)S(1)}, u32[]{:S(2)}, u32[]{:S(2)}) collective-permute-start(bf16[6,4,64,128]{3,2,1,0:T(8,128)(2,1)S(1)} %get-tuple-element.25), channel_id=1, source_target_pairs={{0,16},{16,0},{1,17},{17,1},{2,18},{18,2},{3,19},{19,3},{4,20},{20... | collective-permute-start | bytes 1179656 | tf_op jit(solution)/shard_map/ppermute | solution.py:21
  11.1 14.7 %copy-start.1 = (s32[24]{0:T(128)S(1)}, s32[24]{0:T(128)}, u32[]{:S(2)}) copy-start(s32[24]{0:T(128)} %owners.3) | copy-start | bytes 292
  33.7 22.5 %collective-permute-start.4 = (bf16[3,224,128]{2,1,0:T(8,128)(2,1)S(1)}, bf16[3,224,128]{2,1,0:T(8,128)(2,1)S(1)}, u32[]{:S(2)}, u32[]{:S(2)}) collective-permute-start(bf16[3,224,128]{2,1,0:T(8,128)(2,1)S(1)} %get-tuple-element.37), channel_id=1, source_target_pairs={{0,4},{1,5},{2,6},{3,7},{4,0},{5,1},{6,2},{7,3},{8,12},{9,13},{10,... | collective-permute-start | bytes 516104 | tf_op jit(solution)/shard_map/ppermute | solution.py:538
  37.9 23.9 %collective-permute-start.8 = (bf16[3,224,128]{2,1,0:T(8,128)(2,1)S(1)}, bf16[3,224,128]{2,1,0:T(8,128)(2,1)S(1)}, u32[]{:S(2)}, u32[]{:S(2)}) collective-permute-start(bf16[3,224,128]{2,1,0:T(8,128)(2,1)S(1)} %get-tuple-element.42), channel_id=1, source_target_pairs={{0,5},{1,4},{2,7},{3,6},{4,1},{5,0},{6,3},{7,2},{8,13},{9,12},{10,... | collective-permute-start | bytes 516104 | tf_op jit(solution)/shard_map/ppermute | solution.py:538
  40.4 21.5 %collective-permute-start.9 = (bf16[3,224,128]{2,1,0:T(8,128)(2,1)S(1)}, bf16[3,224,128]{2,1,0:T(8,128)(2,1)S(1)}, u32[]{:S(2)}, u32[]{:S(2)}) collective-permute-start(bf16[3,224,128]{2,1,0:T(8,128)(2,1)S(1)} %get-tuple-element.43), channel_id=1, source_target_pairs={{0,6},{1,7},{2,4},{3,5},{4,2},{5,3},{6,0},{7,1},{8,14},{9,15},{10,... | collective-permute-start | bytes 516104 | tf_op jit(solution)/shard_map/ppermute | solution.py:538
  41.4 20.4 %collective-permute-start.10 = (bf16[3,224,128]{2,1,0:T(8,128)(2,1)S(1)}, bf16[3,224,128]{2,1,0:T(8,128)(2,1)S(1)}, u32[]{:S(2)}, u32[]{:S(2)}) collective-permute-start(bf16[3,224,128]{2,1,0:T(8,128)(2,1)S(1)} %get-tuple-element.44), channel_id=1, source_target_pairs={{0,7},{1,6},{2,5},{3,4},{4,3},{5,2},{6,1},{7,0},{8,15},{9,14},{10,... | collective-permute-start | bytes 516104 | tf_op jit(solution)/shard_map/ppermute | solution.py:538
  57.1 8.5 %collective-permute-start.5 = (bf16[3,224,128]{2,1,0:T(8,128)(2,1)S(1)}, bf16[3,224,128]{2,1,0:T(8,128)(2,1)S(1)}, u32[]{:S(2)}, u32[]{:S(2)}) collective-permute-start(bf16[3,224,128]{2,1,0:T(8,128)(2,1)S(1)} %get-tuple-element.39), channel_id=1, source_target_pairs={{0,1},{1,0},{2,3},{3,2},{4,5},{5,4},{6,7},{7,6},{8,9},{9,8},{10,11... | collective-permute-start | bytes 516104 | tf_op jit(solution)/shard_map/ppermute | solution.py:538
  59.7 5.9 %collective-permute-start.6 = (bf16[3,224,128]{2,1,0:T(8,128)(2,1)S(1)}, bf16[3,224,128]{2,1,0:T(8,128)(2,1)S(1)}, u32[]{:S(2)}, u32[]{:S(2)}) collective-permute-start(bf16[3,224,128]{2,1,0:T(8,128)(2,1)S(1)} %get-tuple-element.40), channel_id=1, source_target_pairs={{0,2},{1,3},{2,0},{3,1},{4,6},{5,7},{6,4},{7,5},{8,10},{9,11},{10,... | collective-permute-start | bytes 516104 | tf_op jit(solution)/shard_map/ppermute | solution.py:538
  61.8 6.5 %collective-permute-start.7 = (bf16[3,224,128]{2,1,0:T(8,128)(2,1)S(1)}, bf16[3,224,128]{2,1,0:T(8,128)(2,1)S(1)}, u32[]{:S(2)}, u32[]{:S(2)}) collective-permute-start(bf16[3,224,128]{2,1,0:T(8,128)(2,1)S(1)} %get-tuple-element.41), channel_id=1, source_target_pairs={{0,3},{1,2},{2,1},{3,0},{4,7},{5,6},{6,5},{7,4},{8,11},{9,10},{10,... | collective-permute-start | bytes 516104 | tf_op jit(solution)/shard_map/ppermute | solution.py:538

commit v12 on v11

--- a/solution.py
+++ b/solution.py
@@ -481,17 +481,20 @@
 
 
 def placed_kernel(place_ref, *refs):
-    parts, (out_ref, stage) = refs[:-2], refs[-2:]
+    parts, (out_ref, stage, laid, done) = refs[:-4], refs[-4:]
     capacity, height = parts[0].shape[0], out_ref.shape[1]
-    for number, rows_ref in enumerate(parts):
-        first = jnp.bitwise_xor(place_ref[2], number) * capacity
-        for q in range(capacity):
-            for s in range(SLOTS):
+    copies = [pltpu.make_async_copy(laid.at[s], out_ref.at[s], done.at[s]) for s in range(SLOTS)]
+    for s in range(SLOTS):
+        for number, rows_ref in enumerate(parts):
+            first = jnp.bitwise_xor(place_ref[2], number) * capacity
+            for q in range(capacity):
                 block = rows_ref[q, HALF * s : HALF * (s + 1), :].astype(jnp.float32)
                 stage[s, pl.ds(first + q, HALF, stride=height), :] = block
-    for s in range(SLOTS):
         for k in range(HALF):
-            out_ref[s, :, LANES * k : LANES * (k + 1)] = stage[s, height * k : height * (k + 1), :].astype(jnp.bfloat16)
+            laid[s, :, LANES * k : LANES * (k + 1)] = stage[s, height * k : height * (k + 1), :].astype(jnp.bfloat16)
+        copies[s].start()
+    for copy in copies:
+        copy.wait()
 
 
 def placed(place, parts, block):
@@ -500,9 +503,13 @@
     return pl.pallas_call(
         placed_kernel,
         in_specs=[pl.BlockSpec(memory_space=pltpu.SMEM)] + [whole] * len(parts),
-        out_specs=whole,
+        out_specs=pl.BlockSpec(memory_space=pl.ANY),
         out_shape=jax.ShapeDtypeStruct((SLOTS, places, block), jnp.bfloat16),
-        scratch_shapes=[pltpu.VMEM((SLOTS, places * HALF, LANES), jnp.float32)],
+        scratch_shapes=[
+            pltpu.VMEM((SLOTS, places * HALF, LANES), jnp.float32),
+            pltpu.VMEM((SLOTS, places, block), jnp.bfloat16),
+            pltpu.SemaphoreType.DMA((SLOTS,)),
+        ],
         compiler_params=pltpu.CompilerParams(vmem_limit_bytes=16 * MIB),
         name="placed",
     )(place, *parts)
@@ -538,7 +545,8 @@
             return lax.ppermute(part, "gz", [(i, i ^ k) for i in range(depth)]) if k else part
 
         far = [swapped_with(part, first_part + k) for k, part in enumerate(outgoing)]
-        near = [swapped_with(part, k) for k, part in enumerate(near_parts(row_owner, place, total, far[0], capacity, first_part, depth))]
+        gate = swapped_with(outgoing[-1][:1, :HALF], 1)
+        near = [swapped_with(part, k) for k, part in enumerate(near_parts(row_owner, place, total, gate, capacity, first_part, depth))]
         parts = near + far
         result = placed(place, parts, block)
     else:

time: 71 us -> 70.4 us (level)
    ppermute x7 -> x8, starting transfers between devices: 12.8 us -> 12.3 us  [swapped_with(): lax.ppermute(part, 'gz', [(i, i ^ k) for i in range(depth)])]
    ppermute x7 -> x8, waiting for transfers between devices: 20.9 us -> 21.2 us  [swapped_with(): lax.ppermute(part, 'gz', [(i, i ^ k) for i in range(depth)])]
  transfers between devices with their start and end apart: 11 -> 12, of which waited for: 4 -> 4; matrix products, arithmetic and copies ran while one was open for 0% -> 0% of each run, Pallas kernels for 22% -> 22%
where the time goes in v12:
time: 70.4 us; the launch traced here: 70.3 us
  Pallas kernels  31.6 us (45%)
  waiting for transfers between devices  21.3 us (30%)
  starting transfers between devices  16.9 us (24%)
    ppermute x8, waiting for transfers between devices, swapped_with(): lax.ppermute(part, 'gz', [(i, i ^ k) for i in range(depth)])  21.2 us
    pallas_call x1, Pallas kernels, interior(): pl.pallas_call(interior_kernel, in_specs=[pl.BlockSpec(memory_space=pltpu...  14.7 us
    ppermute x8, starting transfers between devices, swapped_with(): lax.ppermute(part, 'gz', [(i, i ^ k) for i in range(depth)])  12.3 us
    pallas_call x1, Pallas kernels, border(): pl.pallas_call(functools.partial(border_kernel, capacity, paired, first_p...  7.84 us
    pallas_call x1, Pallas kernels, prepare(): pl.pallas_call(prepare_kernel, grid=(size_x,), in_specs=[pl.BlockSpec(mem...  6.21 us
    ppermute x4, starting transfers between devices, swapped_along(): return lax.ppermute(block, axis, pairs + [(i + 1, i) for i, _ in pairs])  4.64 us
    pallas_call x1, Pallas kernels, placed(): pl.pallas_call(placed_kernel, in_specs=[pl.BlockSpec(memory_space=pltpu.S...  1.94 us
  transfers between devices with their start and end apart: 12, of which 4 were waited for; matrix products, arithmetic and copies ran while one was open for 0% of the time, Pallas kernels for 22%

profile of v12, /device:TPU:0, one launch (start us, length us, event | category | flops | bytes accessed | tf_op | source)
XLA Modules:
  0.0 70.3 jit_solution(11020398743996809709)
XLA Ops:
  0.0 0.1 pad_add_fusion.place_ref
  0.1 0.0 slice-start
  0.1 0.0 copy-start.3
  0.1 0.0 copy-start.2
  0.1 0.0 slice-start.1
  0.1 0.0 copy-start
  0.1 6.2 %prepare.1 = (bf16[24,4,64,128]{3,2,1,0:T(8,128)(2,1)S(1)}, bf16[24,2,128,128]{3,2,1,0:T(8,128)(2,1)S(1)}, bf16[6,4,64,128]{3,2,1,0:T(8,128)(2,1)S(1)}, bf16[4,4...) custom-call(s32[3]{0:T(128)S(1)} %pad_add_fusion.place_ref, ...), custom_call_target="tpu_custom_call" | custom-call | tf_op jit(solution)/shard_map/prepare/pallas_call | solution.py:179
  6.3 3.0 %collective-permute-start.2 = (bf16[12,64,128]{2,1,0:T(8,128)(2,1)S(1)}, bf16[12,64,128]{2,1,0:T(8,128)(2,1)S(1)}, u32[]{:S(2)}, u32[]{:S(2)}) collective-permute-start(bf16[12,64,128]{2,1,0:T(8,128)(2,1)S(1)} %get-tuple-element.27), channel_id=1, source_target_pairs={{0,1},{2,3},{4,5},{6,7},{1,0},{3,2},{5,4},{7,6},{8,9},{10,11},{12,... | collective-permute-start | bytes 589832 | tf_op jit(solution)/shard_map/ppermute | solution.py:21
  9.4 0.7 collective-permute-start.3
  10.0 0.9 %collective-permute-start.1 = (bf16[4,4,64,128]{3,2,1,0:T(8,128)(2,1)S(1)}, bf16[4,4,64,128]{3,2,1,0:T(8,128)(2,1)S(1)}, u32[]{:S(2)}, u32[]{:S(2)}) collective-permute-start(bf16[4,4,64,128]{3,2,1,0:T(8,128)(2,1)S(1)} %get-tuple-element.26), channel_id=1, source_target_pairs={{0,8},{8,0},{1,9},{9,1},{2,10},{10,2},{3,11},{11,3},{4,12},{12,4},... | collective-permute-start | bytes 786440 | tf_op jit(solution)/shard_map/ppermute | solution.py:21
  11.0 0.0 collective-permute-start
  11.0 0.0 copy-done.3
  11.0 0.0 copy-done.2
  11.0 0.0 slice-done
  11.0 0.0 slice-done.1
  11.0 0.0 copy-done
  11.1 0.0 copy-start.1
  11.1 14.7 %interior.1.start_ref = f32[168,32,128]{2,1,0:T(8,128)S(1)} custom-call(s32[7,4,6,8]{3,2,1,0:T(8,128)S(1)} %copy_add_fusion.keys, bf16[24,8,4096]{2,1,0:T(8,128)(2,1)S(1)} %bitcast.19, bf16[3,24,8,4096]{3,2,1,0:T(8,128)(2,1)S(1)} %bitcast.16, bf16[24,4,64,128]{3,2,1,0:T(8,128)(2,1)S(1)} %get-tuple-element.33.natural_ref.natural_x, ...), custom_call_target="tpu_custom_call" | custom-call | flops 704643072 | bytes 9437184 | tf_op jit(solution)/shard_map/interior/pallas_call | solution.py:309
  25.8 0.0 collective-permute-done.2.near_z
  25.8 0.0 collective-permute-done.3.far_z
  25.8 0.0 collective-permute-done.1.got_y
  25.8 0.0 collective-permute-done.got_x
  25.8 0.0 copy-done.1
  25.8 7.8 %border.1 = (bf16[3,224,128]{2,1,0:T(8,128)(2,1)S(1)}, bf16[3,224,128]{2,1,0:T(8,128)(2,1)S(1)}, bf16[3,224,128]{2,1,0:T(8,128)(2,1)S(1)}, bf16[3,224,128]{2,1,0:T(8,128)(2,1)S(1)}, f32[168,32,128]{2,1,0:T(8,128)S(1)}) custom-call(s32[24]{0:T(128)S(1)} %copy-done.1, s32[3]{0:T(128)S(1)} %pad_add_fusion.place_ref, ...), custom_call_target="tpu_custom_call", output_to_operand_aliasing={{4}: (16, {})} | custom-call | tf_op jit(solution)/shard_map/border/pallas_call | solution.py:438
  33.7 4.3 %collective-permute-start.8 = (bf16[3,224,128]{2,1,0:T(8,128)(2,1)S(1)}, bf16[3,224,128]{2,1,0:T(8,128)(2,1)S(1)}, u32[]{:S(2)}, u32[]{:S(2)}) collective-permute-start(bf16[3,224,128]{2,1,0:T(8,128)(2,1)S(1)} %get-tuple-element.42), channel_id=1, source_target_pairs={{0,4},{1,5},{2,6},{3,7},{4,0},{5,1},{6,2},{7,3},{8,12},{9,13},{10,... | collective-permute-start | bytes 516104 | tf_op jit(solution)/shard_map/ppermute | solution.py:545
  37.9 2.4 %collective-permute-start.9 = (bf16[3,224,128]{2,1,0:T(8,128)(2,1)S(1)}, bf16[3,224,128]{2,1,0:T(8,128)(2,1)S(1)}, u32[]{:S(2)}, u32[]{:S(2)}) collective-permute-start(bf16[3,224,128]{2,1,0:T(8,128)(2,1)S(1)} %get-tuple-element.43), channel_id=1, source_target_pairs={{0,5},{1,4},{2,7},{3,6},{4,1},{5,0},{6,3},{7,2},{8,13},{9,12},{10,... | collective-permute-start | bytes 516104 | tf_op jit(solution)/shard_map/ppermute | solution.py:545
  40.4 0.2 collective-permute-start.4
  40.6 2.3 %collective-permute-start.11 = (bf16[3,224,128]{2,1,0:T(8,128)(2,1)S(1)}, bf16[3,224,128]{2,1,0:T(8,128)(2,1)S(1)}, u32[]{:S(2)}, u32[]{:S(2)}) collective-permute-start(bf16[3,224,128]{2,1,0:T(8,128)(2,1)S(1)} %get-tuple-element.37), channel_id=1, source_target_pairs={{0,7},{1,6},{2,5},{3,4},{4,3},{5,2},{6,1},{7,0},{8,15},{9,14},{10,... | collective-permute-start | bytes 516104 | tf_op jit(solution)/shard_map/ppermute | solution.py:545
  42.9 2.7 %collective-permute-start.10 = (bf16[3,224,128]{2,1,0:T(8,128)(2,1)S(1)}, bf16[3,224,128]{2,1,0:T(8,128)(2,1)S(1)}, u32[]{:S(2)}, u32[]{:S(2)}) collective-permute-start(bf16[3,224,128]{2,1,0:T(8,128)(2,1)S(1)} %get-tuple-element.44), channel_id=1, source_target_pairs={{0,6},{1,7},{2,4},{3,5},{4,2},{5,3},{6,0},{7,1},{8,14},{9,15},{10,... | collective-permute-start | bytes 516104 | tf_op jit(solution)/shard_map/ppermute | solution.py:545
  45.7 0.0 collective-permute-done.4.arrived
  45.7 0.9 %near.1 = (bf16[3,224,128]{2,1,0:T(8,128)(2,1)S(1)}, bf16[3,224,128]{2,1,0:T(8,128)(2,1)S(1)}, bf16[3,224,128]{2,1,0:T(8,128)(2,1)S(1)}, bf16[3,224,128]{2,1,0:T(8,128)(2,1)S(1)}) custom-call(s32[24]{0:T(128)S(1)} %copy-done.1, s32[3]{0:T(128)S(1)} %pad_add_fusion.place_ref, f32[168,32,128]{2,1,0:T(8,128)S(1)} %get-tuple-element.36.total, ...), custom_call_target="tpu_custom_call" | custom-call | tf_op jit(solution)/shard_map/near/pallas_call | solution.py:419
  46.6 0.3 collective-permute-start.5
  46.9 9.2 %collective-permute-done.8.refs_4_ = bf16[3,224,128]{2,1,0:T(8,128)(2,1)S(1)} collective-permute-done((bf16[3,224,128]{2,1,0:T(8,128)(2,1)S(1)}, bf16[3,224,128]{2,1,0:T(8,128)(2,1)S(1)}, u32[]{:S(2)}, u32[]{:S(2)}) %collective-permute-start.8) | collective-permute-done | bytes 172064 | tf_op jit(solution)/shard_map/ppermute | solution.py:545
  56.1 0.0 collective-permute-start.6
  56.1 5.7 %collective-permute-done.9.refs_5_ = bf16[3,224,128]{2,1,0:T(8,128)(2,1)S(1)} collective-permute-done((bf16[3,224,128]{2,1,0:T(8,128)(2,1)S(1)}, bf16[3,224,128]{2,1,0:T(8,128)(2,1)S(1)}, u32[]{:S(2)}, u32[]{:S(2)}) %collective-permute-start.9) | collective-permute-done | bytes 172064 | tf_op jit(solution)/shard_map/ppermute | solution.py:545
  61.8 0.0 collective-permute-start.7
  61.9 0.0 collective-permute-done.10.refs_6_
  61.9 0.0 collective-permute-done.11.refs_7_
  61.9 0.0 collective-permute-done.5.refs_1_
  61.9 1.6 %collective-permute-done.6.refs_2_ = bf16[3,224,128]{2,1,0:T(8,128)(2,1)S(1)} collective-permute-done((bf16[3,224,128]{2,1,0:T(8,128)(2,1)S(1)}, bf16[3,224,128]{2,1,0:T(8,128)(2,1)S(1)}, u32[]{:S(2)}, u32[]{:S(2)}) %collective-permute-start.6) | collective-permute-done | bytes 172064 | tf_op jit(solution)/shard_map/ppermute | solution.py:545
  63.5 4.6 %collective-permute-done.7.refs_3_ = bf16[3,224,128]{2,1,0:T(8,128)(2,1)S(1)} collective-permute-done((bf16[3,224,128]{2,1,0:T(8,128)(2,1)S(1)}, bf16[3,224,128]{2,1,0:T(8,128)(2,1)S(1)}, u32[]{:S(2)}, u32[]{:S(2)}) %collective-permute-start.7) | collective-permute-done | bytes 172064 | tf_op jit(solution)/shard_map/ppermute | solution.py:545
  68.2 1.9 %placed.1 = bf16[7,24,4096]{2,1,0:T(8,128)(2,1)} custom-call(s32[3]{0:T(128)S(1)} %pad_add_fusion.place_ref, bf16[3,224,128]{2,1,0:T(8,128)(2,1)S(1)} %get-tuple-element.38.refs_0_, bf16[3,224,128]{2,1,0:T(8,128)(2,1)S(1)} %collective-permute-done.5.refs_1_, bf16[3,224,128]{2,1,0:T(8,128)(2,1)S(1)} %collective-permute-done.6.refs_2_, ...), custom_call_target="tpu_custom_call" | custom-call | tf_op jit(solution)/shard_map/placed/pallas_call | solution.py:503
  (5 shorter events, 0.0 us)
Async XLA Ops:
  0.1 11.0 %slice-start = ((s8[4718592]{0:T(1024)(128)(4,1)}), s8[4194304]{0:T(1024)(128)(4,1)S(1)}, s32[]{:S(2)}) async-start(s8[4718592]{0:T(1024)(128)(4,1)} %bitcast.14), calls=%async_computation | async-start | bytes 8388608
  0.1 10.9 %copy-start.3 = (s32[4,6,8]{2,0,1:T(4,128)S(1)}, s32[4,6,8]{2,0,1:T(4,128)}, u32[]{:S(2)}) copy-start(s32[4,6,8]{2,0,1:T(4,128)} %param.9) | copy-start | bytes 2308
  0.1 10.9 %copy-start.2 = (s32[7,4,6,8]{3,1,2,0:T(4,128)S(1)}, s32[7,4,6,8]{3,1,2,0:T(4,128)}, u32[]{:S(2)}) copy-start(s32[7,4,6,8]{3,1,2,0:T(4,128)} %param.10) | copy-start | bytes 16132
  0.1 11.0 %slice-start.1 = ((s8[4718592]{0:T(1024)(128)(4,1)}), s8[524288]{0:T(1024)(128)(4,1)S(1)}, s32[]{:S(2)}) async-start(s8[4718592]{0:T(1024)(128)(4,1)} %bitcast.14), calls=%async_computation.1 | async-start | bytes 1048576
  0.1 11.0 %copy-start = (bf16[4,6,8,4096]{3,2,1,0:T(8,128)(2,1)S(1)}, bf16[4,6,8,4096]{3,2,1,0:T(8,128)(2,1)}, u32[]{:S(2)}) copy-start(bf16[4,6,8,4096]{3,2,1,0:T(8,128)(2,1)} %param.6) | copy-start | bytes 4718596
  6.3 19.4 %collective-permute-start.2 = (bf16[12,64,128]{2,1,0:T(8,128)(2,1)S(1)}, bf16[12,64,128]{2,1,0:T(8,128)(2,1)S(1)}, u32[]{:S(2)}, u32[]{:S(2)}) collective-permute-start(bf16[12,64,128]{2,1,0:T(8,128)(2,1)S(1)} %get-tuple-element.27), channel_id=1, source_target_pairs={{0,1},{2,3},{4,5},{6,7},{1,0},{3,2},{5,4},{7,6},{8,9},{10,11},{12,... | collective-permute-start | bytes 589832 | tf_op jit(solution)/shard_map/ppermute | solution.py:21
  9.4 16.4 %collective-permute-start.3 = (bf16[12,64,128]{2,1,0:T(8,128)(2,1)S(1)}, bf16[12,64,128]{2,1,0:T(8,128)(2,1)S(1)}, u32[]{:S(2)}, u32[]{:S(2)}) collective-permute-start(bf16[12,64,128]{2,1,0:T(8,128)(2,1)S(1)} %get-tuple-element.28), channel_id=1, source_target_pairs={{1,2},{3,4},{5,6},{2,1},{4,3},{6,5},{9,10},{11,12},{13,14},{10,9},... | collective-permute-start | bytes 589832 | tf_op jit(solution)/shard_map/ppermute | solution.py:21
  10.0 15.8 %collective-permute-start.1 = (bf16[4,4,64,128]{3,2,1,0:T(8,128)(2,1)S(1)}, bf16[4,4,64,128]{3,2,1,0:T(8,128)(2,1)S(1)}, u32[]{:S(2)}, u32[]{:S(2)}) collective-permute-start(bf16[4,4,64,128]{3,2,1,0:T(8,128)(2,1)S(1)} %get-tuple-element.26), channel_id=1, source_target_pairs={{0,8},{8,0},{1,9},{9,1},{2,10},{10,2},{3,11},{11,3},{4,12},{12,4},... | collective-permute-start | bytes 786440 | tf_op jit(solution)/shard_map/ppermute | solution.py:21
  11.0 14.8 %collective-permute-start = (bf16[6,4,64,128]{3,2,1,0:T(8,128)(2,1)S(1)}, bf16[6,4,64,128]{3,2,1,0:T(8,128)(2,1)S(1)}, u32[]{:S(2)}, u32[]{:S(2)}) collective-permute-start(bf16[6,4,64,128]{3,2,1,0:T(8,128)(2,1)S(1)} %get-tuple-element.25), channel_id=1, source_target_pairs={{0,16},{16,0},{1,17},{17,1},{2,18},{18,2},{3,19},{19,3},{4,20},{20... | collective-permute-start | bytes 1179656 | tf_op jit(solution)/shard_map/ppermute | solution.py:21
  11.1 14.7 %copy-start.1 = (s32[24]{0:T(128)S(1)}, s32[24]{0:T(128)}, u32[]{:S(2)}) copy-start(s32[24]{0:T(128)} %owners.3) | copy-start | bytes 292
  33.7 22.5 %collective-permute-start.8 = (bf16[3,224,128]{2,1,0:T(8,128)(2,1)S(1)}, bf16[3,224,128]{2,1,0:T(8,128)(2,1)S(1)}, u32[]{:S(2)}, u32[]{:S(2)}) collective-permute-start(bf16[3,224,128]{2,1,0:T(8,128)(2,1)S(1)} %get-tuple-element.42), channel_id=1, source_target_pairs={{0,4},{1,5},{2,6},{3,7},{4,0},{5,1},{6,2},{7,3},{8,12},{9,13},{10,... | collective-permute-start | bytes 516104 | tf_op jit(solution)/shard_map/ppermute | solution.py:545
  37.9 23.9 %collective-permute-start.9 = (bf16[3,224,128]{2,1,0:T(8,128)(2,1)S(1)}, bf16[3,224,128]{2,1,0:T(8,128)(2,1)S(1)}, u32[]{:S(2)}, u32[]{:S(2)}) collective-permute-start(bf16[3,224,128]{2,1,0:T(8,128)(2,1)S(1)} %get-tuple-element.43), channel_id=1, source_target_pairs={{0,5},{1,4},{2,7},{3,6},{4,1},{5,0},{6,3},{7,2},{8,13},{9,12},{10,... | collective-permute-start | bytes 516104 | tf_op jit(solution)/shard_map/ppermute | solution.py:545
  40.4 5.3 %collective-permute-start.4 = (bf16[1,32,128]{2,1,0:T(8,128)(2,1)S(1)}, bf16[1,32,128]{2,1,0:T(8,128)(2,1)S(1)}, u32[]{:S(2)}, u32[]{:S(2)}) collective-permute-start(bf16[1,32,128]{2,1,0:T(8,128)(2,1)S(1)} %slice.3), channel_id=1, source_target_pairs={{0,1},{1,0},{2,3},{3,2},{4,5},{5,4},{6,7},{7,6},{8,9},{9,8},{10,11... | collective-permute-start | bytes 24584 | tf_op jit(solution)/shard_map/ppermute | solution.py:545
  40.6 21.3 %collective-permute-start.11 = (bf16[3,224,128]{2,1,0:T(8,128)(2,1)S(1)}, bf16[3,224,128]{2,1,0:T(8,128)(2,1)S(1)}, u32[]{:S(2)}, u32[]{:S(2)}) collective-permute-start(bf16[3,224,128]{2,1,0:T(8,128)(2,1)S(1)} %get-tuple-element.37), channel_id=1, source_target_pairs={{0,7},{1,6},{2,5},{3,4},{4,3},{5,2},{6,1},{7,0},{8,15},{9,14},{10,... | collective-permute-start | bytes 516104 | tf_op jit(solution)/shard_map/ppermute | solution.py:545
  42.9 18.9 %collective-permute-start.10 = (bf16[3,224,128]{2,1,0:T(8,128)(2,1)S(1)}, bf16[3,224,128]{2,1,0:T(8,128)(2,1)S(1)}, u32[]{:S(2)}, u32[]{:S(2)}) collective-permute-start(bf16[3,224,128]{2,1,0:T(8,128)(2,1)S(1)} %get-tuple-element.44), channel_id=1, source_target_pairs={{0,6},{1,7},{2,4},{3,5},{4,2},{5,3},{6,0},{7,1},{8,14},{9,15},{10,... | collective-permute-start | bytes 516104 | tf_op jit(solution)/shard_map/ppermute | solution.py:545
  46.6 15.3 %collective-permute-start.5 = (bf16[3,224,128]{2,1,0:T(8,128)(2,1)S(1)}, bf16[3,224,128]{2,1,0:T(8,128)(2,1)S(1)}, u32[]{:S(2)}, u32[]{:S(2)}) collective-permute-start(bf16[3,224,128]{2,1,0:T(8,128)(2,1)S(1)} %get-tuple-element.39), channel_id=1, source_target_pairs={{0,1},{1,0},{2,3},{3,2},{4,5},{5,4},{6,7},{7,6},{8,9},{9,8},{10,11... | collective-permute-start | bytes 516104 | tf_op jit(solution)/shard_map/ppermute | solution.py:545
  56.1 7.4 %collective-permute-start.6 = (bf16[3,224,128]{2,1,0:T(8,128)(2,1)S(1)}, bf16[3,224,128]{2,1,0:T(8,128)(2,1)S(1)}, u32[]{:S(2)}, u32[]{:S(2)}) collective-permute-start(bf16[3,224,128]{2,1,0:T(8,128)(2,1)S(1)} %get-tuple-element.40), channel_id=1, source_target_pairs={{0,2},{1,3},{2,0},{3,1},{4,6},{5,7},{6,4},{7,5},{8,10},{9,11},{10,... | collective-permute-start | bytes 516104 | tf_op jit(solution)/shard_map/ppermute | solution.py:545
  61.8 6.3 %collective-permute-start.7 = (bf16[3,224,128]{2,1,0:T(8,128)(2,1)S(1)}, bf16[3,224,128]{2,1,0:T(8,128)(2,1)S(1)}, u32[]{:S(2)}, u32[]{:S(2)}) collective-permute-start(bf16[3,224,128]{2,1,0:T(8,128)(2,1)S(1)} %get-tuple-element.41), channel_id=1, source_target_pairs={{0,3},{1,2},{2,1},{3,0},{4,7},{5,6},{6,5},{7,4},{8,11},{9,10},{10,... | collective-permute-start | bytes 516104 | tf_op jit(solution)/shard_map/ppermute | solution.py:545

commit v13 on v12

--- a/solution.py
+++ b/solution.py
@@ -384,11 +384,15 @@
                 for updates in batches:
                     add_all(updates)
 
-    emit(capacity, paired, first_part, owners, place_ref, total, out_refs, filled, listed)
-
-
-def emit(capacity, paired, first_part, owners, place_ref, total, out_refs, filled, listed):
-    rows, devices = total.shape[0] // SLOTS, filled.shape[0]
+    list_rows(capacity, paired, owners, place_ref, rows // SLOTS, filled, listed)
+    full = capacity * filled.shape[0] * SLOTS == rows
+    for part, out_ref in enumerate(out_refs):
+        for q in range(capacity):
+            write_row(total, listed[(first_part + part) * capacity + q], full, out_ref, q)
+
+
+def list_rows(capacity, paired, owners, place_ref, rows, filled, listed):
+    devices = filled.shape[0]
     for spot in range(capacity * devices):
         listed[spot] = -1
     for owner in range(devices):
@@ -397,20 +401,25 @@
         owner = owners[r]
         listed[jnp.bitwise_xor(owner, place_ref[2] if paired else 0) * capacity + filled[owner]] = r
         filled[owner] = filled[owner] + 1
-    for part, out_ref in enumerate(out_refs):
+
+
+def write_row(total, row, full, out_ref, spot):
+    for s in range(SLOTS):
+        key = jnp.maximum(row, 0) * SLOTS + s
+        even, odd = [total[key, pl.ds(first, HALF // 2, stride=2), :] for first in (0, 1)]
+        block = straightened(even, odd)
+        if not full:
+            block = jnp.where(row >= 0, block, jnp.zeros_like(block))
+        out_ref[spot, HALF * s : HALF * (s + 1), :] = block.astype(jnp.bfloat16)
+
+
+def near_kernel(capacity, owners, place_ref, total, arrived, out_ref, filled, listed):
+    count = out_ref.shape[0] // capacity
+    list_rows(capacity, True, owners, place_ref, total.shape[0] // SLOTS, filled, listed)
+    for member in range(count):
+        partner = jnp.bitwise_xor(member, place_ref[2] % count)
         for q in range(capacity):
-            row = listed[(first_part + part) * capacity + q]
-            for s in range(SLOTS):
-                key = jnp.maximum(row, 0) * SLOTS + s
-                even, odd = [total[key, pl.ds(first, HALF // 2, stride=2), :] for first in (0, 1)]
-                block = straightened(even, odd)
-                if capacity * devices != rows:
-                    block = jnp.where(row >= 0, block, jnp.zeros_like(block))
-                out_ref[q, HALF * s : HALF * (s + 1), :] = block.astype(jnp.bfloat16)
-
-
-def near_kernel(capacity, owners, place_ref, total, arrived, *refs):
-    emit(capacity, True, 0, owners, place_ref, total, refs[:-2], *refs[-2:])
+            write_row(total, listed[partner * capacity + q], True, out_ref, member * capacity + q)
 
 
 def near_parts(owners, place, total, arrived, capacity, count, devices):
@@ -419,8 +428,8 @@
     return pl.pallas_call(
         functools.partial(near_kernel, capacity),
         in_specs=[smem, smem, whole, pl.BlockSpec(memory_space=pl.ANY)],
-        out_specs=[whole] * count,
-        out_shape=[jax.ShapeDtypeStruct((capacity, SLOTS * HALF, LANES), jnp.bfloat16)] * count,
+        out_specs=whole,
+        out_shape=jax.ShapeDtypeStruct((count * capacity, SLOTS * HALF, LANES), jnp.bfloat16),
         scratch_shapes=[pltpu.SMEM((devices,), jnp.int32), pltpu.SMEM((capacity * devices,), jnp.int32)],
         compiler_params=pltpu.CompilerParams(vmem_limit_bytes=10 * MIB),
         name="near",
@@ -480,16 +489,18 @@
     )(source, rows)
 
 
-def placed_kernel(place_ref, *refs):
+def placed_kernel(capacity, place_ref, near_ref, *refs):
     parts, (out_ref, stage, laid, done) = refs[:-4], refs[-4:]
-    capacity, height = parts[0].shape[0], out_ref.shape[1]
+    height, count = out_ref.shape[1], near_ref.shape[0]
     copies = [pltpu.make_async_copy(laid.at[s], out_ref.at[s], done.at[s]) for s in range(SLOTS)]
+    rows = [(near_ref, row, place_ref[2] // len(parts) * count + row) for row in range(count)]
+    for number, part in enumerate(parts):
+        first = jnp.bitwise_xor(place_ref[2], len(parts) + number) * capacity
+        rows += [(part, q, first + q) for q in range(capacity)]
     for s in range(SLOTS):
-        for number, rows_ref in enumerate(parts):
-            first = jnp.bitwise_xor(place_ref[2], number) * capacity
-            for q in range(capacity):
-                block = rows_ref[q, HALF * s : HALF * (s + 1), :].astype(jnp.float32)
-                stage[s, pl.ds(first + q, HALF, stride=height), :] = block
+        for source, row, spot in rows:
+            block = source[row, HALF * s : HALF * (s + 1), :].astype(jnp.float32)
+            stage[s, pl.ds(spot, HALF, stride=height), :] = block
         for k in range(HALF):
             laid[s, :, LANES * k : LANES * (k + 1)] = stage[s, height * k : height * (k + 1), :].astype(jnp.bfloat16)
         copies[s].start()
@@ -497,12 +508,13 @@
         copy.wait()
 
 
-def placed(place, parts, block):
-    places = parts[0].shape[0] * len(parts)
+def placed(place, near, parts, block):
+    capacity = parts[0].shape[0]
+    places = near.shape[0] + capacity * len(parts)
     whole = pl.BlockSpec(memory_space=pltpu.VMEM)
     return pl.pallas_call(
-        placed_kernel,
-        in_specs=[pl.BlockSpec(memory_space=pltpu.SMEM)] + [whole] * len(parts),
+        functools.partial(placed_kernel, capacity),
+        in_specs=[pl.BlockSpec(memory_space=pltpu.SMEM)] + [whole] * (1 + len(parts)),
         out_specs=pl.BlockSpec(memory_space=pl.ANY),
         out_shape=jax.ShapeDtypeStruct((SLOTS, places, block), jnp.bfloat16),
         scratch_shapes=[
@@ -512,7 +524,7 @@
         ],
         compiler_params=pltpu.CompilerParams(vmem_limit_bytes=16 * MIB),
         name="placed",
-    )(place, *parts)
+    )(place, near, *parts)
 
 
 def shards(a_diag, a_face, prolong, aggregate, pair_slot, row_owner):
@@ -542,13 +554,14 @@
         (first_z, last_z), total, capacity, depth, paired, first_part, sizes)
     if paired:
         def swapped_with(part, k):
-            return lax.ppermute(part, "gz", [(i, i ^ k) for i in range(depth)]) if k else part
+            return lax.ppermute(part, "gz", [(i, i ^ k) for i in range(depth)])
 
         far = [swapped_with(part, first_part + k) for k, part in enumerate(outgoing)]
         gate = swapped_with(outgoing[-1][:1, :HALF], 1)
-        near = [swapped_with(part, k) for k, part in enumerate(near_parts(row_owner, place, total, gate, capacity, first_part, depth))]
-        parts = near + far
-        result = placed(place, parts, block)
+        near = near_parts(row_owner, place, total, gate, capacity, first_part, depth)
+        sides = [list(range(first, first + first_part)) for first in (0, first_part)]
+        near = lax.all_to_all(near, "gz", 0, 0, tiled=True, axis_index_groups=sides)
+        result = placed(place, near, far, block)
     else:
         arrived = lax.all_to_all(jnp.concatenate(outgoing, axis=0), "gz", 0, 0, tiled=True)
         slots = jnp.arange(holding, dtype=jnp.int32)

time: 70.4 us -> 76.7 us (1.089)
  the two profiles are of different devices: /device:TPU:0 before, /device:TPU:16 now
where the time goes in v13:
time: 76.7 us; the launch traced here: 76.5 us
  Pallas kernels  32.4 us (42%)
  waiting for transfers between devices  26.7 us (35%)
  starting transfers between devices  16.9 us (22%)
    ppermute x5, waiting for transfers between devices, swapped_with(): return lax.ppermute(part, 'gz', [(i, i ^ k) for i in range(depth)])  26.6 us
    pallas_call x1, Pallas kernels, interior(): pl.pallas_call(interior_kernel, in_specs=[pl.BlockSpec(memory_space=pltpu...  14.7 us
    ppermute x5, starting transfers between devices, swapped_with(): return lax.ppermute(part, 'gz', [(i, i ^ k) for i in range(depth)])  8.62 us
    pallas_call x1, Pallas kernels, border(): pl.pallas_call(functools.partial(border_kernel, capacity, paired, first_p...  7.84 us
    pallas_call x1, Pallas kernels, prepare(): pl.pallas_call(prepare_kernel, grid=(size_x,), in_specs=[pl.BlockSpec(mem...  6.21 us
    ppermute x4, starting transfers between devices, swapped_along(): return lax.ppermute(block, axis, pairs + [(i + 1, i) for i, _ in pairs])  4.82 us
    all_to_all x1, starting transfers between devices, shards(): near = lax.all_to_all(near, 'gz', 0, 0, tiled=True, axis_index_groups=sides)  3.49 us
    pallas_call x1, Pallas kernels, placed(): pl.pallas_call(functools.partial(placed_kernel, capacity), in_specs=[pl.B...  1.93 us
  transfers between devices with their start and end apart: 10, of which 5 were waited for; matrix products, arithmetic and copies ran while one was open for 0% of the time, Pallas kernels for 19%

profile of v13, /device:TPU:16, one launch (start us, length us, event | category | flops | bytes accessed | tf_op | source)
XLA Modules:
  0.0 76.5 jit_solution(18187764141791266872)
XLA Ops:
  0.0 0.1 pad_add_fusion.place_ref
  0.1 0.0 slice-start
  0.1 0.0 copy-start.3
  0.1 0.0 copy-start.2
  0.1 0.0 slice-start.1
  0.1 0.0 copy-start
  0.1 6.2 %prepare.1 = (bf16[24,4,64,128]{3,2,1,0:T(8,128)(2,1)S(1)}, bf16[24,2,128,128]{3,2,1,0:T(8,128)(2,1)S(1)}, bf16[6,4,64,128]{3,2,1,0:T(8,128)(2,1)S(1)}, bf16[4,4...) custom-call(s32[3]{0:T(128)S(1)} %pad_add_fusion.place_ref, ...), custom_call_target="tpu_custom_call" | custom-call | tf_op jit(solution)/shard_map/prepare/pallas_call | solution.py:179
  6.3 1.6 %collective-permute-start.2 = (bf16[12,64,128]{2,1,0:T(8,128)(2,1)S(1)}, bf16[12,64,128]{2,1,0:T(8,128)(2,1)S(1)}, u32[]{:S(2)}, u32[]{:S(2)}) collective-permute-start(bf16[12,64,128]{2,1,0:T(8,128)(2,1)S(1)} %get-tuple-element.23), channel_id=1, source_target_pairs={{0,1},{2,3},{4,5},{6,7},{1,0},{3,2},{5,4},{7,6},{8,9},{10,11},{12,... | collective-permute-start | bytes 589832 | tf_op jit(solution)/shard_map/ppermute | solution.py:21
  7.9 2.3 %collective-permute-start.3 = (bf16[12,64,128]{2,1,0:T(8,128)(2,1)S(1)}, bf16[12,64,128]{2,1,0:T(8,128)(2,1)S(1)}, u32[]{:S(2)}, u32[]{:S(2)}) collective-permute-start(bf16[12,64,128]{2,1,0:T(8,128)(2,1)S(1)} %get-tuple-element.24), channel_id=1, source_target_pairs={{1,2},{3,4},{5,6},{2,1},{4,3},{6,5},{9,10},{11,12},{13,14},{10,9},... | collective-permute-start | bytes 589832 | tf_op jit(solution)/shard_map/ppermute | solution.py:21
  10.2 0.9 %collective-permute-start.1 = (bf16[4,4,64,128]{3,2,1,0:T(8,128)(2,1)S(1)}, bf16[4,4,64,128]{3,2,1,0:T(8,128)(2,1)S(1)}, u32[]{:S(2)}, u32[]{:S(2)}) collective-permute-start(bf16[4,4,64,128]{3,2,1,0:T(8,128)(2,1)S(1)} %get-tuple-element.22), channel_id=1, source_target_pairs={{0,8},{8,0},{1,9},{9,1},{2,10},{10,2},{3,11},{11,3},{4,12},{12,4},... | collective-permute-start | bytes 786440 | tf_op jit(solution)/shard_map/ppermute | solution.py:21
  11.1 0.0 collective-permute-start
  11.2 0.0 copy-done.3
  11.2 0.0 copy-done.2
  11.2 0.0 slice-done
  11.2 0.0 slice-done.1
  11.2 0.0 copy-done
  11.2 0.0 copy-start.1
  11.3 14.7 %interior.1.start_ref = f32[168,32,128]{2,1,0:T(8,128)S(1)} custom-call(s32[7,4,6,8]{3,2,1,0:T(8,128)S(1)} %copy_add_fusion.keys, bf16[24,8,4096]{2,1,0:T(8,128)(2,1)S(1)} %bitcast.19, bf16[3,24,8,4096]{3,2,1,0:T(8,128)(2,1)S(1)} %bitcast.16, bf16[24,4,64,128]{3,2,1,0:T(8,128)(2,1)S(1)} %get-tuple-element.29.natural_ref.natural_x, ...), custom_call_target="tpu_custom_call" | custom-call | flops 704643072 | bytes 9437184 | tf_op jit(solution)/shard_map/interior/pallas_call | solution.py:309
  25.9 0.0 collective-permute-done.2.near_z
  25.9 0.0 collective-permute-done.3.far_z
  26.0 0.0 collective-permute-done.1.got_y
  26.0 0.0 collective-permute-done.got_x
  26.0 0.0 copy-done.1
  26.0 7.8 %border.1 = (bf16[3,224,128]{2,1,0:T(8,128)(2,1)S(1)}, bf16[3,224,128]{2,1,0:T(8,128)(2,1)S(1)}, bf16[3,224,128]{2,1,0:T(8,128)(2,1)S(1)}, bf16[3,224,128]{2,1,0:T(8,128)(2,1)S(1)}, f32[168,32,128]{2,1,0:T(8,128)S(1)}) custom-call(s32[24]{0:T(128)S(1)} %copy-done.1, s32[3]{0:T(128)S(1)} %pad_add_fusion.place_ref, ...), custom_call_target="tpu_custom_call", output_to_operand_aliasing={{4}: (16, {})} | custom-call | tf_op jit(solution)/shard_map/border/pallas_call | solution.py:447
  33.8 2.7 %collective-permute-start.4 = (bf16[1,32,128]{2,1,0:T(8,128)(2,1)S(1)}, bf16[1,32,128]{2,1,0:T(8,128)(2,1)S(1)}, u32[]{:S(2)}, u32[]{:S(2)}) collective-permute-start(bf16[1,32,128]{2,1,0:T(8,128)(2,1)S(1)} %slice.3), channel_id=1, source_target_pairs={{0,1},{1,0},{2,3},{3,2},{4,5},{5,4},{6,7},{7,6},{8,9},{9,8},{10,11... | collective-permute-start | bytes 24584 | tf_op jit(solution)/shard_map/ppermute | solution.py:557
  36.6 1.6 %collective-permute-done.4.arrived = bf16[1,32,128]{2,1,0:T(8,128)(2,1)S(1)} collective-permute-done((bf16[1,32,128]{2,1,0:T(8,128)(2,1)S(1)}, bf16[1,32,128]{2,1,0:T(8,128)(2,1)S(1)}, u32[]{:S(2)}, u32[]{:S(2)}) %collective-permute-start.4) | collective-permute-done | bytes 8224 | tf_op jit(solution)/shard_map/ppermute | solution.py:557
  38.2 1.8 %near.1 = bf16[12,224,128]{2,1,0:T(8,128)(2,1)} custom-call(s32[24]{0:T(128)S(1)} %copy-done.1, s32[3]{0:T(128)S(1)} %pad_add_fusion.place_ref, f32[168,32,128]{2,1,0:T(8,128)S(1)} %get-tuple-element.32.total, bf16[1,32,128]{2,1,0:T(8,128)(2,1)S(1)} %collective-permute-done.4.arrived), custom_call_target="tpu_custom_call" | custom-call | tf_op jit(solution)/shard_map/near/pallas_call | solution.py:428
  40.0 3.5 %all-to-all-start = ((bf16[12,224,128]{2,1,0:T(8,128)(2,1)}), bf16[12,224,128]{2,1,0:T(8,128)(2,1)S(1)}, u32[]{:S(2)}, u32[]{:S(2)}) async-start(bf16[12,224,128]{2,1,0:T(8,128)(2,1)} %near.1), calls=%async_computation | async-start | bytes 1376256 | tf_op jit(solution)/shard_map/all_to_all | solution.py:563
  43.5 1.1 %collective-permute-start.5 = (bf16[3,224,128]{2,1,0:T(8,128)(2,1)S(1)}, bf16[3,224,128]{2,1,0:T(8,128)(2,1)S(1)}, u32[]{:S(2)}, u32[]{:S(2)}) collective-permute-start(bf16[3,224,128]{2,1,0:T(8,128)(2,1)S(1)} %get-tuple-element.34), channel_id=1, source_target_pairs={{0,4},{1,5},{2,6},{3,7},{4,0},{5,1},{6,2},{7,3},{8,12},{9,13},{10,... | collective-permute-start | bytes 516104 | tf_op jit(solution)/shard_map/ppermute | solution.py:557
  44.6 3.3 %collective-permute-start.6 = (bf16[3,224,128]{2,1,0:T(8,128)(2,1)S(1)}, bf16[3,224,128]{2,1,0:T(8,128)(2,1)S(1)}, u32[]{:S(2)}, u32[]{:S(2)}) collective-permute-start(bf16[3,224,128]{2,1,0:T(8,128)(2,1)S(1)} %get-tuple-element.35), channel_id=1, source_target_pairs={{0,5},{1,4},{2,7},{3,6},{4,1},{5,0},{6,3},{7,2},{8,13},{9,12},{10,... | collective-permute-start | bytes 516104 | tf_op jit(solution)/shard_map/ppermute | solution.py:557
  47.9 1.1 %collective-permute-start.7 = (bf16[3,224,128]{2,1,0:T(8,128)(2,1)S(1)}, bf16[3,224,128]{2,1,0:T(8,128)(2,1)S(1)}, u32[]{:S(2)}, u32[]{:S(2)}) collective-permute-start(bf16[3,224,128]{2,1,0:T(8,128)(2,1)S(1)} %get-tuple-element.36), channel_id=1, source_target_pairs={{0,6},{1,7},{2,4},{3,5},{4,2},{5,3},{6,0},{7,1},{8,14},{9,15},{10,... | collective-permute-start | bytes 516104 | tf_op jit(solution)/shard_map/ppermute | solution.py:557
  49.0 0.4 collective-permute-start.8
  49.4 8.1 %collective-permute-done.5.refs_0_ = bf16[3,224,128]{2,1,0:T(8,128)(2,1)S(1)} collective-permute-done((bf16[3,224,128]{2,1,0:T(8,128)(2,1)S(1)}, bf16[3,224,128]{2,1,0:T(8,128)(2,1)S(1)}, u32[]{:S(2)}, u32[]{:S(2)}) %collective-permute-start.5) | collective-permute-done | bytes 172064 | tf_op jit(solution)/shard_map/ppermute | solution.py:557
  57.5 10.4 %collective-permute-done.6.refs_1_ = bf16[3,224,128]{2,1,0:T(8,128)(2,1)S(1)} collective-permute-done((bf16[3,224,128]{2,1,0:T(8,128)(2,1)S(1)}, bf16[3,224,128]{2,1,0:T(8,128)(2,1)S(1)}, u32[]{:S(2)}, u32[]{:S(2)}) %collective-permute-start.6) | collective-permute-done | bytes 172064 | tf_op jit(solution)/shard_map/ppermute | solution.py:557
  67.9 3.8 %collective-permute-done.7.refs_2_ = bf16[3,224,128]{2,1,0:T(8,128)(2,1)S(1)} collective-permute-done((bf16[3,224,128]{2,1,0:T(8,128)(2,1)S(1)}, bf16[3,224,128]{2,1,0:T(8,128)(2,1)S(1)}, u32[]{:S(2)}, u32[]{:S(2)}) %collective-permute-start.7) | collective-permute-done | bytes 172064 | tf_op jit(solution)/shard_map/ppermute | solution.py:557
  71.7 2.7 %collective-permute-done.8.refs_3_ = bf16[3,224,128]{2,1,0:T(8,128)(2,1)S(1)} collective-permute-done((bf16[3,224,128]{2,1,0:T(8,128)(2,1)S(1)}, bf16[3,224,128]{2,1,0:T(8,128)(2,1)S(1)}, u32[]{:S(2)}, u32[]{:S(2)}) %collective-permute-start.8) | collective-permute-done | bytes 172064 | tf_op jit(solution)/shard_map/ppermute | solution.py:557
  74.4 0.0 all-to-all-done.near_ref
  74.4 1.9 %placed.1 = bf16[7,24,4096]{2,1,0:T(8,128)(2,1)} custom-call(s32[3]{0:T(128)S(1)} %pad_add_fusion.place_ref, bf16[12,224,128]{2,1,0:T(8,128)(2,1)S(1)} %all-to-all-done.near_ref, bf16[3,224,128]{2,1,0:T(8,128)(2,1)S(1)} %collective-permute-done.5.refs_0_, bf16[3,224,128]{2,1,0:T(8,128)(2,1)S(1)} %collective-permute-done.6.refs_1_, ...), custom_call_target="tpu_custom_call" | custom-call | tf_op jit(solution)/shard_map/placed/pallas_call | solution.py:515
  (5 shorter events, 0.0 us)
Async XLA Ops:
  0.1 11.1 %slice-start = ((s8[4718592]{0:T(1024)(128)(4,1)}), s8[4194304]{0:T(1024)(128)(4,1)S(1)}, s32[]{:S(2)}) async-start(s8[4718592]{0:T(1024)(128)(4,1)} %bitcast.14), calls=%async_computation.1 | async-start | bytes 8388608
  0.1 11.1 %copy-start.3 = (s32[4,6,8]{2,0,1:T(4,128)S(1)}, s32[4,6,8]{2,0,1:T(4,128)}, u32[]{:S(2)}) copy-start(s32[4,6,8]{2,0,1:T(4,128)} %param.9) | copy-start | bytes 2308
  0.1 11.1 %copy-start.2 = (s32[7,4,6,8]{3,1,2,0:T(4,128)S(1)}, s32[7,4,6,8]{3,1,2,0:T(4,128)}, u32[]{:S(2)}) copy-start(s32[7,4,6,8]{3,1,2,0:T(4,128)} %param.10) | copy-start | bytes 16132
  0.1 11.1 %slice-start.1 = ((s8[4718592]{0:T(1024)(128)(4,1)}), s8[524288]{0:T(1024)(128)(4,1)S(1)}, s32[]{:S(2)}) async-start(s8[4718592]{0:T(1024)(128)(4,1)} %bitcast.14), calls=%async_computation.2 | async-start | bytes 1048576
  0.1 11.1 %copy-start = (bf16[4,6,8,4096]{3,2,1,0:T(8,128)(2,1)S(1)}, bf16[4,6,8,4096]{3,2,1,0:T(8,128)(2,1)}, u32[]{:S(2)}) copy-start(bf16[4,6,8,4096]{3,2,1,0:T(8,128)(2,1)} %param.6) | copy-start | bytes 4718596
  6.3 19.6 %collective-permute-start.2 = (bf16[12,64,128]{2,1,0:T(8,128)(2,1)S(1)}, bf16[12,64,128]{2,1,0:T(8,128)(2,1)S(1)}, u32[]{:S(2)}, u32[]{:S(2)}) collective-permute-start(bf16[12,64,128]{2,1,0:T(8,128)(2,1)S(1)} %get-tuple-element.23), channel_id=1, source_target_pairs={{0,1},{2,3},{4,5},{6,7},{1,0},{3,2},{5,4},{7,6},{8,9},{10,11},{12,... | collective-permute-start | bytes 589832 | tf_op jit(solution)/shard_map/ppermute | solution.py:21
  7.9 18.0 %collective-permute-start.3 = (bf16[12,64,128]{2,1,0:T(8,128)(2,1)S(1)}, bf16[12,64,128]{2,1,0:T(8,128)(2,1)S(1)}, u32[]{:S(2)}, u32[]{:S(2)}) collective-permute-start(bf16[12,64,128]{2,1,0:T(8,128)(2,1)S(1)} %get-tuple-element.24), channel_id=1, source_target_pairs={{1,2},{3,4},{5,6},{2,1},{4,3},{6,5},{9,10},{11,12},{13,14},{10,9},... | collective-permute-start | bytes 589832 | tf_op jit(solution)/shard_map/ppermute | solution.py:21
  10.2 15.8 %collective-permute-start.1 = (bf16[4,4,64,128]{3,2,1,0:T(8,128)(2,1)S(1)}, bf16[4,4,64,128]{3,2,1,0:T(8,128)(2,1)S(1)}, u32[]{:S(2)}, u32[]{:S(2)}) collective-permute-start(bf16[4,4,64,128]{3,2,1,0:T(8,128)(2,1)S(1)} %get-tuple-element.22), channel_id=1, source_target_pairs={{0,8},{8,0},{1,9},{9,1},{2,10},{10,2},{3,11},{11,3},{4,12},{12,4},... | collective-permute-start | bytes 786440 | tf_op jit(solution)/shard_map/ppermute | solution.py:21
  11.1 14.8 %collective-permute-start = (bf16[6,4,64,128]{3,2,1,0:T(8,128)(2,1)S(1)}, bf16[6,4,64,128]{3,2,1,0:T(8,128)(2,1)S(1)}, u32[]{:S(2)}, u32[]{:S(2)}) collective-permute-start(bf16[6,4,64,128]{3,2,1,0:T(8,128)(2,1)S(1)} %get-tuple-element.21), channel_id=1, source_target_pairs={{0,16},{16,0},{1,17},{17,1},{2,18},{18,2},{3,19},{19,3},{4,20},{20... | collective-permute-start | bytes 1179656 | tf_op jit(solution)/shard_map/ppermute | solution.py:21
  11.2 14.7 %copy-start.1 = (s32[24]{0:T(128)S(1)}, s32[24]{0:T(128)}, u32[]{:S(2)}) copy-start(s32[24]{0:T(128)} %owners.3) | copy-start | bytes 292
  33.8 4.3 %collective-permute-start.4 = (bf16[1,32,128]{2,1,0:T(8,128)(2,1)S(1)}, bf16[1,32,128]{2,1,0:T(8,128)(2,1)S(1)}, u32[]{:S(2)}, u32[]{:S(2)}) collective-permute-start(bf16[1,32,128]{2,1,0:T(8,128)(2,1)S(1)} %slice.3), channel_id=1, source_target_pairs={{0,1},{1,0},{2,3},{3,2},{4,5},{5,4},{6,7},{7,6},{8,9},{9,8},{10,11... | collective-permute-start | bytes 24584 | tf_op jit(solution)/shard_map/ppermute | solution.py:557
  40.0 34.4 %all-to-all-start = ((bf16[12,224,128]{2,1,0:T(8,128)(2,1)}), bf16[12,224,128]{2,1,0:T(8,128)(2,1)S(1)}, u32[]{:S(2)}, u32[]{:S(2)}) async-start(bf16[12,224,128]{2,1,0:T(8,128)(2,1)} %near.1), calls=%async_computation | async-start | bytes 1376256 | tf_op jit(solution)/shard_map/all_to_all | solution.py:563
  43.5 14.0 %collective-permute-start.5 = (bf16[3,224,128]{2,1,0:T(8,128)(2,1)S(1)}, bf16[3,224,128]{2,1,0:T(8,128)(2,1)S(1)}, u32[]{:S(2)}, u32[]{:S(2)}) collective-permute-start(bf16[3,224,128]{2,1,0:T(8,128)(2,1)S(1)} %get-tuple-element.34), channel_id=1, source_target_pairs={{0,4},{1,5},{2,6},{3,7},{4,0},{5,1},{6,2},{7,3},{8,12},{9,13},{10,... | collective-permute-start | bytes 516104 | tf_op jit(solution)/shard_map/ppermute | solution.py:557
  44.6 23.3 %collective-permute-start.6 = (bf16[3,224,128]{2,1,0:T(8,128)(2,1)S(1)}, bf16[3,224,128]{2,1,0:T(8,128)(2,1)S(1)}, u32[]{:S(2)}, u32[]{:S(2)}) collective-permute-start(bf16[3,224,128]{2,1,0:T(8,128)(2,1)S(1)} %get-tuple-element.35), channel_id=1, source_target_pairs={{0,5},{1,4},{2,7},{3,6},{4,1},{5,0},{6,3},{7,2},{8,13},{9,12},{10,... | collective-permute-start | bytes 516104 | tf_op jit(solution)/shard_map/ppermute | solution.py:557
  47.9 23.7 %collective-permute-start.7 = (bf16[3,224,128]{2,1,0:T(8,128)(2,1)S(1)}, bf16[3,224,128]{2,1,0:T(8,128)(2,1)S(1)}, u32[]{:S(2)}, u32[]{:S(2)}) collective-permute-start(bf16[3,224,128]{2,1,0:T(8,128)(2,1)S(1)} %get-tuple-element.36), channel_id=1, source_target_pairs={{0,6},{1,7},{2,4},{3,5},{4,2},{5,3},{6,0},{7,1},{8,14},{9,15},{10,... | collective-permute-start | bytes 516104 | tf_op jit(solution)/shard_map/ppermute | solution.py:557
  49.0 25.4 %collective-permute-start.8 = (bf16[3,224,128]{2,1,0:T(8,128)(2,1)S(1)}, bf16[3,224,128]{2,1,0:T(8,128)(2,1)S(1)}, u32[]{:S(2)}, u32[]{:S(2)}) collective-permute-start(bf16[3,224,128]{2,1,0:T(8,128)(2,1)S(1)} %get-tuple-element.33), channel_id=1, source_target_pairs={{0,7},{1,6},{2,5},{3,4},{4,3},{5,2},{6,1},{7,0},{8,15},{9,14},{10,... | collective-permute-start | bytes 516104 | tf_op jit(solution)/shard_map/ppermute | solution.py:557

commit v14 on v13

--- a/solution.py
+++ b/solution.py
@@ -386,9 +386,14 @@
 
     list_rows(capacity, paired, owners, place_ref, rows // SLOTS, filled, listed)
     full = capacity * filled.shape[0] * SLOTS == rows
-    for part, out_ref in enumerate(out_refs):
+    far_refs = out_refs[1:] if first_part else out_refs
+    for part, out_ref in enumerate(far_refs):
         for q in range(capacity):
             write_row(total, listed[(first_part + part) * capacity + q], full, out_ref, q)
+    for member in range(first_part):
+        partner = jnp.bitwise_xor(member, place_ref[2] % first_part)
+        for q in range(capacity):
+            write_row(total, listed[partner * capacity + q], full, out_refs[0], member * capacity + q)
 
 
 def list_rows(capacity, paired, owners, place_ref, rows, filled, listed):
@@ -413,29 +418,6 @@
         out_ref[spot, HALF * s : HALF * (s + 1), :] = block.astype(jnp.bfloat16)
 
 
-def near_kernel(capacity, owners, place_ref, total, arrived, out_ref, filled, listed):
-    count = out_ref.shape[0] // capacity
-    list_rows(capacity, True, owners, place_ref, total.shape[0] // SLOTS, filled, listed)
-    for member in range(count):
-        partner = jnp.bitwise_xor(member, place_ref[2] % count)
-        for q in range(capacity):
-            write_row(total, listed[partner * capacity + q], True, out_ref, member * capacity + q)
-
-
-def near_parts(owners, place, total, arrived, capacity, count, devices):
-    smem = pl.BlockSpec(memory_space=pltpu.SMEM)
-    whole = pl.BlockSpec(memory_space=pltpu.VMEM)
-    return pl.pallas_call(
-        functools.partial(near_kernel, capacity),
-        in_specs=[smem, smem, whole, pl.BlockSpec(memory_space=pl.ANY)],
-        out_specs=whole,
-        out_shape=jax.ShapeDtypeStruct((count * capacity, SLOTS * HALF, LANES), jnp.bfloat16),
-        scratch_shapes=[pltpu.SMEM((devices,), jnp.int32), pltpu.SMEM((capacity * devices,), jnp.int32)],
-        compiler_params=pltpu.CompilerParams(vmem_limit_bytes=10 * MIB),
-        name="near",
-    )(owners, place, total, arrived)
-
-
 def border(owners, place, keys, operands, turned, natural, ends, total, capacity, devices, paired, first_part, sizes):
     size_x, size_y, depth = sizes
     pairs = depth // 2
@@ -443,7 +425,8 @@
     whole = pl.BlockSpec(memory_space=pltpu.VMEM)
     planes = lambda array: array.reshape((size_x, size_y) + array.shape[1:])
     before = 3 + len(operands) + 4 + len(ends)
-    count = devices - first_part
+    heights = ([first_part * capacity] if first_part else []) + [capacity] * (devices - first_part)
+    count = len(heights)
     return pl.pallas_call(
         functools.partial(border_kernel, capacity, paired, first_part),
         grid=(1,),
@@ -454,7 +437,7 @@
             pl.BlockSpec((size_x, 1, pairs, NODES, LANES), lambda i: (0, 0, 0, 0, 0)),
         ] + [whole] * (len(ends) + 1),
         out_specs=[whole] * (count + 1),
-        out_shape=[jax.ShapeDtypeStruct((capacity, SLOTS * HALF, LANES), jnp.bfloat16)] * count
+        out_shape=[jax.ShapeDtypeStruct((height, SLOTS * HALF, LANES), jnp.bfloat16) for height in heights]
         + [jax.ShapeDtypeStruct(total.shape, total.dtype)],
         input_output_aliases={before: count},
         scratch_shapes=[pltpu.SMEM((devices,), jnp.int32), pltpu.SMEM((capacity * devices,), jnp.int32)],
@@ -549,16 +532,15 @@
     total = interior(keys, diag, faces, natural, turned, sizes)
     paired = holding == AGG_DEV and depth & (depth - 1) == 0
     first_part = depth // 2 if paired else 0
-    *outgoing, total = border(
+    *outgoing, _ = border(
         row_owner, place, keys, (got_x, got_y, near_z, far_z, tail_x, tail_y, tail_z), turned, natural,
         (first_z, last_z), total, capacity, depth, paired, first_part, sizes)
     if paired:
         def swapped_with(part, k):
             return lax.ppermute(part, "gz", [(i, i ^ k) for i in range(depth)])
 
-        far = [swapped_with(part, first_part + k) for k, part in enumerate(outgoing)]
-        gate = swapped_with(outgoing[-1][:1, :HALF], 1)
-        near = near_parts(row_owner, place, total, gate, capacity, first_part, depth)
+        near, *far = outgoing
+        far = [swapped_with(part, first_part + k) for k, part in enumerate(far)]
         sides = [list(range(first, first + first_part)) for first in (0, first_part)]
         near = lax.all_to_all(near, "gz", 0, 0, tiled=True, axis_index_groups=sides)
         result = placed(place, near, far, block)

time: 76.7 us -> 72.8 us (0.949)
  the two profiles are of different devices: /device:TPU:16 before, /device:TPU:12 now
where the time goes in v14:
time: 72.8 us; the launch traced here: 72.6 us
  Pallas kernels  31.7 us (44%)
  waiting for transfers between devices  24.5 us (34%)
  starting transfers between devices  16 us (22%)
    ppermute x4, waiting for transfers between devices, swapped_with(): return lax.ppermute(part, 'gz', [(i, i ^ k) for i in range(depth)])  24.5 us
    pallas_call x1, Pallas kernels, interior(): pl.pallas_call(interior_kernel, in_specs=[pl.BlockSpec(memory_space=pltpu...  14.7 us
    pallas_call x1, Pallas kernels, border(): pl.pallas_call(functools.partial(border_kernel, capacity, paired, first_p...  8.87 us
    pallas_call x1, Pallas kernels, prepare(): pl.pallas_call(prepare_kernel, grid=(size_x,), in_specs=[pl.BlockSpec(mem...  6.21 us
    ppermute x4, starting transfers between devices, swapped_along(): return lax.ppermute(block, axis, pairs + [(i + 1, i) for i, _ in pairs])  5.95 us
    ppermute x4, starting transfers between devices, swapped_with(): return lax.ppermute(part, 'gz', [(i, i ^ k) for i in range(depth)])  5.85 us
    all_to_all x1, starting transfers between devices, shards(): near = lax.all_to_all(near, 'gz', 0, 0, tiled=True, axis_index_groups=sides)  4.19 us
    pallas_call x1, Pallas kernels, placed(): pl.pallas_call(functools.partial(placed_kernel, capacity), in_specs=[pl.B...  1.93 us
  transfers between devices with their start and end apart: 9, of which 4 were waited for; matrix products, arithmetic and copies ran while one was open for 0% of the time, Pallas kernels for 20%

profile of v14, /device:TPU:12, one launch (start us, length us, event | category | flops | bytes accessed | tf_op | source)
XLA Modules:
  0.0 72.6 jit_solution(6756619363933994499)
XLA Ops:
  0.0 0.1 pad_add_fusion.place_ref
  0.1 0.0 slice-start
  0.1 0.0 copy-start.3
  0.1 0.0 copy-start.2
  0.1 0.0 slice-start.1
  0.1 0.0 copy-start
  0.1 6.2 %prepare.1 = (bf16[24,4,64,128]{3,2,1,0:T(8,128)(2,1)S(1)}, bf16[24,2,128,128]{3,2,1,0:T(8,128)(2,1)S(1)}, bf16[6,4,64,128]{3,2,1,0:T(8,128)(2,1)S(1)}, bf16[4,4...) custom-call(s32[3]{0:T(128)S(1)} %pad_add_fusion.place_ref, ...), custom_call_target="tpu_custom_call" | custom-call | tf_op jit(solution)/shard_map/prepare/pallas_call | solution.py:179
  6.3 0.6 collective-permute-start.2
  6.9 4.4 %collective-permute-start.3 = (bf16[12,64,128]{2,1,0:T(8,128)(2,1)S(1)}, bf16[12,64,128]{2,1,0:T(8,128)(2,1)S(1)}, u32[]{:S(2)}, u32[]{:S(2)}) collective-permute-start(bf16[12,64,128]{2,1,0:T(8,128)(2,1)S(1)} %get-tuple-element.24), channel_id=1, source_target_pairs={{1,2},{3,4},{5,6},{2,1},{4,3},{6,5},{9,10},{11,12},{13,14},{10,9},... | collective-permute-start | bytes 589832 | tf_op jit(solution)/shard_map/ppermute | solution.py:21
  11.3 0.9 %collective-permute-start.1 = (bf16[4,4,64,128]{3,2,1,0:T(8,128)(2,1)S(1)}, bf16[4,4,64,128]{3,2,1,0:T(8,128)(2,1)S(1)}, u32[]{:S(2)}, u32[]{:S(2)}) collective-permute-start(bf16[4,4,64,128]{3,2,1,0:T(8,128)(2,1)S(1)} %get-tuple-element.22), channel_id=1, source_target_pairs={{0,8},{8,0},{1,9},{9,1},{2,10},{10,2},{3,11},{11,3},{4,12},{12,4},... | collective-permute-start | bytes 786440 | tf_op jit(solution)/shard_map/ppermute | solution.py:21
  12.3 0.0 collective-permute-start
  12.3 0.0 copy-done.3
  12.3 0.0 copy-done.2
  12.3 0.0 slice-done
  12.3 0.0 slice-done.1
  12.4 0.0 copy-done
  12.4 0.0 copy-start.1
  12.4 14.7 %interior.1.start_ref = f32[168,32,128]{2,1,0:T(8,128)S(1)} custom-call(s32[7,4,6,8]{3,2,1,0:T(8,128)S(1)} %copy_add_fusion.keys, bf16[24,8,4096]{2,1,0:T(8,128)(2,1)S(1)} %bitcast.19, bf16[3,24,8,4096]{3,2,1,0:T(8,128)(2,1)S(1)} %bitcast.16, bf16[24,4,64,128]{3,2,1,0:T(8,128)(2,1)S(1)} %get-tuple-element.29.natural_ref.natural_x, ...), custom_call_target="tpu_custom_call" | custom-call | flops 704643072 | bytes 9437184 | tf_op jit(solution)/shard_map/interior/pallas_call | solution.py:309
  27.1 0.0 collective-permute-done.2.near_z
  27.1 0.0 collective-permute-done.3.far_z
  27.1 0.0 collective-permute-done.1.got_y
  27.1 0.0 collective-permute-done.got_x
  27.1 0.0 copy-done.1
  27.1 8.9 %border.1 = (bf16[12,224,128]{2,1,0:T(8,128)(2,1)}, bf16[3,224,128]{2,1,0:T(8,128)(2,1)S(1)}, bf16[3,224,128]{2,1,0:T(8,128)(2,1)S(1)}, bf16[3,224,128]{2,1,0:T(...) custom-call(s32[24]{0:T(128)S(1)} %copy-done.1, ...), custom_call_target="tpu_custom_call", output_to_operand_aliasing={{5}: (16, {})} | custom-call | tf_op jit(solution)/shard_map/border/pallas_call | solution.py:430
  36.0 4.2 %all-to-all-start = ((bf16[12,224,128]{2,1,0:T(8,128)(2,1)}), bf16[12,224,128]{2,1,0:T(8,128)(2,1)S(1)}, u32[]{:S(2)}, u32[]{:S(2)}) async-start(bf16[12,224,128]{2,1,0:T(8,128)(2,1)} %get-tuple-element.32), calls=%async_computation | async-start | bytes 1376256 | tf_op jit(solution)/shard_map/all_to_all | solution.py:545
  40.2 1.6 %collective-permute-start.4 = (bf16[3,224,128]{2,1,0:T(8,128)(2,1)S(1)}, bf16[3,224,128]{2,1,0:T(8,128)(2,1)S(1)}, u32[]{:S(2)}, u32[]{:S(2)}) collective-permute-start(bf16[3,224,128]{2,1,0:T(8,128)(2,1)S(1)} %get-tuple-element.33), channel_id=1, source_target_pairs={{0,4},{1,5},{2,6},{3,7},{4,0},{5,1},{6,2},{7,3},{8,12},{9,13},{10,... | collective-permute-start | bytes 516104 | tf_op jit(solution)/shard_map/ppermute | solution.py:540
  41.8 1.3 %collective-permute-start.5 = (bf16[3,224,128]{2,1,0:T(8,128)(2,1)S(1)}, bf16[3,224,128]{2,1,0:T(8,128)(2,1)S(1)}, u32[]{:S(2)}, u32[]{:S(2)}) collective-permute-start(bf16[3,224,128]{2,1,0:T(8,128)(2,1)S(1)} %get-tuple-element.34), channel_id=1, source_target_pairs={{0,5},{1,4},{2,7},{3,6},{4,1},{5,0},{6,3},{7,2},{8,13},{9,12},{10,... | collective-permute-start | bytes 516104 | tf_op jit(solution)/shard_map/ppermute | solution.py:540
  43.1 0.1 collective-permute-start.6
  43.2 2.8 %collective-permute-start.7 = (bf16[3,224,128]{2,1,0:T(8,128)(2,1)S(1)}, bf16[3,224,128]{2,1,0:T(8,128)(2,1)S(1)}, u32[]{:S(2)}, u32[]{:S(2)}) collective-permute-start(bf16[3,224,128]{2,1,0:T(8,128)(2,1)S(1)} %get-tuple-element.36), channel_id=1, source_target_pairs={{0,7},{1,6},{2,5},{3,4},{4,3},{5,2},{6,1},{7,0},{8,15},{9,14},{10,... | collective-permute-start | bytes 516104 | tf_op jit(solution)/shard_map/ppermute | solution.py:540
  46.0 14.5 %collective-permute-done.4.refs_0_ = bf16[3,224,128]{2,1,0:T(8,128)(2,1)S(1)} collective-permute-done((bf16[3,224,128]{2,1,0:T(8,128)(2,1)S(1)}, bf16[3,224,128]{2,1,0:T(8,128)(2,1)S(1)}, u32[]{:S(2)}, u32[]{:S(2)}) %collective-permute-start.4) | collective-permute-done | bytes 172064 | tf_op jit(solution)/shard_map/ppermute | solution.py:540
  60.6 3.8 %collective-permute-done.5.refs_1_ = bf16[3,224,128]{2,1,0:T(8,128)(2,1)S(1)} collective-permute-done((bf16[3,224,128]{2,1,0:T(8,128)(2,1)S(1)}, bf16[3,224,128]{2,1,0:T(8,128)(2,1)S(1)}, u32[]{:S(2)}, u32[]{:S(2)}) %collective-permute-start.5) | collective-permute-done | bytes 172064 | tf_op jit(solution)/shard_map/ppermute | solution.py:540
  64.4 3.1 %collective-permute-done.6.refs_2_ = bf16[3,224,128]{2,1,0:T(8,128)(2,1)S(1)} collective-permute-done((bf16[3,224,128]{2,1,0:T(8,128)(2,1)S(1)}, bf16[3,224,128]{2,1,0:T(8,128)(2,1)S(1)}, u32[]{:S(2)}, u32[]{:S(2)}) %collective-permute-start.6) | collective-permute-done | bytes 172064 | tf_op jit(solution)/shard_map/ppermute | solution.py:540
  67.5 3.0 %collective-permute-done.7.refs_3_ = bf16[3,224,128]{2,1,0:T(8,128)(2,1)S(1)} collective-permute-done((bf16[3,224,128]{2,1,0:T(8,128)(2,1)S(1)}, bf16[3,224,128]{2,1,0:T(8,128)(2,1)S(1)}, u32[]{:S(2)}, u32[]{:S(2)}) %collective-permute-start.7) | collective-permute-done | bytes 172064 | tf_op jit(solution)/shard_map/ppermute | solution.py:540
  70.5 0.0 all-to-all-done.near_ref
  70.5 1.9 %placed.1 = bf16[7,24,4096]{2,1,0:T(8,128)(2,1)} custom-call(s32[3]{0:T(128)S(1)} %pad_add_fusion.place_ref, bf16[12,224,128]{2,1,0:T(8,128)(2,1)S(1)} %all-to-all-done.near_ref, bf16[3,224,128]{2,1,0:T(8,128)(2,1)S(1)} %collective-permute-done.4.refs_0_, bf16[3,224,128]{2,1,0:T(8,128)(2,1)S(1)} %collective-permute-done.5.refs_1_, ...), custom_call_target="tpu_custom_call" | custom-call | tf_op jit(solution)/shard_map/placed/pallas_call | solution.py:498
  (4 shorter events, 0.0 us)
Async XLA Ops:
  0.1 12.3 %slice-start = ((s8[4718592]{0:T(1024)(128)(4,1)}), s8[4194304]{0:T(1024)(128)(4,1)S(1)}, s32[]{:S(2)}) async-start(s8[4718592]{0:T(1024)(128)(4,1)} %bitcast.14), calls=%async_computation.1 | async-start | bytes 8388608
  0.1 12.2 %copy-start.3 = (s32[4,6,8]{2,0,1:T(4,128)S(1)}, s32[4,6,8]{2,0,1:T(4,128)}, u32[]{:S(2)}) copy-start(s32[4,6,8]{2,0,1:T(4,128)} %param.9) | copy-start | bytes 2308
  0.1 12.2 %copy-start.2 = (s32[7,4,6,8]{3,1,2,0:T(4,128)S(1)}, s32[7,4,6,8]{3,1,2,0:T(4,128)}, u32[]{:S(2)}) copy-start(s32[7,4,6,8]{3,1,2,0:T(4,128)} %param.10) | copy-start | bytes 16132
  0.1 12.3 %slice-start.1 = ((s8[4718592]{0:T(1024)(128)(4,1)}), s8[524288]{0:T(1024)(128)(4,1)S(1)}, s32[]{:S(2)}) async-start(s8[4718592]{0:T(1024)(128)(4,1)} %bitcast.14), calls=%async_computation.2 | async-start | bytes 1048576
  0.1 12.3 %copy-start = (bf16[4,6,8,4096]{3,2,1,0:T(8,128)(2,1)S(1)}, bf16[4,6,8,4096]{3,2,1,0:T(8,128)(2,1)}, u32[]{:S(2)}) copy-start(bf16[4,6,8,4096]{3,2,1,0:T(8,128)(2,1)} %param.6) | copy-start | bytes 4718596
  6.3 20.7 %collective-permute-start.2 = (bf16[12,64,128]{2,1,0:T(8,128)(2,1)S(1)}, bf16[12,64,128]{2,1,0:T(8,128)(2,1)S(1)}, u32[]{:S(2)}, u32[]{:S(2)}) collective-permute-start(bf16[12,64,128]{2,1,0:T(8,128)(2,1)S(1)} %get-tuple-element.23), channel_id=1, source_target_pairs={{0,1},{2,3},{4,5},{6,7},{1,0},{3,2},{5,4},{7,6},{8,9},{10,11},{12,... | collective-permute-start | bytes 589832 | tf_op jit(solution)/shard_map/ppermute | solution.py:21
  6.9 20.2 %collective-permute-start.3 = (bf16[12,64,128]{2,1,0:T(8,128)(2,1)S(1)}, bf16[12,64,128]{2,1,0:T(8,128)(2,1)S(1)}, u32[]{:S(2)}, u32[]{:S(2)}) collective-permute-start(bf16[12,64,128]{2,1,0:T(8,128)(2,1)S(1)} %get-tuple-element.24), channel_id=1, source_target_pairs={{1,2},{3,4},{5,6},{2,1},{4,3},{6,5},{9,10},{11,12},{13,14},{10,9},... | collective-permute-start | bytes 589832 | tf_op jit(solution)/shard_map/ppermute | solution.py:21
  11.3 15.7 %collective-permute-start.1 = (bf16[4,4,64,128]{3,2,1,0:T(8,128)(2,1)S(1)}, bf16[4,4,64,128]{3,2,1,0:T(8,128)(2,1)S(1)}, u32[]{:S(2)}, u32[]{:S(2)}) collective-permute-start(bf16[4,4,64,128]{3,2,1,0:T(8,128)(2,1)S(1)} %get-tuple-element.22), channel_id=1, source_target_pairs={{0,8},{8,0},{1,9},{9,1},{2,10},{10,2},{3,11},{11,3},{4,12},{12,4},... | collective-permute-start | bytes 786440 | tf_op jit(solution)/shard_map/ppermute | solution.py:21
  12.3 14.8 %collective-permute-start = (bf16[6,4,64,128]{3,2,1,0:T(8,128)(2,1)S(1)}, bf16[6,4,64,128]{3,2,1,0:T(8,128)(2,1)S(1)}, u32[]{:S(2)}, u32[]{:S(2)}) collective-permute-start(bf16[6,4,64,128]{3,2,1,0:T(8,128)(2,1)S(1)} %get-tuple-element.21), channel_id=1, source_target_pairs={{0,16},{16,0},{1,17},{17,1},{2,18},{18,2},{3,19},{19,3},{4,20},{20... | collective-permute-start | bytes 1179656 | tf_op jit(solution)/shard_map/ppermute | solution.py:21
  12.4 14.7 %copy-start.1 = (s32[24]{0:T(128)S(1)}, s32[24]{0:T(128)}, u32[]{:S(2)}) copy-start(s32[24]{0:T(128)} %owners.1) | copy-start | bytes 292
  36.0 34.5 %all-to-all-start = ((bf16[12,224,128]{2,1,0:T(8,128)(2,1)}), bf16[12,224,128]{2,1,0:T(8,128)(2,1)S(1)}, u32[]{:S(2)}, u32[]{:S(2)}) async-start(bf16[12,224,128]{2,1,0:T(8,128)(2,1)} %get-tuple-element.32), calls=%async_computation | async-start | bytes 1376256 | tf_op jit(solution)/shard_map/all_to_all | solution.py:545
  40.2 20.4 %collective-permute-start.4 = (bf16[3,224,128]{2,1,0:T(8,128)(2,1)S(1)}, bf16[3,224,128]{2,1,0:T(8,128)(2,1)S(1)}, u32[]{:S(2)}, u32[]{:S(2)}) collective-permute-start(bf16[3,224,128]{2,1,0:T(8,128)(2,1)S(1)} %get-tuple-element.33), channel_id=1, source_target_pairs={{0,4},{1,5},{2,6},{3,7},{4,0},{5,1},{6,2},{7,3},{8,12},{9,13},{10,... | collective-permute-start | bytes 516104 | tf_op jit(solution)/shard_map/ppermute | solution.py:540
  41.8 22.6 %collective-permute-start.5 = (bf16[3,224,128]{2,1,0:T(8,128)(2,1)S(1)}, bf16[3,224,128]{2,1,0:T(8,128)(2,1)S(1)}, u32[]{:S(2)}, u32[]{:S(2)}) collective-permute-start(bf16[3,224,128]{2,1,0:T(8,128)(2,1)S(1)} %get-tuple-element.34), channel_id=1, source_target_pairs={{0,5},{1,4},{2,7},{3,6},{4,1},{5,0},{6,3},{7,2},{8,13},{9,12},{10,... | collective-permute-start | bytes 516104 | tf_op jit(solution)/shard_map/ppermute | solution.py:540
  43.1 24.4 %collective-permute-start.6 = (bf16[3,224,128]{2,1,0:T(8,128)(2,1)S(1)}, bf16[3,224,128]{2,1,0:T(8,128)(2,1)S(1)}, u32[]{:S(2)}, u32[]{:S(2)}) collective-permute-start(bf16[3,224,128]{2,1,0:T(8,128)(2,1)S(1)} %get-tuple-element.35), channel_id=1, source_target_pairs={{0,6},{1,7},{2,4},{3,5},{4,2},{5,3},{6,0},{7,1},{8,14},{9,15},{10,... | collective-permute-start | bytes 516104 | tf_op jit(solution)/shard_map/ppermute | solution.py:540
  43.2 27.3 %collective-permute-start.7 = (bf16[3,224,128]{2,1,0:T(8,128)(2,1)S(1)}, bf16[3,224,128]{2,1,0:T(8,128)(2,1)S(1)}, u32[]{:S(2)}, u32[]{:S(2)}) collective-permute-start(bf16[3,224,128]{2,1,0:T(8,128)(2,1)S(1)} %get-tuple-element.36), channel_id=1, source_target_pairs={{0,7},{1,6},{2,5},{3,4},{4,3},{5,2},{6,1},{7,0},{8,15},{9,14},{10,... | collective-permute-start | bytes 516104 | tf_op jit(solution)/shard_map/ppermute | solution.py:540

commit v15 on v12

--- a/solution.py
+++ b/solution.py
@@ -314,7 +314,7 @@
         scratch_shapes=[
             pltpu.VMEM((size_y, 4, depth * HALF, LANES), jnp.float32),
             total, total, total, total,
-            pltpu.VMEM((12, LANES, LANES), jnp.float32),
+            pltpu.VMEM((28, LANES, LANES), jnp.float32),
         ],
         compiler_params=pltpu.CompilerParams(vmem_limit_bytes=28 * MIB),
         cost_estimate=pl.CostEstimate(flops=columns * depth * 14 * NODES**3, bytes_accessed=columns * depth * 6 * block * 2, transcendentals=0),

time: 70.4 us -> 69.7 us (0.990)
    pallas_call x1, Pallas kernels: 14.7 us -> 13.9 us  [interior(): pl.pallas_call(interior_kernel, in_specs=[pl.BlockSpec(memory_space=pltpu...]
  transfers between devices with their start and end apart: 12 -> 12, of which waited for: 4 -> 4; matrix products, arithmetic and copies ran while one was open for 0% -> 0% of each run, Pallas kernels for 22% -> 21%
where the time goes in v15:
time: 69.7 us; the launch traced here: 69.5 us
  Pallas kernels  30.9 us (44%)
  waiting for transfers between devices  21.3 us (31%)
  starting transfers between devices  16.9 us (24%)
    ppermute x8, waiting for transfers between devices, swapped_with(): lax.ppermute(part, 'gz', [(i, i ^ k) for i in range(depth)])  21.3 us
    pallas_call x1, Pallas kernels, interior(): pl.pallas_call(interior_kernel, in_specs=[pl.BlockSpec(memory_space=pltpu...  13.9 us
    ppermute x8, starting transfers between devices, swapped_with(): lax.ppermute(part, 'gz', [(i, i ^ k) for i in range(depth)])  12.3 us
    pallas_call x1, Pallas kernels, border(): pl.pallas_call(functools.partial(border_kernel, capacity, paired, first_p...  7.84 us
    pallas_call x1, Pallas kernels, prepare(): pl.pallas_call(prepare_kernel, grid=(size_x,), in_specs=[pl.BlockSpec(mem...  6.21 us
    ppermute x4, starting transfers between devices, swapped_along(): return lax.ppermute(block, axis, pairs + [(i + 1, i) for i, _ in pairs])  4.64 us
    pallas_call x1, Pallas kernels, placed(): pl.pallas_call(placed_kernel, in_specs=[pl.BlockSpec(memory_space=pltpu.S...  1.94 us
  transfers between devices with their start and end apart: 12, of which 4 were waited for; matrix products, arithmetic and copies ran while one was open for 0% of the time, Pallas kernels for 21%

profile of v15, /device:TPU:0, one launch (start us, length us, event | category | flops | bytes accessed | tf_op | source)
XLA Modules:
  0.0 69.5 jit_solution(2141711721477150905)
XLA Ops:
  0.0 0.1 pad_add_fusion.place_ref
  0.1 0.0 slice-start
  0.1 0.0 copy-start.3
  0.1 0.0 copy-start.2
  0.1 0.0 slice-start.1
  0.1 0.0 copy-start
  0.1 6.2 %prepare.1 = (bf16[24,4,64,128]{3,2,1,0:T(8,128)(2,1)S(1)}, bf16[24,2,128,128]{3,2,1,0:T(8,128)(2,1)S(1)}, bf16[6,4,64,128]{3,2,1,0:T(8,128)(2,1)S(1)}, bf16[4,4...) custom-call(s32[3]{0:T(128)S(1)} %pad_add_fusion.place_ref, ...), custom_call_target="tpu_custom_call" | custom-call | tf_op jit(solution)/shard_map/prepare/pallas_call | solution.py:179
  6.3 3.0 %collective-permute-start.2 = (bf16[12,64,128]{2,1,0:T(8,128)(2,1)S(1)}, bf16[12,64,128]{2,1,0:T(8,128)(2,1)S(1)}, u32[]{:S(2)}, u32[]{:S(2)}) collective-permute-start(bf16[12,64,128]{2,1,0:T(8,128)(2,1)S(1)} %get-tuple-element.27), channel_id=1, source_target_pairs={{0,1},{2,3},{4,5},{6,7},{1,0},{3,2},{5,4},{7,6},{8,9},{10,11},{12,... | collective-permute-start | bytes 589832 | tf_op jit(solution)/shard_map/ppermute | solution.py:21
  9.4 0.7 collective-permute-start.3
  10.0 0.9 %collective-permute-start.1 = (bf16[4,4,64,128]{3,2,1,0:T(8,128)(2,1)S(1)}, bf16[4,4,64,128]{3,2,1,0:T(8,128)(2,1)S(1)}, u32[]{:S(2)}, u32[]{:S(2)}) collective-permute-start(bf16[4,4,64,128]{3,2,1,0:T(8,128)(2,1)S(1)} %get-tuple-element.26), channel_id=1, source_target_pairs={{0,8},{8,0},{1,9},{9,1},{2,10},{10,2},{3,11},{11,3},{4,12},{12,4},... | collective-permute-start | bytes 786440 | tf_op jit(solution)/shard_map/ppermute | solution.py:21
  11.0 0.0 collective-permute-start
  11.0 0.0 copy-done.3
  11.0 0.0 copy-done.2
  11.0 0.0 slice-done
  11.0 0.0 slice-done.1
  11.0 0.0 copy-done
  11.1 0.0 copy-start.1
  11.1 13.9 %interior.1.start_ref = f32[168,32,128]{2,1,0:T(8,128)S(1)} custom-call(s32[7,4,6,8]{3,2,1,0:T(8,128)S(1)} %copy_add_fusion.keys, bf16[24,8,4096]{2,1,0:T(8,128)(2,1)S(1)} %bitcast.19, bf16[3,24,8,4096]{3,2,1,0:T(8,128)(2,1)S(1)} %bitcast.16, bf16[24,4,64,128]{3,2,1,0:T(8,128)(2,1)S(1)} %get-tuple-element.33.natural_ref.natural_x, ...), custom_call_target="tpu_custom_call" | custom-call | flops 704643072 | bytes 9437184 | tf_op jit(solution)/shard_map/interior/pallas_call | solution.py:309
  25.0 0.0 collective-permute-done.2.near_z
  25.0 0.0 collective-permute-done.3.far_z
  25.0 0.0 collective-permute-done.1.got_y
  25.0 0.0 collective-permute-done.got_x
  25.0 0.0 copy-done.1
  25.1 7.8 %border.1 = (bf16[3,224,128]{2,1,0:T(8,128)(2,1)S(1)}, bf16[3,224,128]{2,1,0:T(8,128)(2,1)S(1)}, bf16[3,224,128]{2,1,0:T(8,128)(2,1)S(1)}, bf16[3,224,128]{2,1,0:T(8,128)(2,1)S(1)}, f32[168,32,128]{2,1,0:T(8,128)S(1)}) custom-call(s32[24]{0:T(128)S(1)} %copy-done.1, s32[3]{0:T(128)S(1)} %pad_add_fusion.place_ref, ...), custom_call_target="tpu_custom_call", output_to_operand_aliasing={{4}: (16, {})} | custom-call | tf_op jit(solution)/shard_map/border/pallas_call | solution.py:438
  32.9 4.3 %collective-permute-start.8 = (bf16[3,224,128]{2,1,0:T(8,128)(2,1)S(1)}, bf16[3,224,128]{2,1,0:T(8,128)(2,1)S(1)}, u32[]{:S(2)}, u32[]{:S(2)}) collective-permute-start(bf16[3,224,128]{2,1,0:T(8,128)(2,1)S(1)} %get-tuple-element.42), channel_id=1, source_target_pairs={{0,4},{1,5},{2,6},{3,7},{4,0},{5,1},{6,2},{7,3},{8,12},{9,13},{10,... | collective-permute-start | bytes 516104 | tf_op jit(solution)/shard_map/ppermute | solution.py:545
  37.2 2.4 %collective-permute-start.9 = (bf16[3,224,128]{2,1,0:T(8,128)(2,1)S(1)}, bf16[3,224,128]{2,1,0:T(8,128)(2,1)S(1)}, u32[]{:S(2)}, u32[]{:S(2)}) collective-permute-start(bf16[3,224,128]{2,1,0:T(8,128)(2,1)S(1)} %get-tuple-element.43), channel_id=1, source_target_pairs={{0,5},{1,4},{2,7},{3,6},{4,1},{5,0},{6,3},{7,2},{8,13},{9,12},{10,... | collective-permute-start | bytes 516104 | tf_op jit(solution)/shard_map/ppermute | solution.py:545
  39.6 0.2 collective-permute-start.4
  39.8 2.3 %collective-permute-start.11 = (bf16[3,224,128]{2,1,0:T(8,128)(2,1)S(1)}, bf16[3,224,128]{2,1,0:T(8,128)(2,1)S(1)}, u32[]{:S(2)}, u32[]{:S(2)}) collective-permute-start(bf16[3,224,128]{2,1,0:T(8,128)(2,1)S(1)} %get-tuple-element.37), channel_id=1, source_target_pairs={{0,7},{1,6},{2,5},{3,4},{4,3},{5,2},{6,1},{7,0},{8,15},{9,14},{10,... | collective-permute-start | bytes 516104 | tf_op jit(solution)/shard_map/ppermute | solution.py:545
  42.2 2.7 %collective-permute-start.10 = (bf16[3,224,128]{2,1,0:T(8,128)(2,1)S(1)}, bf16[3,224,128]{2,1,0:T(8,128)(2,1)S(1)}, u32[]{:S(2)}, u32[]{:S(2)}) collective-permute-start(bf16[3,224,128]{2,1,0:T(8,128)(2,1)S(1)} %get-tuple-element.44), channel_id=1, source_target_pairs={{0,6},{1,7},{2,4},{3,5},{4,2},{5,3},{6,0},{7,1},{8,14},{9,15},{10,... | collective-permute-start | bytes 516104 | tf_op jit(solution)/shard_map/ppermute | solution.py:545
  44.9 0.0 collective-permute-done.4.arrived
  44.9 0.9 %near.1 = (bf16[3,224,128]{2,1,0:T(8,128)(2,1)S(1)}, bf16[3,224,128]{2,1,0:T(8,128)(2,1)S(1)}, bf16[3,224,128]{2,1,0:T(8,128)(2,1)S(1)}, bf16[3,224,128]{2,1,0:T(8,128)(2,1)S(1)}) custom-call(s32[24]{0:T(128)S(1)} %copy-done.1, s32[3]{0:T(128)S(1)} %pad_add_fusion.place_ref, f32[168,32,128]{2,1,0:T(8,128)S(1)} %get-tuple-element.36.total, ...), custom_call_target="tpu_custom_call" | custom-call | tf_op jit(solution)/shard_map/near/pallas_call | solution.py:419
  45.9 0.3 collective-permute-start.5
  46.1 9.2 %collective-permute-done.8.refs_4_ = bf16[3,224,128]{2,1,0:T(8,128)(2,1)S(1)} collective-permute-done((bf16[3,224,128]{2,1,0:T(8,128)(2,1)S(1)}, bf16[3,224,128]{2,1,0:T(8,128)(2,1)S(1)}, u32[]{:S(2)}, u32[]{:S(2)}) %collective-permute-start.8) | collective-permute-done | bytes 172064 | tf_op jit(solution)/shard_map/ppermute | solution.py:545
  55.4 0.0 collective-permute-start.6
  55.4 5.7 %collective-permute-done.9.refs_5_ = bf16[3,224,128]{2,1,0:T(8,128)(2,1)S(1)} collective-permute-done((bf16[3,224,128]{2,1,0:T(8,128)(2,1)S(1)}, bf16[3,224,128]{2,1,0:T(8,128)(2,1)S(1)}, u32[]{:S(2)}, u32[]{:S(2)}) %collective-permute-start.9) | collective-permute-done | bytes 172064 | tf_op jit(solution)/shard_map/ppermute | solution.py:545
  61.1 0.0 collective-permute-start.7
  61.1 0.0 collective-permute-done.10.refs_6_
  61.1 0.0 collective-permute-done.11.refs_7_
  61.1 0.0 collective-permute-done.5.refs_1_
  61.1 1.6 %collective-permute-done.6.refs_2_ = bf16[3,224,128]{2,1,0:T(8,128)(2,1)S(1)} collective-permute-done((bf16[3,224,128]{2,1,0:T(8,128)(2,1)S(1)}, bf16[3,224,128]{2,1,0:T(8,128)(2,1)S(1)}, u32[]{:S(2)}, u32[]{:S(2)}) %collective-permute-start.6) | collective-permute-done | bytes 172064 | tf_op jit(solution)/shard_map/ppermute | solution.py:545
  62.8 4.6 %collective-permute-done.7.refs_3_ = bf16[3,224,128]{2,1,0:T(8,128)(2,1)S(1)} collective-permute-done((bf16[3,224,128]{2,1,0:T(8,128)(2,1)S(1)}, bf16[3,224,128]{2,1,0:T(8,128)(2,1)S(1)}, u32[]{:S(2)}, u32[]{:S(2)}) %collective-permute-start.7) | collective-permute-done | bytes 172064 | tf_op jit(solution)/shard_map/ppermute | solution.py:545
  67.4 1.9 %placed.1 = bf16[7,24,4096]{2,1,0:T(8,128)(2,1)} custom-call(s32[3]{0:T(128)S(1)} %pad_add_fusion.place_ref, bf16[3,224,128]{2,1,0:T(8,128)(2,1)S(1)} %get-tuple-element.38.refs_0_, bf16[3,224,128]{2,1,0:T(8,128)(2,1)S(1)} %collective-permute-done.5.refs_1_, bf16[3,224,128]{2,1,0:T(8,128)(2,1)S(1)} %collective-permute-done.6.refs_2_, ...), custom_call_target="tpu_custom_call" | custom-call | tf_op jit(solution)/shard_map/placed/pallas_call | solution.py:503
  (5 shorter events, 0.0 us)
Async XLA Ops:
  0.1 11.0 %slice-start = ((s8[4718592]{0:T(1024)(128)(4,1)}), s8[4194304]{0:T(1024)(128)(4,1)S(1)}, s32[]{:S(2)}) async-start(s8[4718592]{0:T(1024)(128)(4,1)} %bitcast.14), calls=%async_computation | async-start | bytes 8388608
  0.1 10.9 %copy-start.3 = (s32[4,6,8]{2,0,1:T(4,128)S(1)}, s32[4,6,8]{2,0,1:T(4,128)}, u32[]{:S(2)}) copy-start(s32[4,6,8]{2,0,1:T(4,128)} %param.9) | copy-start | bytes 2308
  0.1 10.9 %copy-start.2 = (s32[7,4,6,8]{3,1,2,0:T(4,128)S(1)}, s32[7,4,6,8]{3,1,2,0:T(4,128)}, u32[]{:S(2)}) copy-start(s32[7,4,6,8]{3,1,2,0:T(4,128)} %param.10) | copy-start | bytes 16132
  0.1 11.0 %slice-start.1 = ((s8[4718592]{0:T(1024)(128)(4,1)}), s8[524288]{0:T(1024)(128)(4,1)S(1)}, s32[]{:S(2)}) async-start(s8[4718592]{0:T(1024)(128)(4,1)} %bitcast.14), calls=%async_computation.1 | async-start | bytes 1048576
  0.1 11.0 %copy-start = (bf16[4,6,8,4096]{3,2,1,0:T(8,128)(2,1)S(1)}, bf16[4,6,8,4096]{3,2,1,0:T(8,128)(2,1)}, u32[]{:S(2)}) copy-start(bf16[4,6,8,4096]{3,2,1,0:T(8,128)(2,1)} %param.6) | copy-start | bytes 4718596
  6.3 18.7 %collective-permute-start.2 = (bf16[12,64,128]{2,1,0:T(8,128)(2,1)S(1)}, bf16[12,64,128]{2,1,0:T(8,128)(2,1)S(1)}, u32[]{:S(2)}, u32[]{:S(2)}) collective-permute-start(bf16[12,64,128]{2,1,0:T(8,128)(2,1)S(1)} %get-tuple-element.27), channel_id=1, source_target_pairs={{0,1},{2,3},{4,5},{6,7},{1,0},{3,2},{5,4},{7,6},{8,9},{10,11},{12,... | collective-permute-start | bytes 589832 | tf_op jit(solution)/shard_map/ppermute | solution.py:21
  9.4 15.7 %collective-permute-start.3 = (bf16[12,64,128]{2,1,0:T(8,128)(2,1)S(1)}, bf16[12,64,128]{2,1,0:T(8,128)(2,1)S(1)}, u32[]{:S(2)}, u32[]{:S(2)}) collective-permute-start(bf16[12,64,128]{2,1,0:T(8,128)(2,1)S(1)} %get-tuple-element.28), channel_id=1, source_target_pairs={{1,2},{3,4},{5,6},{2,1},{4,3},{6,5},{9,10},{11,12},{13,14},{10,9},... | collective-permute-start | bytes 589832 | tf_op jit(solution)/shard_map/ppermute | solution.py:21
  10.0 15.0 %collective-permute-start.1 = (bf16[4,4,64,128]{3,2,1,0:T(8,128)(2,1)S(1)}, bf16[4,4,64,128]{3,2,1,0:T(8,128)(2,1)S(1)}, u32[]{:S(2)}, u32[]{:S(2)}) collective-permute-start(bf16[4,4,64,128]{3,2,1,0:T(8,128)(2,1)S(1)} %get-tuple-element.26), channel_id=1, source_target_pairs={{0,8},{8,0},{1,9},{9,1},{2,10},{10,2},{3,11},{11,3},{4,12},{12,4},... | collective-permute-start | bytes 786440 | tf_op jit(solution)/shard_map/ppermute | solution.py:21
  11.0 14.1 %collective-permute-start = (bf16[6,4,64,128]{3,2,1,0:T(8,128)(2,1)S(1)}, bf16[6,4,64,128]{3,2,1,0:T(8,128)(2,1)S(1)}, u32[]{:S(2)}, u32[]{:S(2)}) collective-permute-start(bf16[6,4,64,128]{3,2,1,0:T(8,128)(2,1)S(1)} %get-tuple-element.25), channel_id=1, source_target_pairs={{0,16},{16,0},{1,17},{17,1},{2,18},{18,2},{3,19},{19,3},{4,20},{20... | collective-permute-start | bytes 1179656 | tf_op jit(solution)/shard_map/ppermute | solution.py:21
  11.1 14.0 %copy-start.1 = (s32[24]{0:T(128)S(1)}, s32[24]{0:T(128)}, u32[]{:S(2)}) copy-start(s32[24]{0:T(128)} %owners.3) | copy-start | bytes 292
  32.9 22.5 %collective-permute-start.8 = (bf16[3,224,128]{2,1,0:T(8,128)(2,1)S(1)}, bf16[3,224,128]{2,1,0:T(8,128)(2,1)S(1)}, u32[]{:S(2)}, u32[]{:S(2)}) collective-permute-start(bf16[3,224,128]{2,1,0:T(8,128)(2,1)S(1)} %get-tuple-element.42), channel_id=1, source_target_pairs={{0,4},{1,5},{2,6},{3,7},{4,0},{5,1},{6,2},{7,3},{8,12},{9,13},{10,... | collective-permute-start | bytes 516104 | tf_op jit(solution)/shard_map/ppermute | solution.py:545
  37.2 23.9 %collective-permute-start.9 = (bf16[3,224,128]{2,1,0:T(8,128)(2,1)S(1)}, bf16[3,224,128]{2,1,0:T(8,128)(2,1)S(1)}, u32[]{:S(2)}, u32[]{:S(2)}) collective-permute-start(bf16[3,224,128]{2,1,0:T(8,128)(2,1)S(1)} %get-tuple-element.43), channel_id=1, source_target_pairs={{0,5},{1,4},{2,7},{3,6},{4,1},{5,0},{6,3},{7,2},{8,13},{9,12},{10,... | collective-permute-start | bytes 516104 | tf_op jit(solution)/shard_map/ppermute | solution.py:545
  39.6 5.3 %collective-permute-start.4 = (bf16[1,32,128]{2,1,0:T(8,128)(2,1)S(1)}, bf16[1,32,128]{2,1,0:T(8,128)(2,1)S(1)}, u32[]{:S(2)}, u32[]{:S(2)}) collective-permute-start(bf16[1,32,128]{2,1,0:T(8,128)(2,1)S(1)} %slice.3), channel_id=1, source_target_pairs={{0,1},{1,0},{2,3},{3,2},{4,5},{5,4},{6,7},{7,6},{8,9},{9,8},{10,11... | collective-permute-start | bytes 24584 | tf_op jit(solution)/shard_map/ppermute | solution.py:545
  39.8 21.3 %collective-permute-start.11 = (bf16[3,224,128]{2,1,0:T(8,128)(2,1)S(1)}, bf16[3,224,128]{2,1,0:T(8,128)(2,1)S(1)}, u32[]{:S(2)}, u32[]{:S(2)}) collective-permute-start(bf16[3,224,128]{2,1,0:T(8,128)(2,1)S(1)} %get-tuple-element.37), channel_id=1, source_target_pairs={{0,7},{1,6},{2,5},{3,4},{4,3},{5,2},{6,1},{7,0},{8,15},{9,14},{10,... | collective-permute-start | bytes 516104 | tf_op jit(solution)/shard_map/ppermute | solution.py:545
  42.2 18.9 %collective-permute-start.10 = (bf16[3,224,128]{2,1,0:T(8,128)(2,1)S(1)}, bf16[3,224,128]{2,1,0:T(8,128)(2,1)S(1)}, u32[]{:S(2)}, u32[]{:S(2)}) collective-permute-start(bf16[3,224,128]{2,1,0:T(8,128)(2,1)S(1)} %get-tuple-element.44), channel_id=1, source_target_pairs={{0,6},{1,7},{2,4},{3,5},{4,2},{5,3},{6,0},{7,1},{8,14},{9,15},{10,... | collective-permute-start | bytes 516104 | tf_op jit(solution)/shard_map/ppermute | solution.py:545
  45.9 15.3 %collective-permute-start.5 = (bf16[3,224,128]{2,1,0:T(8,128)(2,1)S(1)}, bf16[3,224,128]{2,1,0:T(8,128)(2,1)S(1)}, u32[]{:S(2)}, u32[]{:S(2)}) collective-permute-start(bf16[3,224,128]{2,1,0:T(8,128)(2,1)S(1)} %get-tuple-element.39), channel_id=1, source_target_pairs={{0,1},{1,0},{2,3},{3,2},{4,5},{5,4},{6,7},{7,6},{8,9},{9,8},{10,11... | collective-permute-start | bytes 516104 | tf_op jit(solution)/shard_map/ppermute | solution.py:545
  55.4 7.4 %collective-permute-start.6 = (bf16[3,224,128]{2,1,0:T(8,128)(2,1)S(1)}, bf16[3,224,128]{2,1,0:T(8,128)(2,1)S(1)}, u32[]{:S(2)}, u32[]{:S(2)}) collective-permute-start(bf16[3,224,128]{2,1,0:T(8,128)(2,1)S(1)} %get-tuple-element.40), channel_id=1, source_target_pairs={{0,2},{1,3},{2,0},{3,1},{4,6},{5,7},{6,4},{7,5},{8,10},{9,11},{10,... | collective-permute-start | bytes 516104 | tf_op jit(solution)/shard_map/ppermute | solution.py:545
  61.1 6.3 %collective-permute-start.7 = (bf16[3,224,128]{2,1,0:T(8,128)(2,1)S(1)}, bf16[3,224,128]{2,1,0:T(8,128)(2,1)S(1)}, u32[]{:S(2)}, u32[]{:S(2)}) collective-permute-start(bf16[3,224,128]{2,1,0:T(8,128)(2,1)S(1)} %get-tuple-element.41), channel_id=1, source_target_pairs={{0,3},{1,2},{2,1},{3,0},{4,7},{5,6},{6,5},{7,4},{8,11},{9,10},{10,... | collective-permute-start | bytes 516104 | tf_op jit(solution)/shard_map/ppermute | solution.py:545
